TPU v7x, 512 devices: a whole 4x4x16 slice. The times are simulated.
512 devices in a mesh: view: 32 (over z, core), head: 16 (over y, x).
Axes of the slice: x: 4, y: 4, z: 16, core: 2. Of those that a mesh axis runs over, the one named last changes fastest.
Arguments:
- latents: bfloat16 [1024, 32, 1152], P('head', 'view'), may hold values from -6 to 6
- norm_gain: float32 [1152], replicated, may hold values from 0.25 to 1.75
- qkv_weight: bfloat16 [16, 216, 1152], P('head'), may hold values from -2 to 2
- qk_gain: float32 [16, 2, 72], P('head'), may hold values from 0.5 to 6
- out_weight: bfloat16 [16, 72, 1152], P('head'), may hold values from -0.375 to 0.375
- intersection: int32 [3, 32], P(None, 'view'), may hold values from 0 to 1, as said below
Outputs:
- mixed: bfloat16 [1024, 32, 1152], P('head', 'view')
Inputs may be any that keep to these rules, and one draw needn't show every extreme that they name: intersection is symmetric within a round: intersection[r, g] equals intersection[r, partner of g in round r]; views have from 0 to 3 intersecting partners.
All inputs are finite; a program needn't handle non-finite values.
Results may differ from a plain program's by a relative error of at most 0.0065.
The roundings to bfloat16 on the way count: a program that leaves them out, or rounds other values in their place, can miss the bound.
Values may be sent and summed in bfloat16 or wider, within the bound.
No kernel may reach another device: no remote copies, remote signals or barrier semaphores. Data moves between devices by JAX's collectives and lax.ppermute only.
A program may use at most 64 MiB of HBM per device.

v0:
```python
import jax
import jax.numpy as jnp
from jax import lax
from jax.sharding import PartitionSpec as P


def partner(array, axis, bit):
    return lax.ppermute(array, axis, [(i, i ^ 1 << bit) for i in range(lax.axis_size(axis))])


def normalize(latents, norm_gain):
    values = latents.astype(jnp.float32)
    mean = jnp.mean(values, axis=-1, keepdims=True)
    centred = values - mean
    var = jnp.mean(centred * centred, axis=-1, keepdims=True)
    return (centred * lax.rsqrt(var + 1e-06) * norm_gain).astype(jnp.bfloat16)


def rms_scale(part, gain):
    square = jnp.mean(part * part, axis=-1, keepdims=True) + 1e-06
    return (part * lax.rsqrt(square) * gain).astype(jnp.bfloat16)


def absorb(state, query, keys, values, active, scale):
    best, total, acc = state
    scores = jnp.einsum("hqe,hke->hqk", query, keys, preferred_element_type=jnp.float32) * scale
    newbest = jnp.where(active, jnp.maximum(best, jnp.max(scores, axis=-1)), best)
    weights = jnp.where(active, jnp.exp(scores - newbest[..., None]), jnp.float32(0.0))
    factor = jnp.exp(best - newbest)
    total = total * factor + jnp.sum(weights, axis=-1)
    acc = acc * factor[..., None] + jnp.einsum(
        "hqk,hke->hqe", weights.astype(jnp.bfloat16), values, preferred_element_type=jnp.float32
    )
    return (newbest, total, acc)


def finish(state):
    best, total, acc = state
    return acc / jnp.maximum(total, jnp.float32(1.0))[..., None]


def on_device(latents, norm_gain, qkv_weight, qk_gain, out_weight, intersection):
    normed = normalize(latents, norm_gain)
    loc_len, view_dev, width = normed.shape
    local_heads = qkv_weight.shape[0]
    full_weight = lax.all_gather(qkv_weight, "head", axis=0, tiled=True)
    projected = jnp.dot(
        normed.reshape(-1, width),
        full_weight.reshape(-1, width).T,
        preferred_element_type=jnp.float32,
    )
    projected = projected.astype(jnp.bfloat16).reshape(loc_len, view_dev, full_weight.shape[0], -1)
    qkv = lax.all_to_all(projected, "head", split_axis=2, concat_axis=0, tiled=True)
    head_dim = qkv.shape[-1] // 3
    full_len = qkv.shape[0]
    qkv = qkv.transpose(1, 2, 0, 3)
    query = rms_scale(qkv[..., :head_dim].astype(jnp.float32), qk_gain[:, 0][None, :, None, :])
    keys = rms_scale(
        qkv[..., head_dim : 2 * head_dim].astype(jnp.float32), qk_gain[:, 1][None, :, None, :]
    )
    values = qkv[..., 2 * head_dim :]
    scale = float(head_dim) ** (-0.5)
    start = (
        jnp.full((view_dev, local_heads, full_len), -1e30, jnp.float32),
        jnp.zeros((view_dev, local_heads, full_len), jnp.float32),
        jnp.zeros((view_dev, local_heads, full_len, head_dim), jnp.float32),
    )

    def per_view(inputs):
        state, own_query, some_keys, some_values, active = inputs
        return absorb(state, own_query, some_keys, some_values, active, scale)

    own_state = lax.map(per_view, (start, query, keys, values, jnp.ones((view_dev,), jnp.bool_)))
    cross_state = start
    levels = lax.axis_size("view").bit_length() - 1
    rounds = intersection.shape[0]
    for step in range(rounds):
        bit = step * (levels - 1) // (rounds - 1)
        far_keys, far_values = partner((keys, values), "view", bit)
        active = intersection[step] > 0
        cross_state = lax.map(per_view, (cross_state, query, far_keys, far_values, active))
    attended = (finish(own_state) + finish(cross_state)).astype(jnp.bfloat16)
    attended = attended.transpose(2, 0, 1, 3)
    token_rows = lax.all_to_all(attended, "head", split_axis=0, concat_axis=2, tiled=True)
    mixed = jnp.einsum(
        "tvhe,hed->tvd",
        token_rows,
        lax.all_gather(out_weight, "head", axis=0, tiled=True),
        preferred_element_type=jnp.float32,
    )
    return mixed.astype(jnp.bfloat16)


def solution(mesh):
    placed = (
        P("head", "view", None),
        P(),
        P("head", None, None),
        P("head", None, None),
        P("head", None, None),
        P(None, "view"),
    )
    return jax.shard_map(
        on_device, mesh=mesh, in_specs=placed, out_specs=P("head", "view", None), check_vma=False
    )
```

profile of v0, /device:TPU:1, one launch (start us, length us, event | category | flops | bytes accessed | tf_op | source)
XLA Modules:
  0.0 232.7 jit_solution(17147882652215078773)
XLA Ops:
  7.3 1.0 convert_reduce_fusion
  8.3 1.1 fusion.62
  9.4 90.6 %all-gather.3.cloned.1.call-done = bf16[16,216,1152]{2,1,0:T(8,128)(2,1)} async-done(((bf16[1,216,1152]{2,1,0:T(8,128)(2,1)}), bf16[16,216,1152]{2,1,0:T(8,128)(2,1)}) %all-gather.3.cloned.1.call-update) | async-done | bytes 7962640 | tf_op jit(solution)/shard_map/all_gather | solution.py:46
  100.0 5.9 %convolution_convert_fusion = bf16[64,3456]{1,0:T(8,128)(2,1)S(1)} fusion(bf16[3456,1152]{1,0:T(8,128)(2,1)} %bitcast.88, bf16[64,1,1152]{2,0,1:T(8,128)(2,1)} %param.6, f32[1152]{0:T(1024)} %param.7, f32[64]{0:T(128)S(1)} %add_rsqrt_fusion.2, f32[64]{0:T(128)S(1)} %broadcast_multiply_fusion), kind=kOutput, calls=%fused_computation | convolution fusion | flops 510197760 | bytes 8557568 | tf_op jit(solution)/shard_map/dot_general | solution.py:47
  105.9 1.6 reshape.397
  107.5 1.0 copy.10
  108.5 5.0 %all-to-all-start = ((bf16[64,1,16,216]{3,0,1,2:T(8,128)(2,1)}), bf16[64,1,16,216]{3,0,1,2:T(8,128)(2,1)S(1)}, u32[]{:S(2)}, u32[]{:S(2)}) async-start(bf16[64,1,16,216]{3,0,1,2:T(8,128)(2,1)} %copy.10), calls=%async_computation | async-start | bytes 1048576 | tf_op jit(solution)/shard_map/all_to_all | solution.py:53
  116.6 7.3 %all-to-all-done = bf16[64,1,16,216]{3,0,1,2:T(8,128)(2,1)S(1)} async-done(((bf16[64,1,16,216]{3,0,1,2:T(8,128)(2,1)}), bf16[64,1,16,216]{3,0,1,2:T(8,128)(2,1)S(1)}, u32[]{:S(2)}, u32[]{:S(2)}) %all-to-all-start) | async-done | bytes 442400 | tf_op jit(solution)/shard_map/all_to_all | solution.py:53
  124.7 12.5 %collective-permute-start.4 = (bf16[1,1,1024,72]{3,2,1,0:T(8,128)(2,1)S(1)}, bf16[1,1,1024,72]{3,2,1,0:T(8,128)(2,1)S(1)}, u32[]{:S(2)}, u32[]{:S(2)}) collective-permute-start(bf16[1,1,1024,72]{3,2,1,0:T(8,128)(2,1)S(1)} %fusion.59), channel_id=1, source_target_pairs={{0,256},{16,272},{32,288},{48,304},{64,320},{80,336},{96,352},{112... | collective-permute-start | bytes 442376 | tf_op jit(solution)/shard_map/ppermute | solution.py:8
  137.2 4.2 %collective-permute-start = (bf16[1,1,1024,72]{3,2,1,0:T(8,128)(2,1)S(1)}, bf16[1,1,1024,72]{3,2,1,0:T(8,128)(2,1)S(1)}, u32[]{:S(2)}, u32[]{:S(2)}) collective-permute-start(bf16[1,1,1024,72]{3,2,1,0:T(8,128)(2,1)S(1)} %fusion.59), channel_id=1, source_target_pairs={{0,16},{16,0},{32,48},{48,32},{64,80},{80,64},{96,112},{112,96},{1... | collective-permute-start | bytes 442376 | tf_op jit(solution)/shard_map/ppermute | solution.py:8
  141.4 2.4 %collective-permute-start.2 = (bf16[1,1,1024,72]{3,2,1,0:T(8,128)(2,1)S(1)}, bf16[1,1,1024,72]{3,2,1,0:T(8,128)(2,1)S(1)}, u32[]{:S(2)}, u32[]{:S(2)}) collective-permute-start(bf16[1,1,1024,72]{3,2,1,0:T(8,128)(2,1)S(1)} %fusion.59), channel_id=1, source_target_pairs={{0,64},{16,80},{32,96},{48,112},{64,0},{80,16},{96,32},{112,48},{1... | collective-permute-start | bytes 442376 | tf_op jit(solution)/shard_map/ppermute | solution.py:8
  143.9 3.3 %collective-permute-start.5 = (bf16[1,1,1024,72]{3,2,1,0:T(8,128)(2,1)S(1)}, bf16[1,1,1024,72]{3,2,1,0:T(8,128)(2,1)S(1)}, u32[]{:S(2)}, u32[]{:S(2)}) collective-permute-start(bf16[1,1,1024,72]{3,2,1,0:T(8,128)(2,1)S(1)} %slice.34), channel_id=1, source_target_pairs={{0,256},{16,272},{32,288},{48,304},{64,320},{80,336},{96,352},{112... | collective-permute-start | bytes 442376 | tf_op jit(solution)/shard_map/ppermute | solution.py:8
  147.2 2.5 %collective-permute-start.3 = (bf16[1,1,1024,72]{3,2,1,0:T(8,128)(2,1)S(1)}, bf16[1,1,1024,72]{3,2,1,0:T(8,128)(2,1)S(1)}, u32[]{:S(2)}, u32[]{:S(2)}) collective-permute-start(bf16[1,1,1024,72]{3,2,1,0:T(8,128)(2,1)S(1)} %slice.34), channel_id=1, source_target_pairs={{0,64},{16,80},{32,96},{48,112},{64,0},{80,16},{96,32},{112,48},{1... | collective-permute-start | bytes 442376 | tf_op jit(solution)/shard_map/ppermute | solution.py:8
  151.3 0.9 fusion.24
  152.2 23.0 %collective-permute-start.1 = (bf16[1,1,1024,72]{3,2,1,0:T(8,128)(2,1)S(1)}, bf16[1,1,1024,72]{3,2,1,0:T(8,128)(2,1)S(1)}, u32[]{:S(2)}, u32[]{:S(2)}) collective-permute-start(bf16[1,1,1024,72]{3,2,1,0:T(8,128)(2,1)S(1)} %slice.34), channel_id=1, source_target_pairs={{0,16},{16,0},{32,48},{48,32},{64,80},{80,64},{96,112},{112,96},{1... | collective-permute-start | bytes 442376 | tf_op jit(solution)/shard_map/ppermute | solution.py:8
  176.9 23.9 %collective-permute-done.2 = bf16[1,1,1024,72]{3,2,1,0:T(8,128)(2,1)S(1)} collective-permute-done((bf16[1,1,1024,72]{3,2,1,0:T(8,128)(2,1)S(1)}, bf16[1,1,1024,72]{3,2,1,0:T(8,128)(2,1)S(1)}, u32[]{:S(2)}, u32[]{:S(2)}) %collective-permute-start.2) | collective-permute-done | bytes 147488 | tf_op jit(solution)/shard_map/ppermute | solution.py:8
  201.7 0.9 fusion.12
  203.4 3.0 %collective-permute-done.3 = bf16[1,1,1024,72]{3,2,1,0:T(8,128)(2,1)S(1)} collective-permute-done((bf16[1,1,1024,72]{3,2,1,0:T(8,128)(2,1)S(1)}, bf16[1,1,1024,72]{3,2,1,0:T(8,128)(2,1)S(1)}, u32[]{:S(2)}, u32[]{:S(2)}) %collective-permute-start.3) | collective-permute-done | bytes 147488 | tf_op jit(solution)/shard_map/ppermute | solution.py:8
  206.4 0.9 fusion.14
  207.3 1.6 fusion.4
  209.0 0.9 fusion.51
  211.8 10.1 %all_to_all.30 = bf16[16,2,2304]{2,1,0:T(2,128)(2,1)S(1)} all-to-all(bf16[16,2,2304]{2,1,0:T(2,128)(2,1)S(1)} %reshape.410), channel_id=1, replica_groups=mesh['view'=32,'head'=16] {'head'}, dimensions={0} | all-to-all | bytes 294912 | tf_op jit(solution)/shard_map/all_to_all | solution.py:84
  221.9 0.9 reshape.411
  222.8 3.1 %fusion.9 = bf16[64,1,1152]{2,0,1:T(8,128)(2,1)} fusion(bf16[64,16,72]{2,0,1:T(8,128)(2,1)S(1)} %bitcast.89, bf16[16,72,1152]{2,1,0:T(8,128)(2,1)} %all-gather.5.cloned.1.call-done), kind=kOutput, calls=%fused_computation.19 | convolution fusion | flops 169943040 | bytes 2949120 | tf_op jit(solution)/shard_map/tvhe,hed->tvd/dot_general | solution.py:85
  (38 shorter events, 9.8 us)
Async XLA Ops:
  6.5 93.5 %all-gather.3.cloned.1.call-start = ((), (), s32[]{:S(2)}) async-start(), calls=%async_computation.2 | async-start | bytes 8460288 | tf_op jit(solution)/shard_map/all_gather | solution.py:46
  100.0 14.2 %copy-start = (s32[3,1]{0,1:T(1,128)S(1)}, s32[3,1]{0,1:T(1,128)}, u32[]{:S(2)}) copy-start(s32[3,1]{0,1:T(1,128)} %param.11) | copy-start | bytes 40
  100.0 16.6 %copy-start.1 = (f32[1,2,72]{2,1,0:T(2,128)S(1)}, f32[1,2,72]{2,1,0:T(2,128)}, u32[]{:S(2)}) copy-start(f32[1,2,72]{2,1,0:T(2,128)} %param.9) | copy-start | bytes 1732
  108.5 15.5 %all-to-all-start = ((bf16[64,1,16,216]{3,0,1,2:T(8,128)(2,1)}), bf16[64,1,16,216]{3,0,1,2:T(8,128)(2,1)S(1)}, u32[]{:S(2)}, u32[]{:S(2)}) async-start(bf16[64,1,16,216]{3,0,1,2:T(8,128)(2,1)} %copy.10), calls=%async_computation | async-start | bytes 1048576 | tf_op jit(solution)/shard_map/all_to_all | solution.py:53
  113.5 109.4 %all-gather.5.cloned.1.call-start = ((), (), s32[]{:S(2)}) async-start(), calls=%async_computation.3 | async-start | bytes 2820096 | tf_op jit(solution)/shard_map/all_gather | solution.py:88
  124.7 27.5 %collective-permute-start.4 = (bf16[1,1,1024,72]{3,2,1,0:T(8,128)(2,1)S(1)}, bf16[1,1,1024,72]{3,2,1,0:T(8,128)(2,1)S(1)}, u32[]{:S(2)}, u32[]{:S(2)}) collective-permute-start(bf16[1,1,1024,72]{3,2,1,0:T(8,128)(2,1)S(1)} %fusion.59), channel_id=1, source_target_pairs={{0,256},{16,272},{32,288},{48,304},{64,320},{80,336},{96,352},{112... | collective-permute-start | bytes 442376 | tf_op jit(solution)/shard_map/ppermute | solution.py:8
  137.2 38.8 %collective-permute-start = (bf16[1,1,1024,72]{3,2,1,0:T(8,128)(2,1)S(1)}, bf16[1,1,1024,72]{3,2,1,0:T(8,128)(2,1)S(1)}, u32[]{:S(2)}, u32[]{:S(2)}) collective-permute-start(bf16[1,1,1024,72]{3,2,1,0:T(8,128)(2,1)S(1)} %fusion.59), channel_id=1, source_target_pairs={{0,16},{16,0},{32,48},{48,32},{64,80},{80,64},{96,112},{112,96},{1... | collective-permute-start | bytes 442376 | tf_op jit(solution)/shard_map/ppermute | solution.py:8
  141.4 59.4 %collective-permute-start.2 = (bf16[1,1,1024,72]{3,2,1,0:T(8,128)(2,1)S(1)}, bf16[1,1,1024,72]{3,2,1,0:T(8,128)(2,1)S(1)}, u32[]{:S(2)}, u32[]{:S(2)}) collective-permute-start(bf16[1,1,1024,72]{3,2,1,0:T(8,128)(2,1)S(1)} %fusion.59), channel_id=1, source_target_pairs={{0,64},{16,80},{32,96},{48,112},{64,0},{80,16},{96,32},{112,48},{1... | collective-permute-start | bytes 442376 | tf_op jit(solution)/shard_map/ppermute | solution.py:8
  143.9 57.7 %collective-permute-start.5 = (bf16[1,1,1024,72]{3,2,1,0:T(8,128)(2,1)S(1)}, bf16[1,1,1024,72]{3,2,1,0:T(8,128)(2,1)S(1)}, u32[]{:S(2)}, u32[]{:S(2)}) collective-permute-start(bf16[1,1,1024,72]{3,2,1,0:T(8,128)(2,1)S(1)} %slice.34), channel_id=1, source_target_pairs={{0,256},{16,272},{32,288},{48,304},{64,320},{80,336},{96,352},{112... | collective-permute-start | bytes 442376 | tf_op jit(solution)/shard_map/ppermute | solution.py:8
  147.2 59.2 %collective-permute-start.3 = (bf16[1,1,1024,72]{3,2,1,0:T(8,128)(2,1)S(1)}, bf16[1,1,1024,72]{3,2,1,0:T(8,128)(2,1)S(1)}, u32[]{:S(2)}, u32[]{:S(2)}) collective-permute-start(bf16[1,1,1024,72]{3,2,1,0:T(8,128)(2,1)S(1)} %slice.34), channel_id=1, source_target_pairs={{0,64},{16,80},{32,96},{48,112},{64,0},{80,16},{96,32},{112,48},{1... | collective-permute-start | bytes 442376 | tf_op jit(solution)/shard_map/ppermute | solution.py:8
  152.2 56.7 %collective-permute-start.1 = (bf16[1,1,1024,72]{3,2,1,0:T(8,128)(2,1)S(1)}, bf16[1,1,1024,72]{3,2,1,0:T(8,128)(2,1)S(1)}, u32[]{:S(2)}, u32[]{:S(2)}) collective-permute-start(bf16[1,1,1024,72]{3,2,1,0:T(8,128)(2,1)S(1)} %slice.34), channel_id=1, source_target_pairs={{0,16},{16,0},{32,48},{48,32},{64,80},{80,64},{96,112},{112,96},{1... | collective-permute-start | bytes 442376 | tf_op jit(solution)/shard_map/ppermute | solution.py:8
Sparse Core Ops, SparseCore 0:
  10.4 89.5 all-gather.2
  117.3 63.3 all-gather.4
where the time goes:
time: 233 us
  waiting for transfers between devices  126 us (54%)
  starting transfers between devices  52.8 us (23%)
  matrix products  15.8 us (7%)
  between operations  15.5 us (7%)
  blocking collectives  10.1 us (4%)
  other arithmetic  6.85 us (3%)
  local copies, waits for them, and re-layouts  5.44 us (2%)
    all_gather x1, waiting for transfers between devices, on_device(): full_weight = lax.all_gather(qkv_weight, 'head', axis=0, tiled=True)  90.6 us
    ppermute x6, starting transfers between devices, partner(): lax.ppermute(array, axis, [(i, i ^ 1 << bit) for i in range(lax.axis_size...  47.8 us
    ppermute x6, waiting for transfers between devices, partner(): lax.ppermute(array, axis, [(i, i ^ 1 << bit) for i in range(lax.axis_size...  26.9 us
    all_to_all x1, blocking collectives, on_device(): lax.all_to_all(attended, 'head', split_axis=0, concat_axis=2, tiled=True)  10.1 us
    all_to_all x1, waiting for transfers between devices, on_device(): lax.all_to_all(projected, 'head', split_axis=2, concat_axis=0, tiled=True)  7.35 us
    dot_general x1, matrix products, on_device(): jnp.dot(normed.reshape(-1, width), full_weight.reshape(-1, width).T, pref...  5.87 us
    all_to_all x1, starting transfers between devices, on_device(): lax.all_to_all(projected, 'head', split_axis=2, concat_axis=0, tiled=True)  4.98 us
  transfers between devices with their start and end apart: 9, of which 4 were waited for; matrix products, arithmetic and copies ran while one was open for 7% of the time, Pallas kernels for 0%

commit v1 on v0

v1 whole, which is shorter than its diff:
```python
import functools
import math
import jax
import jax.numpy as jnp
from jax import lax
from jax.experimental import pallas as pl
from jax.experimental.pallas import tpu as pltpu
from jax.sharding import PartitionSpec as P

BLANK = 1e30


def partner(array, bit):
    return lax.ppermute(array, "view", [(i, i ^ 1 << bit) for i in range(lax.axis_size("view"))])


def normalize(latents, norm_gain):
    values = latents.astype(jnp.float32)
    mean = jnp.mean(values, axis=-1, keepdims=True)
    centred = values - mean
    var = jnp.mean(centred * centred, axis=-1, keepdims=True)
    return (centred * lax.rsqrt(var + 1e-06) * norm_gain).astype(jnp.bfloat16)


def gather_tokens(normed):
    heads = lax.axis_size("head")
    copies = jnp.broadcast_to(normed[None], (heads,) + normed.shape)
    rows = lax.all_to_all(copies, "head", split_axis=0, concat_axis=0, tiled=True)
    return rows.reshape(-1, normed.shape[-1])


def rms_rows(part, gain):
    square = jnp.mean(part * part, axis=0, keepdims=True) + 1e-06
    return part * lax.rsqrt(square) * gain


def project_kernel(with_query, rows_ref, weight_ref, gain_ref, *out_refs):
    head_dim = gain_ref.shape[0]
    weight = weight_ref[...]
    flat = lax.dot_general(
        weight, rows_ref[...], (((1,), (1,)), ((), ())), preferred_element_type=jnp.float32
    )
    flat = flat.astype(jnp.bfloat16).astype(jnp.float32)
    if with_query:
        query = rms_rows(flat[:head_dim], gain_ref[:, 0:1])
        out_refs[0][...] = query.T.astype(jnp.bfloat16)
        flat = flat[head_dim:]
    keys = rms_rows(flat[:head_dim], gain_ref[:, 1:2])
    out_refs[-1][...] = jnp.concatenate([keys, flat[head_dim:]], axis=0).astype(jnp.bfloat16)


def project(rows, weight, gain, with_query):
    tokens, width = rows.shape
    head_dim = gain.shape[0]
    out_shape = [jax.ShapeDtypeStruct((2 * head_dim, tokens), jnp.bfloat16)]
    if with_query:
        out_shape = [jax.ShapeDtypeStruct((tokens, head_dim), jnp.bfloat16)] + out_shape
    return pl.pallas_call(
        functools.partial(project_kernel, with_query),
        out_shape=out_shape,
        compiler_params=pltpu.CompilerParams(vmem_limit_bytes=32 << 20),
        cost_estimate=pl.CostEstimate(
            flops=2 * tokens * width * weight.shape[0], bytes_accessed=2 * tokens * width, transcendentals=0
        ),
    )(rows, weight, gain)


def attend_kernel(tile, active_ref, query_ref, own_ref, *refs):
    far_refs, out_ref, values_ref = refs[:-2], refs[-2], refs[-1]
    tokens, head_dim = query_ref.shape
    factor = math.log2(math.e) * float(head_dim) ** (-0.5)
    pair_refs = (own_ref,) + far_refs
    padded = values_ref.shape[-1]
    lane = lax.broadcasted_iota(jnp.int32, (tokens, padded), 1)
    for n, ref in enumerate(pair_refs):
        part = ref[...].astype(jnp.float32)[head_dim:]
        filled = jnp.concatenate([part, jnp.zeros((padded - head_dim, tokens), jnp.float32)], axis=0)
        values_ref[n] = jnp.where(lane == head_dim, 1.0, filled.T).astype(jnp.bfloat16)

    def scores_of(query, ref):
        keys = ref[...][:head_dim]
        return jnp.dot(query, keys, preferred_element_type=jnp.float32) * factor

    def weighted(scores, shift, n):
        weights = jnp.exp2(scores - shift).astype(jnp.bfloat16)
        return jnp.dot(weights, values_ref[n], preferred_element_type=jnp.float32)

    def finish(acc):
        return acc[:, :head_dim] / jnp.maximum(acc[:, head_dim : head_dim + 1], 1.0)

    def step(at, carry):
        rows = pl.ds(pl.multiple_of(at * tile, tile), tile)
        query = query_ref[rows, :]
        scores = scores_of(query, own_ref)
        own = finish(weighted(scores, jnp.max(scores, axis=1, keepdims=True), 0))
        several = [scores_of(query, ref) for ref in far_refs]
        best = jnp.full((tile, 1), -BLANK, jnp.float32)
        for n, scores in enumerate(several):
            most = jnp.max(scores, axis=1, keepdims=True)
            best = jnp.where(active_ref[n] > 0, jnp.maximum(best, most), best)
        acc = jnp.zeros((tile, padded), jnp.float32)
        for n, scores in enumerate(several):
            acc = acc + weighted(scores, jnp.where(active_ref[n] > 0, best, BLANK), n + 1)
        out_ref[rows, :] = (own + finish(acc)).astype(jnp.bfloat16)
        return carry

    lax.fori_loop(0, tokens // tile, step, 0)


def attend(active, query, own, far):
    tokens, head_dim = query.shape
    blocks = 1 + len(far)
    vmem = pl.BlockSpec(memory_space=pltpu.VMEM)
    return pl.pallas_call(
        functools.partial(attend_kernel, 256),
        out_shape=jax.ShapeDtypeStruct((tokens, head_dim), jnp.bfloat16),
        in_specs=[pl.BlockSpec(memory_space=pltpu.SMEM)] + [vmem] * (1 + blocks),
        out_specs=vmem,
        scratch_shapes=[pltpu.VMEM((blocks, tokens, 128), jnp.bfloat16)],
        compiler_params=pltpu.CompilerParams(vmem_limit_bytes=40 << 20),
        cost_estimate=pl.CostEstimate(
            flops=4 * blocks * tokens * tokens * head_dim,
            bytes_accessed=4 * blocks * tokens * head_dim,
            transcendentals=blocks * tokens * tokens,
        ),
    )(active, query, own, *far)


def on_device(latents, norm_gain, qkv_weight, qk_gain, out_weight, intersection):
    loc_len, view_dev, width = latents.shape
    rows = latents.reshape(loc_len, width)
    levels = lax.axis_size("view").bit_length() - 1
    rounds = intersection.shape[0]
    bits = [step * (levels - 1) // (rounds - 1) for step in range(rounds)]
    far_rows = partner(rows, bits[-1])
    gain = qk_gain[0].T
    head_dim = gain.shape[0]
    weight = qkv_weight[0]
    every = gather_tokens(normalize(rows, norm_gain))
    query, own = project(every, weight, gain, True)
    far = [partner(own, bit) for bit in bits[:-1]]
    far_every = gather_tokens(normalize(far_rows, norm_gain))
    far = far + list(project(far_every, weight[head_dim:], gain, False))
    attended = attend(intersection[:, 0], query, own, far)
    token_rows = lax.all_to_all(
        attended.reshape(-1, loc_len, head_dim), "head", split_axis=0, concat_axis=0, tiled=True
    )
    mixed = jnp.einsum(
        "hte,hed->td",
        token_rows,
        lax.all_gather(out_weight, "head", axis=0, tiled=True),
        preferred_element_type=jnp.float32,
    )
    return mixed.astype(jnp.bfloat16).reshape(loc_len, view_dev, width)


def solution(mesh):
    placed = (
        P("head", "view", None),
        P(),
        P("head", None, None),
        P("head", None, None),
        P("head", None, None),
        P(None, "view"),
    )
    return jax.shard_map(
        on_device, mesh=mesh, in_specs=placed, out_specs=P("head", "view", None), check_vma=False
    )
```

time: 233 us -> 153 us (0.66)
  the two profiles are of different devices: /device:TPU:1 before, /device:TPU:32 now
where the time goes in v1:
time: 153 us
  blocking collectives  49.5 us (32%)
  waiting for transfers between devices  44.9 us (29%)
  starting transfers between devices  22.5 us (15%)
  between operations  13.5 us (9%)
  Pallas kernels  10.8 us (7%)
  local copies, waits for them, and re-layouts  4.58 us (3%)
  other arithmetic  3.67 us (2%)
  matrix products  3.05 us (2%)
    all_to_all x1, blocking collectives, gather_tokens(): lax.all_to_all(copies, 'head', split_axis=0, concat_axis=0, tiled=True)  37.5 us
    all_to_all x1, waiting for transfers between devices, gather_tokens(): lax.all_to_all(copies, 'head', split_axis=0, concat_axis=0, tiled=True)  33.7 us
    ppermute x3, starting transfers between devices, partner(): lax.ppermute(array, 'view', [(i, i ^ 1 << bit) for i in range(lax.axis_si...  18.6 us
    all_to_all x1, blocking collectives, on_device(): lax.all_to_all(attended.reshape(-1, loc_len, head_dim), 'head', split_axi...  12.1 us
    ppermute x3, waiting for transfers between devices, partner(): lax.ppermute(array, 'view', [(i, i ^ 1 << bit) for i in range(lax.axis_si...  11.2 us
    pallas_call x1, Pallas kernels, attend(): pl.pallas_call(functools.partial(attend_kernel, 256), out_shape=jax.Shape...  8.87 us
    all_to_all x1, starting transfers between devices, gather_tokens(): lax.all_to_all(copies, 'head', split_axis=0, concat_axis=0, tiled=True)  3.86 us
  transfers between devices with their start and end apart: 5, of which 2 were waited for; matrix products, arithmetic and copies ran while one was open for 4% of the time, Pallas kernels for 7%

profile of v1, /device:TPU:32, one launch (start us, length us, event | category | flops | bytes accessed | tf_op | source)
XLA Modules:
  0.0 152.7 jit_solution(5681466714662009842)
XLA Ops:
  6.5 14.8 %collective-permute-start.2 = (bf16[64,1152]{1,0:T(8,128)(2,1)}, bf16[64,1152]{1,0:T(8,128)(2,1)S(1)}, u32[]{:S(2)}, u32[]{:S(2)}) collective-permute-start(bf16[64,1152]{1,0:T(8,128)(2,1)} %bitcast.31), channel_id=1, source_target_pairs={{0,256},{16,272},{32,288},{48,304},{64,320},{80,336},{96,352},{112... | collective-permute-start | bytes 442376 | tf_op jit(solution)/shard_map/ppermute | solution.py:14
  21.4 0.0 all-gather.2.cloned.1.call-update
  21.4 1.1 convert_reduce_fusion.1
  22.5 1.1 fusion.9
  23.6 11.2 %collective-permute-done.2 = bf16[64,1152]{1,0:T(8,128)(2,1)S(1)} collective-permute-done((bf16[64,1152]{1,0:T(8,128)(2,1)}, bf16[64,1152]{1,0:T(8,128)(2,1)S(1)}, u32[]{:S(2)}, u32[]{:S(2)}) %collective-permute-start.2) | collective-permute-done | bytes 147488 | tf_op jit(solution)/shard_map/ppermute | solution.py:14
  34.8 0.1 convert_reduce_fusion
  34.9 0.2 fusion.6
  35.1 1.2 fusion.8
  36.3 0.3 broadcast_in_dim.4
  36.6 37.5 %all_to_all.15 = bf16[16,64,1152]{2,1,0:T(8,128)(2,1)} all-to-all(bf16[16,64,1152]{2,1,0:T(8,128)(2,1)S(1)} %broadcast_in_dim.4), channel_id=1, replica_groups=mesh['view'=32,'head'=16] {'head'}, dimensions={0} | all-to-all | bytes 4718592 | tf_op jit(solution)/shard_map/all_to_all | solution.py:28
  74.1 1.8 %broadcast_in_dim.5 = bf16[16,64,1152]{2,1,0:T(8,128)(2,1)} broadcast(bf16[64,1152]{1,0:T(8,128)(2,1)S(1)} %get-tuple-element.9), dimensions={1,2} | broadcast | bytes 2506752 | tf_op jit(solution)/shard_map/broadcast_in_dim | solution.py:27
  75.8 3.9 %all-to-all-start.1 = ((bf16[16,64,1152]{2,1,0:T(8,128)(2,1)}), bf16[16,64,1152]{2,1,0:T(8,128)(2,1)S(1)}, u32[]{:S(2)}, u32[]{:S(2)}) async-start(bf16[16,64,1152]{2,1,0:T(8,128)(2,1)} %broadcast_in_dim.5), calls=%async_computation.1 | async-start | bytes 4718592 | tf_op jit(solution)/shard_map/all_to_all | solution.py:28
  79.7 0.1 copy.8
  79.8 1.7 %copy-done = bf16[16,64,1152]{2,1,0:T(8,128)(2,1)S(1)} copy-done((bf16[16,64,1152]{2,1,0:T(8,128)(2,1)S(1)}, bf16[16,64,1152]{2,1,0:T(8,128)(2,1)}, u32[]{:S(2)}) %copy-start) | copy-done | bytes 2359320
  81.5 1.0 shard_map.64
  82.5 0.7 copy-done.2
  83.2 1.9 %collective-permute-start = (bf16[144,1024]{1,0:T(8,128)(2,1)S(1)}, bf16[144,1024]{1,0:T(8,128)(2,1)}, u32[]{:S(2)}, u32[]{:S(2)}) collective-permute-start(bf16[144,1024]{1,0:T(8,128)(2,1)S(1)} %get-tuple-element.8.own_ref), channel_id=1, source_target_pairs={{0,16},{16,0},{32,48},{48,32},{64,80},{80,64},{96,112},{112,96},{1... | collective-permute-start | bytes 884744 | tf_op jit(solution)/shard_map/ppermute | solution.py:14
  85.1 1.9 %collective-permute-start.1 = (bf16[144,1024]{1,0:T(8,128)(2,1)S(1)}, bf16[144,1024]{1,0:T(8,128)(2,1)}, u32[]{:S(2)}, u32[]{:S(2)}) collective-permute-start(bf16[144,1024]{1,0:T(8,128)(2,1)S(1)} %get-tuple-element.8.own_ref), channel_id=1, source_target_pairs={{0,64},{16,80},{32,96},{48,112},{64,0},{80,16},{96,32},{112,48},{1... | collective-permute-start | bytes 884744 | tf_op jit(solution)/shard_map/ppermute | solution.py:14
  87.1 33.7 %all-to-all-done.1 = bf16[16,64,1152]{2,1,0:T(8,128)(2,1)S(1)} async-done(((bf16[16,64,1152]{2,1,0:T(8,128)(2,1)}), bf16[16,64,1152]{2,1,0:T(8,128)(2,1)S(1)}, u32[]{:S(2)}, u32[]{:S(2)}) %all-to-all-start.1) | async-done | bytes 2359328 | tf_op jit(solution)/shard_map/all_to_all | solution.py:28
  120.9 0.9 shard_map.65.refs_2_
  121.8 0.0 collective-permute-done.1.refs_1_
  121.8 8.9 %shard_map.66 = bf16[1024,72]{1,0:T(8,128)(2,1)S(1)} custom-call(s32[3]{0:T(128)S(1)} %bitcast.30, bf16[1024,72]{1,0:T(8,128)(2,1)S(1)} %copy-done.3, bf16[144,1024]{1,0:T(8,128)(2,1)S(1)} %get-tuple-element.8.own_ref, bf16[144,1024]{1,0:T(8,128)(2,1)} %collective-permute-done.refs_0_, bf16[144,1024]{1,0:T(8,128)(2,1)} %collective-permute-done.1.refs_1_, ...), custom_call_target="tpu_custom_call" | custom-call | flops 1207959552 | bytes 1179648 | tf_op jit(solution)/shard_map/pallas_call | solution.py:114
  130.7 12.1 %all_to_all.16 = bf16[16,64,72]{2,1,0:T(8,128)(2,1)S(1)} all-to-all(bf16[16,64,72]{2,1,0:T(8,128)(2,1)S(1)} %bitcast.29), channel_id=1, replica_groups=mesh['view'=32,'head'=16] {'head'}, dimensions={0} | all-to-all | bytes 294912 | tf_op jit(solution)/shard_map/all_to_all | solution.py:145
  142.8 3.1 %fusion.1 = bf16[64,1,1152]{2,0,1:T(8,128)(2,1)} fusion(bf16[16,64,72]{2,1,0:T(8,128)(2,1)S(1)} %all_to_all.16, bf16[16,72,1152]{2,1,0:T(8,128)(2,1)} %all-gather.2.cloned.1.call-done), kind=kOutput, calls=%fused_computation.2 | convolution fusion | flops 169943040 | bytes 2949120 | tf_op jit(solution)/shard_map/hte,hed->td/dot_general | solution.py:148
  (18 shorter events, 0.1 us)
Async XLA Ops:
  6.5 136.2 %all-gather.2.cloned.1.call-start = ((), (), s32[]{:S(2)}) async-start(), calls=%async_computation.3 | async-start | bytes 2820096 | tf_op jit(solution)/shard_map/all_gather | solution.py:151
  6.5 28.2 %collective-permute-start.2 = (bf16[64,1152]{1,0:T(8,128)(2,1)}, bf16[64,1152]{1,0:T(8,128)(2,1)S(1)}, u32[]{:S(2)}, u32[]{:S(2)}) collective-permute-start(bf16[64,1152]{1,0:T(8,128)(2,1)} %bitcast.31), channel_id=1, source_target_pairs={{0,256},{16,272},{32,288},{48,304},{64,320},{80,336},{96,352},{112... | collective-permute-start | bytes 442376 | tf_op jit(solution)/shard_map/ppermute | solution.py:14
  75.8 3.9 %copy-start.5 = (f32[1,2,72]{2,1,0:T(2,128)S(1)}, f32[1,2,72]{2,1,0:T(2,128)}, u32[]{:S(2)}) copy-start(f32[1,2,72]{2,1,0:T(2,128)} %param.9) | copy-start | bytes 1732
  75.8 4.0 %copy-start.1 = (bf16[1,216,1152]{2,1,0:T(8,128)(2,1)S(1)}, bf16[1,216,1152]{2,1,0:T(8,128)(2,1)}, u32[]{:S(2)}) copy-start(bf16[1,216,1152]{2,1,0:T(8,128)(2,1)} %param.8) | copy-start | bytes 1492996
  75.8 45.0 %all-to-all-start.1 = ((bf16[16,64,1152]{2,1,0:T(8,128)(2,1)}), bf16[16,64,1152]{2,1,0:T(8,128)(2,1)S(1)}, u32[]{:S(2)}, u32[]{:S(2)}) async-start(bf16[16,64,1152]{2,1,0:T(8,128)(2,1)} %broadcast_in_dim.5), calls=%async_computation.1 | async-start | bytes 4718592 | tf_op jit(solution)/shard_map/all_to_all | solution.py:28
  79.8 1.7 %copy-start = (bf16[16,64,1152]{2,1,0:T(8,128)(2,1)S(1)}, bf16[16,64,1152]{2,1,0:T(8,128)(2,1)}, u32[]{:S(2)}) copy-start(bf16[16,64,1152]{2,1,0:T(8,128)(2,1)} %all_to_all.15) | copy-start | bytes 7077892
  81.5 40.3 %copy-start.4 = (s32[3,1]{0,1:T(1,128)S(1)}, s32[3,1]{0,1:T(1,128)}, u32[]{:S(2)}) copy-start(s32[3,1]{0,1:T(1,128)} %param.11) | copy-start | bytes 40
  82.5 0.7 copy-start.2
  83.2 38.6 %collective-permute-start = (bf16[144,1024]{1,0:T(8,128)(2,1)S(1)}, bf16[144,1024]{1,0:T(8,128)(2,1)}, u32[]{:S(2)}, u32[]{:S(2)}) collective-permute-start(bf16[144,1024]{1,0:T(8,128)(2,1)S(1)} %get-tuple-element.8.own_ref), channel_id=1, source_target_pairs={{0,16},{16,0},{32,48},{48,32},{64,80},{80,64},{96,112},{112,96},{1... | collective-permute-start | bytes 884744 | tf_op jit(solution)/shard_map/ppermute | solution.py:14
  85.1 36.6 %collective-permute-start.1 = (bf16[144,1024]{1,0:T(8,128)(2,1)S(1)}, bf16[144,1024]{1,0:T(8,128)(2,1)}, u32[]{:S(2)}, u32[]{:S(2)}) collective-permute-start(bf16[144,1024]{1,0:T(8,128)(2,1)S(1)} %get-tuple-element.8.own_ref), channel_id=1, source_target_pairs={{0,64},{16,80},{32,96},{48,112},{64,0},{80,16},{96,32},{112,48},{1... | collective-permute-start | bytes 884744 | tf_op jit(solution)/shard_map/ppermute | solution.py:14
  87.1 34.7 %copy-start.3 = (bf16[1024,72]{1,0:T(8,128)(2,1)S(1)}, bf16[1024,72]{1,0:T(8,128)(2,1)}, u32[]{:S(2)}) copy-start(bf16[1024,72]{1,0:T(8,128)(2,1)} %copy-done.2) | copy-start | bytes 442372
Sparse Core Ops, SparseCore 0:
  21.5 93.0 all-gather.1

commit v2 on v1

v2 whole, which is shorter than its diff:
```python
import functools
import math
import jax
import jax.numpy as jnp
from jax import lax
from jax.experimental import pallas as pl
from jax.experimental.pallas import tpu as pltpu
from jax.sharding import PartitionSpec as P

BLANK = 1e30


def partner(array, bit):
    return lax.ppermute(array, "view", [(i, i ^ 1 << bit) for i in range(lax.axis_size("view"))])


def normalize_kernel(rows_ref, gain_ref, out_ref):
    values = rows_ref[...].astype(jnp.float32)
    mean = jnp.mean(values, axis=-1, keepdims=True)
    centred = values - mean
    var = jnp.mean(centred * centred, axis=-1, keepdims=True)
    out_ref[...] = (centred * lax.rsqrt(var + 1e-06) * gain_ref[...]).astype(jnp.bfloat16)


def normalize(rows, norm_gain):
    return pl.pallas_call(
        normalize_kernel,
        out_shape=jax.ShapeDtypeStruct(rows.shape, jnp.bfloat16),
        compiler_params=pltpu.CompilerParams(vmem_limit_bytes=16 << 20),
        cost_estimate=pl.CostEstimate(
            flops=8 * rows.size, bytes_accessed=4 * rows.size, transcendentals=0
        ),
    )(rows, norm_gain[None])


def gather_tokens(normed):
    heads = lax.axis_size("head")
    copies = jnp.broadcast_to(normed[None], (heads,) + normed.shape)
    rows = lax.all_to_all(copies, "head", split_axis=0, concat_axis=0, tiled=True)
    return rows.reshape(-1, normed.shape[-1])


def rms_rows(part, gain):
    square = jnp.mean(part * part, axis=0, keepdims=True) + 1e-06
    return part * lax.rsqrt(square) * gain


def project_kernel(with_query, rows_ref, weight_ref, gain_ref, *out_refs):
    head_dim = gain_ref.shape[0]
    weight = weight_ref[...]
    flat = lax.dot_general(
        weight, rows_ref[...], (((1,), (1,)), ((), ())), preferred_element_type=jnp.float32
    )
    flat = flat.astype(jnp.bfloat16).astype(jnp.float32)
    if with_query:
        query = rms_rows(flat[:head_dim], gain_ref[:, 0:1])
        out_refs[0][...] = query.T.astype(jnp.bfloat16)
        flat = flat[head_dim:]
    keys = rms_rows(flat[:head_dim], gain_ref[:, 1:2])
    out_refs[-1][...] = jnp.concatenate([keys, flat[head_dim:]], axis=0).astype(jnp.bfloat16)


def project(rows, weight, gain, with_query):
    tokens, width = rows.shape
    head_dim = gain.shape[0]
    out_shape = [jax.ShapeDtypeStruct((2 * head_dim, tokens), jnp.bfloat16)]
    if with_query:
        out_shape = [jax.ShapeDtypeStruct((tokens, head_dim), jnp.bfloat16)] + out_shape
    return pl.pallas_call(
        functools.partial(project_kernel, with_query),
        out_shape=out_shape,
        compiler_params=pltpu.CompilerParams(vmem_limit_bytes=32 << 20),
        cost_estimate=pl.CostEstimate(
            flops=2 * tokens * width * weight.shape[0], bytes_accessed=2 * tokens * width, transcendentals=0
        ),
    )(rows, weight, gain)


def scores_of(query, pair_ref):
    head_dim = query.shape[1]
    factor = math.log2(math.e) * float(head_dim) ** (-0.5)
    keys = pair_ref[...][:head_dim]
    return jnp.dot(query, keys, preferred_element_type=jnp.float32) * factor


def weighted(scores, shift, values):
    weights = jnp.exp2(scores - shift).astype(jnp.bfloat16)
    return jnp.dot(weights, values, preferred_element_type=jnp.float32)


def finish(acc, head_dim):
    return acc[:, :head_dim] / jnp.maximum(acc[:, head_dim : head_dim + 1], 1.0)


def spread_values(pair_ref, head_dim, padded):
    part = pair_ref[...].astype(jnp.float32)[head_dim:]
    tokens = part.shape[1]
    lane = lax.broadcasted_iota(jnp.int32, (tokens, padded), 1)
    filled = jnp.concatenate([part, jnp.zeros((padded - head_dim, tokens), jnp.float32)], axis=0)
    return jnp.where(lane == head_dim, 1.0, filled.T).astype(jnp.bfloat16)


def cross_update(active_ref, first, query, far_refs, values_ref, slot, best, acc):
    several = [scores_of(query, ref) for ref in far_refs]
    newbest = best
    for n, scores in enumerate(several):
        most = jnp.max(scores, axis=1, keepdims=True)
        newbest = jnp.where(active_ref[first + n] > 0, jnp.maximum(newbest, most), newbest)
    if acc is not None:
        acc = acc * jnp.exp2(best - newbest)
    for n, scores in enumerate(several):
        shift = jnp.where(active_ref[first + n] > 0, newbest, BLANK)
        term = weighted(scores, shift, values_ref[slot + n])
        acc = term if acc is None else acc + term
    return newbest, acc


def near_kernel(tile, active_ref, query_ref, own_ref, *refs):
    far_refs, own_out_ref, state_ref, values_ref = refs[:-3], refs[-3], refs[-2], refs[-1]
    tokens, head_dim = query_ref.shape
    padded = values_ref.shape[-1]
    for n, ref in enumerate((own_ref,) + far_refs):
        values_ref[n] = spread_values(ref, head_dim, padded)

    def step(at, carry):
        rows = pl.ds(pl.multiple_of(at * tile, tile), tile)
        query = query_ref[rows, :]
        scores = scores_of(query, own_ref)
        acc = weighted(scores, jnp.max(scores, axis=1, keepdims=True), values_ref[0])
        own_out_ref[rows, :] = finish(acc, head_dim)
        start = jnp.full((tile, 1), -BLANK, jnp.float32)
        best, acc = cross_update(active_ref, 0, query, far_refs, values_ref, 1, start, None)
        lane = lax.broadcasted_iota(jnp.int32, (tile, padded), 1)
        state_ref[rows, :] = jnp.where(lane == head_dim + 1, best, acc)
        return carry

    lax.fori_loop(0, tokens // tile, step, 0)


def last_kernel(tile, first, active_ref, query_ref, own_in_ref, state_ref, *refs):
    far_refs, out_ref, values_ref = refs[:-2], refs[-2], refs[-1]
    tokens, head_dim = query_ref.shape
    padded = values_ref.shape[-1]
    for n, ref in enumerate(far_refs):
        values_ref[n] = spread_values(ref, head_dim, padded)

    def step(at, carry):
        rows = pl.ds(pl.multiple_of(at * tile, tile), tile)
        query = query_ref[rows, :]
        acc = state_ref[rows, :]
        best = acc[:, head_dim + 1 : head_dim + 2]
        best, acc = cross_update(active_ref, first, query, far_refs, values_ref, 0, best, acc)
        out_ref[rows, :] = (own_in_ref[rows, :] + finish(acc, head_dim)).astype(jnp.bfloat16)
        return carry

    lax.fori_loop(0, tokens // tile, step, 0)


PADDED = 128


def call_attend(kernel, out_shape, blocks, tokens, head_dim, arrays):
    vmem = pl.BlockSpec(memory_space=pltpu.VMEM)
    several = isinstance(out_shape, list)
    return pl.pallas_call(
        kernel,
        out_shape=out_shape,
        in_specs=[pl.BlockSpec(memory_space=pltpu.SMEM)] + [vmem] * (len(arrays) - 1),
        out_specs=[vmem] * len(out_shape) if several else vmem,
        scratch_shapes=[pltpu.VMEM((blocks, tokens, PADDED), jnp.bfloat16)],
        compiler_params=pltpu.CompilerParams(vmem_limit_bytes=40 << 20),
        cost_estimate=pl.CostEstimate(
            flops=4 * blocks * tokens * tokens * 256,
            bytes_accessed=4 * blocks * tokens * head_dim,
            transcendentals=blocks * tokens * tokens,
        ),
    )(*arrays)


def attend_near(active, query, own, far):
    tokens, head_dim = query.shape
    out_shape = [
        jax.ShapeDtypeStruct((tokens, head_dim), jnp.float32),
        jax.ShapeDtypeStruct((tokens, PADDED), jnp.float32),
    ]
    arrays = (active, query, own, *far)
    return call_attend(
        functools.partial(near_kernel, 256), out_shape, 1 + len(far), tokens, head_dim, arrays
    )


def attend_last(active, first, query, own_result, state, far):
    tokens, head_dim = query.shape
    out_shape = jax.ShapeDtypeStruct((tokens, head_dim), jnp.bfloat16)
    arrays = (active, query, own_result, state, *far)
    return call_attend(
        functools.partial(last_kernel, 256, first), out_shape, len(far), tokens, head_dim, arrays
    )


def gather_out_half(out_weight):
    head_dim, width = out_weight.shape
    half = width // 2
    core = lax.axis_index("view") % 2
    mine = lax.dynamic_slice_in_dim(out_weight, core * half, half, axis=1)
    return lax.all_gather(mine, "head", axis=0, tiled=True)


def swap_halves(mine):
    core = lax.axis_index("view") % 2
    other = partner(mine, 0)
    pair = jnp.where(core == 0, jnp.stack([mine, other]), jnp.stack([other, mine]))
    return jnp.concatenate([pair[0], pair[1]], axis=1)


def on_device(latents, norm_gain, qkv_weight, qk_gain, out_weight, intersection):
    loc_len, view_dev, width = latents.shape
    rows = latents.reshape(loc_len, width)
    levels = lax.axis_size("view").bit_length() - 1
    rounds = intersection.shape[0]
    bits = [step * (levels - 1) // (rounds - 1) for step in range(rounds)]
    gain = qk_gain[0].T
    head_dim = gain.shape[0]
    weight = qkv_weight[0]
    active = intersection[:, 0]
    normed = normalize(rows, norm_gain)
    far_normed = partner(normed, bits[-1])
    every = gather_tokens(normed)
    query, own = project(every, weight, gain, True)
    near = [partner(own, bit) for bit in bits[:-1]]
    far_every = gather_tokens(far_normed)
    out_half = gather_out_half(out_weight[0])
    own_result, state = attend_near(active, query, own, near)
    out_half, own_result, state = lax.optimization_barrier((out_half, own_result, state))
    full_out = swap_halves(out_half).reshape(-1, head_dim, width)
    far_every, full_out = lax.optimization_barrier((far_every, full_out))
    far = list(project(far_every, weight[head_dim:], gain, False))
    attended = attend_last(active, rounds - 1, query, own_result, state, far)
    token_rows = lax.all_to_all(
        attended.reshape(-1, loc_len, head_dim), "head", split_axis=0, concat_axis=0, tiled=True
    )
    mixed = jnp.einsum("hte,hed->td", token_rows, full_out, preferred_element_type=jnp.float32)
    return mixed.astype(jnp.bfloat16).reshape(loc_len, view_dev, width)


def solution(mesh):
    placed = (
        P("head", "view", None),
        P(),
        P("head", None, None),
        P("head", None, None),
        P("head", None, None),
        P(None, "view"),
    )
    return jax.shard_map(
        on_device, mesh=mesh, in_specs=placed, out_specs=P("head", "view", None), check_vma=False
    )
```

time: 153 us -> 186 us (1.22)
  the two profiles are of different devices: /device:TPU:32 before, /device:TPU:192 now
where the time goes in v2:
time: 186 us
  waiting for transfers between devices  102 us (55%)
  starting transfers between devices  24.1 us (13%)
  local copies, waits for them, and re-layouts  14.1 us (8%)
  between operations  13.6 us (7%)
  Pallas kernels  12.8 us (7%)
  blocking collectives  12.1 us (7%)
  other arithmetic  5.87 us (3%)
    all_to_all x2, waiting for transfers between devices, gather_tokens(): lax.all_to_all(copies, 'head', split_axis=0, concat_axis=0, tiled=True)  62.6 us
    ppermute x4, waiting for transfers between devices, partner(): lax.ppermute(array, 'view', [(i, i ^ 1 << bit) for i in range(lax.axis_si...  33.4 us
    all_to_all x2, starting transfers between devices, gather_tokens(): lax.all_to_all(copies, 'head', split_axis=0, concat_axis=0, tiled=True)  12.1 us
    all_to_all x1, blocking collectives, on_device(): lax.all_to_all(attended.reshape(-1, loc_len, head_dim), 'head', split_axi...  12.1 us
    ppermute x4, starting transfers between devices, partner(): lax.ppermute(array, 'view', [(i, i ^ 1 << bit) for i in range(lax.axis_si...  12 us
    pallas_call x2, Pallas kernels, call_attend(): pl.pallas_call(kernel, out_shape=out_shape, in_specs=[pl.BlockSpec(memory...  10.7 us
    all_gather x1, waiting for transfers between devices, gather_out_half(): return lax.all_gather(mine, 'head', axis=0, tiled=True)  5.7 us
  transfers between devices with their start and end apart: 7, of which 5 were waited for; matrix products, arithmetic and copies ran while one was open for 6% of the time, Pallas kernels for 4%

profile of v2, /device:TPU:192, one launch (start us, length us, event | category | flops | bytes accessed | tf_op | source)
XLA Modules:
  0.0 185.6 jit_solution(14932674153773569336)
XLA Ops:
  7.3 0.9 copy-done.2
  8.4 1.8 broadcast_in_dim.7
  10.2 7.2 %all-to-all-start = ((bf16[16,64,1152]{2,1,0:T(8,128)(2,1)}), bf16[16,64,1152]{2,1,0:T(8,128)(2,1)S(1)}, u32[]{:S(2)}, u32[]{:S(2)}) async-start(bf16[16,64,1152]{2,1,0:T(8,128)(2,1)} %broadcast_in_dim.7), calls=%async_computation | async-start | bytes 4718592 | tf_op jit(solution)/shard_map/all_to_all | solution.py:39
  18.3 35.5 %all-to-all-done = bf16[16,64,1152]{2,1,0:T(8,128)(2,1)S(1)} async-done(((bf16[16,64,1152]{2,1,0:T(8,128)(2,1)}), bf16[16,64,1152]{2,1,0:T(8,128)(2,1)S(1)}, u32[]{:S(2)}, u32[]{:S(2)}) %all-to-all-start) | async-done | bytes 2359328 | tf_op jit(solution)/shard_map/all_to_all | solution.py:39
  53.8 1.0 shard_map.65
  54.8 1.9 %collective-permute-start = (bf16[144,1024]{1,0:T(8,128)(2,1)S(1)}, bf16[144,1024]{1,0:T(8,128)(2,1)S(1)}, u32[]{:S(2)}, u32[]{:S(2)}) collective-permute-start(bf16[144,1024]{1,0:T(8,128)(2,1)S(1)} %get-tuple-element.15.own_ref), channel_id=1, source_target_pairs={{0,16},{16,0},{32,48},{48,32},{64,80},{80,64},{96,112},{112,96},{1... | collective-permute-start | bytes 884744 | tf_op jit(solution)/shard_map/ppermute | solution.py:14
  56.7 1.9 %collective-permute-start.1 = (bf16[144,1024]{1,0:T(8,128)(2,1)S(1)}, bf16[144,1024]{1,0:T(8,128)(2,1)S(1)}, u32[]{:S(2)}, u32[]{:S(2)}) collective-permute-start(bf16[144,1024]{1,0:T(8,128)(2,1)S(1)} %get-tuple-element.15.own_ref), channel_id=1, source_target_pairs={{0,64},{16,80},{32,96},{48,112},{64,0},{80,16},{96,32},{112,48},{1... | collective-permute-start | bytes 884744 | tf_op jit(solution)/shard_map/ppermute | solution.py:14
  58.7 13.5 %collective-permute-done.1.refs_1_ = bf16[144,1024]{1,0:T(8,128)(2,1)S(1)} collective-permute-done((bf16[144,1024]{1,0:T(8,128)(2,1)S(1)}, bf16[144,1024]{1,0:T(8,128)(2,1)S(1)}, u32[]{:S(2)}, u32[]{:S(2)}) %collective-permute-start.1) | collective-permute-done | bytes 294944 | tf_op jit(solution)/shard_map/ppermute | solution.py:14
  72.2 6.7 %shard_map.66 = (f32[1024,72]{1,0:T(8,128)S(1)}, f32[1024,128]{1,0:T(8,128)S(1)}) custom-call(s32[3]{0:T(128)S(1)} %bitcast.33, bf16[1024,72]{1,0:T(8,128)(2,1)S(1)} %get-tuple-element.14.query_ref, bf16[144,1024]{1,0:T(8,128)(2,1)S(1)} %get-tuple-element.15.own_ref, bf16[144,1024]{1,0:T(8,128)(2,1)S(1)} %collective-permute-done.refs_0_, ...), custom_call_target="tpu_custom_call" | custom-call | flops 3221225472 | bytes 884736 | tf_op jit(solution)/shard_map/pallas_call | solution.py:165
  81.1 5.7 %all-gather.3.cloned.1.call-done = bf16[1,1152,576]{2,1,0:T(8,128)(2,1)} async-done(((bf16[1,72,576]{2,1,0:T(8,128)(2,1)}), bf16[1,1152,576]{2,1,0:T(8,128)(2,1)}) %all-gather.3.cloned.1.call-update) | async-done | bytes 1327120 | tf_op jit(solution)/shard_map/all_gather | solution.py:206
  86.8 2.6 %copy.13 = bf16[1152,576]{0,1:T(8,128)(2,1)} copy(bf16[1152,576]{1,0:T(8,128)(2,1)} %bitcast.35) | data formatting | bytes 2654208 | tf_op jit(solution)/shard_map/optimization_barrier | solution.py:234
  89.4 1.9 %collective-permute-start.3 = (bf16[1152,576]{0,1:T(8,128)(2,1)}, bf16[1152,576]{0,1:T(8,128)(2,1)}, u32[]{:S(2)}, u32[]{:S(2)}) collective-permute-start(bf16[1152,576]{0,1:T(8,128)(2,1)} %copy.13), channel_id=1, source_target_pairs={{0,16},{16,0},{32,48},{48,32},{64,80},{80,64},{96,112},{112,96},{1... | collective-permute-start | bytes 3981320 | tf_op jit(solution)/shard_map/ppermute | solution.py:14
  91.4 6.2 %collective-permute-start.2 = (bf16[64,1152]{1,0:T(8,128)(2,1)S(1)}, bf16[64,1152]{1,0:T(8,128)(2,1)S(1)}, u32[]{:S(2)}, u32[]{:S(2)}) collective-permute-start(bf16[64,1152]{1,0:T(8,128)(2,1)S(1)} %shard_map.64), channel_id=1, source_target_pairs={{0,256},{16,272},{32,288},{48,304},{64,320},{80,336},{96,352},{112... | collective-permute-start | bytes 442376 | tf_op jit(solution)/shard_map/ppermute | solution.py:14
  97.6 19.9 %collective-permute-done.2 = bf16[64,1152]{1,0:T(8,128)(2,1)S(1)} collective-permute-done((bf16[64,1152]{1,0:T(8,128)(2,1)S(1)}, bf16[64,1152]{1,0:T(8,128)(2,1)S(1)}, u32[]{:S(2)}, u32[]{:S(2)}) %collective-permute-start.2) | collective-permute-done | bytes 147488 | tf_op jit(solution)/shard_map/ppermute | solution.py:14
  117.5 1.8 broadcast_in_dim.8
  119.2 5.0 %all-to-all-start.1 = ((bf16[16,64,1152]{2,1,0:T(8,128)(2,1)}), bf16[16,64,1152]{2,1,0:T(8,128)(2,1)S(1)}, u32[]{:S(2)}, u32[]{:S(2)}) async-start(bf16[16,64,1152]{2,1,0:T(8,128)(2,1)} %broadcast_in_dim.8), calls=%async_computation.1 | async-start | bytes 4718592 | tf_op jit(solution)/shard_map/all_to_all | solution.py:39
  124.3 2.6 %copy.14 = bf16[1152,576]{1,0:T(8,128)(2,1)} copy(bf16[1152,576]{0,1:T(8,128)(2,1)} %collective-permute-done.3) | data formatting | bytes 2654208 | tf_op jit(solution)/shard_map/ppermute | solution.py:14
  126.9 3.5 %maximum_select_fusion = bf16[2,1152,576]{2,1,0:T(8,128)(2,1)S(1)} fusion(bf16[1,1152,576]{2,1,0:T(8,128)(2,1)} %bitcast.36, bf16[1,1152,576]{2,1,0:T(8,128)(2,1)} %all-gather.3.cloned.1.call-done, pred[]{:T(512)S(6)} %eq.6), kind=kLoop, calls=%fused_computation | loop fusion | flops 3981312 | bytes 5308417 | tf_op jit(solution)/shard_map/jit(_where)/select_n | solution.py:212
  130.7 2.4 %pad_maximum_fusion = bf16[16,72,1152]{2,1,0:T(8,128)(2,1)} fusion(bf16[16,72,576]{2,1,0:T(8,128)(2,1)S(1)} %bitcast.38, bf16[16,72,576]{2,1,0:T(8,128)(2,1)S(1)} %bitcast.37), kind=kLoop, calls=%fused_computation.1 | loop fusion | flops 5308416 | bytes 5308416 | tf_op jit(solution)/shard_map/concatenate | solution.py:213
  133.0 27.1 %all-to-all-done.1 = bf16[16,64,1152]{2,1,0:T(8,128)(2,1)S(1)} async-done(((bf16[16,64,1152]{2,1,0:T(8,128)(2,1)}), bf16[16,64,1152]{2,1,0:T(8,128)(2,1)S(1)}, u32[]{:S(2)}, u32[]{:S(2)}) %all-to-all-start.1) | async-done | bytes 2359328 | tf_op jit(solution)/shard_map/all_to_all | solution.py:39
  160.1 0.9 shard_map.67.refs_0_
  161.3 4.0 %shard_map.68 = bf16[1024,72]{1,0:T(8,128)(2,1)S(1)} custom-call(s32[3]{0:T(128)S(1)} %bitcast.34, bf16[1024,72]{1,0:T(8,128)(2,1)S(1)} %copy-done.4, f32[1024,72]{1,0:T(8,128)S(1)} %copy-done.7, f32[1024,128]{1,0:T(8,128)S(1)} %copy-done.9, bf16[144,1024]{1,0:T(8,128)(2,1)S(1)} %shard_map.67.refs_0_), custom_call_target="tpu_custom_call" | custom-call | flops 1073741824 | bytes 294912 | tf_op jit(solution)/shard_map/pallas_call | solution.py:165
  165.4 12.1 %all_to_all.15 = bf16[16,64,72]{2,1,0:T(8,128)(2,1)S(1)} all-to-all(bf16[16,64,72]{2,1,0:T(8,128)(2,1)S(1)} %bitcast.31), channel_id=1, replica_groups=mesh['view'=32,'head'=16] {'head'}, dimensions={0} | all-to-all | bytes 294912 | tf_op jit(solution)/shard_map/all_to_all | solution.py:239
  177.4 1.3 fusion.1
  (33 shorter events, 4.7 us)
Async XLA Ops:
  6.5 10.9 %copy-start = (bf16[1,72,1152]{2,1,0:T(8,128)(2,1)S(1)}, bf16[1,72,1152]{2,1,0:T(8,128)(2,1)}, u32[]{:S(2)}) copy-start(bf16[1,72,1152]{2,1,0:T(8,128)(2,1)} %param.10) | copy-start | bytes 497668
  7.3 0.9 copy-start.2
  10.2 8.0 %copy-start.11 = (f32[1,2,72]{2,1,0:T(2,128)S(1)}, f32[1,2,72]{2,1,0:T(2,128)}, u32[]{:S(2)}) copy-start(f32[1,2,72]{2,1,0:T(2,128)} %param.9) | copy-start | bytes 1732
  10.2 43.6 %copy-start.1 = (bf16[1,216,1152]{2,1,0:T(8,128)(2,1)S(1)}, bf16[1,216,1152]{2,1,0:T(8,128)(2,1)}, u32[]{:S(2)}) copy-start(bf16[1,216,1152]{2,1,0:T(8,128)(2,1)} %param.8) | copy-start | bytes 1492996
  10.2 43.6 %all-to-all-start = ((bf16[16,64,1152]{2,1,0:T(8,128)(2,1)}), bf16[16,64,1152]{2,1,0:T(8,128)(2,1)S(1)}, u32[]{:S(2)}, u32[]{:S(2)}) async-start(bf16[16,64,1152]{2,1,0:T(8,128)(2,1)} %broadcast_in_dim.7), calls=%async_computation | async-start | bytes 4718592 | tf_op jit(solution)/shard_map/all_to_all | solution.py:39
  17.3 54.8 %copy-start.5 = (s32[3,1]{0,1:T(1,128)S(1)}, s32[3,1]{0,1:T(1,128)}, u32[]{:S(2)}) copy-start(s32[3,1]{0,1:T(1,128)} %param.11) | copy-start | bytes 40
  17.4 69.5 %all-gather.3.cloned.1.call-start = ((), (), s32[]{:S(2)}) async-start(), calls=%async_computation.3 | async-start | bytes 1566720 | tf_op jit(solution)/shard_map/all_gather | solution.py:206
  54.8 3.8 %collective-permute-start = (bf16[144,1024]{1,0:T(8,128)(2,1)S(1)}, bf16[144,1024]{1,0:T(8,128)(2,1)S(1)}, u32[]{:S(2)}, u32[]{:S(2)}) collective-permute-start(bf16[144,1024]{1,0:T(8,128)(2,1)S(1)} %get-tuple-element.15.own_ref), channel_id=1, source_target_pairs={{0,16},{16,0},{32,48},{48,32},{64,80},{80,64},{96,112},{112,96},{1... | collective-permute-start | bytes 884744 | tf_op jit(solution)/shard_map/ppermute | solution.py:14
  56.7 15.4 %collective-permute-start.1 = (bf16[144,1024]{1,0:T(8,128)(2,1)S(1)}, bf16[144,1024]{1,0:T(8,128)(2,1)S(1)}, u32[]{:S(2)}, u32[]{:S(2)}) collective-permute-start(bf16[144,1024]{1,0:T(8,128)(2,1)S(1)} %get-tuple-element.15.own_ref), channel_id=1, source_target_pairs={{0,64},{16,80},{32,96},{48,112},{64,0},{80,16},{96,32},{112,48},{1... | collective-permute-start | bytes 884744 | tf_op jit(solution)/shard_map/ppermute | solution.py:14
  78.8 0.7 copy-start.3
  79.5 0.8 copy-start.6
  80.3 0.8 copy-start.8
  89.4 34.8 %collective-permute-start.3 = (bf16[1152,576]{0,1:T(8,128)(2,1)}, bf16[1152,576]{0,1:T(8,128)(2,1)}, u32[]{:S(2)}, u32[]{:S(2)}) collective-permute-start(bf16[1152,576]{0,1:T(8,128)(2,1)} %copy.13), channel_id=1, source_target_pairs={{0,16},{16,0},{32,48},{48,32},{64,80},{80,64},{96,112},{112,96},{1... | collective-permute-start | bytes 3981320 | tf_op jit(solution)/shard_map/ppermute | solution.py:14
  91.4 26.1 %collective-permute-start.2 = (bf16[64,1152]{1,0:T(8,128)(2,1)S(1)}, bf16[64,1152]{1,0:T(8,128)(2,1)S(1)}, u32[]{:S(2)}, u32[]{:S(2)}) collective-permute-start(bf16[64,1152]{1,0:T(8,128)(2,1)S(1)} %shard_map.64), channel_id=1, source_target_pairs={{0,256},{16,272},{32,288},{48,304},{64,320},{80,336},{96,352},{112... | collective-permute-start | bytes 442376 | tf_op jit(solution)/shard_map/ppermute | solution.py:14
  119.2 40.9 %all-to-all-start.1 = ((bf16[16,64,1152]{2,1,0:T(8,128)(2,1)}), bf16[16,64,1152]{2,1,0:T(8,128)(2,1)S(1)}, u32[]{:S(2)}, u32[]{:S(2)}) async-start(bf16[16,64,1152]{2,1,0:T(8,128)(2,1)} %broadcast_in_dim.8), calls=%async_computation.1 | async-start | bytes 4718592 | tf_op jit(solution)/shard_map/all_to_all | solution.py:39
  133.0 28.0 %copy-start.4 = (bf16[1024,72]{1,0:T(8,128)(2,1)S(1)}, bf16[1024,72]{1,0:T(8,128)(2,1)}, u32[]{:S(2)}) copy-start(bf16[1024,72]{1,0:T(8,128)(2,1)} %copy-done.3) | copy-start | bytes 442372
  160.1 1.0 copy-start.7
  160.1 1.2 copy-start.9
  161.3 16.1 %copy-start.10 = (bf16[16,72,1152]{2,1,0:T(8,128)(2,1)S(1)}, bf16[16,72,1152]{2,1,0:T(8,128)(2,1)}, u32[]{:S(2)}) copy-start(bf16[16,72,1152]{2,1,0:T(8,128)(2,1)} %pad_maximum_fusion) | copy-start | bytes 7962628
Sparse Core Ops, SparseCore 0:
  21.2 65.5 all-gather.2

commit v3 on v2

--- a/solution.py
+++ b/solution.py
@@ -206,11 +206,22 @@
     return lax.all_gather(mine, "head", axis=0, tiled=True)
 
 
-def swap_halves(mine):
+def project_out(token_rows, mine):
     core = lax.axis_index("view") % 2
+    heads, loc_len, head_dim = token_rows.shape
+    mine = mine.reshape(heads, head_dim, -1)
     other = partner(mine, 0)
-    pair = jnp.where(core == 0, jnp.stack([mine, other]), jnp.stack([other, mine]))
-    return jnp.concatenate([pair[0], pair[1]], axis=1)
+    halves = [
+        jnp.einsum("hte,hed->td", token_rows, part, preferred_element_type=jnp.float32)
+        for part in (mine, other)
+    ]
+    halves = [part.astype(jnp.bfloat16) for part in halves]
+    first, second = halves
+    return jnp.where(
+        core == 0,
+        jnp.concatenate([first, second], axis=1),
+        jnp.concatenate([second, first], axis=1),
+    )
 
 
 def on_device(latents, norm_gain, qkv_weight, qk_gain, out_weight, intersection):
@@ -226,21 +237,19 @@
     normed = normalize(rows, norm_gain)
     far_normed = partner(normed, bits[-1])
     every = gather_tokens(normed)
+    far_every = gather_tokens(far_normed)
     query, own = project(every, weight, gain, True)
     near = [partner(own, bit) for bit in bits[:-1]]
-    far_every = gather_tokens(far_normed)
-    out_half = gather_out_half(out_weight[0])
     own_result, state = attend_near(active, query, own, near)
-    out_half, own_result, state = lax.optimization_barrier((out_half, own_result, state))
-    full_out = swap_halves(out_half).reshape(-1, head_dim, width)
-    far_every, full_out = lax.optimization_barrier((far_every, full_out))
+    far_every, own_result, state = lax.optimization_barrier((far_every, own_result, state))
     far = list(project(far_every, weight[head_dim:], gain, False))
     attended = attend_last(active, rounds - 1, query, own_result, state, far)
+    out_half, attended = lax.optimization_barrier((gather_out_half(out_weight[0]), attended))
     token_rows = lax.all_to_all(
         attended.reshape(-1, loc_len, head_dim), "head", split_axis=0, concat_axis=0, tiled=True
     )
-    mixed = jnp.einsum("hte,hed->td", token_rows, full_out, preferred_element_type=jnp.float32)
-    return mixed.astype(jnp.bfloat16).reshape(loc_len, view_dev, width)
+    mixed = project_out(token_rows, out_half)
+    return mixed.reshape(loc_len, view_dev, width)
 
 
 def solution(mesh):

time: 186 us -> 131 us (0.70)
  the two profiles are of different devices: /device:TPU:192 before, /device:TPU:448 now
where the time goes in v3:
time: 131 us; the launch traced here: 130 us
  waiting for transfers between devices  64.4 us (49%)
  starting transfers between devices  27.8 us (21%)
  Pallas kernels  15.2 us (12%)
  between operations  13.6 us (10%)
  local copies, waits for them, and re-layouts  6 us (5%)
  matrix products  2.27 us (2%)
    ppermute x4, waiting for transfers between devices, partner(): lax.ppermute(array, 'view', [(i, i ^ 1 << bit) for i in range(lax.axis_si...  32.3 us
    all_to_all x2, waiting for transfers between devices, gather_tokens(): lax.all_to_all(copies, 'head', split_axis=0, concat_axis=0, tiled=True)  22.4 us
    ppermute x4, starting transfers between devices, partner(): lax.ppermute(array, 'view', [(i, i ^ 1 << bit) for i in range(lax.axis_si...  12.6 us
    all_to_all x2, starting transfers between devices, gather_tokens(): lax.all_to_all(copies, 'head', split_axis=0, concat_axis=0, tiled=True)  11.6 us
    pallas_call x2, Pallas kernels, call_attend(): pl.pallas_call(kernel, out_shape=out_shape, in_specs=[pl.BlockSpec(memory...  11.4 us
    all_to_all x1, waiting for transfers between devices, on_device(): lax.all_to_all(attended.reshape(-1, loc_len, head_dim), 'head', split_axi...  9.58 us
    pallas_call x2, Pallas kernels, project(): pl.pallas_call(functools.partial(project_kernel, with_query), out_shape=o...  3.63 us
    all_to_all x1, starting transfers between devices, on_device(): lax.all_to_all(attended.reshape(-1, loc_len, head_dim), 'head', split_axi...  3.54 us
  transfers between devices with their start and end apart: 8, of which 5 were waited for; matrix products, arithmetic and copies ran while one was open for 3% of the time, Pallas kernels for 12%

profile of v3, /device:TPU:448, one launch (start us, length us, event | category | flops | bytes accessed | tf_op | source)
XLA Modules:
  0.0 130.0 jit_solution(17993067179922141063)
XLA Ops:
  6.5 0.7 broadcast_in_dim.6.gain_ref
  7.3 0.9 copy-done.2
  8.4 1.7 %broadcast_in_dim.7 = bf16[16,64,1152]{2,1,0:T(8,128)(2,1)} broadcast(bf16[64,1152]{1,0:T(8,128)(2,1)S(1)} %shard_map.64), dimensions={1,2} | broadcast | bytes 2506752 | tf_op jit(solution)/shard_map/broadcast_in_dim | solution.py:38
  10.1 7.0 %all-to-all-start = ((bf16[16,64,1152]{2,1,0:T(8,128)(2,1)}), bf16[16,64,1152]{2,1,0:T(8,128)(2,1)S(1)}, u32[]{:S(2)}, u32[]{:S(2)}) async-start(bf16[16,64,1152]{2,1,0:T(8,128)(2,1)} %broadcast_in_dim.7), calls=%async_computation | async-start | bytes 4718592 | tf_op jit(solution)/shard_map/all_to_all | solution.py:39
  17.2 5.4 %collective-permute-start = (bf16[64,1152]{1,0:T(8,128)(2,1)S(1)}, bf16[64,1152]{1,0:T(8,128)(2,1)S(1)}, u32[]{:S(2)}, u32[]{:S(2)}) collective-permute-start(bf16[64,1152]{1,0:T(8,128)(2,1)S(1)} %shard_map.64), channel_id=1, source_target_pairs={{0,256},{16,272},{32,288},{48,304},{64,320},{80,336},{96,352},{112... | collective-permute-start | bytes 442376 | tf_op jit(solution)/shard_map/ppermute | solution.py:14
  22.7 0.7 constant_dynamic-slice_fusion
  23.5 19.1 %collective-permute-done = bf16[64,1152]{1,0:T(8,128)(2,1)S(1)} collective-permute-done((bf16[64,1152]{1,0:T(8,128)(2,1)S(1)}, bf16[64,1152]{1,0:T(8,128)(2,1)S(1)}, u32[]{:S(2)}, u32[]{:S(2)}) %collective-permute-start) | collective-permute-done | bytes 147488 | tf_op jit(solution)/shard_map/ppermute | solution.py:14
  42.6 11.0 %all-to-all-done = bf16[16,64,1152]{2,1,0:T(8,128)(2,1)S(1)} async-done(((bf16[16,64,1152]{2,1,0:T(8,128)(2,1)}), bf16[16,64,1152]{2,1,0:T(8,128)(2,1)S(1)}, u32[]{:S(2)}, u32[]{:S(2)}) %all-to-all-start) | async-done | bytes 2359328 | tf_op jit(solution)/shard_map/all_to_all | solution.py:39
  53.6 1.7 %broadcast_in_dim.8 = bf16[16,64,1152]{2,1,0:T(8,128)(2,1)} broadcast(bf16[64,1152]{1,0:T(8,128)(2,1)S(1)} %collective-permute-done), dimensions={1,2} | broadcast | bytes 2506752 | tf_op jit(solution)/shard_map/broadcast_in_dim | solution.py:38
  55.3 4.6 %all-to-all-start.1 = ((bf16[16,64,1152]{2,1,0:T(8,128)(2,1)}), bf16[16,64,1152]{2,1,0:T(8,128)(2,1)}, u32[]{:S(2)}, u32[]{:S(2)}) async-start(bf16[16,64,1152]{2,1,0:T(8,128)(2,1)} %broadcast_in_dim.8), calls=%async_computation.1 | async-start | bytes 4718592 | tf_op jit(solution)/shard_map/all_to_all | solution.py:39
  60.0 1.0 shard_map.65
  61.1 1.9 %collective-permute-start.1 = (bf16[144,1024]{1,0:T(8,128)(2,1)S(1)}, bf16[144,1024]{1,0:T(8,128)(2,1)S(1)}, u32[]{:S(2)}, u32[]{:S(2)}) collective-permute-start(bf16[144,1024]{1,0:T(8,128)(2,1)S(1)} %get-tuple-element.15.own_ref), channel_id=1, source_target_pairs={{0,16},{16,0},{32,48},{48,32},{64,80},{80,64},{96,112},{112,96},{1... | collective-permute-start | bytes 884744 | tf_op jit(solution)/shard_map/ppermute | solution.py:14
  63.0 3.4 %collective-permute-start.2 = (bf16[144,1024]{1,0:T(8,128)(2,1)S(1)}, bf16[144,1024]{1,0:T(8,128)(2,1)S(1)}, u32[]{:S(2)}, u32[]{:S(2)}) collective-permute-start(bf16[144,1024]{1,0:T(8,128)(2,1)S(1)} %get-tuple-element.15.own_ref), channel_id=1, source_target_pairs={{0,64},{16,80},{32,96},{48,112},{64,0},{80,16},{96,32},{112,48},{1... | collective-permute-start | bytes 884744 | tf_op jit(solution)/shard_map/ppermute | solution.py:14
  66.4 13.2 %collective-permute-done.2.refs_1_ = bf16[144,1024]{1,0:T(8,128)(2,1)S(1)} collective-permute-done((bf16[144,1024]{1,0:T(8,128)(2,1)S(1)}, bf16[144,1024]{1,0:T(8,128)(2,1)S(1)}, u32[]{:S(2)}, u32[]{:S(2)}) %collective-permute-start.2) | collective-permute-done | bytes 294944 | tf_op jit(solution)/shard_map/ppermute | solution.py:14
  79.6 6.7 %shard_map.66 = (f32[1024,72]{1,0:T(8,128)S(1)}, f32[1024,128]{1,0:T(8,128)S(1)}) custom-call(s32[3]{0:T(128)S(1)} %bitcast.38, bf16[1024,72]{1,0:T(8,128)(2,1)S(1)} %get-tuple-element.14.query_ref, bf16[144,1024]{1,0:T(8,128)(2,1)S(1)} %get-tuple-element.15.own_ref, bf16[144,1024]{1,0:T(8,128)(2,1)S(1)} %collective-permute-done.1.refs_0_, ...), custom_call_target="tpu_custom_call" | custom-call | flops 3221225472 | bytes 884736 | tf_op jit(solution)/shard_map/pallas_call | solution.py:165
  86.2 11.5 %all-to-all-done.1 = bf16[16,64,1152]{2,1,0:T(8,128)(2,1)} async-done(((bf16[16,64,1152]{2,1,0:T(8,128)(2,1)}), bf16[16,64,1152]{2,1,0:T(8,128)(2,1)}, u32[]{:S(2)}, u32[]{:S(2)}) %all-to-all-start.1) | async-done | bytes 2359328 | tf_op jit(solution)/shard_map/all_to_all | solution.py:39
  97.7 2.6 %shard_map.67.refs_0_ = bf16[144,1024]{1,0:T(8,128)(2,1)S(1)} custom-call(bf16[1024,1152]{1,0:T(8,128)(2,1)} %bitcast.7.rows_ref, bf16[144,1152]{1,0:T(8,128)(2,1)S(1)} %slice_bitcast_fusion.weight_ref, f32[72,2]{1,0:T(8,128)S(1)} %bitcast.36), custom_call_target="tpu_custom_call" | custom-call | flops 339738624 | bytes 2359296 | tf_op jit(solution)/shard_map/pallas_call | solution.py:69
  100.3 4.7 %shard_map.68 = bf16[1024,72]{1,0:T(8,128)(2,1)} custom-call(s32[3]{0:T(128)S(1)} %bitcast.39, bf16[1024,72]{1,0:T(8,128)(2,1)S(1)} %get-tuple-element.14.query_ref, f32[1024,72]{1,0:T(8,128)S(1)} %get-tuple-element.18.own_in_ref, f32[1024,128]{1,0:T(8,128)S(1)} %get-tuple-element.19.state_ref, bf16[144,1024]{1,0:T(8,128)(2,1)S(1)} %shard_map.67.refs_0_), custom_call_target="tpu_custom_call" | custom-call | flops 1073741824 | bytes 294912 | tf_op jit(solution)/shard_map/pallas_call | solution.py:165
  105.1 1.9 %collective-permute-start.3 = (bf16[16,72,576]{2,1,0:T(8,128)(2,1)}, bf16[16,72,576]{2,1,0:T(8,128)(2,1)S(1)}, u32[]{:S(2)}, u32[]{:S(2)}) collective-permute-start(bf16[16,72,576]{2,1,0:T(8,128)(2,1)} %bitcast.40), channel_id=1, source_target_pairs={{0,16},{16,0},{32,48},{48,32},{64,80},{80,64},{96,112},{112,96},{1... | collective-permute-start | bytes 3981320 | tf_op jit(solution)/shard_map/ppermute | solution.py:14
  107.0 3.5 %all-to-all-start.2 = ((bf16[16,64,72]{2,1,0:T(8,128)(2,1)}), bf16[16,64,72]{2,1,0:T(8,128)(2,1)S(1)}, u32[]{:S(2)}, u32[]{:S(2)}) async-start(bf16[16,64,72]{2,1,0:T(8,128)(2,1)} %bitcast.10), calls=%async_computation.2 | async-start | bytes 524288 | tf_op jit(solution)/shard_map/all_to_all | solution.py:248
  110.5 9.6 %all-to-all-done.2 = bf16[16,64,72]{2,1,0:T(8,128)(2,1)S(1)} async-done(((bf16[16,64,72]{2,1,0:T(8,128)(2,1)}), bf16[16,64,72]{2,1,0:T(8,128)(2,1)S(1)}, u32[]{:S(2)}, u32[]{:S(2)}) %all-to-all-start.2) | async-done | bytes 147488 | tf_op jit(solution)/shard_map/all_to_all | solution.py:248
  120.1 1.8 %fusion.3 = bf16[64,1,576]{2,0,1:T(8,128)(2,1)S(1)} fusion(bf16[16,64,72]{2,1,0:T(8,128)(2,1)S(1)} %all-to-all-done.2, bf16[16,72,576]{2,1,0:T(8,128)(2,1)} %bitcast.41), kind=kOutput, calls=%fused_computation.5 | convolution fusion | flops 84971520 | bytes 1548288 | tf_op jit(solution)/shard_map/hte,hed->td/dot_general | solution.py:215
  121.9 0.4 fusion.2
  122.4 0.8 maximum_select_fusion
  (17 shorter events, 0.4 us)
Async XLA Ops:
  6.5 16.2 %copy-start = (bf16[1,72,1152]{2,1,0:T(8,128)(2,1)S(1)}, bf16[1,72,1152]{2,1,0:T(8,128)(2,1)}, u32[]{:S(2)}) copy-start(bf16[1,72,1152]{2,1,0:T(8,128)(2,1)} %param.10) | copy-start | bytes 497668
  7.3 0.9 copy-start.2
  10.1 43.4 %all-to-all-start = ((bf16[16,64,1152]{2,1,0:T(8,128)(2,1)}), bf16[16,64,1152]{2,1,0:T(8,128)(2,1)S(1)}, u32[]{:S(2)}, u32[]{:S(2)}) async-start(bf16[16,64,1152]{2,1,0:T(8,128)(2,1)} %broadcast_in_dim.7), calls=%async_computation | async-start | bytes 4718592 | tf_op jit(solution)/shard_map/all_to_all | solution.py:39
  17.2 87.9 %all-gather.3.cloned.1.call-start = ((), (), s32[]{:S(2)}) async-start(), calls=%async_computation.3 | async-start | bytes 1566720 | tf_op jit(solution)/shard_map/all_gather | solution.py:206
  17.2 25.4 %collective-permute-start = (bf16[64,1152]{1,0:T(8,128)(2,1)S(1)}, bf16[64,1152]{1,0:T(8,128)(2,1)S(1)}, u32[]{:S(2)}, u32[]{:S(2)}) collective-permute-start(bf16[64,1152]{1,0:T(8,128)(2,1)S(1)} %shard_map.64), channel_id=1, source_target_pairs={{0,256},{16,272},{32,288},{48,304},{64,320},{80,336},{96,352},{112... | collective-permute-start | bytes 442376 | tf_op jit(solution)/shard_map/ppermute | solution.py:14
  55.3 4.6 %copy-start.4 = (f32[1,2,72]{2,1,0:T(2,128)S(1)}, f32[1,2,72]{2,1,0:T(2,128)}, u32[]{:S(2)}) copy-start(f32[1,2,72]{2,1,0:T(2,128)} %param.9) | copy-start | bytes 1732
  55.3 4.7 %copy-start.1 = (bf16[1,216,1152]{2,1,0:T(8,128)(2,1)S(1)}, bf16[1,216,1152]{2,1,0:T(8,128)(2,1)}, u32[]{:S(2)}) copy-start(bf16[1,216,1152]{2,1,0:T(8,128)(2,1)} %param.8) | copy-start | bytes 1492996
  55.3 42.4 %all-to-all-start.1 = ((bf16[16,64,1152]{2,1,0:T(8,128)(2,1)}), bf16[16,64,1152]{2,1,0:T(8,128)(2,1)}, u32[]{:S(2)}, u32[]{:S(2)}) async-start(bf16[16,64,1152]{2,1,0:T(8,128)(2,1)} %broadcast_in_dim.8), calls=%async_computation.1 | async-start | bytes 4718592 | tf_op jit(solution)/shard_map/all_to_all | solution.py:39
  60.0 19.6 %copy-start.3 = (s32[3,1]{0,1:T(1,128)S(1)}, s32[3,1]{0,1:T(1,128)}, u32[]{:S(2)}) copy-start(s32[3,1]{0,1:T(1,128)} %param.11) | copy-start | bytes 40
  61.1 5.3 %collective-permute-start.1 = (bf16[144,1024]{1,0:T(8,128)(2,1)S(1)}, bf16[144,1024]{1,0:T(8,128)(2,1)S(1)}, u32[]{:S(2)}, u32[]{:S(2)}) collective-permute-start(bf16[144,1024]{1,0:T(8,128)(2,1)S(1)} %get-tuple-element.15.own_ref), channel_id=1, source_target_pairs={{0,16},{16,0},{32,48},{48,32},{64,80},{80,64},{96,112},{112,96},{1... | collective-permute-start | bytes 884744 | tf_op jit(solution)/shard_map/ppermute | solution.py:14
  63.0 16.6 %collective-permute-start.2 = (bf16[144,1024]{1,0:T(8,128)(2,1)S(1)}, bf16[144,1024]{1,0:T(8,128)(2,1)S(1)}, u32[]{:S(2)}, u32[]{:S(2)}) collective-permute-start(bf16[144,1024]{1,0:T(8,128)(2,1)S(1)} %get-tuple-element.15.own_ref), channel_id=1, source_target_pairs={{0,64},{16,80},{32,96},{48,112},{64,0},{80,16},{96,32},{112,48},{1... | collective-permute-start | bytes 884744 | tf_op jit(solution)/shard_map/ppermute | solution.py:14
  105.1 16.9 %collective-permute-start.3 = (bf16[16,72,576]{2,1,0:T(8,128)(2,1)}, bf16[16,72,576]{2,1,0:T(8,128)(2,1)S(1)}, u32[]{:S(2)}, u32[]{:S(2)}) collective-permute-start(bf16[16,72,576]{2,1,0:T(8,128)(2,1)} %bitcast.40), channel_id=1, source_target_pairs={{0,16},{16,0},{32,48},{48,32},{64,80},{80,64},{96,112},{112,96},{1... | collective-permute-start | bytes 3981320 | tf_op jit(solution)/shard_map/ppermute | solution.py:14
  107.0 13.1 %all-to-all-start.2 = ((bf16[16,64,72]{2,1,0:T(8,128)(2,1)}), bf16[16,64,72]{2,1,0:T(8,128)(2,1)S(1)}, u32[]{:S(2)}, u32[]{:S(2)}) async-start(bf16[16,64,72]{2,1,0:T(8,128)(2,1)} %bitcast.10), calls=%async_computation.2 | async-start | bytes 524288 | tf_op jit(solution)/shard_map/all_to_all | solution.py:248
Sparse Core Ops, SparseCore 0:
  23.6 74.0 all-gather.2

commit v4 on v2

v4 whole, which is shorter than its diff:
```python
import functools
import math
import jax
import jax.numpy as jnp
from jax import lax
from jax.experimental import pallas as pl
from jax.experimental.pallas import tpu as pltpu
from jax.sharding import PartitionSpec as P

BLANK = 1e30


def partner(array, bit):
    return lax.ppermute(array, "view", [(i, i ^ 1 << bit) for i in range(lax.axis_size("view"))])


def beside(array):
    return lax.ppermute(array, "head", [(i, i ^ 1) for i in range(lax.axis_size("head"))])


def traded(*arrays):
    views, heads = lax.axis_size("view"), lax.axis_size("head")
    pairs = []
    for view in range(views):
        for head in range(heads):
            if view % 2 != head % 2:
                pairs.append(((view ^ 1) * heads + (head ^ 1), view * heads + head))
    same = lax.axis_index("view") % 2 == lax.axis_index("head") % 2
    return [
        jnp.where(same, array, lax.ppermute(array, ("view", "head"), pairs)) for array in arrays
    ]


def by_core(first, second, axis):
    core = lax.axis_index("view") % 2
    return jnp.where(
        core == 0, jnp.stack([first, second], axis), jnp.stack([second, first], axis)
    )


def normalize_kernel(core_ref, rows_ref, gain_ref, keep_ref, give_ref):
    values = rows_ref[...].astype(jnp.float32)
    mean = jnp.mean(values, axis=-1, keepdims=True)
    centred = values - mean
    var = jnp.mean(centred * centred, axis=-1, keepdims=True)
    normed = centred * lax.rsqrt(var + 1e-06) * gain_ref[...]
    half = normed.shape[0] // 2
    first = core_ref[0] == 0
    keep_ref[...] = jnp.where(first, normed[:half], normed[half:]).astype(jnp.bfloat16)
    give_ref[...] = jnp.where(first, normed[half:], normed[:half]).astype(jnp.bfloat16)


def normalize(core, rows, norm_gain):
    half = jax.ShapeDtypeStruct((rows.shape[0] // 2, rows.shape[1]), jnp.bfloat16)
    vmem = pl.BlockSpec(memory_space=pltpu.VMEM)
    return pl.pallas_call(
        normalize_kernel,
        out_shape=[half, half],
        in_specs=[pl.BlockSpec(memory_space=pltpu.SMEM), vmem, vmem],
        out_specs=[vmem, vmem],
        compiler_params=pltpu.CompilerParams(vmem_limit_bytes=16 << 20),
        cost_estimate=pl.CostEstimate(
            flops=8 * rows.size, bytes_accessed=4 * rows.size, transcendentals=0
        ),
    )(core, rows, norm_gain[None])


def gather_tokens(pair):
    heads = lax.axis_size("head")
    slots = jnp.broadcast_to(pair[None], (heads // 2,) + pair.shape)
    slots = slots.reshape((heads,) + pair.shape[1:])
    rows = lax.all_to_all(slots, "head", split_axis=0, concat_axis=0, tiled=True)
    return rows.reshape(-1, pair.shape[-1])


def rms_rows(part, gain):
    square = jnp.mean(part * part, axis=0, keepdims=True) + 1e-06
    return part * lax.rsqrt(square) * gain


def project_kernel(with_query, mine_ref, other_ref, weight_ref, gain_ref, *out_refs):
    head_dim = gain_ref.shape[0]
    weight = weight_ref[...]
    for n, rows_ref in enumerate((mine_ref, other_ref)):
        tokens = rows_ref.shape[0]
        flat = lax.dot_general(
            weight, rows_ref[...], (((1,), (1,)), ((), ())), preferred_element_type=jnp.float32
        )
        flat = flat.astype(jnp.bfloat16).astype(jnp.float32)
        at = pl.ds(n * tokens, tokens)
        if with_query:
            query = rms_rows(flat[:head_dim], gain_ref[:, 0:1])
            out_refs[0][at, :] = query.T.astype(jnp.bfloat16)
            flat = flat[head_dim:]
        keys = rms_rows(flat[:head_dim], gain_ref[:, 1:2])
        pair = jnp.concatenate([keys, flat[head_dim:]], axis=0)
        out_refs[-1][:, at] = pair.astype(jnp.bfloat16)


def project(mine, other, weight, gain, with_query):
    tokens, width = 2 * mine.shape[0], mine.shape[1]
    head_dim = gain.shape[0]
    out_shape = [jax.ShapeDtypeStruct((2 * head_dim, tokens), jnp.bfloat16)]
    if with_query:
        out_shape = [jax.ShapeDtypeStruct((tokens, head_dim), jnp.bfloat16)] + out_shape
    return pl.pallas_call(
        functools.partial(project_kernel, with_query),
        out_shape=out_shape,
        compiler_params=pltpu.CompilerParams(vmem_limit_bytes=16 << 20),
        cost_estimate=pl.CostEstimate(
            flops=2 * tokens * width * weight.shape[0], bytes_accessed=2 * tokens * width, transcendentals=0
        ),
    )(mine, other, weight, gain)


def scores_of(query, pair_ref):
    head_dim = query.shape[1]
    factor = math.log2(math.e) * float(head_dim) ** (-0.5)
    keys = pair_ref[...][:head_dim]
    return jnp.dot(query, keys, preferred_element_type=jnp.float32) * factor


def weighted(scores, shift, values):
    weights = jnp.exp2(scores - shift).astype(jnp.bfloat16)
    return jnp.dot(weights, values, preferred_element_type=jnp.float32)


def finish(acc, head_dim):
    return acc[:, :head_dim] / jnp.maximum(acc[:, head_dim : head_dim + 1], 1.0)


def spread_values(pair_ref, head_dim, padded):
    part = pair_ref[...].astype(jnp.float32)[head_dim:]
    tokens = part.shape[1]
    lane = lax.broadcasted_iota(jnp.int32, (tokens, padded), 1)
    filled = jnp.concatenate([part, jnp.zeros((padded - head_dim, tokens), jnp.float32)], axis=0)
    return jnp.where(lane == head_dim, 1.0, filled.T).astype(jnp.bfloat16)


def cross_update(active_ref, first, query, far_refs, values_ref, slot, best, acc):
    several = [scores_of(query, ref) for ref in far_refs]
    newbest = best
    for n, scores in enumerate(several):
        most = jnp.max(scores, axis=1, keepdims=True)
        newbest = jnp.where(active_ref[first + n] > 0, jnp.maximum(newbest, most), newbest)
    if acc is not None:
        acc = acc * jnp.exp2(best - newbest)
    for n, scores in enumerate(several):
        shift = jnp.where(active_ref[first + n] > 0, newbest, BLANK)
        term = weighted(scores, shift, values_ref[slot + n])
        acc = term if acc is None else acc + term
    return newbest, acc


def near_kernel(tile, active_ref, query_ref, own_ref, *refs):
    far_refs, own_out_ref, state_ref, values_ref = refs[:-3], refs[-3], refs[-2], refs[-1]
    tokens, head_dim = query_ref.shape
    padded = values_ref.shape[-1]
    for n, ref in enumerate((own_ref,) + far_refs):
        values_ref[n] = spread_values(ref, head_dim, padded)

    def step(at, carry):
        rows = pl.ds(pl.multiple_of(at * tile, tile), tile)
        query = query_ref[rows, :]
        scores = scores_of(query, own_ref)
        acc = weighted(scores, jnp.max(scores, axis=1, keepdims=True), values_ref[0])
        own_out_ref[rows, :] = finish(acc, head_dim)
        start = jnp.full((tile, 1), -BLANK, jnp.float32)
        best, acc = cross_update(active_ref, 0, query, far_refs, values_ref, 1, start, None)
        lane = lax.broadcasted_iota(jnp.int32, (tile, padded), 1)
        state_ref[rows, :] = jnp.where(lane == head_dim + 1, best, acc)
        return carry

    lax.fori_loop(0, tokens // tile, step, 0, unroll=True)


def last_kernel(tile, first, core_ref, active_ref, query_ref, own_in_ref, state_ref, *refs):
    far_refs, out_ref, values_ref = refs[:-2], refs[-2], refs[-1]
    tokens, head_dim = query_ref.shape
    padded = values_ref.shape[-1]
    for n, ref in enumerate(far_refs):
        values_ref[n] = spread_values(ref, head_dim, padded)

    slots, loc_len, _ = out_ref.shape
    half = loc_len // 2
    for at in range(tokens // tile):
        rows = pl.ds(at * tile, tile)
        query = query_ref[rows, :]
        acc = state_ref[rows, :]
        best = acc[:, head_dim + 1 : head_dim + 2]
        best, acc = cross_update(active_ref, first, query, far_refs, values_ref, 0, best, acc)
        result = own_in_ref[rows, :] + finish(acc, head_dim)
        result = result.reshape(tile // half, half, head_dim).astype(jnp.bfloat16)
        second, block = divmod(at * tile // half, slots)
        side = core_ref[0] if second == 0 else 1 - core_ref[0]
        place = pl.ds(pl.multiple_of(side * half, half), half)
        out_ref[pl.ds(block, tile // half), place, :] = result


PADDED = 128


def call_attend(kernel, out_shape, blocks, tokens, head_dim, scalars, arrays):
    smem, vmem = pl.BlockSpec(memory_space=pltpu.SMEM), pl.BlockSpec(memory_space=pltpu.VMEM)
    several = isinstance(out_shape, list)
    return pl.pallas_call(
        kernel,
        out_shape=out_shape,
        in_specs=[smem] * len(scalars) + [vmem] * len(arrays),
        out_specs=[vmem] * len(out_shape) if several else vmem,
        scratch_shapes=[pltpu.VMEM((blocks, tokens, PADDED), jnp.bfloat16)],
        compiler_params=pltpu.CompilerParams(vmem_limit_bytes=24 << 20),
        cost_estimate=pl.CostEstimate(
            flops=blocks * tokens * tokens * head_dim // 4,
            bytes_accessed=4 * blocks * tokens * head_dim,
            transcendentals=0,
        ),
    )(*scalars, *arrays)


def attend_near(active, query, own, far):
    tokens, head_dim = query.shape
    out_shape = [
        jax.ShapeDtypeStruct((tokens, head_dim), jnp.float32),
        jax.ShapeDtypeStruct((tokens, PADDED), jnp.float32),
    ]
    kernel = functools.partial(near_kernel, 256)
    arrays = (query, own, *far)
    return call_attend(kernel, out_shape, 1 + len(far), tokens, head_dim, (active,), arrays)


def attend_last(core, active, first, query, own_result, state, far):
    tokens, head_dim = query.shape
    heads = lax.axis_size("head")
    out_shape = jax.ShapeDtypeStruct((heads, tokens // heads, head_dim), jnp.bfloat16)
    kernel = functools.partial(last_kernel, 256, first)
    arrays = (query, own_result, state, *far)
    return call_attend(kernel, out_shape, len(far), tokens, head_dim, (core, active), arrays)


def return_tokens(attended):
    heads, loc_len, head_dim = attended.shape
    core = lax.axis_index("view") % 2
    came = lax.all_to_all(attended, "head", split_axis=0, concat_axis=0, tiled=True)
    came = came.reshape(heads // 2, 2, loc_len, head_dim)
    mine = jnp.where(core == 0, came[:, 0], came[:, 1])
    other = partner(jnp.where(core == 0, came[:, 1], came[:, 0]), 0)
    return by_core(mine, other, 1).reshape(heads, loc_len, head_dim)


def on_device(latents, norm_gain, qkv_weight, qk_gain, out_weight, intersection):
    loc_len, view_dev, width = latents.shape
    rows = latents.reshape(loc_len, width)
    levels = lax.axis_size("view").bit_length() - 1
    rounds = intersection.shape[0]
    bits = [step * (levels - 1) // (rounds - 1) for step in range(rounds)]
    head_dim = qk_gain.shape[-1]
    core = (lax.axis_index("view") % 2).astype(jnp.int32)[None]
    flags = jnp.broadcast_to(intersection.astype(jnp.float32), (rounds, head_dim))
    weight, small = traded(qkv_weight[0], jnp.concatenate([qk_gain[0], flags], axis=0))
    keep, give = normalize(core, rows, norm_gain)
    pair = by_core(keep, partner(give, 0), 0)
    far_pair = partner(pair, bits[-1])
    mine = gather_tokens(pair)
    mine, far_pair, weight, small = lax.optimization_barrier((mine, far_pair, weight, small))
    gain, active = small[:2].T, small[2:, 0].astype(jnp.int32)
    far_mine = gather_tokens(far_pair)
    query, own = project(mine, partner(mine, 0), weight, gain, True)
    near = beside(own)
    middle = [partner(own, bit) for bit in bits[1:-1]]
    own_result, state = attend_near(active, query, own, [near])
    far_mine, own_result, state, middle = lax.optimization_barrier(
        (far_mine, own_result, state, middle)
    )
    far = list(project(far_mine, partner(far_mine, 0), weight[head_dim:], gain, False))
    attended = attend_last(core, active, 1, query, own_result, state, middle + far)
    full_out = lax.all_gather(out_weight, "head", axis=0, tiled=True)
    full_out, attended = lax.optimization_barrier((full_out, attended))
    token_rows = return_tokens(attended)
    mixed = jnp.einsum("hte,hed->td", token_rows, full_out, preferred_element_type=jnp.float32)
    return mixed.astype(jnp.bfloat16).reshape(loc_len, view_dev, width)


def solution(mesh):
    placed = (
        P("head", "view", None),
        P(),
        P("head", None, None),
        P("head", None, None),
        P("head", None, None),
        P(None, "view"),
    )
    return jax.shard_map(
        on_device, mesh=mesh, in_specs=placed, out_specs=P("head", "view", None), check_vma=False
    )
```

time: 186 us -> 145 us (0.78)
  the two profiles are of different devices: /device:TPU:192 before, /device:TPU:1 now
where the time goes in v4:
time: 145 us; the launch traced here: 144 us
  starting transfers between devices  55.9 us (39%)
  waiting for transfers between devices  40.6 us (28%)
  between operations  13.7 us (9%)
  blocking collectives  12.8 us (9%)
  Pallas kernels  12.6 us (9%)
  local copies, waits for them, and re-layouts  4.92 us (3%)
  matrix products  3.05 us (2%)
    ppermute x6, starting transfers between devices, partner(): lax.ppermute(array, 'view', [(i, i ^ 1 << bit) for i in range(lax.axis_si...  32.8 us
    ppermute x1, waiting for transfers between devices, beside(): lax.ppermute(array, 'head', [(i, i ^ 1) for i in range(lax.axis_size('hea...  19.1 us
    ppermute x2, waiting for transfers between devices, traded(): lax.ppermute(array, ('view', 'head'), pairs)  14.6 us
    all_to_all x2, starting transfers between devices, gather_tokens(): lax.all_to_all(slots, 'head', split_axis=0, concat_axis=0, tiled=True)  14.4 us
    all_to_all x1, blocking collectives, return_tokens(): lax.all_to_all(attended, 'head', split_axis=0, concat_axis=0, tiled=True)  12.8 us
    pallas_call x2, Pallas kernels, call_attend(): pl.pallas_call(kernel, out_shape=out_shape, in_specs=[smem] * len(scalars...  9.19 us
    ppermute x6, waiting for transfers between devices, partner(): lax.ppermute(array, 'view', [(i, i ^ 1 << bit) for i in range(lax.axis_si...  6.08 us
    ppermute x2, starting transfers between devices, traded(): lax.ppermute(array, ('view', 'head'), pairs)  5.45 us
  transfers between devices with their start and end apart: 12, of which 5 were waited for; matrix products, arithmetic and copies ran while one was open for 2% of the time, Pallas kernels for 9%

profile of v4, /device:TPU:1, one launch (start us, length us, event | category | flops | bytes accessed | tf_op | source)
XLA Modules:
  0.0 143.9 jit_solution(8265784661833844400)
XLA Ops:
  9.1 8.8 %collective-permute-start = (bf16[32,1152]{1,0:T(8,128)(2,1)S(1)}, bf16[32,1152]{1,0:T(8,128)(2,1)S(1)}, u32[]{:S(2)}, u32[]{:S(2)}) collective-permute-start(bf16[32,1152]{1,0:T(8,128)(2,1)S(1)} %get-tuple-element.22), channel_id=1, source_target_pairs={{0,16},{16,0},{32,48},{48,32},{64,80},{80,64},{96,112},{112,96},{1... | collective-permute-start | bytes 221192 | tf_op jit(solution)/shard_map/ppermute | solution.py:14
  17.9 1.9 %collective-permute-start.2 = (bf16[216,1152]{1,0:T(8,128)(2,1)}, bf16[216,1152]{1,0:T(8,128)(2,1)S(1)}, u32[]{:S(2)}, u32[]{:S(2)}) collective-permute-start(bf16[216,1152]{1,0:T(8,128)(2,1)} %bitcast.52), channel_id=1, source_target_pairs={{16,1},{18,3},{20,5},{22,7},{24,9},{26,11},{28,13},{30,15},{1,16},... | collective-permute-start | bytes 1493000 | tf_op jit(solution)/shard_map/ppermute | solution.py:30
  19.9 1.1 broadcast_in_dim.27
  21.0 3.8 %all-to-all-start = ((bf16[16,32,1152]{2,1,0:T(8,128)(2,1)}), bf16[16,32,1152]{2,1,0:T(8,128)(2,1)S(1)}, u32[]{:S(2)}, u32[]{:S(2)}) async-start(bf16[16,32,1152]{2,1,0:T(8,128)(2,1)} %bitcast.4), calls=%async_computation | async-start | bytes 2359296 | tf_op jit(solution)/shard_map/all_to_all | solution.py:72
  25.1 3.5 %collective-permute-start.3 = (f32[5,72]{0,1:T(8,128)S(1)}, f32[5,72]{0,1:T(8,128)S(1)}, u32[]{:S(2)}, u32[]{:S(2)}) collective-permute-start(f32[5,72]{0,1:T(8,128)S(1)} %copy.14), channel_id=1, source_target_pairs={{16,1},{18,3},{20,5},{22,7},{24,9},{26,11},{28,13},{30,15},{1,16},... | collective-permute-start | bytes 4328 | tf_op jit(solution)/shard_map/ppermute | solution.py:30
  28.7 14.6 %collective-permute-done.3 = f32[5,72]{0,1:T(8,128)S(1)} collective-permute-done((f32[5,72]{0,1:T(8,128)S(1)}, f32[5,72]{0,1:T(8,128)S(1)}, u32[]{:S(2)}, u32[]{:S(2)}) %collective-permute-start.3) | collective-permute-done | bytes 1472 | tf_op jit(solution)/shard_map/ppermute | solution.py:30
  43.3 12.8 %collective-permute-start.1 = (bf16[2,32,1152]{2,1,0:T(8,128)(2,1)S(1)}, bf16[2,32,1152]{2,1,0:T(8,128)(2,1)S(1)}, u32[]{:S(2)}, u32[]{:S(2)}) collective-permute-start(bf16[2,32,1152]{2,1,0:T(8,128)(2,1)S(1)} %maximum_select_fusion.1), channel_id=1, source_target_pairs={{0,256},{16,272},{32,288},{48,304},{64,320},{80,336},{96,352},{112... | collective-permute-start | bytes 442376 | tf_op jit(solution)/shard_map/ppermute | solution.py:14
  56.2 2.7 %collective-permute-done.1 = bf16[2,32,1152]{2,1,0:T(8,128)(2,1)S(1)} collective-permute-done((bf16[2,32,1152]{2,1,0:T(8,128)(2,1)S(1)}, bf16[2,32,1152]{2,1,0:T(8,128)(2,1)S(1)}, u32[]{:S(2)}, u32[]{:S(2)}) %collective-permute-start.1) | collective-permute-done | bytes 147488 | tf_op jit(solution)/shard_map/ppermute | solution.py:14
  58.9 1.9 %collective-permute-start.4 = (bf16[512,1152]{1,0:T(8,128)(2,1)S(1)}, bf16[512,1152]{1,0:T(8,128)(2,1)}, u32[]{:S(2)}, u32[]{:S(2)}) collective-permute-start(bf16[512,1152]{1,0:T(8,128)(2,1)S(1)} %bitcast.42), channel_id=1, source_target_pairs={{0,16},{16,0},{32,48},{48,32},{64,80},{80,64},{96,112},{112,96},{1... | collective-permute-start | bytes 3538952 | tf_op jit(solution)/shard_map/ppermute | solution.py:14
  60.9 1.1 broadcast_in_dim.30
  62.0 10.6 %all-to-all-start.1 = ((bf16[16,32,1152]{2,1,0:T(8,128)(2,1)}), bf16[16,32,1152]{2,1,0:T(8,128)(2,1)S(1)}, u32[]{:S(2)}, u32[]{:S(2)}) async-start(bf16[16,32,1152]{2,1,0:T(8,128)(2,1)} %bitcast.48), calls=%async_computation.1 | async-start | bytes 2359296 | tf_op jit(solution)/shard_map/all_to_all | solution.py:72
  72.6 2.3 %shard_map.65 = (bf16[1024,72]{1,0:T(8,128)(2,1)S(1)}, bf16[144,1024]{1,0:T(8,128)(2,1)S(1)}) custom-call(bf16[512,1152]{1,0:T(8,128)(2,1)S(1)} %bitcast.43, bf16[512,1152]{1,0:T(8,128)(2,1)} %collective-permute-done.4.other_ref, bf16[216,1152]{1,0:T(8,128)(2,1)S(1)} %broadcast_select_fusion.weight_ref, f32[72,2]{1,0:T(8,128)S(1)} %slice_bitcast_fusion.gain_ref), custom_call_target="tpu_custom_call" | custom-call | flops 509607936 | bytes 2359296 | tf_op jit(solution)/shard_map/pallas_call | solution.py:106
  74.9 3.3 %collective-permute-start.5 = (bf16[144,1024]{1,0:T(8,128)(2,1)S(1)}, bf16[144,1024]{1,0:T(8,128)(2,1)S(1)}, u32[]{:S(2)}, u32[]{:S(2)}) collective-permute-start(bf16[144,1024]{1,0:T(8,128)(2,1)S(1)} %get-tuple-element.28.own_ref), channel_id=1, source_target_pairs={{0,1},{1,0},{2,3},{3,2},{4,5},{5,4},{6,7},{7,6},{8,9},{9,8},{10,11... | collective-permute-start | bytes 884744 | tf_op jit(solution)/shard_map/ppermute | solution.py:18
  78.2 3.3 %collective-permute-start.6 = (bf16[144,1024]{1,0:T(8,128)(2,1)S(1)}, bf16[144,1024]{1,0:T(8,128)(2,1)S(1)}, u32[]{:S(2)}, u32[]{:S(2)}) collective-permute-start(bf16[144,1024]{1,0:T(8,128)(2,1)S(1)} %get-tuple-element.28.own_ref), channel_id=1, source_target_pairs={{0,64},{16,80},{32,96},{48,112},{64,0},{80,16},{96,32},{112,48},{1... | collective-permute-start | bytes 884744 | tf_op jit(solution)/shard_map/ppermute | solution.py:14
  81.5 19.1 %collective-permute-done.5.refs_0_ = bf16[144,1024]{1,0:T(8,128)(2,1)S(1)} collective-permute-done((bf16[144,1024]{1,0:T(8,128)(2,1)S(1)}, bf16[144,1024]{1,0:T(8,128)(2,1)S(1)}, u32[]{:S(2)}, u32[]{:S(2)}) %collective-permute-start.5) | collective-permute-done | bytes 294944 | tf_op jit(solution)/shard_map/ppermute | solution.py:18
  100.6 4.6 %shard_map.66 = (f32[1024,72]{1,0:T(8,128)S(1)}, f32[1024,128]{1,0:T(8,128)S(1)}) custom-call(s32[3]{0:T(128)S(1)} %convert_bitcast_fusion.active_ref, bf16[1024,72]{1,0:T(8,128)(2,1)S(1)} %get-tuple-element.26.query_ref, bf16[144,1024]{1,0:T(8,128)(2,1)S(1)} %get-tuple-element.28.own_ref, bf16[144,1024]{1,0:T(8,128)(2,1)S(1)} %collective-permute-done.5.refs_0_), custom_call_target="tpu_custom_call" | custom-call | flops 37748736 | bytes 589824 | tf_op jit(solution)/shard_map/pallas_call | solution.py:206
  106.0 2.6 %collective-permute-start.7 = (bf16[512,1152]{1,0:T(8,128)(2,1)S(1)}, bf16[512,1152]{1,0:T(8,128)(2,1)S(1)}, u32[]{:S(2)}, u32[]{:S(2)}) collective-permute-start(bf16[512,1152]{1,0:T(8,128)(2,1)S(1)} %bitcast.44), channel_id=1, source_target_pairs={{0,16},{16,0},{32,48},{48,32},{64,80},{80,64},{96,112},{112,96},{1... | collective-permute-start | bytes 3538952 | tf_op jit(solution)/shard_map/ppermute | solution.py:14
  108.6 2.4 %collective-permute-done.7.other_ref = bf16[512,1152]{1,0:T(8,128)(2,1)S(1)} collective-permute-done((bf16[512,1152]{1,0:T(8,128)(2,1)S(1)}, bf16[512,1152]{1,0:T(8,128)(2,1)S(1)}, u32[]{:S(2)}, u32[]{:S(2)}) %collective-permute-start.7) | collective-permute-done | bytes 1179680 | tf_op jit(solution)/shard_map/ppermute | solution.py:14
  111.1 0.9 shard_map.67.refs_1_
  112.0 4.6 %shard_map.68 = bf16[16,64,72]{2,1,0:T(8,128)(2,1)S(1)} custom-call(s32[1]{0:T(128)} %bitcast.core_ref, s32[3]{0:T(128)S(1)} %convert_bitcast_fusion.active_ref, bf16[1024,72]{1,0:T(8,128)(2,1)S(1)} %get-tuple-element.26.query_ref, f32[1024,72]{1,0:T(8,128)S(1)} %get-tuple-element.31.own_in_ref, f32[1024,128]{1,0:T(8,128)S(1)} %copy-done.1, ...), custom_call_target="tpu_custom_call" | custom-call | flops 37748736 | bytes 589824 | tf_op jit(solution)/shard_map/pallas_call | solution.py:206
  116.6 12.8 %all_to_all.15 = bf16[16,64,72]{2,1,0:T(8,128)(2,1)S(1)} all-to-all(bf16[16,64,72]{2,1,0:T(8,128)(2,1)S(1)} %shard_map.68), channel_id=1, replica_groups=mesh['view'=32,'head'=16] {'head'}, dimensions={0} | all-to-all | bytes 294912 | tf_op jit(solution)/shard_map/all_to_all | solution.py:244
  129.4 3.4 %collective-permute-start.8 = (bf16[8,64,72]{2,1,0:T(8,128)(2,1)S(1)}, bf16[8,64,72]{2,1,0:T(8,128)(2,1)S(1)}, u32[]{:S(2)}, u32[]{:S(2)}) collective-permute-start(bf16[8,64,72]{2,1,0:T(8,128)(2,1)S(1)} %fusion.2), channel_id=1, source_target_pairs={{0,16},{16,0},{32,48},{48,32},{64,80},{80,64},{96,112},{112,96},{1... | collective-permute-start | bytes 221192 | tf_op jit(solution)/shard_map/ppermute | solution.py:14
  132.9 0.9 collective-permute-done.8
  134.0 3.1 %fusion.1 = bf16[64,1,1152]{2,0,1:T(8,128)(2,1)} fusion(bf16[16,64,72]{2,1,0:T(8,128)(2,1)S(1)} %bitcast.51, bf16[16,72,1152]{2,1,0:T(8,128)(2,1)} %all-gather.2.cloned.1.call-done), kind=kOutput, calls=%fused_computation.2 | convolution fusion | flops 169943040 | bytes 2949120 | tf_op jit(solution)/shard_map/hte,hed->td/dot_general | solution.py:280
  (37 shorter events, 4.0 us)
Async XLA Ops:
  6.5 110.1 %all-gather.2.cloned.1.call-start = ((), (), s32[]{:S(2)}) async-start(), calls=%async_computation.3 | async-start | bytes 2820096 | tf_op jit(solution)/shard_map/all_gather | solution.py:277
  8.0 0.9 copy-start.2
  9.1 10.7 %collective-permute-start = (bf16[32,1152]{1,0:T(8,128)(2,1)S(1)}, bf16[32,1152]{1,0:T(8,128)(2,1)S(1)}, u32[]{:S(2)}, u32[]{:S(2)}) collective-permute-start(bf16[32,1152]{1,0:T(8,128)(2,1)S(1)} %get-tuple-element.22), channel_id=1, source_target_pairs={{0,16},{16,0},{32,48},{48,32},{64,80},{80,64},{96,112},{112,96},{1... | collective-permute-start | bytes 221192 | tf_op jit(solution)/shard_map/ppermute | solution.py:14
  17.9 38.2 %collective-permute-start.2 = (bf16[216,1152]{1,0:T(8,128)(2,1)}, bf16[216,1152]{1,0:T(8,128)(2,1)S(1)}, u32[]{:S(2)}, u32[]{:S(2)}) collective-permute-start(bf16[216,1152]{1,0:T(8,128)(2,1)} %bitcast.52), channel_id=1, source_target_pairs={{16,1},{18,3},{20,5},{22,7},{24,9},{26,11},{28,13},{30,15},{1,16},... | collective-permute-start | bytes 1493000 | tf_op jit(solution)/shard_map/ppermute | solution.py:30
  21.0 3.8 %copy-start.5 = (s32[3,1]{0,1:T(1,128)S(1)}, s32[3,1]{0,1:T(1,128)}, u32[]{:S(2)}) copy-start(s32[3,1]{0,1:T(1,128)} %param.11) | copy-start | bytes 40
  21.0 3.9 %copy-start.4 = (f32[1,2,72]{2,1,0:T(2,128)S(1)}, f32[1,2,72]{2,1,0:T(2,128)}, u32[]{:S(2)}) copy-start(f32[1,2,72]{2,1,0:T(2,128)} %param.9) | copy-start | bytes 1732
  21.0 35.1 %copy-start.3 = (bf16[1,216,1152]{2,1,0:T(8,128)(2,1)S(1)}, bf16[1,216,1152]{2,1,0:T(8,128)(2,1)}, u32[]{:S(2)}) copy-start(bf16[1,216,1152]{2,1,0:T(8,128)(2,1)} %param.8) | copy-start | bytes 1492996
  21.0 37.9 %all-to-all-start = ((bf16[16,32,1152]{2,1,0:T(8,128)(2,1)}), bf16[16,32,1152]{2,1,0:T(8,128)(2,1)S(1)}, u32[]{:S(2)}, u32[]{:S(2)}) async-start(bf16[16,32,1152]{2,1,0:T(8,128)(2,1)} %bitcast.4), calls=%async_computation | async-start | bytes 2359296 | tf_op jit(solution)/shard_map/all_to_all | solution.py:72
  25.1 18.2 %collective-permute-start.3 = (f32[5,72]{0,1:T(8,128)S(1)}, f32[5,72]{0,1:T(8,128)S(1)}, u32[]{:S(2)}, u32[]{:S(2)}) collective-permute-start(f32[5,72]{0,1:T(8,128)S(1)} %copy.14), channel_id=1, source_target_pairs={{16,1},{18,3},{20,5},{22,7},{24,9},{26,11},{28,13},{30,15},{1,16},... | collective-permute-start | bytes 4328 | tf_op jit(solution)/shard_map/ppermute | solution.py:30
  43.3 15.6 %collective-permute-start.1 = (bf16[2,32,1152]{2,1,0:T(8,128)(2,1)S(1)}, bf16[2,32,1152]{2,1,0:T(8,128)(2,1)S(1)}, u32[]{:S(2)}, u32[]{:S(2)}) collective-permute-start(bf16[2,32,1152]{2,1,0:T(8,128)(2,1)S(1)} %maximum_select_fusion.1), channel_id=1, source_target_pairs={{0,256},{16,272},{32,288},{48,304},{64,320},{80,336},{96,352},{112... | collective-permute-start | bytes 442376 | tf_op jit(solution)/shard_map/ppermute | solution.py:14
  58.9 13.6 %collective-permute-start.4 = (bf16[512,1152]{1,0:T(8,128)(2,1)S(1)}, bf16[512,1152]{1,0:T(8,128)(2,1)}, u32[]{:S(2)}, u32[]{:S(2)}) collective-permute-start(bf16[512,1152]{1,0:T(8,128)(2,1)S(1)} %bitcast.42), channel_id=1, source_target_pairs={{0,16},{16,0},{32,48},{48,32},{64,80},{80,64},{96,112},{112,96},{1... | collective-permute-start | bytes 3538952 | tf_op jit(solution)/shard_map/ppermute | solution.py:14
  62.0 44.0 %all-to-all-start.1 = ((bf16[16,32,1152]{2,1,0:T(8,128)(2,1)}), bf16[16,32,1152]{2,1,0:T(8,128)(2,1)S(1)}, u32[]{:S(2)}, u32[]{:S(2)}) async-start(bf16[16,32,1152]{2,1,0:T(8,128)(2,1)} %bitcast.48), calls=%async_computation.1 | async-start | bytes 2359296 | tf_op jit(solution)/shard_map/all_to_all | solution.py:72
  74.9 25.7 %collective-permute-start.5 = (bf16[144,1024]{1,0:T(8,128)(2,1)S(1)}, bf16[144,1024]{1,0:T(8,128)(2,1)S(1)}, u32[]{:S(2)}, u32[]{:S(2)}) collective-permute-start(bf16[144,1024]{1,0:T(8,128)(2,1)S(1)} %get-tuple-element.28.own_ref), channel_id=1, source_target_pairs={{0,1},{1,0},{2,3},{3,2},{4,5},{5,4},{6,7},{7,6},{8,9},{9,8},{10,11... | collective-permute-start | bytes 884744 | tf_op jit(solution)/shard_map/ppermute | solution.py:18
  78.2 27.8 %collective-permute-start.6 = (bf16[144,1024]{1,0:T(8,128)(2,1)S(1)}, bf16[144,1024]{1,0:T(8,128)(2,1)S(1)}, u32[]{:S(2)}, u32[]{:S(2)}) collective-permute-start(bf16[144,1024]{1,0:T(8,128)(2,1)S(1)} %get-tuple-element.28.own_ref), channel_id=1, source_target_pairs={{0,64},{16,80},{32,96},{48,112},{64,0},{80,16},{96,32},{112,48},{1... | collective-permute-start | bytes 884744 | tf_op jit(solution)/shard_map/ppermute | solution.py:14
  105.2 0.8 copy-start
  106.0 5.1 %collective-permute-start.7 = (bf16[512,1152]{1,0:T(8,128)(2,1)S(1)}, bf16[512,1152]{1,0:T(8,128)(2,1)S(1)}, u32[]{:S(2)}, u32[]{:S(2)}) collective-permute-start(bf16[512,1152]{1,0:T(8,128)(2,1)S(1)} %bitcast.44), channel_id=1, source_target_pairs={{0,16},{16,0},{32,48},{48,32},{64,80},{80,64},{96,112},{112,96},{1... | collective-permute-start | bytes 3538952 | tf_op jit(solution)/shard_map/ppermute | solution.py:14
  108.6 3.3 %copy-start.1 = (f32[1024,128]{1,0:T(8,128)S(1)}, f32[1024,128]{1,0:T(8,128)}, u32[]{:S(2)}) copy-start(f32[1024,128]{1,0:T(8,128)} %copy-done) | copy-start | bytes 1572868
  129.4 4.4 %collective-permute-start.8 = (bf16[8,64,72]{2,1,0:T(8,128)(2,1)S(1)}, bf16[8,64,72]{2,1,0:T(8,128)(2,1)S(1)}, u32[]{:S(2)}, u32[]{:S(2)}) collective-permute-start(bf16[8,64,72]{2,1,0:T(8,128)(2,1)S(1)} %fusion.2), channel_id=1, source_target_pairs={{0,16},{16,0},{32,48},{48,32},{64,80},{80,64},{96,112},{112,96},{1... | collective-permute-start | bytes 221192 | tf_op jit(solution)/shard_map/ppermute | solution.py:14
Sparse Core Ops, SparseCore 0:
  10.4 82.5 all-gather.1

commit v5 on v3

--- a/solution.py
+++ b/solution.py
@@ -33,11 +33,40 @@
     )(rows, norm_gain[None])
 
 
+def groups(which):
+    heads = lax.axis_size("head")
+    side = math.isqrt(heads)
+    table = [[side * i + j for j in range(side)] for i in range(side)]
+    return table if which == 0 else [list(column) for column in zip(*table)]
+
+
+def exchange(slots, which):
+    return lax.all_to_all(
+        slots, "head", split_axis=0, concat_axis=0, tiled=True, axis_index_groups=groups(which)
+    )
+
+
 def gather_tokens(normed):
-    heads = lax.axis_size("head")
-    copies = jnp.broadcast_to(normed[None], (heads,) + normed.shape)
-    rows = lax.all_to_all(copies, "head", split_axis=0, concat_axis=0, tiled=True)
-    return rows.reshape(-1, normed.shape[-1])
+    side = len(groups(0))
+    copies = jnp.broadcast_to(normed[None], (side,) + normed.shape)
+    return exchange(copies, 0).reshape(-1, normed.shape[-1])
+
+
+def gather_weights(weight):
+    views, heads = lax.axis_size("view"), lax.axis_size("head")
+    side = len(groups(0))
+    core = lax.axis_index("view") % 2
+    rows = weight.shape[0]
+    part = (rows // 2 + 15) // 16 * 16
+    pairs = []
+    for view in range(views):
+        step = side if view % 2 == 0 else -side
+        for head in range(heads):
+            pairs.append((view * heads + (head + step) % heads, view * heads + head))
+    nearby = lax.ppermute(weight, ("view", "head"), pairs)
+    sent = jnp.where(core == 0, weight[:part], weight[rows - part :])
+    across = [(head, (head + heads // 2) % heads) for head in range(heads)]
+    return jnp.concatenate([nearby, lax.ppermute(sent, "head", across)], axis=0)
 
 
 def rms_rows(part, gain):
@@ -45,35 +74,71 @@
     return part * lax.rsqrt(square) * gain
 
 
-def project_kernel(with_query, rows_ref, weight_ref, gain_ref, *out_refs):
+def project_kernel(skip, place_ref, rows_ref, weight_ref, mine_ref, other_ref, out_ref):
+    tokens = rows_ref[...]
+    rows = weight_ref.shape[0]
+    part = mine_ref.shape[0] - rows
+
+    def product(weight):
+        return lax.dot_general(
+            weight, tokens, (((1,), (1,)), ((), ())), preferred_element_type=jnp.float32
+        )
+
+    mine, other = product(mine_ref[...]), product(other_ref[...])
+    own = product(weight_ref[...])
+    first = place_ref[4] == 0
+    low = jnp.where(first, mine[rows:], other[rows:])
+    high = jnp.where(first, other[rows:], mine[rows:])
+    far = jnp.concatenate([low[: rows - part], high], axis=0)
+    for n, flat in enumerate((own, mine[:rows], other[:rows], far)):
+        out_ref[place_ref[n]] = flat[skip:].astype(jnp.bfloat16)
+
+
+def project(place, tokens, weight, mine, other, skip):
+    rows, width = weight.shape
+    side = len(groups(0))
+    smem, vmem = pl.BlockSpec(memory_space=pltpu.SMEM), pl.BlockSpec(memory_space=pltpu.VMEM)
+    return pl.pallas_call(
+        functools.partial(project_kernel, skip),
+        out_shape=jax.ShapeDtypeStruct((side, rows - skip, tokens.shape[0]), jnp.bfloat16),
+        in_specs=[smem] + [vmem] * 4,
+        out_specs=vmem,
+        compiler_params=pltpu.CompilerParams(vmem_limit_bytes=16 << 20),
+        cost_estimate=pl.CostEstimate(
+            flops=2 * side * rows * width * tokens.shape[0], bytes_accessed=4 * rows * width, transcendentals=0
+        ),
+    )(place, tokens, weight, mine, other)
+
+
+def settle_kernel(with_query, parts_ref, gain_ref, *out_refs):
     head_dim = gain_ref.shape[0]
-    weight = weight_ref[...]
-    flat = lax.dot_general(
-        weight, rows_ref[...], (((1,), (1,)), ((), ())), preferred_element_type=jnp.float32
-    )
-    flat = flat.astype(jnp.bfloat16).astype(jnp.float32)
-    if with_query:
-        query = rms_rows(flat[:head_dim], gain_ref[:, 0:1])
-        out_refs[0][...] = query.T.astype(jnp.bfloat16)
-        flat = flat[head_dim:]
-    keys = rms_rows(flat[:head_dim], gain_ref[:, 1:2])
-    out_refs[-1][...] = jnp.concatenate([keys, flat[head_dim:]], axis=0).astype(jnp.bfloat16)
-
-
-def project(rows, weight, gain, with_query):
-    tokens, width = rows.shape
+    blocks, _, tokens = parts_ref.shape
+    for n in range(blocks):
+        flat = parts_ref[n].astype(jnp.float32)
+        at = pl.ds(n * tokens, tokens)
+        if with_query:
+            query = rms_rows(flat[:head_dim], gain_ref[:, 0:1])
+            out_refs[0][at, :] = query.T.astype(jnp.bfloat16)
+            flat = flat[head_dim:]
+        keys = rms_rows(flat[:head_dim], gain_ref[:, 1:2])
+        pair = jnp.concatenate([keys, flat[head_dim:]], axis=0)
+        out_refs[-1][:, at] = pair.astype(jnp.bfloat16)
+
+
+def settle(parts, gain, with_query):
     head_dim = gain.shape[0]
+    tokens = parts.shape[0] * parts.shape[2]
     out_shape = [jax.ShapeDtypeStruct((2 * head_dim, tokens), jnp.bfloat16)]
     if with_query:
         out_shape = [jax.ShapeDtypeStruct((tokens, head_dim), jnp.bfloat16)] + out_shape
     return pl.pallas_call(
-        functools.partial(project_kernel, with_query),
+        functools.partial(settle_kernel, with_query),
         out_shape=out_shape,
-        compiler_params=pltpu.CompilerParams(vmem_limit_bytes=32 << 20),
+        compiler_params=pltpu.CompilerParams(vmem_limit_bytes=16 << 20),
         cost_estimate=pl.CostEstimate(
-            flops=2 * tokens * width * weight.shape[0], bytes_accessed=2 * tokens * width, transcendentals=0
+            flops=8 * parts.size, bytes_accessed=4 * parts.size, transcendentals=0
         ),
-    )(rows, weight, gain)
+    )(parts, gain)
 
 
 def scores_of(query, pair_ref):
@@ -134,7 +199,7 @@
         state_ref[rows, :] = jnp.where(lane == head_dim + 1, best, acc)
         return carry
 
-    lax.fori_loop(0, tokens // tile, step, 0)
+    lax.fori_loop(0, tokens // tile, step, 0, unroll=True)
 
 
 def last_kernel(tile, first, active_ref, query_ref, own_in_ref, state_ref, *refs):
@@ -153,7 +218,7 @@
         out_ref[rows, :] = (own_in_ref[rows, :] + finish(acc, head_dim)).astype(jnp.bfloat16)
         return carry
 
-    lax.fori_loop(0, tokens // tile, step, 0)
+    lax.fori_loop(0, tokens // tile, step, 0, unroll=True)
 
 
 PADDED = 128
@@ -168,7 +233,7 @@
         in_specs=[pl.BlockSpec(memory_space=pltpu.SMEM)] + [vmem] * (len(arrays) - 1),
         out_specs=[vmem] * len(out_shape) if several else vmem,
         scratch_shapes=[pltpu.VMEM((blocks, tokens, PADDED), jnp.bfloat16)],
-        compiler_params=pltpu.CompilerParams(vmem_limit_bytes=40 << 20),
+        compiler_params=pltpu.CompilerParams(vmem_limit_bytes=20 << 20),
         cost_estimate=pl.CostEstimate(
             flops=4 * blocks * tokens * tokens * 256,
             bytes_accessed=4 * blocks * tokens * head_dim,
@@ -234,16 +299,33 @@
     head_dim = gain.shape[0]
     weight = qkv_weight[0]
     active = intersection[:, 0]
+    core = lax.axis_index("view") % 2
+    heads, side = lax.axis_size("head"), len(groups(0))
+    line = lax.axis_index("head") // side
+    turn = jnp.where(core == 0, 1, side - 1)
+    place = jnp.stack([line, line + turn, line + side - turn, line + side // 2]) % side
+    place = jnp.concatenate([place, core[None]]).astype(jnp.int32)
+    mine_weight = gather_weights(weight)
     normed = normalize(rows, norm_gain)
     far_normed = partner(normed, bits[-1])
-    every = gather_tokens(normed)
-    far_every = gather_tokens(far_normed)
-    query, own = project(every, weight, gain, True)
-    near = [partner(own, bit) for bit in bits[:-1]]
-    own_result, state = attend_near(active, query, own, near)
-    far_every, own_result, state = lax.optimization_barrier((far_every, own_result, state))
-    far = list(project(far_every, weight[head_dim:], gain, False))
-    attended = attend_last(active, rounds - 1, query, own_result, state, far)
+    tokens, mine_weight, far_normed = lax.optimization_barrier(
+        (gather_tokens(normed), mine_weight, far_normed)
+    )
+    other_weight = partner(mine_weight, 0)
+    parts = exchange(project(place, tokens, weight, mine_weight, other_weight, 0), 1)
+    query, own = settle(parts, gain, True)
+    near = partner(own, bits[0])
+    middle = [partner(own, bit) for bit in bits[1:-1]]
+    far_normed, query, own = lax.optimization_barrier((far_normed, query, own))
+    far_tokens = gather_tokens(far_normed)
+    far_parts = project(place, far_tokens, weight, mine_weight, other_weight, head_dim)
+    far_parts = exchange(far_parts, 1)
+    own_result, state = attend_near(active, query, own, [near])
+    far_parts, own_result, state, middle = lax.optimization_barrier(
+        (far_parts, own_result, state, middle)
+    )
+    far = list(settle(far_parts, gain, False))
+    attended = attend_last(active, 1, query, own_result, state, middle + far)
     out_half, attended = lax.optimization_barrier((gather_out_half(out_weight[0]), attended))
     token_rows = lax.all_to_all(
         attended.reshape(-1, loc_len, head_dim), "head", split_axis=0, concat_axis=0, tiled=True

time: 131 us -> 135 us (1.031)
  the two profiles are of different devices: /device:TPU:448 before, /device:TPU:32 now
where the time goes in v5:
time: 135 us; the launch traced here: 134 us
  starting transfers between devices  45.9 us (34%)
  waiting for transfers between devices  35.9 us (27%)
  Pallas kernels  14.6 us (11%)
  blocking collectives  14 us (10%)
  between operations  13.7 us (10%)
  local copies, waits for them, and re-layouts  5.83 us (4%)
  matrix products  2.26 us (2%)
  other arithmetic  2.11 us (2%)
    ppermute x5, starting transfers between devices, partner(): lax.ppermute(array, 'view', [(i, i ^ 1 << bit) for i in range(lax.axis_si...  22.5 us
    all_to_all x4, waiting for transfers between devices, exchange(): lax.all_to_all(slots, 'head', split_axis=0, concat_axis=0, tiled=True, ax...  20.8 us
    all_to_all x4, starting transfers between devices, exchange(): lax.all_to_all(slots, 'head', split_axis=0, concat_axis=0, tiled=True, ax...  15.9 us
    ppermute x5, waiting for transfers between devices, partner(): lax.ppermute(array, 'view', [(i, i ^ 1 << bit) for i in range(lax.axis_si...  15.1 us
    all_to_all x1, blocking collectives, on_device(): lax.all_to_all(attended.reshape(-1, loc_len, head_dim), 'head', split_axi...  14 us
    pallas_call x2, Pallas kernels, call_attend(): pl.pallas_call(kernel, out_shape=out_shape, in_specs=[pl.BlockSpec(memory...  9.66 us
    ppermute x1, starting transfers between devices, gather_weights(): nearby = lax.ppermute(weight, ('view', 'head'), pairs)  5.04 us
    pallas_call x2, Pallas kernels, project(): pl.pallas_call(functools.partial(project_kernel, skip), out_shape=jax.Sha...  4.25 us
  transfers between devices with their start and end apart: 12, of which 5 were waited for; matrix products, arithmetic and copies ran while one was open for 5% of the time, Pallas kernels for 11%

profile of v5, /device:TPU:32, one launch (start us, length us, event | category | flops | bytes accessed | tf_op | source)
XLA Modules:
  0.0 134.4 jit_solution(18164382230485174456)
XLA Ops:
  6.5 5.0 %collective-permute-start = (bf16[216,1152]{1,0:T(8,128)(2,1)}, bf16[216,1152]{1,0:T(8,128)(2,1)S(1)}, u32[]{:S(2)}, u32[]{:S(2)}) collective-permute-start(bf16[216,1152]{1,0:T(8,128)(2,1)} %bitcast.38), channel_id=1, source_target_pairs={{4,0},{5,1},{6,2},{7,3},{8,4},{9,5},{10,6},{11,7},{12,8},{13,9},{1... | collective-permute-start | bytes 1493000 | tf_op jit(solution)/shard_map/ppermute | solution.py:66
  11.6 1.1 select_bitcast_fusion
  12.7 2.6 %collective-permute-start.1 = (bf16[112,1152]{1,0:T(8,128)(2,1)S(1)}, bf16[112,1152]{1,0:T(8,128)(2,1)S(1)}, u32[]{:S(2)}, u32[]{:S(2)}) collective-permute-start(bf16[112,1152]{1,0:T(8,128)(2,1)S(1)} %select_bitcast_fusion), channel_id=1, source_target_pairs={{0,8},{1,9},{2,10},{3,11},{4,12},{5,13},{6,14},{7,15},{8,0},{9,1},... | collective-permute-start | bytes 774152 | tf_op jit(solution)/shard_map/ppermute | solution.py:69
  16.0 0.9 copy-done.2
  18.0 4.4 %all-to-all-start = ((bf16[4,64,1152]{2,1,0:T(8,128)(2,1)}), bf16[4,64,1152]{2,1,0:T(8,128)(2,1)S(1)}, u32[]{:S(2)}, u32[]{:S(2)}) async-start(bf16[4,64,1152]{2,1,0:T(8,128)(2,1)} %broadcast_in_dim.9), calls=%async_computation | async-start | bytes 1179648 | tf_op jit(solution)/shard_map/all_to_all | solution.py:44
  23.2 14.8 %collective-permute-start.2 = (bf16[64,1152]{1,0:T(8,128)(2,1)S(1)}, bf16[64,1152]{1,0:T(8,128)(2,1)S(1)}, u32[]{:S(2)}, u32[]{:S(2)}) collective-permute-start(bf16[64,1152]{1,0:T(8,128)(2,1)S(1)} %shard_map.64), channel_id=1, source_target_pairs={{0,256},{16,272},{32,288},{48,304},{64,320},{80,336},{96,352},{112... | collective-permute-start | bytes 442376 | tf_op jit(solution)/shard_map/ppermute | solution.py:14
  38.1 13.1 %collective-permute-done.2 = bf16[64,1152]{1,0:T(8,128)(2,1)S(1)} collective-permute-done((bf16[64,1152]{1,0:T(8,128)(2,1)S(1)}, bf16[64,1152]{1,0:T(8,128)(2,1)S(1)}, u32[]{:S(2)}, u32[]{:S(2)}) %collective-permute-start.2) | collective-permute-done | bytes 147488 | tf_op jit(solution)/shard_map/ppermute | solution.py:14
  51.2 1.9 %collective-permute-start.3 = (bf16[328,1152]{1,0:T(8,128)(2,1)S(1)}, bf16[328,1152]{1,0:T(8,128)(2,1)S(1)}, u32[]{:S(2)}, u32[]{:S(2)}) collective-permute-start(bf16[328,1152]{1,0:T(8,128)(2,1)S(1)} %pad_maximum_fusion.mine_ref), channel_id=1, source_target_pairs={{0,16},{16,0},{32,48},{48,32},{64,80},{80,64},{96,112},{112,96},{1... | collective-permute-start | bytes 2267144 | tf_op jit(solution)/shard_map/ppermute | solution.py:14
  53.3 2.0 %collective-permute-done.3.other_ref = bf16[328,1152]{1,0:T(8,128)(2,1)S(1)} collective-permute-done((bf16[328,1152]{1,0:T(8,128)(2,1)S(1)}, bf16[328,1152]{1,0:T(8,128)(2,1)S(1)}, u32[]{:S(2)}, u32[]{:S(2)}) %collective-permute-start.3) | collective-permute-done | bytes 755744 | tf_op jit(solution)/shard_map/ppermute | solution.py:14
  55.3 2.2 %shard_map.65 = bf16[4,216,256]{2,1,0:T(8,128)(2,1)} custom-call(s32[5]{0:T(128)S(1)} %pad_add_fusion.place_ref, bf16[256,1152]{1,0:T(8,128)(2,1)S(1)} %bitcast.41, bf16[216,1152]{1,0:T(8,128)(2,1)S(1)} %bitcast.39, bf16[328,1152]{1,0:T(8,128)(2,1)S(1)} %pad_maximum_fusion.mine_ref, bf16[328,1152]{1,0:T(8,128)(2,1)S(1)} %collective-permute-done.3.other_ref), custom_call_target="tpu_custom_call" | custom-call | flops 509607936 | bytes 995328 | tf_op jit(solution)/shard_map/pallas_call | solution.py:101
  57.5 3.5 %all-to-all-start.1 = ((bf16[4,216,256]{2,1,0:T(8,128)(2,1)}), bf16[4,216,256]{2,1,0:T(8,128)(2,1)S(1)}, u32[]{:S(2)}, u32[]{:S(2)}) async-start(bf16[4,216,256]{2,1,0:T(8,128)(2,1)} %shard_map.65), calls=%async_computation.1 | async-start | bytes 884736 | tf_op jit(solution)/shard_map/all_to_all | solution.py:44
  61.1 9.0 %all-to-all-done.1.parts_ref = bf16[4,216,256]{2,1,0:T(8,128)(2,1)S(1)} async-done(((bf16[4,216,256]{2,1,0:T(8,128)(2,1)}), bf16[4,216,256]{2,1,0:T(8,128)(2,1)S(1)}, u32[]{:S(2)}, u32[]{:S(2)}) %all-to-all-start.1) | async-done | bytes 442400 | tf_op jit(solution)/shard_map/all_to_all | solution.py:44
  72.1 4.5 %all-to-all-start.2 = ((bf16[4,64,1152]{2,1,0:T(8,128)(2,1)}), bf16[4,64,1152]{2,1,0:T(8,128)(2,1)S(1)}, u32[]{:S(2)}, u32[]{:S(2)}) async-start(bf16[4,64,1152]{2,1,0:T(8,128)(2,1)} %broadcast_in_dim.21), calls=%async_computation.2 | async-start | bytes 1179648 | tf_op jit(solution)/shard_map/all_to_all | solution.py:44
  76.6 1.9 %collective-permute-start.4 = (bf16[144,1024]{1,0:T(8,128)(2,1)S(1)}, bf16[144,1024]{1,0:T(8,128)(2,1)}, u32[]{:S(2)}, u32[]{:S(2)}) collective-permute-start(bf16[144,1024]{1,0:T(8,128)(2,1)S(1)} %get-tuple-element.28.own_ref), channel_id=1, source_target_pairs={{0,16},{16,0},{32,48},{48,32},{64,80},{80,64},{96,112},{112,96},{1... | collective-permute-start | bytes 884744 | tf_op jit(solution)/shard_map/ppermute | solution.py:14
  78.5 1.9 %collective-permute-start.5 = (bf16[144,1024]{1,0:T(8,128)(2,1)S(1)}, bf16[144,1024]{1,0:T(8,128)(2,1)S(1)}, u32[]{:S(2)}, u32[]{:S(2)}) collective-permute-start(bf16[144,1024]{1,0:T(8,128)(2,1)S(1)} %get-tuple-element.28.own_ref), channel_id=1, source_target_pairs={{0,64},{16,80},{32,96},{48,112},{64,0},{80,16},{96,32},{112,48},{1... | collective-permute-start | bytes 884744 | tf_op jit(solution)/shard_map/ppermute | solution.py:14
  80.4 10.9 %all-to-all-done.2 = bf16[4,64,1152]{2,1,0:T(8,128)(2,1)S(1)} async-done(((bf16[4,64,1152]{2,1,0:T(8,128)(2,1)}), bf16[4,64,1152]{2,1,0:T(8,128)(2,1)S(1)}, u32[]{:S(2)}, u32[]{:S(2)}) %all-to-all-start.2) | async-done | bytes 589856 | tf_op jit(solution)/shard_map/all_to_all | solution.py:44
  91.4 2.1 %shard_map.67 = bf16[4,144,256]{2,1,0:T(8,128)(2,1)} custom-call(s32[5]{0:T(128)S(1)} %pad_add_fusion.place_ref, bf16[256,1152]{1,0:T(8,128)(2,1)S(1)} %bitcast.42, bf16[216,1152]{1,0:T(8,128)(2,1)S(1)} %bitcast.40, bf16[328,1152]{1,0:T(8,128)(2,1)S(1)} %pad_maximum_fusion.mine_ref, bf16[328,1152]{1,0:T(8,128)(2,1)S(1)} %collective-permute-done.3.other_ref), custom_call_target="tpu_custom_call" | custom-call | flops 509607936 | bytes 995328 | tf_op jit(solution)/shard_map/pallas_call | solution.py:101
  93.4 3.5 %all-to-all-start.3 = ((bf16[4,144,256]{2,1,0:T(8,128)(2,1)}), bf16[4,144,256]{2,1,0:T(8,128)(2,1)S(1)}, u32[]{:S(2)}, u32[]{:S(2)}) async-start(bf16[4,144,256]{2,1,0:T(8,128)(2,1)} %shard_map.67), calls=%async_computation.3 | async-start | bytes 589824 | tf_op jit(solution)/shard_map/all_to_all | solution.py:44
  96.9 0.9 copy-done.4
  97.9 5.0 %shard_map.68 = (f32[1024,72]{1,0:T(8,128)S(1)}, f32[1024,128]{1,0:T(8,128)S(1)}) custom-call(s32[3]{0:T(128)S(1)} %bitcast.47, bf16[1024,72]{1,0:T(8,128)(2,1)S(1)} %copy-done.4, bf16[144,1024]{1,0:T(8,128)(2,1)S(1)} %get-tuple-element.28.own_ref, bf16[144,1024]{1,0:T(8,128)(2,1)} %collective-permute-done.4.refs_0_), custom_call_target="tpu_custom_call" | custom-call | flops 2147483648 | bytes 589824 | tf_op jit(solution)/shard_map/pallas_call | solution.py:230
  103.8 4.6 %shard_map.70 = bf16[1024,72]{1,0:T(8,128)(2,1)S(1)} custom-call(s32[3]{0:T(128)S(1)} %bitcast.48, bf16[1024,72]{1,0:T(8,128)(2,1)S(1)} %copy-done.5, f32[1024,72]{1,0:T(8,128)S(1)} %get-tuple-element.31.own_in_ref, f32[1024,128]{1,0:T(8,128)S(1)} %get-tuple-element.32.state_ref, bf16[144,1024]{1,0:T(8,128)(2,1)S(1)} %collective-permute-done.5.refs_0_, ...), custom_call_target="tpu_custom_call" | custom-call | flops 2147483648 | bytes 589824 | tf_op jit(solution)/shard_map/pallas_call | solution.py:230
  108.5 1.9 %collective-permute-start.6 = (bf16[16,72,576]{2,1,0:T(8,128)(2,1)}, bf16[16,72,576]{2,1,0:T(8,128)(2,1)S(1)}, u32[]{:S(2)}, u32[]{:S(2)}) collective-permute-start(bf16[16,72,576]{2,1,0:T(8,128)(2,1)} %bitcast.49), channel_id=1, source_target_pairs={{0,16},{16,0},{32,48},{48,32},{64,80},{80,64},{96,112},{112,96},{1... | collective-permute-start | bytes 3981320 | tf_op jit(solution)/shard_map/ppermute | solution.py:14
  110.4 14.0 %all_to_all.25 = bf16[16,64,72]{2,1,0:T(8,128)(2,1)S(1)} all-to-all(bf16[16,64,72]{2,1,0:T(8,128)(2,1)S(1)} %bitcast.45), channel_id=1, replica_groups=mesh['view'=32,'head'=16] {'head'}, dimensions={0} | all-to-all | bytes 294912 | tf_op jit(solution)/shard_map/all_to_all | solution.py:330
  124.4 1.8 %fusion.3 = bf16[64,1,576]{2,0,1:T(8,128)(2,1)S(1)} fusion(bf16[16,64,72]{2,1,0:T(8,128)(2,1)S(1)} %all_to_all.25, bf16[16,72,576]{2,1,0:T(8,128)(2,1)} %bitcast.50), kind=kOutput, calls=%fused_computation.5 | convolution fusion | flops 84971520 | bytes 1548288 | tf_op jit(solution)/shard_map/hte,hed->td/dot_general | solution.py:280
  (37 shorter events, 7.0 us)
Async XLA Ops:
  6.5 15.9 %copy-start = (bf16[1,72,1152]{2,1,0:T(8,128)(2,1)S(1)}, bf16[1,72,1152]{2,1,0:T(8,128)(2,1)}, u32[]{:S(2)}) copy-start(bf16[1,72,1152]{2,1,0:T(8,128)(2,1)} %param.10) | copy-start | bytes 497668
  6.5 31.5 %collective-permute-start = (bf16[216,1152]{1,0:T(8,128)(2,1)}, bf16[216,1152]{1,0:T(8,128)(2,1)S(1)}, u32[]{:S(2)}, u32[]{:S(2)}) collective-permute-start(bf16[216,1152]{1,0:T(8,128)(2,1)} %bitcast.38), channel_id=1, source_target_pairs={{4,0},{5,1},{6,2},{7,3},{8,4},{9,5},{10,6},{11,7},{12,8},{13,9},{1... | collective-permute-start | bytes 1493000 | tf_op jit(solution)/shard_map/ppermute | solution.py:66
  12.7 25.3 %collective-permute-start.1 = (bf16[112,1152]{1,0:T(8,128)(2,1)S(1)}, bf16[112,1152]{1,0:T(8,128)(2,1)S(1)}, u32[]{:S(2)}, u32[]{:S(2)}) collective-permute-start(bf16[112,1152]{1,0:T(8,128)(2,1)S(1)} %select_bitcast_fusion), channel_id=1, source_target_pairs={{0,8},{1,9},{2,10},{3,11},{4,12},{5,13},{6,14},{7,15},{8,0},{9,1},... | collective-permute-start | bytes 774152 | tf_op jit(solution)/shard_map/ppermute | solution.py:69
  16.0 0.9 copy-start.2
  18.0 37.3 %copy-start.1 = (bf16[1,216,1152]{2,1,0:T(8,128)(2,1)S(1)}, bf16[1,216,1152]{2,1,0:T(8,128)(2,1)}, u32[]{:S(2)}) copy-start(bf16[1,216,1152]{2,1,0:T(8,128)(2,1)} %param.8) | copy-start | bytes 1492996
  18.0 33.2 %all-to-all-start = ((bf16[4,64,1152]{2,1,0:T(8,128)(2,1)}), bf16[4,64,1152]{2,1,0:T(8,128)(2,1)S(1)}, u32[]{:S(2)}, u32[]{:S(2)}) async-start(bf16[4,64,1152]{2,1,0:T(8,128)(2,1)} %broadcast_in_dim.9), calls=%async_computation | async-start | bytes 1179648 | tf_op jit(solution)/shard_map/all_to_all | solution.py:44
  22.4 86.1 %all-gather.3.cloned.1.call-start = ((), (), s32[]{:S(2)}) async-start(), calls=%async_computation.5 | async-start | bytes 1566720 | tf_op jit(solution)/shard_map/all_gather | solution.py:271
  23.2 28.0 %collective-permute-start.2 = (bf16[64,1152]{1,0:T(8,128)(2,1)S(1)}, bf16[64,1152]{1,0:T(8,128)(2,1)S(1)}, u32[]{:S(2)}, u32[]{:S(2)}) collective-permute-start(bf16[64,1152]{1,0:T(8,128)(2,1)S(1)} %shard_map.64), channel_id=1, source_target_pairs={{0,256},{16,272},{32,288},{48,304},{64,320},{80,336},{96,352},{112... | collective-permute-start | bytes 442376 | tf_op jit(solution)/shard_map/ppermute | solution.py:14
  51.2 4.1 %collective-permute-start.3 = (bf16[328,1152]{1,0:T(8,128)(2,1)S(1)}, bf16[328,1152]{1,0:T(8,128)(2,1)S(1)}, u32[]{:S(2)}, u32[]{:S(2)}) collective-permute-start(bf16[328,1152]{1,0:T(8,128)(2,1)S(1)} %pad_maximum_fusion.mine_ref), channel_id=1, source_target_pairs={{0,16},{16,0},{32,48},{48,32},{64,80},{80,64},{96,112},{112,96},{1... | collective-permute-start | bytes 2267144 | tf_op jit(solution)/shard_map/ppermute | solution.py:14
  53.3 7.7 %copy-start.7 = (f32[1,2,72]{2,1,0:T(2,128)S(1)}, f32[1,2,72]{2,1,0:T(2,128)}, u32[]{:S(2)}) copy-start(f32[1,2,72]{2,1,0:T(2,128)} %param.9) | copy-start | bytes 1732
  57.5 12.6 %all-to-all-start.1 = ((bf16[4,216,256]{2,1,0:T(8,128)(2,1)}), bf16[4,216,256]{2,1,0:T(8,128)(2,1)S(1)}, u32[]{:S(2)}, u32[]{:S(2)}) async-start(bf16[4,216,256]{2,1,0:T(8,128)(2,1)} %shard_map.65), calls=%async_computation.1 | async-start | bytes 884736 | tf_op jit(solution)/shard_map/all_to_all | solution.py:44
  70.5 0.7 copy-start.3
  72.1 19.3 %all-to-all-start.2 = ((bf16[4,64,1152]{2,1,0:T(8,128)(2,1)}), bf16[4,64,1152]{2,1,0:T(8,128)(2,1)S(1)}, u32[]{:S(2)}, u32[]{:S(2)}) async-start(bf16[4,64,1152]{2,1,0:T(8,128)(2,1)} %broadcast_in_dim.21), calls=%async_computation.2 | async-start | bytes 1179648 | tf_op jit(solution)/shard_map/all_to_all | solution.py:44
  76.6 20.3 %collective-permute-start.4 = (bf16[144,1024]{1,0:T(8,128)(2,1)S(1)}, bf16[144,1024]{1,0:T(8,128)(2,1)}, u32[]{:S(2)}, u32[]{:S(2)}) collective-permute-start(bf16[144,1024]{1,0:T(8,128)(2,1)S(1)} %get-tuple-element.28.own_ref), channel_id=1, source_target_pairs={{0,16},{16,0},{32,48},{48,32},{64,80},{80,64},{96,112},{112,96},{1... | collective-permute-start | bytes 884744 | tf_op jit(solution)/shard_map/ppermute | solution.py:14
  78.5 24.4 %collective-permute-start.5 = (bf16[144,1024]{1,0:T(8,128)(2,1)S(1)}, bf16[144,1024]{1,0:T(8,128)(2,1)S(1)}, u32[]{:S(2)}, u32[]{:S(2)}) collective-permute-start(bf16[144,1024]{1,0:T(8,128)(2,1)S(1)} %get-tuple-element.28.own_ref), channel_id=1, source_target_pairs={{0,64},{16,80},{32,96},{48,112},{64,0},{80,16},{96,32},{112,48},{1... | collective-permute-start | bytes 884744 | tf_op jit(solution)/shard_map/ppermute | solution.py:14
  91.3 5.6 %copy-start.6 = (s32[3,1]{0,1:T(1,128)S(1)}, s32[3,1]{0,1:T(1,128)}, u32[]{:S(2)}) copy-start(s32[3,1]{0,1:T(1,128)} %param.11) | copy-start | bytes 40
  93.4 10.3 %all-to-all-start.3 = ((bf16[4,144,256]{2,1,0:T(8,128)(2,1)}), bf16[4,144,256]{2,1,0:T(8,128)(2,1)S(1)}, u32[]{:S(2)}, u32[]{:S(2)}) async-start(bf16[4,144,256]{2,1,0:T(8,128)(2,1)} %shard_map.67), calls=%async_computation.3 | async-start | bytes 589824 | tf_op jit(solution)/shard_map/all_to_all | solution.py:44
  96.9 1.0 copy-start.4
  97.9 6.0 %copy-start.5 = (bf16[1024,72]{1,0:T(8,128)(2,1)S(1)}, bf16[1024,72]{1,0:T(8,128)(2,1)}, u32[]{:S(2)}) copy-start(bf16[1024,72]{1,0:T(8,128)(2,1)} %copy-done.3) | copy-start | bytes 442372
  108.5 17.8 %collective-permute-start.6 = (bf16[16,72,576]{2,1,0:T(8,128)(2,1)}, bf16[16,72,576]{2,1,0:T(8,128)(2,1)S(1)}, u32[]{:S(2)}, u32[]{:S(2)}) collective-permute-start(bf16[16,72,576]{2,1,0:T(8,128)(2,1)} %bitcast.49), channel_id=1, source_target_pairs={{0,16},{16,0},{32,48},{48,32},{64,80},{80,64},{96,112},{112,96},{1... | collective-permute-start | bytes 3981320 | tf_op jit(solution)/shard_map/ppermute | solution.py:14
Sparse Core Ops, SparseCore 0:
  26.2 65.7 all-gather.2

commit v6 on v2

--- a/solution.py
+++ b/solution.py
@@ -69,7 +69,7 @@
     return pl.pallas_call(
         functools.partial(project_kernel, with_query),
         out_shape=out_shape,
-        compiler_params=pltpu.CompilerParams(vmem_limit_bytes=32 << 20),
+        compiler_params=pltpu.CompilerParams(vmem_limit_bytes=16 << 20),
         cost_estimate=pl.CostEstimate(
             flops=2 * tokens * width * weight.shape[0], bytes_accessed=2 * tokens * width, transcendentals=0
         ),
@@ -134,7 +134,7 @@
         state_ref[rows, :] = jnp.where(lane == head_dim + 1, best, acc)
         return carry
 
-    lax.fori_loop(0, tokens // tile, step, 0)
+    lax.fori_loop(0, tokens // tile, step, 0, unroll=True)
 
 
 def last_kernel(tile, first, active_ref, query_ref, own_in_ref, state_ref, *refs):
@@ -144,16 +144,14 @@
     for n, ref in enumerate(far_refs):
         values_ref[n] = spread_values(ref, head_dim, padded)
 
-    def step(at, carry):
-        rows = pl.ds(pl.multiple_of(at * tile, tile), tile)
+    for at in range(tokens // tile):
+        rows = pl.ds(at * tile, tile)
         query = query_ref[rows, :]
         acc = state_ref[rows, :]
         best = acc[:, head_dim + 1 : head_dim + 2]
         best, acc = cross_update(active_ref, first, query, far_refs, values_ref, 0, best, acc)
-        out_ref[rows, :] = (own_in_ref[rows, :] + finish(acc, head_dim)).astype(jnp.bfloat16)
-        return carry
-
-    lax.fori_loop(0, tokens // tile, step, 0)
+        result = own_in_ref[rows, :] + finish(acc, head_dim)
+        out_ref[at] = result.T.astype(jnp.bfloat16)
 
 
 PADDED = 128
@@ -168,7 +166,7 @@
         in_specs=[pl.BlockSpec(memory_space=pltpu.SMEM)] + [vmem] * (len(arrays) - 1),
         out_specs=[vmem] * len(out_shape) if several else vmem,
         scratch_shapes=[pltpu.VMEM((blocks, tokens, PADDED), jnp.bfloat16)],
-        compiler_params=pltpu.CompilerParams(vmem_limit_bytes=40 << 20),
+        compiler_params=pltpu.CompilerParams(vmem_limit_bytes=20 << 20),
         cost_estimate=pl.CostEstimate(
             flops=4 * blocks * tokens * tokens * 256,
             bytes_accessed=4 * blocks * tokens * head_dim,
@@ -191,26 +189,66 @@
 
 def attend_last(active, first, query, own_result, state, far):
     tokens, head_dim = query.shape
-    out_shape = jax.ShapeDtypeStruct((tokens, head_dim), jnp.bfloat16)
+    side = len(groups(0))
+    out_shape = jax.ShapeDtypeStruct((side, head_dim, tokens // side), jnp.bfloat16)
     arrays = (active, query, own_result, state, *far)
     return call_attend(
-        functools.partial(last_kernel, 256, first), out_shape, len(far), tokens, head_dim, arrays
-    )
-
-
-def gather_out_half(out_weight):
-    head_dim, width = out_weight.shape
-    half = width // 2
-    core = lax.axis_index("view") % 2
-    mine = lax.dynamic_slice_in_dim(out_weight, core * half, half, axis=1)
-    return lax.all_gather(mine, "head", axis=0, tiled=True)
-
-
-def swap_halves(mine):
-    core = lax.axis_index("view") % 2
-    other = partner(mine, 0)
-    pair = jnp.where(core == 0, jnp.stack([mine, other]), jnp.stack([other, mine]))
-    return jnp.concatenate([pair[0], pair[1]], axis=1)
+        functools.partial(last_kernel, tokens // side, first), out_shape, len(far), tokens, head_dim, arrays
+    )
+
+
+def groups(which):
+    heads = lax.axis_size("head")
+    side = math.isqrt(heads)
+    table = [[side * i + j for j in range(side)] for i in range(side)]
+    return table if which == 0 else [list(column) for column in zip(*table)]
+
+
+def exchange(slots, which):
+    return lax.all_to_all(
+        slots, "head", split_axis=0, concat_axis=0, tiled=True, axis_index_groups=groups(which)
+    )
+
+
+def column_weights(weight):
+    heads = lax.axis_size("head")
+    side = len(groups(0))
+    return [
+        lax.ppermute(weight, "head", [((head + step * side) % heads, head) for head in range(heads)])
+        for step in range(1, side)
+    ]
+
+
+def project_out_kernel(line_ref, parts_ref, *refs):
+    weight_refs, out_ref = refs[:-1], refs[-1]
+    side = len(weight_refs)
+    total = None
+    for step, weight_ref in enumerate(weight_refs):
+        part = parts_ref[lax.rem(line_ref[0] + step, side)]
+        term = lax.dot_general(
+            part, weight_ref[...], (((0,), (0,)), ((), ())), preferred_element_type=jnp.float32
+        )
+        total = term if total is None else total + term
+    out_ref[...] = total.reshape(out_ref.shape).astype(jnp.bfloat16)
+
+
+def project_out(parts, weights):
+    side, head_dim, tokens = parts.shape
+    width = weights[0].shape[1]
+    line = (lax.axis_index("head") // side).astype(jnp.int32)[None]
+    smem, vmem = pl.BlockSpec(memory_space=pltpu.SMEM), pl.BlockSpec(memory_space=pltpu.VMEM)
+    partial = pl.pallas_call(
+        project_out_kernel,
+        out_shape=jax.ShapeDtypeStruct((side, tokens // side, width), jnp.bfloat16),
+        in_specs=[smem] + [vmem] * (1 + len(weights)),
+        out_specs=vmem,
+        compiler_params=pltpu.CompilerParams(vmem_limit_bytes=16 << 20),
+        cost_estimate=pl.CostEstimate(
+            flops=2 * parts.size * width, bytes_accessed=2 * (side * head_dim + tokens) * width, transcendentals=0
+        ),
+    )(line, parts, *weights)
+    partial = exchange(partial, 0)
+    return jnp.sum(partial.astype(jnp.float32), axis=0).astype(jnp.bfloat16)
 
 
 def on_device(latents, norm_gain, qkv_weight, qk_gain, out_weight, intersection):
@@ -225,22 +263,19 @@
     active = intersection[:, 0]
     normed = normalize(rows, norm_gain)
     far_normed = partner(normed, bits[-1])
+    far_normed, out_weights = lax.optimization_barrier(
+        (far_normed, column_weights(out_weight[0]))
+    )
     every = gather_tokens(normed)
+    far_every = gather_tokens(far_normed)
     query, own = project(every, weight, gain, True)
     near = [partner(own, bit) for bit in bits[:-1]]
-    far_every = gather_tokens(far_normed)
-    out_half = gather_out_half(out_weight[0])
     own_result, state = attend_near(active, query, own, near)
-    out_half, own_result, state = lax.optimization_barrier((out_half, own_result, state))
-    full_out = swap_halves(out_half).reshape(-1, head_dim, width)
-    far_every, full_out = lax.optimization_barrier((far_every, full_out))
+    far_every, own_result, state = lax.optimization_barrier((far_every, own_result, state))
     far = list(project(far_every, weight[head_dim:], gain, False))
     attended = attend_last(active, rounds - 1, query, own_result, state, far)
-    token_rows = lax.all_to_all(
-        attended.reshape(-1, loc_len, head_dim), "head", split_axis=0, concat_axis=0, tiled=True
-    )
-    mixed = jnp.einsum("hte,hed->td", token_rows, full_out, preferred_element_type=jnp.float32)
-    return mixed.astype(jnp.bfloat16).reshape(loc_len, view_dev, width)
+    mixed = project_out(exchange(attended, 1), [out_weight[0]] + out_weights)
+    return mixed.reshape(loc_len, view_dev, width)
 
 
 def solution(mesh):

time: 186 us -> 119 us (0.64)
  the two profiles are of different devices: /device:TPU:192 before, /device:TPU:448 now
where the time goes in v6:
time: 119 us; the launch traced here: 118 us
  waiting for transfers between devices  48.7 us (41%)
  starting transfers between devices  37 us (31%)
  Pallas kernels  14.7 us (12%)
  blocking collectives  10.8 us (9%)
  local copies, waits for them, and re-layouts  5.89 us (5%)
    ppermute x3, waiting for transfers between devices, partner(): lax.ppermute(array, 'view', [(i, i ^ 1 << bit) for i in range(lax.axis_si...  31.9 us
    all_to_all x2, starting transfers between devices, gather_tokens(): lax.all_to_all(copies, 'head', split_axis=0, concat_axis=0, tiled=True)  12.3 us
    all_to_all x1, blocking collectives, exchange(): lax.all_to_all(slots, 'head', split_axis=0, concat_axis=0, tiled=True, ax...  10.8 us
    ppermute x3, starting transfers between devices, partner(): lax.ppermute(array, 'view', [(i, i ^ 1 << bit) for i in range(lax.axis_si...  10.7 us
    ppermute x3, starting transfers between devices, column_weights(): lax.ppermute(weight, 'head', [((head + step * side) % heads, head) for he...  10.6 us
    pallas_call x2, Pallas kernels, call_attend(): pl.pallas_call(kernel, out_shape=out_shape, in_specs=[pl.BlockSpec(memory...  10 us
    all_to_all x2, waiting for transfers between devices, gather_tokens(): lax.all_to_all(copies, 'head', split_axis=0, concat_axis=0, tiled=True)  9.39 us
    all_to_all x1, waiting for transfers between devices, exchange(): lax.all_to_all(slots, 'head', split_axis=0, concat_axis=0, tiled=True, ax...  6.01 us
  transfers between devices with their start and end apart: 9, of which 5 were waited for; matrix products, arithmetic and copies ran while one was open for 0% of the time, Pallas kernels for 6%

profile of v6, /device:TPU:448, one launch (start us, length us, event | category | flops | bytes accessed | tf_op | source)
XLA Modules:
  0.0 118.0 jit_solution(10172040606360198922)
XLA Ops:
  0.7 0.9 copy-done.4
  1.8 1.7 %broadcast_in_dim.20 = bf16[16,64,1152]{2,1,0:T(8,128)(2,1)} broadcast(bf16[64,1152]{1,0:T(8,128)(2,1)S(1)} %shard_map.64), dimensions={1,2} | broadcast | bytes 2506752 | tf_op jit(solution)/shard_map/broadcast_in_dim | solution.py:38
  3.6 7.2 %all-to-all-start = ((bf16[16,64,1152]{2,1,0:T(8,128)(2,1)}), bf16[16,64,1152]{2,1,0:T(8,128)(2,1)S(1)}, u32[]{:S(2)}, u32[]{:S(2)}) async-start(bf16[16,64,1152]{2,1,0:T(8,128)(2,1)} %broadcast_in_dim.20), calls=%async_computation | async-start | bytes 4718592 | tf_op jit(solution)/shard_map/all_to_all | solution.py:39
  10.8 5.0 %collective-permute-start.1 = (bf16[72,1152]{1,0:T(8,128)(2,1)S(1)}, bf16[72,1152]{1,0:T(8,128)(2,1)S(1)}, u32[]{:S(2)}, u32[]{:S(2)}) collective-permute-start(bf16[72,1152]{1,0:T(8,128)(2,1)S(1)} %bitcast.17), channel_id=1, source_target_pairs={{4,0},{5,1},{6,2},{7,3},{8,4},{9,5},{10,6},{11,7},{12,8},{13,9},{1... | collective-permute-start | bytes 497672 | tf_op jit(solution)/shard_map/ppermute | solution.py:217
  15.8 2.8 %collective-permute-start.2 = (bf16[72,1152]{1,0:T(8,128)(2,1)S(1)}, bf16[72,1152]{1,0:T(8,128)(2,1)S(1)}, u32[]{:S(2)}, u32[]{:S(2)}) collective-permute-start(bf16[72,1152]{1,0:T(8,128)(2,1)S(1)} %bitcast.18), channel_id=1, source_target_pairs={{8,0},{9,1},{10,2},{11,3},{12,4},{13,5},{14,6},{15,7},{0,8},{1,9},... | collective-permute-start | bytes 497672 | tf_op jit(solution)/shard_map/ppermute | solution.py:217
  18.6 2.8 %collective-permute-start.3 = (bf16[72,1152]{1,0:T(8,128)(2,1)S(1)}, bf16[72,1152]{1,0:T(8,128)(2,1)S(1)}, u32[]{:S(2)}, u32[]{:S(2)}) collective-permute-start(bf16[72,1152]{1,0:T(8,128)(2,1)S(1)} %bitcast.19), channel_id=1, source_target_pairs={{12,0},{13,1},{14,2},{15,3},{0,4},{1,5},{2,6},{3,7},{4,8},{5,9},{6... | collective-permute-start | bytes 497672 | tf_op jit(solution)/shard_map/ppermute | solution.py:217
  21.4 5.4 %collective-permute-start = (bf16[64,1152]{1,0:T(8,128)(2,1)S(1)}, bf16[64,1152]{1,0:T(8,128)(2,1)S(1)}, u32[]{:S(2)}, u32[]{:S(2)}) collective-permute-start(bf16[64,1152]{1,0:T(8,128)(2,1)S(1)} %shard_map.64), channel_id=1, source_target_pairs={{0,256},{16,272},{32,288},{48,304},{64,320},{80,336},{96,352},{112... | collective-permute-start | bytes 442376 | tf_op jit(solution)/shard_map/ppermute | solution.py:14
  26.8 18.7 %collective-permute-done = bf16[64,1152]{1,0:T(8,128)(2,1)S(1)} collective-permute-done((bf16[64,1152]{1,0:T(8,128)(2,1)S(1)}, bf16[64,1152]{1,0:T(8,128)(2,1)S(1)}, u32[]{:S(2)}, u32[]{:S(2)}) %collective-permute-start) | collective-permute-done | bytes 147488 | tf_op jit(solution)/shard_map/ppermute | solution.py:14
  45.5 1.4 %collective-permute-done.3.refs_3_ = bf16[72,1152]{1,0:T(8,128)(2,1)S(1)} collective-permute-done((bf16[72,1152]{1,0:T(8,128)(2,1)S(1)}, bf16[72,1152]{1,0:T(8,128)(2,1)S(1)}, u32[]{:S(2)}, u32[]{:S(2)}) %collective-permute-start.3) | collective-permute-done | bytes 165920 | tf_op jit(solution)/shard_map/ppermute | solution.py:217
  47.6 1.7 %broadcast_in_dim.21 = bf16[16,64,1152]{2,1,0:T(8,128)(2,1)} broadcast(bf16[64,1152]{1,0:T(8,128)(2,1)S(1)} %collective-permute-done), dimensions={1,2} | broadcast | bytes 2506752 | tf_op jit(solution)/shard_map/broadcast_in_dim | solution.py:38
  49.3 5.2 %all-to-all-start.1 = ((bf16[16,64,1152]{2,1,0:T(8,128)(2,1)}), bf16[16,64,1152]{2,1,0:T(8,128)(2,1)}, u32[]{:S(2)}, u32[]{:S(2)}) async-start(bf16[16,64,1152]{2,1,0:T(8,128)(2,1)} %broadcast_in_dim.21), calls=%async_computation.1 | async-start | bytes 4718592 | tf_op jit(solution)/shard_map/all_to_all | solution.py:39
  54.6 1.0 shard_map.65
  55.6 1.9 %collective-permute-start.4 = (bf16[144,1024]{1,0:T(8,128)(2,1)S(1)}, bf16[144,1024]{1,0:T(8,128)(2,1)S(1)}, u32[]{:S(2)}, u32[]{:S(2)}) collective-permute-start(bf16[144,1024]{1,0:T(8,128)(2,1)S(1)} %get-tuple-element.18.own_ref), channel_id=1, source_target_pairs={{0,16},{16,0},{32,48},{48,32},{64,80},{80,64},{96,112},{112,96},{1... | collective-permute-start | bytes 884744 | tf_op jit(solution)/shard_map/ppermute | solution.py:14
  57.6 3.4 %collective-permute-start.5 = (bf16[144,1024]{1,0:T(8,128)(2,1)S(1)}, bf16[144,1024]{1,0:T(8,128)(2,1)S(1)}, u32[]{:S(2)}, u32[]{:S(2)}) collective-permute-start(bf16[144,1024]{1,0:T(8,128)(2,1)S(1)} %get-tuple-element.18.own_ref), channel_id=1, source_target_pairs={{0,64},{16,80},{32,96},{48,112},{64,0},{80,16},{96,32},{112,48},{1... | collective-permute-start | bytes 884744 | tf_op jit(solution)/shard_map/ppermute | solution.py:14
  61.0 13.2 %collective-permute-done.5.refs_1_ = bf16[144,1024]{1,0:T(8,128)(2,1)S(1)} collective-permute-done((bf16[144,1024]{1,0:T(8,128)(2,1)S(1)}, bf16[144,1024]{1,0:T(8,128)(2,1)S(1)}, u32[]{:S(2)}, u32[]{:S(2)}) %collective-permute-start.5) | collective-permute-done | bytes 294944 | tf_op jit(solution)/shard_map/ppermute | solution.py:14
  74.2 6.1 %shard_map.66 = (f32[1024,72]{1,0:T(8,128)S(1)}, f32[1024,128]{1,0:T(8,128)S(1)}) custom-call(s32[3]{0:T(128)S(1)} %bitcast.22, bf16[1024,72]{1,0:T(8,128)(2,1)S(1)} %get-tuple-element.16.query_ref, bf16[144,1024]{1,0:T(8,128)(2,1)S(1)} %get-tuple-element.18.own_ref, bf16[144,1024]{1,0:T(8,128)(2,1)S(1)} %collective-permute-done.4.refs_0_, ...), custom_call_target="tpu_custom_call" | custom-call | flops 3221225472 | bytes 884736 | tf_op jit(solution)/shard_map/pallas_call | solution.py:163
  80.3 9.4 %all-to-all-done.1 = bf16[16,64,1152]{2,1,0:T(8,128)(2,1)} async-done(((bf16[16,64,1152]{2,1,0:T(8,128)(2,1)}), bf16[16,64,1152]{2,1,0:T(8,128)(2,1)}, u32[]{:S(2)}, u32[]{:S(2)}) %all-to-all-start.1) | async-done | bytes 2359328 | tf_op jit(solution)/shard_map/all_to_all | solution.py:39
  89.7 2.6 %shard_map.67.refs_0_ = bf16[144,1024]{1,0:T(8,128)(2,1)S(1)} custom-call(bf16[1024,1152]{1,0:T(8,128)(2,1)} %bitcast.8.rows_ref, bf16[144,1152]{1,0:T(8,128)(2,1)S(1)} %slice_bitcast_fusion.weight_ref, f32[72,2]{1,0:T(8,128)S(1)} %bitcast.16), custom_call_target="tpu_custom_call" | custom-call | flops 339738624 | bytes 2359296 | tf_op jit(solution)/shard_map/pallas_call | solution.py:69
  92.3 3.9 %shard_map.68 = bf16[4,72,256]{2,1,0:T(8,128)(2,1)} custom-call(s32[3]{0:T(128)S(1)} %bitcast.23, bf16[1024,72]{1,0:T(8,128)(2,1)S(1)} %copy-done.6, f32[1024,72]{1,0:T(8,128)S(1)} %get-tuple-element.21.own_in_ref, f32[1024,128]{1,0:T(8,128)S(1)} %get-tuple-element.22.state_ref, bf16[144,1024]{1,0:T(8,128)(2,1)S(1)} %shard_map.67.refs_0_), custom_call_target="tpu_custom_call" | custom-call | flops 1073741824 | bytes 294912 | tf_op jit(solution)/shard_map/pallas_call | solution.py:163
  96.2 3.3 %all-to-all-start.2 = ((bf16[4,72,256]{2,1,0:T(8,128)(2,1)}), bf16[4,72,256]{2,1,0:T(8,128)(2,1)S(1)}, u32[]{:S(2)}, u32[]{:S(2)}) async-start(bf16[4,72,256]{2,1,0:T(8,128)(2,1)} %shard_map.68), calls=%async_computation.2 | async-start | bytes 294912 | tf_op jit(solution)/shard_map/all_to_all | solution.py:208
  99.6 6.0 %all-to-all-done.2.parts_ref = bf16[4,72,256]{2,1,0:T(8,128)(2,1)S(1)} async-done(((bf16[4,72,256]{2,1,0:T(8,128)(2,1)}), bf16[4,72,256]{2,1,0:T(8,128)(2,1)S(1)}, u32[]{:S(2)}, u32[]{:S(2)}) %all-to-all-start.2) | async-done | bytes 147488 | tf_op jit(solution)/shard_map/all_to_all | solution.py:208
  105.6 0.8 shard_map.69
  106.4 10.8 %all_to_all.20 = bf16[4,64,1152]{2,1,0:T(8,128)(2,1)S(1)} all-to-all(bf16[4,64,1152]{2,1,0:T(8,128)(2,1)S(1)} %shard_map.69), channel_id=1, replica_groups={{0,1,2,3},{4,5,6,7},{8,9,10,11},{12,13,14,15},{16,17,18,19},{20,21,22,2..., dimensions={0} | all-to-all | bytes 1179648 | tf_op jit(solution)/shard_map/all_to_all | solution.py:208
  117.2 0.8 reduce_sum.12
  (25 shorter events, 1.8 us)
Async XLA Ops:
  0.7 0.9 copy-start.4
  3.6 7.2 %copy-start.1 = (bf16[1,72,1152]{2,1,0:T(8,128)(2,1)S(1)}, bf16[1,72,1152]{2,1,0:T(8,128)(2,1)}, u32[]{:S(2)}) copy-start(bf16[1,72,1152]{2,1,0:T(8,128)(2,1)} %param.10) | copy-start | bytes 497668
  3.6 44.0 %all-to-all-start = ((bf16[16,64,1152]{2,1,0:T(8,128)(2,1)}), bf16[16,64,1152]{2,1,0:T(8,128)(2,1)S(1)}, u32[]{:S(2)}, u32[]{:S(2)}) async-start(bf16[16,64,1152]{2,1,0:T(8,128)(2,1)} %broadcast_in_dim.20), calls=%async_computation | async-start | bytes 4718592 | tf_op jit(solution)/shard_map/all_to_all | solution.py:39
  10.8 34.7 %collective-permute-start.1 = (bf16[72,1152]{1,0:T(8,128)(2,1)S(1)}, bf16[72,1152]{1,0:T(8,128)(2,1)S(1)}, u32[]{:S(2)}, u32[]{:S(2)}) collective-permute-start(bf16[72,1152]{1,0:T(8,128)(2,1)S(1)} %bitcast.17), channel_id=1, source_target_pairs={{4,0},{5,1},{6,2},{7,3},{8,4},{9,5},{10,6},{11,7},{12,8},{13,9},{1... | collective-permute-start | bytes 497672 | tf_op jit(solution)/shard_map/ppermute | solution.py:217
  15.8 29.7 %collective-permute-start.2 = (bf16[72,1152]{1,0:T(8,128)(2,1)S(1)}, bf16[72,1152]{1,0:T(8,128)(2,1)S(1)}, u32[]{:S(2)}, u32[]{:S(2)}) collective-permute-start(bf16[72,1152]{1,0:T(8,128)(2,1)S(1)} %bitcast.18), channel_id=1, source_target_pairs={{8,0},{9,1},{10,2},{11,3},{12,4},{13,5},{14,6},{15,7},{0,8},{1,9},... | collective-permute-start | bytes 497672 | tf_op jit(solution)/shard_map/ppermute | solution.py:217
  18.6 28.3 %collective-permute-start.3 = (bf16[72,1152]{1,0:T(8,128)(2,1)S(1)}, bf16[72,1152]{1,0:T(8,128)(2,1)S(1)}, u32[]{:S(2)}, u32[]{:S(2)}) collective-permute-start(bf16[72,1152]{1,0:T(8,128)(2,1)S(1)} %bitcast.19), channel_id=1, source_target_pairs={{12,0},{13,1},{14,2},{15,3},{0,4},{1,5},{2,6},{3,7},{4,8},{5,9},{6... | collective-permute-start | bytes 497672 | tf_op jit(solution)/shard_map/ppermute | solution.py:217
  21.4 24.1 %collective-permute-start = (bf16[64,1152]{1,0:T(8,128)(2,1)S(1)}, bf16[64,1152]{1,0:T(8,128)(2,1)S(1)}, u32[]{:S(2)}, u32[]{:S(2)}) collective-permute-start(bf16[64,1152]{1,0:T(8,128)(2,1)S(1)} %shard_map.64), channel_id=1, source_target_pairs={{0,256},{16,272},{32,288},{48,304},{64,320},{80,336},{96,352},{112... | collective-permute-start | bytes 442376 | tf_op jit(solution)/shard_map/ppermute | solution.py:14
  46.9 0.7 copy-start.2
  49.3 5.2 %copy-start.8 = (f32[1,2,72]{2,1,0:T(2,128)S(1)}, f32[1,2,72]{2,1,0:T(2,128)}, u32[]{:S(2)}) copy-start(f32[1,2,72]{2,1,0:T(2,128)} %param.9) | copy-start | bytes 1732
  49.3 5.3 %copy-start = (bf16[1,216,1152]{2,1,0:T(8,128)(2,1)S(1)}, bf16[1,216,1152]{2,1,0:T(8,128)(2,1)}, u32[]{:S(2)}) copy-start(bf16[1,216,1152]{2,1,0:T(8,128)(2,1)} %param.8) | copy-start | bytes 1492996
  49.3 40.4 %all-to-all-start.1 = ((bf16[16,64,1152]{2,1,0:T(8,128)(2,1)}), bf16[16,64,1152]{2,1,0:T(8,128)(2,1)}, u32[]{:S(2)}, u32[]{:S(2)}) async-start(bf16[16,64,1152]{2,1,0:T(8,128)(2,1)} %broadcast_in_dim.21), calls=%async_computation.1 | async-start | bytes 4718592 | tf_op jit(solution)/shard_map/all_to_all | solution.py:39
  54.5 19.7 %copy-start.7 = (s32[3,1]{0,1:T(1,128)S(1)}, s32[3,1]{0,1:T(1,128)}, u32[]{:S(2)}) copy-start(s32[3,1]{0,1:T(1,128)} %param.11) | copy-start | bytes 40
  55.6 18.5 %copy-start.5 = (bf16[1024,72]{1,0:T(8,128)(2,1)}, bf16[1024,72]{1,0:T(8,128)(2,1)S(1)}, u32[]{:S(2)}) copy-start(bf16[1024,72]{1,0:T(8,128)(2,1)S(1)} %get-tuple-element.16.query_ref) | copy-start | bytes 442372
  55.6 5.3 %collective-permute-start.4 = (bf16[144,1024]{1,0:T(8,128)(2,1)S(1)}, bf16[144,1024]{1,0:T(8,128)(2,1)S(1)}, u32[]{:S(2)}, u32[]{:S(2)}) collective-permute-start(bf16[144,1024]{1,0:T(8,128)(2,1)S(1)} %get-tuple-element.18.own_ref), channel_id=1, source_target_pairs={{0,16},{16,0},{32,48},{48,32},{64,80},{80,64},{96,112},{112,96},{1... | collective-permute-start | bytes 884744 | tf_op jit(solution)/shard_map/ppermute | solution.py:14
  57.6 16.6 %collective-permute-start.5 = (bf16[144,1024]{1,0:T(8,128)(2,1)S(1)}, bf16[144,1024]{1,0:T(8,128)(2,1)S(1)}, u32[]{:S(2)}, u32[]{:S(2)}) collective-permute-start(bf16[144,1024]{1,0:T(8,128)(2,1)S(1)} %get-tuple-element.18.own_ref), channel_id=1, source_target_pairs={{0,64},{16,80},{32,96},{48,112},{64,0},{80,16},{96,32},{112,48},{1... | collective-permute-start | bytes 884744 | tf_op jit(solution)/shard_map/ppermute | solution.py:14
  80.3 12.0 %copy-start.6 = (bf16[1024,72]{1,0:T(8,128)(2,1)S(1)}, bf16[1024,72]{1,0:T(8,128)(2,1)}, u32[]{:S(2)}) copy-start(bf16[1024,72]{1,0:T(8,128)(2,1)} %copy-done.5) | copy-start | bytes 442372
  92.3 13.3 %copy-start.3 = (bf16[72,1152]{1,0:T(8,128)(2,1)S(1)}, bf16[72,1152]{1,0:T(8,128)(2,1)}, u32[]{:S(2)}) copy-start(bf16[72,1152]{1,0:T(8,128)(2,1)} %copy-done.2) | copy-start | bytes 497668
  96.2 9.4 %all-to-all-start.2 = ((bf16[4,72,256]{2,1,0:T(8,128)(2,1)}), bf16[4,72,256]{2,1,0:T(8,128)(2,1)S(1)}, u32[]{:S(2)}, u32[]{:S(2)}) async-start(bf16[4,72,256]{2,1,0:T(8,128)(2,1)} %shard_map.68), calls=%async_computation.2 | async-start | bytes 294912 | tf_op jit(solution)/shard_map/all_to_all | solution.py:208

commit v7 on v6

--- a/solution.py
+++ b/solution.py
@@ -14,30 +14,59 @@
     return lax.ppermute(array, "view", [(i, i ^ 1 << bit) for i in range(lax.axis_size("view"))])
 
 
-def normalize_kernel(rows_ref, gain_ref, out_ref):
+def spread(source_ref, slots_ref, sems):
+    copies = [
+        pltpu.make_async_copy(source_ref, slots_ref.at[n], sems.at[n]) for n in range(slots_ref.shape[0])
+    ]
+    for copy in copies:
+        copy.start()
+    for copy in copies:
+        copy.wait()
+
+
+def normalize_kernel(rows_ref, gain_ref, out_ref, slots_ref, sems):
     values = rows_ref[...].astype(jnp.float32)
     mean = jnp.mean(values, axis=-1, keepdims=True)
     centred = values - mean
     var = jnp.mean(centred * centred, axis=-1, keepdims=True)
-    out_ref[...] = (centred * lax.rsqrt(var + 1e-06) * gain_ref[...]).astype(jnp.bfloat16)
-
-
-def normalize(rows, norm_gain):
+    gain = gain_ref[...].reshape(1, -1)
+    out_ref[...] = (centred * lax.rsqrt(var + 1e-06) * gain).astype(jnp.bfloat16)
+    spread(out_ref, slots_ref, sems)
+
+
+def normalize(rows, norm_gain, slots):
+    vmem = pl.BlockSpec(memory_space=pltpu.VMEM)
     return pl.pallas_call(
         normalize_kernel,
-        out_shape=jax.ShapeDtypeStruct(rows.shape, jnp.bfloat16),
+        out_shape=[
+            jax.ShapeDtypeStruct(rows.shape, jnp.bfloat16),
+            pltpu.HBM((slots,) + rows.shape, jnp.bfloat16),
+        ],
+        in_specs=[vmem, vmem],
+        out_specs=[vmem, pl.BlockSpec(memory_space=pltpu.HBM)],
+        scratch_shapes=[pltpu.SemaphoreType.DMA((slots,))],
         compiler_params=pltpu.CompilerParams(vmem_limit_bytes=16 << 20),
         cost_estimate=pl.CostEstimate(
-            flops=8 * rows.size, bytes_accessed=4 * rows.size, transcendentals=0
+            flops=8 * rows.size, bytes_accessed=2 * slots * rows.size, transcendentals=0
         ),
-    )(rows, norm_gain[None])
-
-
-def gather_tokens(normed):
-    heads = lax.axis_size("head")
-    copies = jnp.broadcast_to(normed[None], (heads,) + normed.shape)
-    rows = lax.all_to_all(copies, "head", split_axis=0, concat_axis=0, tiled=True)
-    return rows.reshape(-1, normed.shape[-1])
+    )(rows, norm_gain)
+
+
+def copies_of(rows, slots):
+    return pl.pallas_call(
+        spread,
+        out_shape=pltpu.HBM((slots,) + rows.shape, rows.dtype),
+        in_specs=[pl.BlockSpec(memory_space=pltpu.VMEM)],
+        out_specs=pl.BlockSpec(memory_space=pltpu.HBM),
+        scratch_shapes=[pltpu.SemaphoreType.DMA((slots,))],
+        compiler_params=pltpu.CompilerParams(vmem_limit_bytes=16 << 20),
+        cost_estimate=pl.CostEstimate(flops=0, bytes_accessed=2 * slots * rows.size, transcendentals=0),
+    )(rows)
+
+
+def gather_tokens(slots):
+    rows = lax.all_to_all(slots, "head", split_axis=0, concat_axis=0, tiled=True)
+    return rows.reshape(-1, slots.shape[-1])
 
 
 def rms_rows(part, gain):
@@ -63,13 +92,23 @@
 def project(rows, weight, gain, with_query):
     tokens, width = rows.shape
     head_dim = gain.shape[0]
+    block = tokens if with_query else tokens // 4
     out_shape = [jax.ShapeDtypeStruct((2 * head_dim, tokens), jnp.bfloat16)]
+    out_specs = [pl.BlockSpec((2 * head_dim, block), lambda n: (0, n))]
     if with_query:
         out_shape = [jax.ShapeDtypeStruct((tokens, head_dim), jnp.bfloat16)] + out_shape
+        out_specs = [pl.BlockSpec((block, head_dim), lambda n: (n, 0))] + out_specs
     return pl.pallas_call(
         functools.partial(project_kernel, with_query),
+        grid=(tokens // block,),
         out_shape=out_shape,
-        compiler_params=pltpu.CompilerParams(vmem_limit_bytes=16 << 20),
+        in_specs=[
+            pl.BlockSpec((block, width), lambda n: (n, 0)),
+            pl.BlockSpec(weight.shape, lambda n: (0, 0)),
+            pl.BlockSpec(gain.shape, lambda n: (0, 0)),
+        ],
+        out_specs=out_specs,
+        compiler_params=pltpu.CompilerParams(vmem_limit_bytes=20 << 20),
         cost_estimate=pl.CostEstimate(
             flops=2 * tokens * width * weight.shape[0], bytes_accessed=2 * tokens * width, transcendentals=0
         ),
@@ -211,42 +250,61 @@
 
 
 def column_weights(weight):
-    heads = lax.axis_size("head")
+    views, heads = lax.axis_size("view"), lax.axis_size("head")
     side = len(groups(0))
-    return [
-        lax.ppermute(weight, "head", [((head + step * side) % heads, head) for head in range(heads)])
-        for step in range(1, side)
-    ]
-
-
-def project_out_kernel(line_ref, parts_ref, *refs):
-    weight_refs, out_ref = refs[:-1], refs[-1]
-    side = len(weight_refs)
-    total = None
-    for step, weight_ref in enumerate(weight_refs):
-        part = parts_ref[lax.rem(line_ref[0] + step, side)]
-        term = lax.dot_general(
-            part, weight_ref[...], (((0,), (0,)), ((), ())), preferred_element_type=jnp.float32
+    core = lax.axis_index("view") % 2
+    width = weight.shape[1]
+    part = (width // 2 + 127) // 128 * 128
+    pairs = []
+    for view in range(views):
+        step = side if view % 2 == 0 else -side
+        for head in range(heads):
+            pairs.append((view * heads + (head + step) % heads, view * heads + head))
+    beside = lax.ppermute(weight, ("view", "head"), pairs)
+    sent = jnp.where(core == 0, weight[:, :part], weight[:, width - part :])
+    across = [(head, (head + heads // 2) % heads) for head in range(heads)]
+    mine = jnp.concatenate([beside, lax.ppermute(sent, "head", across)], axis=1)
+    return mine, partner(mine, 0)
+
+
+def project_out_kernel(place_ref, parts_ref, weight_ref, mine_ref, other_ref, out_ref):
+    side = parts_ref.shape[0]
+    line, core = place_ref[0], place_ref[1]
+    width = weight_ref.shape[1]
+    part = mine_ref.shape[1] - width
+
+    def product(step, weight):
+        rows = parts_ref[lax.rem(line + step, side)]
+        return lax.dot_general(
+            rows, weight, (((0,), (0,)), ((), ())), preferred_element_type=jnp.float32
         )
-        total = term if total is None else total + term
+
+    turn = jnp.where(core == 0, 1, side - 1)
+    total = product(0, weight_ref[...])
+    total = total + product(turn, mine_ref[:, :width])
+    total = total + product(side - turn, other_ref[:, :width])
+    mine, other = product(side // 2, mine_ref[:, width:]), product(side // 2, other_ref[:, width:])
+    low, high = jnp.where(core == 0, mine, other), jnp.where(core == 0, other, mine)
+    total = total + jnp.concatenate([low[:, : width - part], high], axis=1)
     out_ref[...] = total.reshape(out_ref.shape).astype(jnp.bfloat16)
 
 
-def project_out(parts, weights):
+def project_out(parts, weight, mine, other):
     side, head_dim, tokens = parts.shape
-    width = weights[0].shape[1]
-    line = (lax.axis_index("head") // side).astype(jnp.int32)[None]
+    width = weight.shape[1]
+    line, core = lax.axis_index("head") // side, lax.axis_index("view") % 2
+    place = jnp.stack([line, core]).astype(jnp.int32)
     smem, vmem = pl.BlockSpec(memory_space=pltpu.SMEM), pl.BlockSpec(memory_space=pltpu.VMEM)
     partial = pl.pallas_call(
         project_out_kernel,
         out_shape=jax.ShapeDtypeStruct((side, tokens // side, width), jnp.bfloat16),
-        in_specs=[smem] + [vmem] * (1 + len(weights)),
+        in_specs=[smem] + [vmem] * 4,
         out_specs=vmem,
         compiler_params=pltpu.CompilerParams(vmem_limit_bytes=16 << 20),
         cost_estimate=pl.CostEstimate(
             flops=2 * parts.size * width, bytes_accessed=2 * (side * head_dim + tokens) * width, transcendentals=0
         ),
-    )(line, parts, *weights)
+    )(place, parts, weight, mine, other)
     partial = exchange(partial, 0)
     return jnp.sum(partial.astype(jnp.float32), axis=0).astype(jnp.bfloat16)
 
@@ -261,20 +319,23 @@
     head_dim = gain.shape[0]
     weight = qkv_weight[0]
     active = intersection[:, 0]
-    normed = normalize(rows, norm_gain)
-    far_normed = partner(normed, bits[-1])
-    far_normed, out_weights = lax.optimization_barrier(
-        (far_normed, column_weights(out_weight[0]))
-    )
-    every = gather_tokens(normed)
-    far_every = gather_tokens(far_normed)
+    heads = lax.axis_size("head")
+    normed, slots = normalize(rows, norm_gain, heads)
+    far_slots = copies_of(partner(normed, bits[-1]), heads)
+    every, far_slots = lax.optimization_barrier((gather_tokens(slots), far_slots))
+    far_every = gather_tokens(far_slots)
     query, own = project(every, weight, gain, True)
     near = [partner(own, bit) for bit in bits[:-1]]
+    near[0], out_rows = lax.optimization_barrier((near[0], out_weight[0]))
+    mine, other = column_weights(out_rows)
     own_result, state = attend_near(active, query, own, near)
-    far_every, own_result, state = lax.optimization_barrier((far_every, own_result, state))
+    far_every, own_result, state, mine, other = lax.optimization_barrier(
+        (far_every, own_result, state, mine, other)
+    )
+    far_every = pltpu.with_memory_space_constraint(far_every, pltpu.HBM)
     far = list(project(far_every, weight[head_dim:], gain, False))
     attended = attend_last(active, rounds - 1, query, own_result, state, far)
-    mixed = project_out(exchange(attended, 1), [out_weight[0]] + out_weights)
+    mixed = project_out(exchange(attended, 1), out_weight[0], mine, other)
     return mixed.reshape(loc_len, view_dev, width)
 
 

time: 119 us -> 124 us (1.042)
  the two profiles are of different devices: /device:TPU:448 before, /device:TPU:32 now
where the time goes in v7:
time: 124 us; the launch traced here: 123 us
  starting transfers between devices  48 us (39%)
  waiting for transfers between devices  38.4 us (31%)
  Pallas kernels  19.2 us (15%)
  blocking collectives  14.6 us (12%)
  local copies, waits for them, and re-layouts  1.78 us (1%)
    ppermute x4, starting transfers between devices, partner(): lax.ppermute(array, 'view', [(i, i ^ 1 << bit) for i in range(lax.axis_si...  24.2 us
    all_to_all x1, blocking collectives, exchange(): lax.all_to_all(slots, 'head', split_axis=0, concat_axis=0, tiled=True, ax...  14.6 us
    ppermute x1, waiting for transfers between devices, column_weights(): beside = lax.ppermute(weight, ('view', 'head'), pairs)  13.3 us
    ppermute x4, waiting for transfers between devices, partner(): lax.ppermute(array, 'view', [(i, i ^ 1 << bit) for i in range(lax.axis_si...  12.9 us
    all_to_all x2, starting transfers between devices, gather_tokens(): lax.all_to_all(slots, 'head', split_axis=0, concat_axis=0, tiled=True)  11.6 us
    pallas_call x2, Pallas kernels, call_attend(): pl.pallas_call(kernel, out_shape=out_shape, in_specs=[pl.BlockSpec(memory...  10.1 us
    all_to_all x2, waiting for transfers between devices, gather_tokens(): lax.all_to_all(slots, 'head', split_axis=0, concat_axis=0, tiled=True)  6.17 us
    all_to_all x1, waiting for transfers between devices, exchange(): lax.all_to_all(slots, 'head', split_axis=0, concat_axis=0, tiled=True, ax...  6.04 us
  transfers between devices with their start and end apart: 9, of which 4 were waited for; matrix products, arithmetic and copies ran while one was open for 0% of the time, Pallas kernels for 7%

profile of v7, /device:TPU:32, one launch (start us, length us, event | category | flops | bytes accessed | tf_op | source)
XLA Modules:
  0.0 123.0 jit_solution(4755115403005022911)
XLA Ops:
  0.0 0.9 copy-done.2
  0.9 0.7 copy-done.3
  1.6 1.8 %shard_map.64 = (bf16[64,1152]{1,0:T(8,128)(2,1)S(1)}, bf16[16,64,1152]{2,1,0:T(8,128)(2,1)}) custom-call(bf16[64,1152]{1,0:T(8,128)(2,1)S(1)} %bitcast.21, f32[1152]{0:T(1024)S(1)} %copy-done.3), custom_call_target="tpu_custom_call" | custom-call | flops 589824 | bytes 2359296 | tf_op jit(solution)/shard_map/pallas_call | solution.py:39
  3.4 7.0 %all-to-all-start = ((bf16[16,64,1152]{2,1,0:T(8,128)(2,1)}), bf16[16,64,1152]{2,1,0:T(8,128)(2,1)S(1)}, u32[]{:S(2)}, u32[]{:S(2)}) async-start(bf16[16,64,1152]{2,1,0:T(8,128)(2,1)} %get-tuple-element.20), calls=%async_computation | async-start | bytes 4718592 | tf_op jit(solution)/shard_map/all_to_all | solution.py:68
  10.4 14.8 %collective-permute-start = (bf16[64,1152]{1,0:T(8,128)(2,1)S(1)}, bf16[64,1152]{1,0:T(8,128)(2,1)S(1)}, u32[]{:S(2)}, u32[]{:S(2)}) collective-permute-start(bf16[64,1152]{1,0:T(8,128)(2,1)S(1)} %get-tuple-element.21), channel_id=1, source_target_pairs={{0,256},{16,272},{32,288},{48,304},{64,320},{80,336},{96,352},{112... | collective-permute-start | bytes 442376 | tf_op jit(solution)/shard_map/ppermute | solution.py:14
  25.3 12.9 %collective-permute-done.source_ref = bf16[64,1152]{1,0:T(8,128)(2,1)S(1)} collective-permute-done((bf16[64,1152]{1,0:T(8,128)(2,1)S(1)}, bf16[64,1152]{1,0:T(8,128)(2,1)S(1)}, u32[]{:S(2)}, u32[]{:S(2)}) %collective-permute-start) | collective-permute-done | bytes 147488 | tf_op jit(solution)/shard_map/ppermute | solution.py:14
  38.2 1.6 %shard_map.65 = bf16[16,64,1152]{2,1,0:T(8,128)(2,1)} custom-call(bf16[64,1152]{1,0:T(8,128)(2,1)S(1)} %collective-permute-done.source_ref), custom_call_target="tpu_custom_call" | custom-call | bytes 2359296 | tf_op jit(solution)/shard_map/pallas_call | solution.py:56
  39.8 6.2 %all-to-all-done = bf16[16,64,1152]{2,1,0:T(8,128)(2,1)S(1)} async-done(((bf16[16,64,1152]{2,1,0:T(8,128)(2,1)}), bf16[16,64,1152]{2,1,0:T(8,128)(2,1)S(1)}, u32[]{:S(2)}, u32[]{:S(2)}) %all-to-all-start) | async-done | bytes 2359328 | tf_op jit(solution)/shard_map/all_to_all | solution.py:68
  45.9 4.6 %all-to-all-start.1 = ((bf16[16,64,1152]{2,1,0:T(8,128)(2,1)}), bf16[16,64,1152]{2,1,0:T(8,128)(2,1)}, u32[]{:S(2)}, u32[]{:S(2)}) async-start(bf16[16,64,1152]{2,1,0:T(8,128)(2,1)} %shard_map.65), calls=%async_computation.1 | async-start | bytes 4718592 | tf_op jit(solution)/shard_map/all_to_all | solution.py:68
  50.7 1.0 shard_map.66
  51.7 1.9 %collective-permute-start.1 = (bf16[144,1024]{1,0:T(8,128)(2,1)S(1)}, bf16[144,1024]{1,0:T(8,128)(2,1)S(1)}, u32[]{:S(2)}, u32[]{:S(2)}) collective-permute-start(bf16[144,1024]{1,0:T(8,128)(2,1)S(1)} %get-tuple-element.25.own_ref), channel_id=1, source_target_pairs={{0,16},{16,0},{32,48},{48,32},{64,80},{80,64},{96,112},{112,96},{1... | collective-permute-start | bytes 884744 | tf_op jit(solution)/shard_map/ppermute | solution.py:14
  53.7 5.2 %collective-permute-start.2 = (bf16[144,1024]{1,0:T(8,128)(2,1)S(1)}, bf16[144,1024]{1,0:T(8,128)(2,1)S(1)}, u32[]{:S(2)}, u32[]{:S(2)}) collective-permute-start(bf16[144,1024]{1,0:T(8,128)(2,1)S(1)} %get-tuple-element.25.own_ref), channel_id=1, source_target_pairs={{0,64},{16,80},{32,96},{48,112},{64,0},{80,16},{96,32},{112,48},{1... | collective-permute-start | bytes 884744 | tf_op jit(solution)/shard_map/ppermute | solution.py:14
  58.9 4.9 %collective-permute-start.3 = (bf16[72,1152]{1,0:T(8,128)(2,1)S(1)}, bf16[72,1152]{1,0:T(8,128)(2,1)S(1)}, u32[]{:S(2)}, u32[]{:S(2)}) collective-permute-start(bf16[72,1152]{1,0:T(8,128)(2,1)S(1)} %bitcast.16), channel_id=1, source_target_pairs={{4,0},{5,1},{6,2},{7,3},{8,4},{9,5},{10,6},{11,7},{12,8},{13,9},{1... | collective-permute-start | bytes 497672 | tf_op jit(solution)/shard_map/ppermute | solution.py:263
  63.9 2.7 %collective-permute-start.4 = (bf16[72,640]{1,0:T(8,128)(2,1)S(1)}, bf16[72,640]{1,0:T(8,128)(2,1)S(1)}, u32[]{:S(2)}, u32[]{:S(2)}) collective-permute-start(bf16[72,640]{1,0:T(8,128)(2,1)S(1)} %slice_select_fusion), channel_id=1, source_target_pairs={{0,8},{1,9},{2,10},{3,11},{4,12},{5,13},{6,14},{7,15},{8,0},{9,1},... | collective-permute-start | bytes 276488 | tf_op jit(solution)/shard_map/ppermute | solution.py:266
  66.6 13.3 %collective-permute-done.3 = bf16[72,1152]{1,0:T(8,128)(2,1)S(1)} collective-permute-done((bf16[72,1152]{1,0:T(8,128)(2,1)S(1)}, bf16[72,1152]{1,0:T(8,128)(2,1)S(1)}, u32[]{:S(2)}, u32[]{:S(2)}) %collective-permute-start.3) | collective-permute-done | bytes 165920 | tf_op jit(solution)/shard_map/ppermute | solution.py:263
  79.9 2.3 %collective-permute-start.5 = (bf16[72,1792]{1,0:T(8,128)(2,1)S(1)}, bf16[72,1792]{1,0:T(8,128)(2,1)S(1)}, u32[]{:S(2)}, u32[]{:S(2)}) collective-permute-start(bf16[72,1792]{1,0:T(8,128)(2,1)S(1)} %constant_dynamic-update-slice_fusion.mine_ref), channel_id=1, source_target_pairs={{0,16},{16,0},{32,48},{48,32},{64,80},{80,64},{96,112},{112,96},{1... | collective-permute-start | bytes 774152 | tf_op jit(solution)/shard_map/ppermute | solution.py:14
  82.2 6.1 %shard_map.67 = (f32[1024,72]{1,0:T(8,128)S(1)}, f32[1024,128]{1,0:T(8,128)S(1)}) custom-call(s32[3]{0:T(128)S(1)} %bitcast.22, bf16[1024,72]{1,0:T(8,128)(2,1)S(1)} %get-tuple-element.23.query_ref, bf16[144,1024]{1,0:T(8,128)(2,1)S(1)} %get-tuple-element.25.own_ref, bf16[144,1024]{1,0:T(8,128)(2,1)S(1)} %collective-permute-done.1.refs_0_, ...), custom_call_target="tpu_custom_call" | custom-call | flops 3221225472 | bytes 884736 | tf_op jit(solution)/shard_map/pallas_call | solution.py:202
  88.4 3.3 %shard_map.68.refs_0_ = bf16[144,1024]{1,0:T(8,128)(2,1)S(1)} custom-call(bf16[1024,1152]{1,0:T(8,128)(2,1)} %bitcast.8.rows_ref, bf16[144,1152]{1,0:T(8,128)(2,1)S(1)} %slice_bitcast_fusion.weight_ref, f32[72,2]{1,0:T(8,128)S(1)} %bitcast.20), custom_call_target="tpu_custom_call" | custom-call | flops 339738624 | bytes 2359296 | tf_op jit(solution)/shard_map/pallas_call | solution.py:101
  91.7 4.0 %shard_map.69 = bf16[4,72,256]{2,1,0:T(8,128)(2,1)} custom-call(s32[3]{0:T(128)S(1)} %bitcast.23, bf16[1024,72]{1,0:T(8,128)(2,1)S(1)} %get-tuple-element.23.query_ref, f32[1024,72]{1,0:T(8,128)S(1)} %get-tuple-element.30.own_in_ref, f32[1024,128]{1,0:T(8,128)S(1)} %get-tuple-element.31.state_ref, bf16[144,1024]{1,0:T(8,128)(2,1)S(1)} %shard_map.68.refs_0_), custom_call_target="tpu_custom_call" | custom-call | flops 1073741824 | bytes 294912 | tf_op jit(solution)/shard_map/pallas_call | solution.py:202
  95.7 4.5 %all-to-all-start.2 = ((bf16[4,72,256]{2,1,0:T(8,128)(2,1)}), bf16[4,72,256]{2,1,0:T(8,128)(2,1)S(1)}, u32[]{:S(2)}, u32[]{:S(2)}) async-start(bf16[4,72,256]{2,1,0:T(8,128)(2,1)} %shard_map.69), calls=%async_computation.2 | async-start | bytes 294912 | tf_op jit(solution)/shard_map/all_to_all | solution.py:247
  100.3 6.0 %all-to-all-done.2.parts_ref = bf16[4,72,256]{2,1,0:T(8,128)(2,1)S(1)} async-done(((bf16[4,72,256]{2,1,0:T(8,128)(2,1)}), bf16[4,72,256]{2,1,0:T(8,128)(2,1)S(1)}, u32[]{:S(2)}, u32[]{:S(2)}) %all-to-all-start.2) | async-done | bytes 147488 | tf_op jit(solution)/shard_map/all_to_all | solution.py:247
  106.3 1.4 %shard_map.70 = bf16[4,64,1152]{2,1,0:T(8,128)(2,1)S(1)} custom-call(s32[2]{0:T(128)S(1)} %pad_add_fusion.place_ref, bf16[4,72,256]{2,1,0:T(8,128)(2,1)S(1)} %all-to-all-done.2.parts_ref, bf16[72,1152]{1,0:T(8,128)(2,1)S(1)} %bitcast.18, bf16[72,1792]{1,0:T(8,128)(2,1)S(1)} %constant_dynamic-update-slice_fusion.mine_ref, ...), custom_call_target="tpu_custom_call" | custom-call | flops 169869312 | bytes 1253376 | tf_op jit(solution)/shard_map/pallas_call | solution.py:298
  107.7 14.6 %all_to_all.20 = bf16[4,64,1152]{2,1,0:T(8,128)(2,1)S(1)} all-to-all(bf16[4,64,1152]{2,1,0:T(8,128)(2,1)S(1)} %shard_map.70), channel_id=1, replica_groups={{0,1,2,3},{4,5,6,7},{8,9,10,11},{12,13,14,15},{16,17,18,19},{20,21,22,2..., dimensions={0} | all-to-all | bytes 1179648 | tf_op jit(solution)/shard_map/all_to_all | solution.py:247
  122.3 0.8 reduce_sum.12
  (21 shorter events, 0.3 us)
Async XLA Ops:
  0.0 0.9 copy-start.2
  0.9 0.7 copy-start.3
  3.4 42.6 %all-to-all-start = ((bf16[16,64,1152]{2,1,0:T(8,128)(2,1)}), bf16[16,64,1152]{2,1,0:T(8,128)(2,1)S(1)}, u32[]{:S(2)}, u32[]{:S(2)}) async-start(bf16[16,64,1152]{2,1,0:T(8,128)(2,1)} %get-tuple-element.20), calls=%async_computation | async-start | bytes 4718592 | tf_op jit(solution)/shard_map/all_to_all | solution.py:68
  10.4 27.8 %collective-permute-start = (bf16[64,1152]{1,0:T(8,128)(2,1)S(1)}, bf16[64,1152]{1,0:T(8,128)(2,1)S(1)}, u32[]{:S(2)}, u32[]{:S(2)}) collective-permute-start(bf16[64,1152]{1,0:T(8,128)(2,1)S(1)} %get-tuple-element.21), channel_id=1, source_target_pairs={{0,256},{16,272},{32,288},{48,304},{64,320},{80,336},{96,352},{112... | collective-permute-start | bytes 442376 | tf_op jit(solution)/shard_map/ppermute | solution.py:14
  45.9 4.6 %copy-start.5 = (f32[1,2,72]{2,1,0:T(2,128)S(1)}, f32[1,2,72]{2,1,0:T(2,128)}, u32[]{:S(2)}) copy-start(f32[1,2,72]{2,1,0:T(2,128)} %param.9) | copy-start | bytes 1732
  45.9 4.7 %copy-start = (bf16[1,216,1152]{2,1,0:T(8,128)(2,1)S(1)}, bf16[1,216,1152]{2,1,0:T(8,128)(2,1)}, u32[]{:S(2)}) copy-start(bf16[1,216,1152]{2,1,0:T(8,128)(2,1)} %param.8) | copy-start | bytes 1492996
  45.9 42.4 %all-to-all-start.1 = ((bf16[16,64,1152]{2,1,0:T(8,128)(2,1)}), bf16[16,64,1152]{2,1,0:T(8,128)(2,1)}, u32[]{:S(2)}, u32[]{:S(2)}) async-start(bf16[16,64,1152]{2,1,0:T(8,128)(2,1)} %shard_map.65), calls=%async_computation.1 | async-start | bytes 4718592 | tf_op jit(solution)/shard_map/all_to_all | solution.py:68
  50.5 8.3 %copy-start.1 = (bf16[1,72,1152]{2,1,0:T(8,128)(2,1)S(1)}, bf16[1,72,1152]{2,1,0:T(8,128)(2,1)}, u32[]{:S(2)}) copy-start(bf16[1,72,1152]{2,1,0:T(8,128)(2,1)} %param.10) | copy-start | bytes 497668
  50.5 31.7 %copy-start.4 = (s32[3,1]{0,1:T(1,128)S(1)}, s32[3,1]{0,1:T(1,128)}, u32[]{:S(2)}) copy-start(s32[3,1]{0,1:T(1,128)} %param.11) | copy-start | bytes 40
  51.7 7.1 %collective-permute-start.1 = (bf16[144,1024]{1,0:T(8,128)(2,1)S(1)}, bf16[144,1024]{1,0:T(8,128)(2,1)S(1)}, u32[]{:S(2)}, u32[]{:S(2)}) collective-permute-start(bf16[144,1024]{1,0:T(8,128)(2,1)S(1)} %get-tuple-element.25.own_ref), channel_id=1, source_target_pairs={{0,16},{16,0},{32,48},{48,32},{64,80},{80,64},{96,112},{112,96},{1... | collective-permute-start | bytes 884744 | tf_op jit(solution)/shard_map/ppermute | solution.py:14
  53.7 28.5 %collective-permute-start.2 = (bf16[144,1024]{1,0:T(8,128)(2,1)S(1)}, bf16[144,1024]{1,0:T(8,128)(2,1)S(1)}, u32[]{:S(2)}, u32[]{:S(2)}) collective-permute-start(bf16[144,1024]{1,0:T(8,128)(2,1)S(1)} %get-tuple-element.25.own_ref), channel_id=1, source_target_pairs={{0,64},{16,80},{32,96},{48,112},{64,0},{80,16},{96,32},{112,48},{1... | collective-permute-start | bytes 884744 | tf_op jit(solution)/shard_map/ppermute | solution.py:14
  58.9 21.0 %collective-permute-start.3 = (bf16[72,1152]{1,0:T(8,128)(2,1)S(1)}, bf16[72,1152]{1,0:T(8,128)(2,1)S(1)}, u32[]{:S(2)}, u32[]{:S(2)}) collective-permute-start(bf16[72,1152]{1,0:T(8,128)(2,1)S(1)} %bitcast.16), channel_id=1, source_target_pairs={{4,0},{5,1},{6,2},{7,3},{8,4},{9,5},{10,6},{11,7},{12,8},{13,9},{1... | collective-permute-start | bytes 497672 | tf_op jit(solution)/shard_map/ppermute | solution.py:263
  63.9 16.0 %collective-permute-start.4 = (bf16[72,640]{1,0:T(8,128)(2,1)S(1)}, bf16[72,640]{1,0:T(8,128)(2,1)S(1)}, u32[]{:S(2)}, u32[]{:S(2)}) collective-permute-start(bf16[72,640]{1,0:T(8,128)(2,1)S(1)} %slice_select_fusion), channel_id=1, source_target_pairs={{0,8},{1,9},{2,10},{3,11},{4,12},{5,13},{6,14},{7,15},{8,0},{9,1},... | collective-permute-start | bytes 276488 | tf_op jit(solution)/shard_map/ppermute | solution.py:266
  79.9 8.5 %collective-permute-start.5 = (bf16[72,1792]{1,0:T(8,128)(2,1)S(1)}, bf16[72,1792]{1,0:T(8,128)(2,1)S(1)}, u32[]{:S(2)}, u32[]{:S(2)}) collective-permute-start(bf16[72,1792]{1,0:T(8,128)(2,1)S(1)} %constant_dynamic-update-slice_fusion.mine_ref), channel_id=1, source_target_pairs={{0,16},{16,0},{32,48},{48,32},{64,80},{80,64},{96,112},{112,96},{1... | collective-permute-start | bytes 774152 | tf_op jit(solution)/shard_map/ppermute | solution.py:14
  95.7 10.6 %all-to-all-start.2 = ((bf16[4,72,256]{2,1,0:T(8,128)(2,1)}), bf16[4,72,256]{2,1,0:T(8,128)(2,1)S(1)}, u32[]{:S(2)}, u32[]{:S(2)}) async-start(bf16[4,72,256]{2,1,0:T(8,128)(2,1)} %shard_map.69), calls=%async_computation.2 | async-start | bytes 294912 | tf_op jit(solution)/shard_map/all_to_all | solution.py:247

commit v8 on v7

--- a/solution.py
+++ b/solution.py
@@ -74,40 +74,70 @@
     return part * lax.rsqrt(square) * gain
 
 
-def project_kernel(with_query, rows_ref, weight_ref, gain_ref, *out_refs):
+def project_kernel(rows_ref, weight_ref, gain_ref, query_ref, pair_ref):
     head_dim = gain_ref.shape[0]
-    weight = weight_ref[...]
     flat = lax.dot_general(
-        weight, rows_ref[...], (((1,), (1,)), ((), ())), preferred_element_type=jnp.float32
+        weight_ref[...], rows_ref[...], (((1,), (1,)), ((), ())), preferred_element_type=jnp.float32
     )
     flat = flat.astype(jnp.bfloat16).astype(jnp.float32)
-    if with_query:
-        query = rms_rows(flat[:head_dim], gain_ref[:, 0:1])
-        out_refs[0][...] = query.T.astype(jnp.bfloat16)
-        flat = flat[head_dim:]
-    keys = rms_rows(flat[:head_dim], gain_ref[:, 1:2])
-    out_refs[-1][...] = jnp.concatenate([keys, flat[head_dim:]], axis=0).astype(jnp.bfloat16)
-
-
-def project(rows, weight, gain, with_query):
+    query_ref[...] = rms_rows(flat[:head_dim], gain_ref[:, 0:1]).T.astype(jnp.bfloat16)
+    keys = rms_rows(flat[head_dim : 2 * head_dim], gain_ref[:, 1:2])
+    pair = jnp.concatenate([keys, flat[2 * head_dim :]], axis=0)
+    pair_ref[...] = pair.astype(jnp.bfloat16)
+
+
+def project_far_kernel(rows_ref, weight_ref, gain_ref, pair_ref, held_ref, sems):
+    head_dim = gain_ref.shape[0]
+    skip = head_dim // 16 * 16
+    blocks, block = held_ref.shape[:2]
+    copies = [
+        pltpu.make_async_copy(rows_ref.at[pl.ds(n * block, block)], held_ref.at[n], sems.at[n])
+        for n in range(blocks)
+    ]
+    for copy in copies:
+        copy.start()
+    for n in range(blocks):
+        copies[n].wait()
+        flat = lax.dot_general(
+            weight_ref[skip:], held_ref[n], (((1,), (1,)), ((), ())), preferred_element_type=jnp.float32
+        )
+        flat = flat[head_dim - skip :].astype(jnp.bfloat16).astype(jnp.float32)
+        keys = rms_rows(flat[:head_dim], gain_ref[:, 1:2])
+        pair = jnp.concatenate([keys, flat[head_dim:]], axis=0)
+        pair_ref[:, pl.ds(n * block, block)] = pair.astype(jnp.bfloat16)
+
+
+def project(rows, weight, gain):
     tokens, width = rows.shape
     head_dim = gain.shape[0]
-    block = tokens if with_query else tokens // 4
-    out_shape = [jax.ShapeDtypeStruct((2 * head_dim, tokens), jnp.bfloat16)]
-    out_specs = [pl.BlockSpec((2 * head_dim, block), lambda n: (0, n))]
-    if with_query:
-        out_shape = [jax.ShapeDtypeStruct((tokens, head_dim), jnp.bfloat16)] + out_shape
-        out_specs = [pl.BlockSpec((block, head_dim), lambda n: (n, 0))] + out_specs
     return pl.pallas_call(
-        functools.partial(project_kernel, with_query),
-        grid=(tokens // block,),
-        out_shape=out_shape,
-        in_specs=[
-            pl.BlockSpec((block, width), lambda n: (n, 0)),
-            pl.BlockSpec(weight.shape, lambda n: (0, 0)),
-            pl.BlockSpec(gain.shape, lambda n: (0, 0)),
+        project_kernel,
+        out_shape=[
+            jax.ShapeDtypeStruct((tokens, head_dim), jnp.bfloat16),
+            jax.ShapeDtypeStruct((2 * head_dim, tokens), jnp.bfloat16),
         ],
-        out_specs=out_specs,
+        compiler_params=pltpu.CompilerParams(vmem_limit_bytes=16 << 20),
+        cost_estimate=pl.CostEstimate(
+            flops=2 * tokens * width * weight.shape[0], bytes_accessed=2 * tokens * width, transcendentals=0
+        ),
+    )(rows, weight, gain)
+
+
+def project_far(rows, weight, gain):
+    tokens, width = rows.shape
+    head_dim = gain.shape[0]
+    blocks = 2
+    vmem = pl.BlockSpec(memory_space=pltpu.VMEM)
+    rows = pltpu.with_memory_space_constraint(rows, pltpu.HBM)
+    return pl.pallas_call(
+        project_far_kernel,
+        out_shape=jax.ShapeDtypeStruct((2 * head_dim, tokens), jnp.bfloat16),
+        in_specs=[pl.BlockSpec(memory_space=pltpu.HBM), vmem, vmem],
+        out_specs=vmem,
+        scratch_shapes=[
+            pltpu.VMEM((blocks, tokens // blocks, width), jnp.bfloat16),
+            pltpu.SemaphoreType.DMA((blocks,)),
+        ],
         compiler_params=pltpu.CompilerParams(vmem_limit_bytes=20 << 20),
         cost_estimate=pl.CostEstimate(
             flops=2 * tokens * width * weight.shape[0], bytes_accessed=2 * tokens * width, transcendentals=0
@@ -174,6 +204,23 @@
         return carry
 
     lax.fori_loop(0, tokens // tile, step, 0, unroll=True)
+
+
+def middle_kernel(tile, first, active_ref, query_ref, state_ref, *refs):
+    far_refs, out_ref, values_ref = refs[:-2], refs[-2], refs[-1]
+    tokens, head_dim = query_ref.shape
+    padded = values_ref.shape[-1]
+    for n, ref in enumerate(far_refs):
+        values_ref[n] = spread_values(ref, head_dim, padded)
+    lane = lax.broadcasted_iota(jnp.int32, (tile, padded), 1)
+    for at in range(tokens // tile):
+        rows = pl.ds(at * tile, tile)
+        acc = state_ref[rows, :]
+        best = acc[:, head_dim + 1 : head_dim + 2]
+        best, acc = cross_update(
+            active_ref, first, query_ref[rows, :], far_refs, values_ref, 0, best, acc
+        )
+        out_ref[rows, :] = jnp.where(lane == head_dim + 1, best, acc)
 
 
 def last_kernel(tile, first, active_ref, query_ref, own_in_ref, state_ref, *refs):
@@ -226,6 +273,15 @@
     )
 
 
+def attend_middle(active, first, query, state, far):
+    tokens, head_dim = query.shape
+    out_shape = jax.ShapeDtypeStruct((tokens, PADDED), jnp.float32)
+    arrays = (active, query, state, *far)
+    return call_attend(
+        functools.partial(middle_kernel, 256, first), out_shape, len(far), tokens, head_dim, arrays
+    )
+
+
 def attend_last(active, first, query, own_result, state, far):
     tokens, head_dim = query.shape
     side = len(groups(0))
@@ -263,8 +319,7 @@
     beside = lax.ppermute(weight, ("view", "head"), pairs)
     sent = jnp.where(core == 0, weight[:, :part], weight[:, width - part :])
     across = [(head, (head + heads // 2) % heads) for head in range(heads)]
-    mine = jnp.concatenate([beside, lax.ppermute(sent, "head", across)], axis=1)
-    return mine, partner(mine, 0)
+    return jnp.concatenate([beside, lax.ppermute(sent, "head", across)], axis=1)
 
 
 def project_out_kernel(place_ref, parts_ref, weight_ref, mine_ref, other_ref, out_ref):
@@ -321,19 +376,22 @@
     active = intersection[:, 0]
     heads = lax.axis_size("head")
     normed, slots = normalize(rows, norm_gain, heads)
-    far_slots = copies_of(partner(normed, bits[-1]), heads)
+    far_normed, mine, gain, active = lax.optimization_barrier(
+        (partner(normed, bits[-1]), column_weights(out_weight[0]), gain, active)
+    )
+    far_slots = copies_of(far_normed, heads)
     every, far_slots = lax.optimization_barrier((gather_tokens(slots), far_slots))
     far_every = gather_tokens(far_slots)
-    query, own = project(every, weight, gain, True)
+    query, own = project(every, weight, gain)
     near = [partner(own, bit) for bit in bits[:-1]]
-    near[0], out_rows = lax.optimization_barrier((near[0], out_weight[0]))
-    mine, other = column_weights(out_rows)
-    own_result, state = attend_near(active, query, own, near)
-    far_every, own_result, state, mine, other = lax.optimization_barrier(
-        (far_every, own_result, state, mine, other)
-    )
-    far_every = pltpu.with_memory_space_constraint(far_every, pltpu.HBM)
-    far = list(project(far_every, weight[head_dim:], gain, False))
+    near[0], mine = lax.optimization_barrier((near[0], mine))
+    other = partner(mine, 0)
+    own_result, state = attend_near(active, query, own, near[:1])
+    state = attend_middle(active, 1, query, state, near[1:])
+    far_every, own_result, state, other = lax.optimization_barrier(
+        (far_every, own_result, state, other)
+    )
+    far = [project_far(far_every, weight, gain)]
     attended = attend_last(active, rounds - 1, query, own_result, state, far)
     mixed = project_out(exchange(attended, 1), out_weight[0], mine, other)
     return mixed.reshape(loc_len, view_dev, width)

time: 124 us -> 115 us (0.927)
  waiting for transfers between devices: 38.4 us -> 32.9 us
  blocking collectives: 14.6 us -> 10.8 us
  starting transfers between devices: 48 us -> 45.6 us
  Pallas kernels: 19.2 us -> 20.9 us
  local copies, waits for them, and re-layouts: 1.78 us -> 3.38 us
    ppermute x1, waiting for transfers between devices: 13.3 us -> 1.03 us  [column_weights(): beside = lax.ppermute(weight, ('view', 'head'), pairs)]
    ppermute x1, waiting for transfers between devices: 0.01 us -> 6.51 us  [column_weights(): return jnp.concatenate([beside, lax.ppermute(sent, 'head', across)], axis=1)]
    all_to_all x1, blocking collectives: 14.6 us -> 10.8 us  [exchange(): lax.all_to_all(slots, 'head', split_axis=0, concat_axis=0, tiled=True, ax...]
    all_to_all x2, waiting for transfers between devices: 6.17 us -> 9.47 us  [gather_tokens(): lax.all_to_all(slots, 'head', split_axis=0, concat_axis=0, tiled=True)]
    ppermute x4, waiting for transfers between devices: 12.9 us -> 9.92 us  [partner(): lax.ppermute(array, 'view', [(i, i ^ 1 << bit) for i in range(lax.axis_si...]
    ppermute x4, starting transfers between devices: 24.2 us -> 21.8 us  [partner(): lax.ppermute(array, 'view', [(i, i ^ 1 << bit) for i in range(lax.axis_si...]
    pallas_call x2 -> x3, Pallas kernels: 10.1 us -> 12 us  [call_attend(): pl.pallas_call(kernel, out_shape=out_shape, in_specs=[pl.BlockSpec(memory...]
    unnamed x14 -> x19, local copies, waits for them, and re-layouts: 1.74 us -> 3.38 us
  transfers between devices with their start and end apart: 9 -> 9, of which waited for: 4 -> 6; matrix products, arithmetic and copies ran while one was open for 0% -> 0% of each run, Pallas kernels for 7% -> 10%
where the time goes in v8:
time: 115 us
  starting transfers between devices  45.6 us (40%)
  waiting for transfers between devices  32.9 us (29%)
  Pallas kernels  20.9 us (18%)
  blocking collectives  10.8 us (9%)
  local copies, waits for them, and re-layouts  3.38 us (3%)
    ppermute x4, starting transfers between devices, partner(): lax.ppermute(array, 'view', [(i, i ^ 1 << bit) for i in range(lax.axis_si...  21.8 us
    all_to_all x2, starting transfers between devices, gather_tokens(): lax.all_to_all(slots, 'head', split_axis=0, concat_axis=0, tiled=True)  12.7 us
    pallas_call x3, Pallas kernels, call_attend(): pl.pallas_call(kernel, out_shape=out_shape, in_specs=[pl.BlockSpec(memory...  12 us
    all_to_all x1, blocking collectives, exchange(): lax.all_to_all(slots, 'head', split_axis=0, concat_axis=0, tiled=True, ax...  10.8 us
    ppermute x4, waiting for transfers between devices, partner(): lax.ppermute(array, 'view', [(i, i ^ 1 << bit) for i in range(lax.axis_si...  9.92 us
    all_to_all x2, waiting for transfers between devices, gather_tokens(): lax.all_to_all(slots, 'head', split_axis=0, concat_axis=0, tiled=True)  9.47 us
    ppermute x1, waiting for transfers between devices, column_weights(): return jnp.concatenate([beside, lax.ppermute(sent, 'head', across)], axis=1)  6.51 us
    all_to_all x1, waiting for transfers between devices, exchange(): lax.all_to_all(slots, 'head', split_axis=0, concat_axis=0, tiled=True, ax...  5.95 us
  transfers between devices with their start and end apart: 9, of which 6 were waited for; matrix products, arithmetic and copies ran while one was open for 0% of the time, Pallas kernels for 10%

profile of v8, /device:TPU:32, one launch (start us, length us, event | category | flops | bytes accessed | tf_op | source)
XLA Modules:
  0.0 114.7 jit_solution(8727399798745704020)
XLA Ops:
  1.6 1.8 %shard_map.64 = (bf16[64,1152]{1,0:T(8,128)(2,1)S(1)}, bf16[16,64,1152]{2,1,0:T(8,128)(2,1)}) custom-call(bf16[64,1152]{1,0:T(8,128)(2,1)S(1)} %bitcast.20, f32[1152]{0:T(1024)S(1)} %copy-done.3), custom_call_target="tpu_custom_call" | custom-call | flops 589824 | bytes 2359296 | tf_op jit(solution)/shard_map/pallas_call | solution.py:39
  3.4 7.2 %all-to-all-start = ((bf16[16,64,1152]{2,1,0:T(8,128)(2,1)}), bf16[16,64,1152]{2,1,0:T(8,128)(2,1)S(1)}, u32[]{:S(2)}, u32[]{:S(2)}) async-start(bf16[16,64,1152]{2,1,0:T(8,128)(2,1)} %get-tuple-element.25), calls=%async_computation | async-start | bytes 4718592 | tf_op jit(solution)/shard_map/all_to_all | solution.py:68
  10.6 5.0 %collective-permute-start.1 = (bf16[72,1152]{1,0:T(8,128)(2,1)S(1)}, bf16[72,1152]{1,0:T(8,128)(2,1)S(1)}, u32[]{:S(2)}, u32[]{:S(2)}) collective-permute-start(bf16[72,1152]{1,0:T(8,128)(2,1)S(1)} %bitcast.15), channel_id=1, source_target_pairs={{4,0},{5,1},{6,2},{7,3},{8,4},{9,5},{10,6},{11,7},{12,8},{13,9},{1... | collective-permute-start | bytes 497672 | tf_op jit(solution)/shard_map/ppermute | solution.py:319
  15.7 2.8 %collective-permute-start.2 = (bf16[72,640]{1,0:T(8,128)(2,1)S(1)}, bf16[72,640]{1,0:T(8,128)(2,1)S(1)}, u32[]{:S(2)}, u32[]{:S(2)}) collective-permute-start(bf16[72,640]{1,0:T(8,128)(2,1)S(1)} %slice_select_fusion), channel_id=1, source_target_pairs={{0,8},{1,9},{2,10},{3,11},{4,12},{5,13},{6,14},{7,15},{8,0},{9,1},... | collective-permute-start | bytes 276488 | tf_op jit(solution)/shard_map/ppermute | solution.py:322
  18.5 14.8 %collective-permute-start = (bf16[64,1152]{1,0:T(8,128)(2,1)S(1)}, bf16[64,1152]{1,0:T(8,128)(2,1)S(1)}, u32[]{:S(2)}, u32[]{:S(2)}) collective-permute-start(bf16[64,1152]{1,0:T(8,128)(2,1)S(1)} %get-tuple-element.23), channel_id=1, source_target_pairs={{0,256},{16,272},{32,288},{48,304},{64,320},{80,336},{96,352},{112... | collective-permute-start | bytes 442376 | tf_op jit(solution)/shard_map/ppermute | solution.py:14
  33.4 6.5 %collective-permute-done.2 = bf16[72,640]{1,0:T(8,128)(2,1)S(1)} collective-permute-done((bf16[72,640]{1,0:T(8,128)(2,1)S(1)}, bf16[72,640]{1,0:T(8,128)(2,1)S(1)}, u32[]{:S(2)}, u32[]{:S(2)}) %collective-permute-start.2) | collective-permute-done | bytes 92192 | tf_op jit(solution)/shard_map/ppermute | solution.py:322
  39.9 1.0 collective-permute-done.1
  41.0 5.0 %collective-permute-done.source_ref = bf16[64,1152]{1,0:T(8,128)(2,1)S(1)} collective-permute-done((bf16[64,1152]{1,0:T(8,128)(2,1)S(1)}, bf16[64,1152]{1,0:T(8,128)(2,1)S(1)}, u32[]{:S(2)}, u32[]{:S(2)}) %collective-permute-start) | collective-permute-done | bytes 147488 | tf_op jit(solution)/shard_map/ppermute | solution.py:14
  45.9 1.6 %shard_map.65 = bf16[16,64,1152]{2,1,0:T(8,128)(2,1)} custom-call(bf16[64,1152]{1,0:T(8,128)(2,1)S(1)} %collective-permute-done.source_ref), custom_call_target="tpu_custom_call" | custom-call | bytes 2359296 | tf_op jit(solution)/shard_map/pallas_call | solution.py:56
  47.5 5.5 %all-to-all-start.1 = ((bf16[16,64,1152]{2,1,0:T(8,128)(2,1)}), bf16[16,64,1152]{2,1,0:T(8,128)(2,1)}, u32[]{:S(2)}, u32[]{:S(2)}) async-start(bf16[16,64,1152]{2,1,0:T(8,128)(2,1)} %shard_map.65), calls=%async_computation.1 | async-start | bytes 4718592 | tf_op jit(solution)/shard_map/all_to_all | solution.py:68
  53.1 1.8 %shard_map.66 = (bf16[1024,72]{1,0:T(8,128)(2,1)S(1)}, bf16[144,1024]{1,0:T(8,128)(2,1)}) custom-call(bf16[1024,1152]{1,0:T(8,128)(2,1)S(1)} %bitcast.12, bf16[216,1152]{1,0:T(8,128)(2,1)S(1)} %bitcast.13, f32[72,2]{1,0:T(8,128)S(1)} %bitcast.18), custom_call_target="tpu_custom_call" | custom-call | flops 509607936 | bytes 2359296 | tf_op jit(solution)/shard_map/pallas_call | solution.py:113
  55.5 1.9 %collective-permute-start.3 = (bf16[144,1024]{1,0:T(8,128)(2,1)}, bf16[144,1024]{1,0:T(8,128)(2,1)S(1)}, u32[]{:S(2)}, u32[]{:S(2)}) collective-permute-start(bf16[144,1024]{1,0:T(8,128)(2,1)} %get-tuple-element.31.own_ref), channel_id=1, source_target_pairs={{0,16},{16,0},{32,48},{48,32},{64,80},{80,64},{96,112},{112,96},{1... | collective-permute-start | bytes 884744 | tf_op jit(solution)/shard_map/ppermute | solution.py:14
  57.4 3.0 %collective-permute-start.4 = (bf16[144,1024]{1,0:T(8,128)(2,1)}, bf16[144,1024]{1,0:T(8,128)(2,1)S(1)}, u32[]{:S(2)}, u32[]{:S(2)}) collective-permute-start(bf16[144,1024]{1,0:T(8,128)(2,1)} %get-tuple-element.31.own_ref), channel_id=1, source_target_pairs={{0,64},{16,80},{32,96},{48,112},{64,0},{80,16},{96,32},{112,48},{1... | collective-permute-start | bytes 884744 | tf_op jit(solution)/shard_map/ppermute | solution.py:14
  60.4 2.1 %collective-permute-start.5 = (bf16[72,1792]{1,0:T(8,128)(2,1)S(1)}, bf16[72,1792]{1,0:T(8,128)(2,1)S(1)}, u32[]{:S(2)}, u32[]{:S(2)}) collective-permute-start(bf16[72,1792]{1,0:T(8,128)(2,1)S(1)} %pad_maximum_fusion.mine_ref), channel_id=1, source_target_pairs={{0,16},{16,0},{32,48},{48,32},{64,80},{80,64},{96,112},{112,96},{1... | collective-permute-start | bytes 774152 | tf_op jit(solution)/shard_map/ppermute | solution.py:14
  63.5 5.0 %shard_map.67 = (f32[1024,72]{1,0:T(8,128)S(1)}, f32[1024,128]{1,0:T(8,128)S(1)}) custom-call(s32[3]{0:T(128)S(1)} %bitcast.21, bf16[1024,72]{1,0:T(8,128)(2,1)S(1)} %copy-done.5, bf16[144,1024]{1,0:T(8,128)(2,1)} %get-tuple-element.31.own_ref, bf16[144,1024]{1,0:T(8,128)(2,1)S(1)} %collective-permute-done.3.refs_0_), custom_call_target="tpu_custom_call" | custom-call | flops 2147483648 | bytes 589824 | tf_op jit(solution)/shard_map/pallas_call | solution.py:249
  68.5 5.0 %collective-permute-done.4.refs_0_ = bf16[144,1024]{1,0:T(8,128)(2,1)S(1)} collective-permute-done((bf16[144,1024]{1,0:T(8,128)(2,1)}, bf16[144,1024]{1,0:T(8,128)(2,1)S(1)}, u32[]{:S(2)}, u32[]{:S(2)}) %collective-permute-start.4) | collective-permute-done | bytes 294944 | tf_op jit(solution)/shard_map/ppermute | solution.py:14
  73.5 3.1 %shard_map.68.state_ref = f32[1024,128]{1,0:T(8,128)S(1)} custom-call(s32[3]{0:T(128)S(1)} %bitcast.22, bf16[1024,72]{1,0:T(8,128)(2,1)S(1)} %copy-done.5, f32[1024,128]{1,0:T(8,128)S(1)} %get-tuple-element.35.state_ref, bf16[144,1024]{1,0:T(8,128)(2,1)S(1)} %collective-permute-done.4.refs_0_), custom_call_target="tpu_custom_call" | custom-call | flops 1073741824 | bytes 294912 | tf_op jit(solution)/shard_map/pallas_call | solution.py:249
  76.6 9.5 %all-to-all-done.1 = bf16[16,64,1152]{2,1,0:T(8,128)(2,1)} async-done(((bf16[16,64,1152]{2,1,0:T(8,128)(2,1)}), bf16[16,64,1152]{2,1,0:T(8,128)(2,1)}, u32[]{:S(2)}, u32[]{:S(2)}) %all-to-all-start.1) | async-done | bytes 2359328 | tf_op jit(solution)/shard_map/all_to_all | solution.py:68
  86.1 2.4 %shard_map.69.refs_0_ = bf16[144,1024]{1,0:T(8,128)(2,1)S(1)} custom-call(bf16[1024,1152]{1,0:T(8,128)(2,1)} %bitcast.9.rows_ref, bf16[216,1152]{1,0:T(8,128)(2,1)S(1)} %bitcast.14, f32[72,2]{1,0:T(8,128)S(1)} %bitcast.19), custom_call_target="tpu_custom_call" | custom-call | flops 509607936 | bytes 2359296 | tf_op jit(solution)/shard_map/pallas_call | solution.py:132
  88.5 3.9 %shard_map.70 = bf16[4,72,256]{2,1,0:T(8,128)(2,1)} custom-call(s32[3]{0:T(128)S(1)} %bitcast.23, bf16[1024,72]{1,0:T(8,128)(2,1)S(1)} %copy-done.6, f32[1024,72]{1,0:T(8,128)S(1)} %get-tuple-element.37.own_in_ref, f32[1024,128]{1,0:T(8,128)S(1)} %shard_map.68.state_ref, bf16[144,1024]{1,0:T(8,128)(2,1)S(1)} %shard_map.69.refs_0_), custom_call_target="tpu_custom_call" | custom-call | flops 1073741824 | bytes 294912 | tf_op jit(solution)/shard_map/pallas_call | solution.py:249
  92.4 3.3 %all-to-all-start.2 = ((bf16[4,72,256]{2,1,0:T(8,128)(2,1)}), bf16[4,72,256]{2,1,0:T(8,128)(2,1)S(1)}, u32[]{:S(2)}, u32[]{:S(2)}) async-start(bf16[4,72,256]{2,1,0:T(8,128)(2,1)} %shard_map.70), calls=%async_computation.2 | async-start | bytes 294912 | tf_op jit(solution)/shard_map/all_to_all | solution.py:303
  95.8 6.0 %all-to-all-done.2.parts_ref = bf16[4,72,256]{2,1,0:T(8,128)(2,1)S(1)} async-done(((bf16[4,72,256]{2,1,0:T(8,128)(2,1)}), bf16[4,72,256]{2,1,0:T(8,128)(2,1)S(1)}, u32[]{:S(2)}, u32[]{:S(2)}) %all-to-all-start.2) | async-done | bytes 147488 | tf_op jit(solution)/shard_map/all_to_all | solution.py:303
  101.8 1.4 %shard_map.71 = bf16[4,64,1152]{2,1,0:T(8,128)(2,1)S(1)} custom-call(s32[2]{0:T(128)S(1)} %pad_add_fusion.place_ref, bf16[4,72,256]{2,1,0:T(8,128)(2,1)S(1)} %all-to-all-done.2.parts_ref, bf16[72,1152]{1,0:T(8,128)(2,1)S(1)} %bitcast.17, bf16[72,1792]{1,0:T(8,128)(2,1)S(1)} %pad_maximum_fusion.mine_ref, bf16[72,1792]{1,0:T(8,128)(2,1)S(1)} %collective-permute-done.5.other_ref), custom_call_target="tpu_custom_call" | custom-call | flops 169869312 | bytes 1253376 | tf_op jit(solution)/shard_map/pallas_call | solution.py:353
  103.2 10.8 %all_to_all.20 = bf16[4,64,1152]{2,1,0:T(8,128)(2,1)S(1)} all-to-all(bf16[4,64,1152]{2,1,0:T(8,128)(2,1)S(1)} %shard_map.71), channel_id=1, replica_groups={{0,1,2,3},{4,5,6,7},{8,9,10,11},{12,13,14,15},{16,17,18,19},{20,21,22,2..., dimensions={0} | all-to-all | bytes 1179648 | tf_op jit(solution)/shard_map/all_to_all | solution.py:303
  (26 shorter events, 4.3 us)
Async XLA Ops:
  0.0 0.9 copy-start.2
  0.9 0.7 copy-start.3
  3.4 7.2 %copy-start.1 = (bf16[1,72,1152]{2,1,0:T(8,128)(2,1)S(1)}, bf16[1,72,1152]{2,1,0:T(8,128)(2,1)}, u32[]{:S(2)}) copy-start(bf16[1,72,1152]{2,1,0:T(8,128)(2,1)} %param.10) | copy-start | bytes 497668
  3.4 29.9 %copy-start.8 = (f32[1,2,72]{2,1,0:T(2,128)S(1)}, f32[1,2,72]{2,1,0:T(2,128)}, u32[]{:S(2)}) copy-start(f32[1,2,72]{2,1,0:T(2,128)} %param.9) | copy-start | bytes 1732
  3.4 44.1 %all-to-all-start = ((bf16[16,64,1152]{2,1,0:T(8,128)(2,1)}), bf16[16,64,1152]{2,1,0:T(8,128)(2,1)S(1)}, u32[]{:S(2)}, u32[]{:S(2)}) async-start(bf16[16,64,1152]{2,1,0:T(8,128)(2,1)} %get-tuple-element.25), calls=%async_computation | async-start | bytes 4718592 | tf_op jit(solution)/shard_map/all_to_all | solution.py:68
  10.6 30.3 %collective-permute-start.1 = (bf16[72,1152]{1,0:T(8,128)(2,1)S(1)}, bf16[72,1152]{1,0:T(8,128)(2,1)S(1)}, u32[]{:S(2)}, u32[]{:S(2)}) collective-permute-start(bf16[72,1152]{1,0:T(8,128)(2,1)S(1)} %bitcast.15), channel_id=1, source_target_pairs={{4,0},{5,1},{6,2},{7,3},{8,4},{9,5},{10,6},{11,7},{12,8},{13,9},{1... | collective-permute-start | bytes 497672 | tf_op jit(solution)/shard_map/ppermute | solution.py:319
  15.7 24.2 %collective-permute-start.2 = (bf16[72,640]{1,0:T(8,128)(2,1)S(1)}, bf16[72,640]{1,0:T(8,128)(2,1)S(1)}, u32[]{:S(2)}, u32[]{:S(2)}) collective-permute-start(bf16[72,640]{1,0:T(8,128)(2,1)S(1)} %slice_select_fusion), channel_id=1, source_target_pairs={{0,8},{1,9},{2,10},{3,11},{4,12},{5,13},{6,14},{7,15},{8,0},{9,1},... | collective-permute-start | bytes 276488 | tf_op jit(solution)/shard_map/ppermute | solution.py:322
  18.5 27.5 %collective-permute-start = (bf16[64,1152]{1,0:T(8,128)(2,1)S(1)}, bf16[64,1152]{1,0:T(8,128)(2,1)S(1)}, u32[]{:S(2)}, u32[]{:S(2)}) collective-permute-start(bf16[64,1152]{1,0:T(8,128)(2,1)S(1)} %get-tuple-element.23), channel_id=1, source_target_pairs={{0,256},{16,272},{32,288},{48,304},{64,320},{80,336},{96,352},{112... | collective-permute-start | bytes 442376 | tf_op jit(solution)/shard_map/ppermute | solution.py:14
  47.5 5.5 %copy-start = (bf16[1,216,1152]{2,1,0:T(8,128)(2,1)S(1)}, bf16[1,216,1152]{2,1,0:T(8,128)(2,1)}, u32[]{:S(2)}) copy-start(bf16[1,216,1152]{2,1,0:T(8,128)(2,1)} %param.8) | copy-start | bytes 1492996
  47.5 38.5 %all-to-all-start.1 = ((bf16[16,64,1152]{2,1,0:T(8,128)(2,1)}), bf16[16,64,1152]{2,1,0:T(8,128)(2,1)}, u32[]{:S(2)}, u32[]{:S(2)}) async-start(bf16[16,64,1152]{2,1,0:T(8,128)(2,1)} %shard_map.65), calls=%async_computation.1 | async-start | bytes 4718592 | tf_op jit(solution)/shard_map/all_to_all | solution.py:68
  53.1 9.5 %copy-start.7 = (s32[3,1]{0,1:T(1,128)S(1)}, s32[3,1]{0,1:T(1,128)}, u32[]{:S(2)}) copy-start(s32[3,1]{0,1:T(1,128)} %param.11) | copy-start | bytes 40
  54.8 0.7 copy-start.4
  55.5 4.9 %collective-permute-start.3 = (bf16[144,1024]{1,0:T(8,128)(2,1)}, bf16[144,1024]{1,0:T(8,128)(2,1)S(1)}, u32[]{:S(2)}, u32[]{:S(2)}) collective-permute-start(bf16[144,1024]{1,0:T(8,128)(2,1)} %get-tuple-element.31.own_ref), channel_id=1, source_target_pairs={{0,16},{16,0},{32,48},{48,32},{64,80},{80,64},{96,112},{112,96},{1... | collective-permute-start | bytes 884744 | tf_op jit(solution)/shard_map/ppermute | solution.py:14
  57.4 16.0 %collective-permute-start.4 = (bf16[144,1024]{1,0:T(8,128)(2,1)}, bf16[144,1024]{1,0:T(8,128)(2,1)S(1)}, u32[]{:S(2)}, u32[]{:S(2)}) collective-permute-start(bf16[144,1024]{1,0:T(8,128)(2,1)} %get-tuple-element.31.own_ref), channel_id=1, source_target_pairs={{0,64},{16,80},{32,96},{48,112},{64,0},{80,16},{96,32},{112,48},{1... | collective-permute-start | bytes 884744 | tf_op jit(solution)/shard_map/ppermute | solution.py:14
  60.4 16.1 %collective-permute-start.5 = (bf16[72,1792]{1,0:T(8,128)(2,1)S(1)}, bf16[72,1792]{1,0:T(8,128)(2,1)S(1)}, u32[]{:S(2)}, u32[]{:S(2)}) collective-permute-start(bf16[72,1792]{1,0:T(8,128)(2,1)S(1)} %pad_maximum_fusion.mine_ref), channel_id=1, source_target_pairs={{0,16},{16,0},{32,48},{48,32},{64,80},{80,64},{96,112},{112,96},{1... | collective-permute-start | bytes 774152 | tf_op jit(solution)/shard_map/ppermute | solution.py:14
  62.6 1.0 copy-start.5
  76.6 11.9 %copy-start.6 = (bf16[1024,72]{1,0:T(8,128)(2,1)S(1)}, bf16[1024,72]{1,0:T(8,128)(2,1)}, u32[]{:S(2)}) copy-start(bf16[1024,72]{1,0:T(8,128)(2,1)} %copy-done.4) | copy-start | bytes 442372
  92.4 9.4 %all-to-all-start.2 = ((bf16[4,72,256]{2,1,0:T(8,128)(2,1)}), bf16[4,72,256]{2,1,0:T(8,128)(2,1)S(1)}, u32[]{:S(2)}, u32[]{:S(2)}) async-start(bf16[4,72,256]{2,1,0:T(8,128)(2,1)} %shard_map.70), calls=%async_computation.2 | async-start | bytes 294912 | tf_op jit(solution)/shard_map/all_to_all | solution.py:303

commit v9 on v8

--- a/solution.py
+++ b/solution.py
@@ -24,27 +24,42 @@
         copy.wait()
 
 
-def normalize_kernel(rows_ref, gain_ref, out_ref, slots_ref, sems):
-    values = rows_ref[...].astype(jnp.float32)
+def normalize_kernel(rows_ref, gain_ref, out_ref, slots_ref, held_ref, held_gain_ref, read_sems, sems):
+    reads = [
+        pltpu.make_async_copy(rows_ref, held_ref, read_sems.at[0]),
+        pltpu.make_async_copy(gain_ref, held_gain_ref, read_sems.at[1]),
+    ]
+    for read in reads:
+        read.start()
+    for read in reads:
+        read.wait()
+    values = held_ref[...].astype(jnp.float32)
     mean = jnp.mean(values, axis=-1, keepdims=True)
     centred = values - mean
     var = jnp.mean(centred * centred, axis=-1, keepdims=True)
-    gain = gain_ref[...].reshape(1, -1)
+    gain = held_gain_ref[...].reshape(1, -1)
     out_ref[...] = (centred * lax.rsqrt(var + 1e-06) * gain).astype(jnp.bfloat16)
     spread(out_ref, slots_ref, sems)
 
 
 def normalize(rows, norm_gain, slots):
-    vmem = pl.BlockSpec(memory_space=pltpu.VMEM)
+    vmem, hbm = pl.BlockSpec(memory_space=pltpu.VMEM), pl.BlockSpec(memory_space=pltpu.HBM)
+    rows = pltpu.with_memory_space_constraint(rows, pltpu.HBM)
+    norm_gain = pltpu.with_memory_space_constraint(norm_gain, pltpu.HBM)
     return pl.pallas_call(
         normalize_kernel,
         out_shape=[
             jax.ShapeDtypeStruct(rows.shape, jnp.bfloat16),
             pltpu.HBM((slots,) + rows.shape, jnp.bfloat16),
         ],
-        in_specs=[vmem, vmem],
-        out_specs=[vmem, pl.BlockSpec(memory_space=pltpu.HBM)],
-        scratch_shapes=[pltpu.SemaphoreType.DMA((slots,))],
+        in_specs=[hbm, hbm],
+        out_specs=[vmem, hbm],
+        scratch_shapes=[
+            pltpu.VMEM(rows.shape, rows.dtype),
+            pltpu.VMEM(norm_gain.shape, norm_gain.dtype),
+            pltpu.SemaphoreType.DMA((2,)),
+            pltpu.SemaphoreType.DMA((slots,)),
+        ],
         compiler_params=pltpu.CompilerParams(vmem_limit_bytes=16 << 20),
         cost_estimate=pl.CostEstimate(
             flops=8 * rows.size, bytes_accessed=2 * slots * rows.size, transcendentals=0
@@ -86,27 +101,6 @@
     pair_ref[...] = pair.astype(jnp.bfloat16)
 
 
-def project_far_kernel(rows_ref, weight_ref, gain_ref, pair_ref, held_ref, sems):
-    head_dim = gain_ref.shape[0]
-    skip = head_dim // 16 * 16
-    blocks, block = held_ref.shape[:2]
-    copies = [
-        pltpu.make_async_copy(rows_ref.at[pl.ds(n * block, block)], held_ref.at[n], sems.at[n])
-        for n in range(blocks)
-    ]
-    for copy in copies:
-        copy.start()
-    for n in range(blocks):
-        copies[n].wait()
-        flat = lax.dot_general(
-            weight_ref[skip:], held_ref[n], (((1,), (1,)), ((), ())), preferred_element_type=jnp.float32
-        )
-        flat = flat[head_dim - skip :].astype(jnp.bfloat16).astype(jnp.float32)
-        keys = rms_rows(flat[:head_dim], gain_ref[:, 1:2])
-        pair = jnp.concatenate([keys, flat[head_dim:]], axis=0)
-        pair_ref[:, pl.ds(n * block, block)] = pair.astype(jnp.bfloat16)
-
-
 def project(rows, weight, gain):
     tokens, width = rows.shape
     head_dim = gain.shape[0]
@@ -117,28 +111,6 @@
             jax.ShapeDtypeStruct((2 * head_dim, tokens), jnp.bfloat16),
         ],
         compiler_params=pltpu.CompilerParams(vmem_limit_bytes=16 << 20),
-        cost_estimate=pl.CostEstimate(
-            flops=2 * tokens * width * weight.shape[0], bytes_accessed=2 * tokens * width, transcendentals=0
-        ),
-    )(rows, weight, gain)
-
-
-def project_far(rows, weight, gain):
-    tokens, width = rows.shape
-    head_dim = gain.shape[0]
-    blocks = 2
-    vmem = pl.BlockSpec(memory_space=pltpu.VMEM)
-    rows = pltpu.with_memory_space_constraint(rows, pltpu.HBM)
-    return pl.pallas_call(
-        project_far_kernel,
-        out_shape=jax.ShapeDtypeStruct((2 * head_dim, tokens), jnp.bfloat16),
-        in_specs=[pl.BlockSpec(memory_space=pltpu.HBM), vmem, vmem],
-        out_specs=vmem,
-        scratch_shapes=[
-            pltpu.VMEM((blocks, tokens // blocks, width), jnp.bfloat16),
-            pltpu.SemaphoreType.DMA((blocks,)),
-        ],
-        compiler_params=pltpu.CompilerParams(vmem_limit_bytes=20 << 20),
         cost_estimate=pl.CostEstimate(
             flops=2 * tokens * width * weight.shape[0], bytes_accessed=2 * tokens * width, transcendentals=0
         ),
@@ -223,19 +195,46 @@
         out_ref[rows, :] = jnp.where(lane == head_dim + 1, best, acc)
 
 
-def last_kernel(tile, first, active_ref, query_ref, own_in_ref, state_ref, *refs):
-    far_refs, out_ref, values_ref = refs[:-2], refs[-2], refs[-1]
+def last_kernel(
+    tile, which, active_ref, query_ref, own_in_ref, state_ref, rows_ref, weight_ref, gain_ref,
+    out_ref, held_ref, keys_ref, values_ref, sems,
+):
     tokens, head_dim = query_ref.shape
     padded = values_ref.shape[-1]
-    for n, ref in enumerate(far_refs):
-        values_ref[n] = spread_values(ref, head_dim, padded)
-
+    blocks, block, width = held_ref.shape
+    copies = [
+        pltpu.make_async_copy(rows_ref.at[pl.ds(n * block, block)], held_ref.at[n], sems.at[n])
+        for n in range(blocks)
+    ]
+    for copy in copies:
+        copy.start()
+    even = head_dim // 16 * 16
+    value_weight = weight_ref[2 * head_dim :].astype(jnp.float32)
+    blank = jnp.zeros((padded - head_dim, width), jnp.float32)
+    value_weight = jnp.concatenate([value_weight, blank], axis=0).astype(jnp.bfloat16)
+    lane = lax.broadcasted_iota(jnp.int32, (block, padded), 1)
+    across = (((1,), (1,)), ((), ()))
+    for n in range(blocks):
+        copies[n].wait()
+        at = pl.ds(n * block, block)
+        rows = held_ref[n]
+        keys = lax.dot_general(
+            weight_ref[even : 2 * head_dim], rows, across, preferred_element_type=jnp.float32
+        )
+        keys = keys[head_dim - even :].astype(jnp.bfloat16).astype(jnp.float32)
+        keys_ref[:, at] = rms_rows(keys, gain_ref[:, 1:2]).astype(jnp.bfloat16)
+        values = lax.dot_general(rows, value_weight, across, preferred_element_type=jnp.float32)
+        values_ref[at, :] = jnp.where(lane == head_dim, 1.0, values).astype(jnp.bfloat16)
     for at in range(tokens // tile):
         rows = pl.ds(at * tile, tile)
-        query = query_ref[rows, :]
         acc = state_ref[rows, :]
         best = acc[:, head_dim + 1 : head_dim + 2]
-        best, acc = cross_update(active_ref, first, query, far_refs, values_ref, 0, best, acc)
+        factor = math.log2(math.e) * float(head_dim) ** (-0.5)
+        scores = jnp.dot(query_ref[rows, :], keys_ref[...], preferred_element_type=jnp.float32) * factor
+        most = jnp.maximum(best, jnp.max(scores, axis=1, keepdims=True))
+        newbest = jnp.where(active_ref[which] > 0, most, best)
+        shift = jnp.where(active_ref[which] > 0, newbest, BLANK)
+        acc = acc * jnp.exp2(best - newbest) + weighted(scores, shift, values_ref[...])
         result = own_in_ref[rows, :] + finish(acc, head_dim)
         out_ref[at] = result.T.astype(jnp.bfloat16)
 
@@ -282,14 +281,31 @@
     )
 
 
-def attend_last(active, first, query, own_result, state, far):
+def attend_last(active, which, query, own_result, state, rows, weight, gain):
     tokens, head_dim = query.shape
+    width = rows.shape[1]
     side = len(groups(0))
-    out_shape = jax.ShapeDtypeStruct((side, head_dim, tokens // side), jnp.bfloat16)
-    arrays = (active, query, own_result, state, *far)
-    return call_attend(
-        functools.partial(last_kernel, tokens // side, first), out_shape, len(far), tokens, head_dim, arrays
-    )
+    blocks = 2
+    smem, vmem = pl.BlockSpec(memory_space=pltpu.SMEM), pl.BlockSpec(memory_space=pltpu.VMEM)
+    rows = pltpu.with_memory_space_constraint(rows, pltpu.HBM)
+    return pl.pallas_call(
+        functools.partial(last_kernel, tokens // side, which),
+        out_shape=jax.ShapeDtypeStruct((side, head_dim, tokens // side), jnp.bfloat16),
+        in_specs=[smem] + [vmem] * 3 + [pl.BlockSpec(memory_space=pltpu.HBM)] + [vmem] * 2,
+        out_specs=vmem,
+        scratch_shapes=[
+            pltpu.VMEM((blocks, tokens // blocks, width), jnp.bfloat16),
+            pltpu.VMEM((head_dim, tokens), jnp.bfloat16),
+            pltpu.VMEM((tokens, PADDED), jnp.bfloat16),
+            pltpu.SemaphoreType.DMA((blocks,)),
+        ],
+        compiler_params=pltpu.CompilerParams(vmem_limit_bytes=24 << 20),
+        cost_estimate=pl.CostEstimate(
+            flops=2 * tokens * width * weight.shape[0] + 4 * tokens * tokens * 256,
+            bytes_accessed=2 * tokens * width,
+            transcendentals=tokens * tokens,
+        ),
+    )(active, query, own_result, state, rows, weight, gain)
 
 
 def groups(which):
@@ -376,23 +392,20 @@
     active = intersection[:, 0]
     heads = lax.axis_size("head")
     normed, slots = normalize(rows, norm_gain, heads)
-    far_normed, mine, gain, active = lax.optimization_barrier(
-        (partner(normed, bits[-1]), column_weights(out_weight[0]), gain, active)
-    )
+    far_normed, gain, active = lax.optimization_barrier((partner(normed, bits[-1]), gain, active))
     far_slots = copies_of(far_normed, heads)
     every, far_slots = lax.optimization_barrier((gather_tokens(slots), far_slots))
     far_every = gather_tokens(far_slots)
     query, own = project(every, weight, gain)
     near = [partner(own, bit) for bit in bits[:-1]]
-    near[0], mine = lax.optimization_barrier((near[0], mine))
-    other = partner(mine, 0)
+    near[0], out_rows = lax.optimization_barrier((near[0], out_weight[0]))
+    mine = column_weights(out_rows)
     own_result, state = attend_near(active, query, own, near[:1])
     state = attend_middle(active, 1, query, state, near[1:])
-    far_every, own_result, state, other = lax.optimization_barrier(
-        (far_every, own_result, state, other)
-    )
-    far = [project_far(far_every, weight, gain)]
-    attended = attend_last(active, rounds - 1, query, own_result, state, far)
+    state, mine = lax.optimization_barrier((state, mine))
+    other = partner(mine, 0)
+    far_every, own_result, state = lax.optimization_barrier((far_every, own_result, state))
+    attended = attend_last(active, rounds - 1, query, own_result, state, far_every, weight, gain)
     mixed = project_out(exchange(attended, 1), out_weight[0], mine, other)
     return mixed.reshape(loc_len, view_dev, width)
 

time: 115 us -> 117 us (1.017)
  the two profiles are of different devices: /device:TPU:32 before, /device:TPU:128 now
where the time goes in v9:
time: 117 us; the launch traced here: 116 us
  starting transfers between devices  42.9 us (37%)
  waiting for transfers between devices  34.5 us (29%)
  Pallas kernels  21.5 us (18%)
  blocking collectives  14.5 us (12%)
  local copies, waits for them, and re-layouts  1.78 us (2%)
    ppermute x4, starting transfers between devices, partner(): lax.ppermute(array, 'view', [(i, i ^ 1 << bit) for i in range(lax.axis_si...  20.3 us
    all_to_all x1, blocking collectives, exchange(): lax.all_to_all(slots, 'head', split_axis=0, concat_axis=0, tiled=True, ax...  14.5 us
    ppermute x4, waiting for transfers between devices, partner(): lax.ppermute(array, 'view', [(i, i ^ 1 << bit) for i in range(lax.axis_si...  13.3 us
    all_to_all x2, waiting for transfers between devices, gather_tokens(): lax.all_to_all(slots, 'head', split_axis=0, concat_axis=0, tiled=True)  12 us
    all_to_all x2, starting transfers between devices, gather_tokens(): lax.all_to_all(slots, 'head', split_axis=0, concat_axis=0, tiled=True)  11.6 us
    pallas_call x2, Pallas kernels, call_attend(): pl.pallas_call(kernel, out_shape=out_shape, in_specs=[pl.BlockSpec(memory...  7.67 us
    pallas_call x1, Pallas kernels, attend_last(): pl.pallas_call(functools.partial(last_kernel, tokens // side, which), out...  7.11 us
    all_to_all x1, waiting for transfers between devices, exchange(): lax.all_to_all(slots, 'head', split_axis=0, concat_axis=0, tiled=True, ax...  5.95 us
  transfers between devices with their start and end apart: 9, of which 7 were waited for; matrix products, arithmetic and copies ran while one was open for 0% of the time, Pallas kernels for 15%

profile of v9, /device:TPU:128, one launch (start us, length us, event | category | flops | bytes accessed | tf_op | source)
XLA Modules:
  0.0 116.3 jit_solution(8995487674376446659)
XLA Ops:
  0.0 2.7 %shard_map.64 = (bf16[64,1152]{1,0:T(8,128)(2,1)S(1)}, bf16[16,64,1152]{2,1,0:T(8,128)(2,1)}) custom-call(bf16[64,1152]{1,0:T(8,128)(2,1)} %bitcast.23, f32[1152]{0:T(1024)} %gain_ref.1), custom_call_target="tpu_custom_call" | custom-call | flops 589824 | bytes 2359296 | tf_op jit(solution)/shard_map/pallas_call | solution.py:49
  2.7 7.0 %all-to-all-start = ((bf16[16,64,1152]{2,1,0:T(8,128)(2,1)}), bf16[16,64,1152]{2,1,0:T(8,128)(2,1)S(1)}, u32[]{:S(2)}, u32[]{:S(2)}) async-start(bf16[16,64,1152]{2,1,0:T(8,128)(2,1)} %get-tuple-element.25), calls=%async_computation | async-start | bytes 4718592 | tf_op jit(solution)/shard_map/all_to_all | solution.py:83
  9.8 10.9 %collective-permute-start = (bf16[64,1152]{1,0:T(8,128)(2,1)S(1)}, bf16[64,1152]{1,0:T(8,128)(2,1)S(1)}, u32[]{:S(2)}, u32[]{:S(2)}) collective-permute-start(bf16[64,1152]{1,0:T(8,128)(2,1)S(1)} %get-tuple-element.23), channel_id=1, source_target_pairs={{0,256},{16,272},{32,288},{48,304},{64,320},{80,336},{96,352},{112... | collective-permute-start | bytes 442376 | tf_op jit(solution)/shard_map/ppermute | solution.py:14
  20.8 12.5 %collective-permute-done.source_ref = bf16[64,1152]{1,0:T(8,128)(2,1)S(1)} collective-permute-done((bf16[64,1152]{1,0:T(8,128)(2,1)S(1)}, bf16[64,1152]{1,0:T(8,128)(2,1)S(1)}, u32[]{:S(2)}, u32[]{:S(2)}) %collective-permute-start) | collective-permute-done | bytes 147488 | tf_op jit(solution)/shard_map/ppermute | solution.py:14
  33.3 1.6 %shard_map.65 = bf16[16,64,1152]{2,1,0:T(8,128)(2,1)} custom-call(bf16[64,1152]{1,0:T(8,128)(2,1)S(1)} %collective-permute-done.source_ref), custom_call_target="tpu_custom_call" | custom-call | bytes 2359296 | tf_op jit(solution)/shard_map/pallas_call | solution.py:71
  34.9 10.4 %all-to-all-done = bf16[16,64,1152]{2,1,0:T(8,128)(2,1)S(1)} async-done(((bf16[16,64,1152]{2,1,0:T(8,128)(2,1)}), bf16[16,64,1152]{2,1,0:T(8,128)(2,1)S(1)}, u32[]{:S(2)}, u32[]{:S(2)}) %all-to-all-start) | async-done | bytes 2359328 | tf_op jit(solution)/shard_map/all_to_all | solution.py:83
  45.3 4.6 %all-to-all-start.1 = ((bf16[16,64,1152]{2,1,0:T(8,128)(2,1)}), bf16[16,64,1152]{2,1,0:T(8,128)(2,1)}, u32[]{:S(2)}, u32[]{:S(2)}) async-start(bf16[16,64,1152]{2,1,0:T(8,128)(2,1)} %shard_map.65), calls=%async_computation.1 | async-start | bytes 4718592 | tf_op jit(solution)/shard_map/all_to_all | solution.py:83
  49.9 1.0 shard_map.66
  51.7 1.9 %collective-permute-start.1 = (bf16[144,1024]{1,0:T(8,128)(2,1)S(1)}, bf16[144,1024]{1,0:T(8,128)(2,1)S(1)}, u32[]{:S(2)}, u32[]{:S(2)}) collective-permute-start(bf16[144,1024]{1,0:T(8,128)(2,1)S(1)} %get-tuple-element.31.own_ref), channel_id=1, source_target_pairs={{0,16},{16,0},{32,48},{48,32},{64,80},{80,64},{96,112},{112,96},{1... | collective-permute-start | bytes 884744 | tf_op jit(solution)/shard_map/ppermute | solution.py:14
  53.6 5.2 %collective-permute-start.2 = (bf16[144,1024]{1,0:T(8,128)(2,1)S(1)}, bf16[144,1024]{1,0:T(8,128)(2,1)S(1)}, u32[]{:S(2)}, u32[]{:S(2)}) collective-permute-start(bf16[144,1024]{1,0:T(8,128)(2,1)S(1)} %get-tuple-element.31.own_ref), channel_id=1, source_target_pairs={{0,64},{16,80},{32,96},{48,112},{64,0},{80,16},{96,32},{112,48},{1... | collective-permute-start | bytes 884744 | tf_op jit(solution)/shard_map/ppermute | solution.py:14
  58.8 4.9 %collective-permute-start.3 = (bf16[72,1152]{1,0:T(8,128)(2,1)S(1)}, bf16[72,1152]{1,0:T(8,128)(2,1)S(1)}, u32[]{:S(2)}, u32[]{:S(2)}) collective-permute-start(bf16[72,1152]{1,0:T(8,128)(2,1)S(1)} %bitcast.13), channel_id=1, source_target_pairs={{4,0},{5,1},{6,2},{7,3},{8,4},{9,5},{10,6},{11,7},{12,8},{13,9},{1... | collective-permute-start | bytes 497672 | tf_op jit(solution)/shard_map/ppermute | solution.py:335
  63.8 2.7 %collective-permute-start.4 = (bf16[72,640]{1,0:T(8,128)(2,1)S(1)}, bf16[72,640]{1,0:T(8,128)(2,1)S(1)}, u32[]{:S(2)}, u32[]{:S(2)}) collective-permute-start(bf16[72,640]{1,0:T(8,128)(2,1)S(1)} %slice_select_fusion), channel_id=1, source_target_pairs={{0,8},{1,9},{2,10},{3,11},{4,12},{5,13},{6,14},{7,15},{8,0},{9,1},... | collective-permute-start | bytes 276488 | tf_op jit(solution)/shard_map/ppermute | solution.py:338
  66.5 0.9 copy-done.3
  67.5 4.6 %shard_map.67 = (f32[1024,72]{1,0:T(8,128)S(1)}, f32[1024,128]{1,0:T(8,128)S(1)}) custom-call(s32[3]{0:T(128)S(1)} %bitcast.20, bf16[1024,72]{1,0:T(8,128)(2,1)S(1)} %copy-done.3, bf16[144,1024]{1,0:T(8,128)(2,1)S(1)} %get-tuple-element.31.own_ref, bf16[144,1024]{1,0:T(8,128)(2,1)S(1)} %collective-permute-done.1.refs_0_), custom_call_target="tpu_custom_call" | custom-call | flops 2147483648 | bytes 589824 | tf_op jit(solution)/shard_map/pallas_call | solution.py:248
  72.8 3.1 %shard_map.68.state_ref = f32[1024,128]{1,0:T(8,128)S(1)} custom-call(s32[3]{0:T(128)S(1)} %bitcast.21, bf16[1024,72]{1,0:T(8,128)(2,1)S(1)} %copy-done.4, f32[1024,128]{1,0:T(8,128)S(1)} %get-tuple-element.34.state_ref, bf16[144,1024]{1,0:T(8,128)(2,1)S(1)} %collective-permute-done.2.refs_0_), custom_call_target="tpu_custom_call" | custom-call | flops 1073741824 | bytes 294912 | tf_op jit(solution)/shard_map/pallas_call | solution.py:248
  75.9 1.7 %collective-permute-done.4 = bf16[72,640]{1,0:T(8,128)(2,1)S(1)} collective-permute-done((bf16[72,640]{1,0:T(8,128)(2,1)S(1)}, bf16[72,640]{1,0:T(8,128)(2,1)S(1)}, u32[]{:S(2)}, u32[]{:S(2)}) %collective-permute-start.4) | collective-permute-done | bytes 92192 | tf_op jit(solution)/shard_map/ppermute | solution.py:338
  77.6 1.6 %collective-permute-done.3 = bf16[72,1152]{1,0:T(8,128)(2,1)S(1)} collective-permute-done((bf16[72,1152]{1,0:T(8,128)(2,1)S(1)}, bf16[72,1152]{1,0:T(8,128)(2,1)S(1)}, u32[]{:S(2)}, u32[]{:S(2)}) %collective-permute-start.3) | collective-permute-done | bytes 165920 | tf_op jit(solution)/shard_map/ppermute | solution.py:335
  79.2 2.3 %collective-permute-start.5 = (bf16[72,1792]{1,0:T(8,128)(2,1)S(1)}, bf16[72,1792]{1,0:T(8,128)(2,1)S(1)}, u32[]{:S(2)}, u32[]{:S(2)}) collective-permute-start(bf16[72,1792]{1,0:T(8,128)(2,1)S(1)} %pad_maximum_fusion.mine_ref), channel_id=1, source_target_pairs={{0,16},{16,0},{32,48},{48,32},{64,80},{80,64},{96,112},{112,96},{1... | collective-permute-start | bytes 774152 | tf_op jit(solution)/shard_map/ppermute | solution.py:14
  81.5 1.6 %all-to-all-done.1 = bf16[16,64,1152]{2,1,0:T(8,128)(2,1)} async-done(((bf16[16,64,1152]{2,1,0:T(8,128)(2,1)}), bf16[16,64,1152]{2,1,0:T(8,128)(2,1)}, u32[]{:S(2)}, u32[]{:S(2)}) %all-to-all-start.1) | async-done | bytes 2359328 | tf_op jit(solution)/shard_map/all_to_all | solution.py:83
  83.1 7.1 %shard_map.69 = bf16[4,72,256]{2,1,0:T(8,128)(2,1)} custom-call(s32[3]{0:T(128)S(1)} %bitcast.22, bf16[1024,72]{1,0:T(8,128)(2,1)S(1)} %copy-done.4, f32[1024,72]{1,0:T(8,128)S(1)} %get-tuple-element.37.own_in_ref, f32[1024,128]{1,0:T(8,128)S(1)} %shard_map.68.state_ref, bf16[1024,1152]{1,0:T(8,128)(2,1)} %bitcast.8.rows_ref, ...), custom_call_target="tpu_custom_call" | custom-call | flops 1583349760 | bytes 2359296 | tf_op jit(solution)/shard_map/pallas_call | solution.py:291
  90.3 3.3 %all-to-all-start.2 = ((bf16[4,72,256]{2,1,0:T(8,128)(2,1)}), bf16[4,72,256]{2,1,0:T(8,128)(2,1)S(1)}, u32[]{:S(2)}, u32[]{:S(2)}) async-start(bf16[4,72,256]{2,1,0:T(8,128)(2,1)} %shard_map.69), calls=%async_computation.2 | async-start | bytes 294912 | tf_op jit(solution)/shard_map/all_to_all | solution.py:319
  93.7 5.9 %all-to-all-done.2.parts_ref = bf16[4,72,256]{2,1,0:T(8,128)(2,1)S(1)} async-done(((bf16[4,72,256]{2,1,0:T(8,128)(2,1)}), bf16[4,72,256]{2,1,0:T(8,128)(2,1)S(1)}, u32[]{:S(2)}, u32[]{:S(2)}) %all-to-all-start.2) | async-done | bytes 147488 | tf_op jit(solution)/shard_map/all_to_all | solution.py:319
  99.6 1.4 %shard_map.70 = bf16[4,64,1152]{2,1,0:T(8,128)(2,1)S(1)} custom-call(s32[2]{0:T(128)S(1)} %pad_add_fusion.place_ref, bf16[4,72,256]{2,1,0:T(8,128)(2,1)S(1)} %all-to-all-done.2.parts_ref, bf16[72,1152]{1,0:T(8,128)(2,1)S(1)} %bitcast.15, bf16[72,1792]{1,0:T(8,128)(2,1)S(1)} %pad_maximum_fusion.mine_ref, bf16[72,1792]{1,0:T(8,128)(2,1)S(1)} %collective-permute-done.5.other_ref), custom_call_target="tpu_custom_call" | custom-call | flops 169869312 | bytes 1253376 | tf_op jit(solution)/shard_map/pallas_call | solution.py:369
  101.0 14.5 %all_to_all.20 = bf16[4,64,1152]{2,1,0:T(8,128)(2,1)S(1)} all-to-all(bf16[4,64,1152]{2,1,0:T(8,128)(2,1)S(1)} %shard_map.70), channel_id=1, replica_groups={{0,1,2,3},{4,5,6,7},{8,9,10,11},{12,13,14,15},{16,17,18,19},{20,21,22,2..., dimensions={0} | all-to-all | bytes 1179648 | tf_op jit(solution)/shard_map/all_to_all | solution.py:319
  (21 shorter events, 2.4 us)
Async XLA Ops:
  2.7 18.0 %copy-start.6 = (f32[1,2,72]{2,1,0:T(2,128)S(1)}, f32[1,2,72]{2,1,0:T(2,128)}, u32[]{:S(2)}) copy-start(f32[1,2,72]{2,1,0:T(2,128)} %param.9) | copy-start | bytes 1732
  2.7 42.6 %all-to-all-start = ((bf16[16,64,1152]{2,1,0:T(8,128)(2,1)}), bf16[16,64,1152]{2,1,0:T(8,128)(2,1)S(1)}, u32[]{:S(2)}, u32[]{:S(2)}) async-start(bf16[16,64,1152]{2,1,0:T(8,128)(2,1)} %get-tuple-element.25), calls=%async_computation | async-start | bytes 4718592 | tf_op jit(solution)/shard_map/all_to_all | solution.py:83
  9.8 23.6 %collective-permute-start = (bf16[64,1152]{1,0:T(8,128)(2,1)S(1)}, bf16[64,1152]{1,0:T(8,128)(2,1)S(1)}, u32[]{:S(2)}, u32[]{:S(2)}) collective-permute-start(bf16[64,1152]{1,0:T(8,128)(2,1)S(1)} %get-tuple-element.23), channel_id=1, source_target_pairs={{0,256},{16,272},{32,288},{48,304},{64,320},{80,336},{96,352},{112... | collective-permute-start | bytes 442376 | tf_op jit(solution)/shard_map/ppermute | solution.py:14
  45.3 4.6 %copy-start.1 = (bf16[1,216,1152]{2,1,0:T(8,128)(2,1)S(1)}, bf16[1,216,1152]{2,1,0:T(8,128)(2,1)}, u32[]{:S(2)}) copy-start(bf16[1,216,1152]{2,1,0:T(8,128)(2,1)} %param.8) | copy-start | bytes 1492996
  45.3 37.8 %all-to-all-start.1 = ((bf16[16,64,1152]{2,1,0:T(8,128)(2,1)}), bf16[16,64,1152]{2,1,0:T(8,128)(2,1)}, u32[]{:S(2)}, u32[]{:S(2)}) async-start(bf16[16,64,1152]{2,1,0:T(8,128)(2,1)} %shard_map.65), calls=%async_computation.1 | async-start | bytes 4718592 | tf_op jit(solution)/shard_map/all_to_all | solution.py:83
  49.9 8.9 %copy-start = (bf16[1,72,1152]{2,1,0:T(8,128)(2,1)S(1)}, bf16[1,72,1152]{2,1,0:T(8,128)(2,1)}, u32[]{:S(2)}) copy-start(bf16[1,72,1152]{2,1,0:T(8,128)(2,1)} %param.10) | copy-start | bytes 497668
  49.9 16.6 %copy-start.5 = (s32[3,1]{0,1:T(1,128)S(1)}, s32[3,1]{0,1:T(1,128)}, u32[]{:S(2)}) copy-start(s32[3,1]{0,1:T(1,128)} %param.11) | copy-start | bytes 40
  50.9 0.7 copy-start.2
  51.7 7.1 %collective-permute-start.1 = (bf16[144,1024]{1,0:T(8,128)(2,1)S(1)}, bf16[144,1024]{1,0:T(8,128)(2,1)S(1)}, u32[]{:S(2)}, u32[]{:S(2)}) collective-permute-start(bf16[144,1024]{1,0:T(8,128)(2,1)S(1)} %get-tuple-element.31.own_ref), channel_id=1, source_target_pairs={{0,16},{16,0},{32,48},{48,32},{64,80},{80,64},{96,112},{112,96},{1... | collective-permute-start | bytes 884744 | tf_op jit(solution)/shard_map/ppermute | solution.py:14
  53.6 19.2 %collective-permute-start.2 = (bf16[144,1024]{1,0:T(8,128)(2,1)S(1)}, bf16[144,1024]{1,0:T(8,128)(2,1)S(1)}, u32[]{:S(2)}, u32[]{:S(2)}) collective-permute-start(bf16[144,1024]{1,0:T(8,128)(2,1)S(1)} %get-tuple-element.31.own_ref), channel_id=1, source_target_pairs={{0,64},{16,80},{32,96},{48,112},{64,0},{80,16},{96,32},{112,48},{1... | collective-permute-start | bytes 884744 | tf_op jit(solution)/shard_map/ppermute | solution.py:14
  58.8 20.4 %collective-permute-start.3 = (bf16[72,1152]{1,0:T(8,128)(2,1)S(1)}, bf16[72,1152]{1,0:T(8,128)(2,1)S(1)}, u32[]{:S(2)}, u32[]{:S(2)}) collective-permute-start(bf16[72,1152]{1,0:T(8,128)(2,1)S(1)} %bitcast.13), channel_id=1, source_target_pairs={{4,0},{5,1},{6,2},{7,3},{8,4},{9,5},{10,6},{11,7},{12,8},{13,9},{1... | collective-permute-start | bytes 497672 | tf_op jit(solution)/shard_map/ppermute | solution.py:335
  63.8 13.8 %collective-permute-start.4 = (bf16[72,640]{1,0:T(8,128)(2,1)S(1)}, bf16[72,640]{1,0:T(8,128)(2,1)S(1)}, u32[]{:S(2)}, u32[]{:S(2)}) collective-permute-start(bf16[72,640]{1,0:T(8,128)(2,1)S(1)} %slice_select_fusion), channel_id=1, source_target_pairs={{0,8},{1,9},{2,10},{3,11},{4,12},{5,13},{6,14},{7,15},{8,0},{9,1},... | collective-permute-start | bytes 276488 | tf_op jit(solution)/shard_map/ppermute | solution.py:338
  66.5 1.0 copy-start.3
  67.5 5.3 %copy-start.4 = (bf16[1024,72]{1,0:T(8,128)(2,1)S(1)}, bf16[1024,72]{1,0:T(8,128)(2,1)}, u32[]{:S(2)}) copy-start(bf16[1024,72]{1,0:T(8,128)(2,1)} %copy-done.2) | copy-start | bytes 442372
  79.2 14.5 %collective-permute-start.5 = (bf16[72,1792]{1,0:T(8,128)(2,1)S(1)}, bf16[72,1792]{1,0:T(8,128)(2,1)S(1)}, u32[]{:S(2)}, u32[]{:S(2)}) collective-permute-start(bf16[72,1792]{1,0:T(8,128)(2,1)S(1)} %pad_maximum_fusion.mine_ref), channel_id=1, source_target_pairs={{0,16},{16,0},{32,48},{48,32},{64,80},{80,64},{96,112},{112,96},{1... | collective-permute-start | bytes 774152 | tf_op jit(solution)/shard_map/ppermute | solution.py:14
  90.3 9.4 %all-to-all-start.2 = ((bf16[4,72,256]{2,1,0:T(8,128)(2,1)}), bf16[4,72,256]{2,1,0:T(8,128)(2,1)S(1)}, u32[]{:S(2)}, u32[]{:S(2)}) async-start(bf16[4,72,256]{2,1,0:T(8,128)(2,1)} %shard_map.69), calls=%async_computation.2 | async-start | bytes 294912 | tf_op jit(solution)/shard_map/all_to_all | solution.py:319

commit v10 on v8

--- a/solution.py
+++ b/solution.py
@@ -24,27 +24,42 @@
         copy.wait()
 
 
-def normalize_kernel(rows_ref, gain_ref, out_ref, slots_ref, sems):
-    values = rows_ref[...].astype(jnp.float32)
+def normalize_kernel(rows_ref, gain_ref, out_ref, slots_ref, held_ref, held_gain_ref, read_sems, sems):
+    reads = [
+        pltpu.make_async_copy(rows_ref, held_ref, read_sems.at[0]),
+        pltpu.make_async_copy(gain_ref, held_gain_ref, read_sems.at[1]),
+    ]
+    for read in reads:
+        read.start()
+    for read in reads:
+        read.wait()
+    values = held_ref[...].astype(jnp.float32)
     mean = jnp.mean(values, axis=-1, keepdims=True)
     centred = values - mean
     var = jnp.mean(centred * centred, axis=-1, keepdims=True)
-    gain = gain_ref[...].reshape(1, -1)
+    gain = held_gain_ref[...].reshape(1, -1)
     out_ref[...] = (centred * lax.rsqrt(var + 1e-06) * gain).astype(jnp.bfloat16)
     spread(out_ref, slots_ref, sems)
 
 
 def normalize(rows, norm_gain, slots):
-    vmem = pl.BlockSpec(memory_space=pltpu.VMEM)
+    vmem, hbm = pl.BlockSpec(memory_space=pltpu.VMEM), pl.BlockSpec(memory_space=pltpu.HBM)
+    rows = pltpu.with_memory_space_constraint(rows, pltpu.HBM)
+    norm_gain = pltpu.with_memory_space_constraint(norm_gain, pltpu.HBM)
     return pl.pallas_call(
         normalize_kernel,
         out_shape=[
             jax.ShapeDtypeStruct(rows.shape, jnp.bfloat16),
             pltpu.HBM((slots,) + rows.shape, jnp.bfloat16),
         ],
-        in_specs=[vmem, vmem],
-        out_specs=[vmem, pl.BlockSpec(memory_space=pltpu.HBM)],
-        scratch_shapes=[pltpu.SemaphoreType.DMA((slots,))],
+        in_specs=[hbm, hbm],
+        out_specs=[vmem, hbm],
+        scratch_shapes=[
+            pltpu.VMEM(rows.shape, rows.dtype),
+            pltpu.VMEM(norm_gain.shape, norm_gain.dtype),
+            pltpu.SemaphoreType.DMA((2,)),
+            pltpu.SemaphoreType.DMA((slots,)),
+        ],
         compiler_params=pltpu.CompilerParams(vmem_limit_bytes=16 << 20),
         cost_estimate=pl.CostEstimate(
             flops=8 * rows.size, bytes_accessed=2 * slots * rows.size, transcendentals=0
@@ -306,60 +321,42 @@
 
 
 def column_weights(weight):
-    views, heads = lax.axis_size("view"), lax.axis_size("head")
+    heads = lax.axis_size("head")
     side = len(groups(0))
-    core = lax.axis_index("view") % 2
-    width = weight.shape[1]
-    part = (width // 2 + 127) // 128 * 128
-    pairs = []
-    for view in range(views):
-        step = side if view % 2 == 0 else -side
-        for head in range(heads):
-            pairs.append((view * heads + (head + step) % heads, view * heads + head))
-    beside = lax.ppermute(weight, ("view", "head"), pairs)
-    sent = jnp.where(core == 0, weight[:, :part], weight[:, width - part :])
-    across = [(head, (head + heads // 2) % heads) for head in range(heads)]
-    return jnp.concatenate([beside, lax.ppermute(sent, "head", across)], axis=1)
-
-
-def project_out_kernel(place_ref, parts_ref, weight_ref, mine_ref, other_ref, out_ref):
-    side = parts_ref.shape[0]
-    line, core = place_ref[0], place_ref[1]
-    width = weight_ref.shape[1]
-    part = mine_ref.shape[1] - width
-
-    def product(step, weight):
-        rows = parts_ref[lax.rem(line + step, side)]
-        return lax.dot_general(
-            rows, weight, (((0,), (0,)), ((), ())), preferred_element_type=jnp.float32
+    return [
+        lax.ppermute(weight, "head", [((head + step * side) % heads, head) for head in range(heads)])
+        for step in range(1, side)
+    ]
+
+
+def project_out_kernel(line_ref, parts_ref, *refs):
+    weight_refs, out_ref = refs[:-1], refs[-1]
+    side = len(weight_refs)
+    total = None
+    for step, weight_ref in enumerate(weight_refs):
+        part = parts_ref[lax.rem(line_ref[0] + step, side)]
+        term = lax.dot_general(
+            part, weight_ref[...], (((0,), (0,)), ((), ())), preferred_element_type=jnp.float32
         )
-
-    turn = jnp.where(core == 0, 1, side - 1)
-    total = product(0, weight_ref[...])
-    total = total + product(turn, mine_ref[:, :width])
-    total = total + product(side - turn, other_ref[:, :width])
-    mine, other = product(side // 2, mine_ref[:, width:]), product(side // 2, other_ref[:, width:])
-    low, high = jnp.where(core == 0, mine, other), jnp.where(core == 0, other, mine)
-    total = total + jnp.concatenate([low[:, : width - part], high], axis=1)
+        total = term if total is None else total + term
     out_ref[...] = total.reshape(out_ref.shape).astype(jnp.bfloat16)
 
 
-def project_out(parts, weight, mine, other):
+def project_out(parts, weights):
     side, head_dim, tokens = parts.shape
-    width = weight.shape[1]
-    line, core = lax.axis_index("head") // side, lax.axis_index("view") % 2
-    place = jnp.stack([line, core]).astype(jnp.int32)
+    width = weights[0].shape[1]
+    line = (lax.axis_index("head") // side).astype(jnp.int32)[None]
     smem, vmem = pl.BlockSpec(memory_space=pltpu.SMEM), pl.BlockSpec(memory_space=pltpu.VMEM)
     partial = pl.pallas_call(
         project_out_kernel,
         out_shape=jax.ShapeDtypeStruct((side, tokens // side, width), jnp.bfloat16),
-        in_specs=[smem] + [vmem] * 4,
+        in_specs=[smem] + [vmem] * (1 + len(weights)),
         out_specs=vmem,
         compiler_params=pltpu.CompilerParams(vmem_limit_bytes=16 << 20),
         cost_estimate=pl.CostEstimate(
             flops=2 * parts.size * width, bytes_accessed=2 * (side * head_dim + tokens) * width, transcendentals=0
         ),
-    )(place, parts, weight, mine, other)
+    )(line, parts, *weights)
     partial = exchange(partial, 0)
     return jnp.sum(partial.astype(jnp.float32), axis=0).astype(jnp.bfloat16)
 
@@ -376,24 +373,20 @@
     active = intersection[:, 0]
     heads = lax.axis_size("head")
     normed, slots = normalize(rows, norm_gain, heads)
-    far_normed, mine, gain, active = lax.optimization_barrier(
-        (partner(normed, bits[-1]), column_weights(out_weight[0]), gain, active)
-    )
+    far_normed, gain, active = lax.optimization_barrier((partner(normed, bits[-1]), gain, active))
     far_slots = copies_of(far_normed, heads)
     every, far_slots = lax.optimization_barrier((gather_tokens(slots), far_slots))
     far_every = gather_tokens(far_slots)
     query, own = project(every, weight, gain)
     near = [partner(own, bit) for bit in bits[:-1]]
-    near[0], mine = lax.optimization_barrier((near[0], mine))
-    other = partner(mine, 0)
+    near[0], out_rows = lax.optimization_barrier((near[0], out_weight[0]))
+    out_weights = [out_weight[0]] + column_weights(out_rows)
     own_result, state = attend_near(active, query, own, near[:1])
     state = attend_middle(active, 1, query, state, near[1:])
-    far_every, own_result, state, other = lax.optimization_barrier(
-        (far_every, own_result, state, other)
-    )
+    far_every, own_result, state = lax.optimization_barrier((far_every, own_result, state))
     far = [project_far(far_every, weight, gain)]
     attended = attend_last(active, rounds - 1, query, own_result, state, far)
-    mixed = project_out(exchange(attended, 1), out_weight[0], mine, other)
+    mixed = project_out(exchange(attended, 1), out_weights)
     return mixed.reshape(loc_len, view_dev, width)
 
 

time: 115 us -> 113 us (0.983)
  the two profiles are of different devices: /device:TPU:32 before, /device:TPU:96 now
where the time goes in v10:
time: 113 us
  starting transfers between devices  43.5 us (38%)
  waiting for transfers between devices  37 us (33%)
  Pallas kernels  20.1 us (18%)
  blocking collectives  10.8 us (10%)
    all_to_all x2, waiting for transfers between devices, gather_tokens(): lax.all_to_all(slots, 'head', split_axis=0, concat_axis=0, tiled=True)  27.3 us
    ppermute x3, starting transfers between devices, partner(): lax.ppermute(array, 'view', [(i, i ^ 1 << bit) for i in range(lax.axis_si...  16.9 us
    ppermute x3, starting transfers between devices, column_weights(): lax.ppermute(weight, 'head', [((head + step * side) % heads, head) for he...  11.7 us
    all_to_all x2, starting transfers between devices, gather_tokens(): lax.all_to_all(slots, 'head', split_axis=0, concat_axis=0, tiled=True)  11.6 us
    pallas_call x3, Pallas kernels, call_attend(): pl.pallas_call(kernel, out_shape=out_shape, in_specs=[pl.BlockSpec(memory...  11.6 us
    all_to_all x1, blocking collectives, exchange(): lax.all_to_all(slots, 'head', split_axis=0, concat_axis=0, tiled=True, ax...  10.8 us
    all_to_all x1, waiting for transfers between devices, exchange(): lax.all_to_all(slots, 'head', split_axis=0, concat_axis=0, tiled=True, ax...  5.98 us
    ppermute x3, waiting for transfers between devices, partner(): lax.ppermute(array, 'view', [(i, i ^ 1 << bit) for i in range(lax.axis_si...  3.75 us
  transfers between devices with their start and end apart: 9, of which 4 were waited for; matrix products, arithmetic and copies ran while one was open for 0% of the time, Pallas kernels for 15%

profile of v10, /device:TPU:96, one launch (start us, length us, event | category | flops | bytes accessed | tf_op | source)
XLA Modules:
  0.0 112.5 jit_solution(9156459748822176261)
XLA Ops:
  0.0 2.7 %shard_map.64 = (bf16[64,1152]{1,0:T(8,128)(2,1)S(1)}, bf16[16,64,1152]{2,1,0:T(8,128)(2,1)}) custom-call(bf16[64,1152]{1,0:T(8,128)(2,1)} %bitcast.23, f32[1152]{0:T(1024)} %gain_ref.1), custom_call_target="tpu_custom_call" | custom-call | flops 589824 | bytes 2359296 | tf_op jit(solution)/shard_map/pallas_call | solution.py:49
  2.7 7.0 %all-to-all-start = ((bf16[16,64,1152]{2,1,0:T(8,128)(2,1)}), bf16[16,64,1152]{2,1,0:T(8,128)(2,1)S(1)}, u32[]{:S(2)}, u32[]{:S(2)}) async-start(bf16[16,64,1152]{2,1,0:T(8,128)(2,1)} %get-tuple-element.23), calls=%async_computation | async-start | bytes 4718592 | tf_op jit(solution)/shard_map/all_to_all | solution.py:83
  9.8 13.0 %collective-permute-start = (bf16[64,1152]{1,0:T(8,128)(2,1)S(1)}, bf16[64,1152]{1,0:T(8,128)(2,1)S(1)}, u32[]{:S(2)}, u32[]{:S(2)}) collective-permute-start(bf16[64,1152]{1,0:T(8,128)(2,1)S(1)} %get-tuple-element.21), channel_id=1, source_target_pairs={{0,256},{16,272},{32,288},{48,304},{64,320},{80,336},{96,352},{112... | collective-permute-start | bytes 442376 | tf_op jit(solution)/shard_map/ppermute | solution.py:14
  22.8 0.1 copy.7
  22.9 3.7 %collective-permute-done.source_ref = bf16[64,1152]{1,0:T(8,128)(2,1)S(1)} collective-permute-done((bf16[64,1152]{1,0:T(8,128)(2,1)S(1)}, bf16[64,1152]{1,0:T(8,128)(2,1)S(1)}, u32[]{:S(2)}, u32[]{:S(2)}) %collective-permute-start) | collective-permute-done | bytes 147488 | tf_op jit(solution)/shard_map/ppermute | solution.py:14
  26.7 1.6 %shard_map.65 = bf16[16,64,1152]{2,1,0:T(8,128)(2,1)} custom-call(bf16[64,1152]{1,0:T(8,128)(2,1)S(1)} %collective-permute-done.source_ref), custom_call_target="tpu_custom_call" | custom-call | bytes 2359296 | tf_op jit(solution)/shard_map/pallas_call | solution.py:71
  28.2 17.0 %all-to-all-done = bf16[16,64,1152]{2,1,0:T(8,128)(2,1)S(1)} async-done(((bf16[16,64,1152]{2,1,0:T(8,128)(2,1)}), bf16[16,64,1152]{2,1,0:T(8,128)(2,1)S(1)}, u32[]{:S(2)}, u32[]{:S(2)}) %all-to-all-start) | async-done | bytes 2359328 | tf_op jit(solution)/shard_map/all_to_all | solution.py:83
  45.3 4.6 %all-to-all-start.1 = ((bf16[16,64,1152]{2,1,0:T(8,128)(2,1)}), bf16[16,64,1152]{2,1,0:T(8,128)(2,1)}, u32[]{:S(2)}, u32[]{:S(2)}) async-start(bf16[16,64,1152]{2,1,0:T(8,128)(2,1)} %shard_map.65), calls=%async_computation.1 | async-start | bytes 4718592 | tf_op jit(solution)/shard_map/all_to_all | solution.py:83
  49.9 1.0 shard_map.66
  50.9 1.9 %collective-permute-start.1 = (bf16[144,1024]{1,0:T(8,128)(2,1)S(1)}, bf16[144,1024]{1,0:T(8,128)(2,1)S(1)}, u32[]{:S(2)}, u32[]{:S(2)}) collective-permute-start(bf16[144,1024]{1,0:T(8,128)(2,1)S(1)} %get-tuple-element.29.own_ref), channel_id=1, source_target_pairs={{0,16},{16,0},{32,48},{48,32},{64,80},{80,64},{96,112},{112,96},{1... | collective-permute-start | bytes 884744 | tf_op jit(solution)/shard_map/ppermute | solution.py:14
  52.8 1.9 %collective-permute-start.2 = (bf16[144,1024]{1,0:T(8,128)(2,1)S(1)}, bf16[144,1024]{1,0:T(8,128)(2,1)S(1)}, u32[]{:S(2)}, u32[]{:S(2)}) collective-permute-start(bf16[144,1024]{1,0:T(8,128)(2,1)S(1)} %get-tuple-element.29.own_ref), channel_id=1, source_target_pairs={{0,64},{16,80},{32,96},{48,112},{64,0},{80,16},{96,32},{112,48},{1... | collective-permute-start | bytes 884744 | tf_op jit(solution)/shard_map/ppermute | solution.py:14
  54.8 3.7 %collective-permute-start.5 = (bf16[72,1152]{1,0:T(8,128)(2,1)S(1)}, bf16[72,1152]{1,0:T(8,128)(2,1)S(1)}, u32[]{:S(2)}, u32[]{:S(2)}) collective-permute-start(bf16[72,1152]{1,0:T(8,128)(2,1)S(1)} %bitcast.16), channel_id=1, source_target_pairs={{12,0},{13,1},{14,2},{15,3},{0,4},{1,5},{2,6},{3,7},{4,8},{5,9},{6... | collective-permute-start | bytes 497672 | tf_op jit(solution)/shard_map/ppermute | solution.py:327
  58.5 4.6 %collective-permute-start.4 = (bf16[72,1152]{1,0:T(8,128)(2,1)S(1)}, bf16[72,1152]{1,0:T(8,128)(2,1)S(1)}, u32[]{:S(2)}, u32[]{:S(2)}) collective-permute-start(bf16[72,1152]{1,0:T(8,128)(2,1)S(1)} %bitcast.17), channel_id=1, source_target_pairs={{8,0},{9,1},{10,2},{11,3},{12,4},{13,5},{14,6},{15,7},{0,8},{1,9},... | collective-permute-start | bytes 497672 | tf_op jit(solution)/shard_map/ppermute | solution.py:327
  63.1 3.3 %collective-permute-start.3 = (bf16[72,1152]{1,0:T(8,128)(2,1)S(1)}, bf16[72,1152]{1,0:T(8,128)(2,1)S(1)}, u32[]{:S(2)}, u32[]{:S(2)}) collective-permute-start(bf16[72,1152]{1,0:T(8,128)(2,1)S(1)} %bitcast.18), channel_id=1, source_target_pairs={{4,0},{5,1},{6,2},{7,3},{8,4},{9,5},{10,6},{11,7},{12,8},{13,9},{1... | collective-permute-start | bytes 497672 | tf_op jit(solution)/shard_map/ppermute | solution.py:327
  66.5 4.6 %shard_map.67 = (f32[1024,72]{1,0:T(8,128)S(1)}, f32[1024,128]{1,0:T(8,128)S(1)}) custom-call(s32[3]{0:T(128)S(1)} %bitcast.20, bf16[1024,72]{1,0:T(8,128)(2,1)S(1)} %get-tuple-element.27.query_ref, bf16[144,1024]{1,0:T(8,128)(2,1)S(1)} %get-tuple-element.29.own_ref, bf16[144,1024]{1,0:T(8,128)(2,1)S(1)} %collective-permute-done.1.refs_0_), custom_call_target="tpu_custom_call" | custom-call | flops 2147483648 | bytes 589824 | tf_op jit(solution)/shard_map/pallas_call | solution.py:264
  71.1 3.1 %shard_map.68.state_ref = f32[1024,128]{1,0:T(8,128)S(1)} custom-call(s32[3]{0:T(128)S(1)} %bitcast.21, bf16[1024,72]{1,0:T(8,128)(2,1)S(1)} %get-tuple-element.27.query_ref, f32[1024,128]{1,0:T(8,128)S(1)} %get-tuple-element.32.state_ref, bf16[144,1024]{1,0:T(8,128)(2,1)S(1)} %collective-permute-done.2.refs_0_), custom_call_target="tpu_custom_call" | custom-call | flops 1073741824 | bytes 294912 | tf_op jit(solution)/shard_map/pallas_call | solution.py:264
  74.1 10.2 %all-to-all-done.1 = bf16[16,64,1152]{2,1,0:T(8,128)(2,1)} async-done(((bf16[16,64,1152]{2,1,0:T(8,128)(2,1)}), bf16[16,64,1152]{2,1,0:T(8,128)(2,1)}, u32[]{:S(2)}, u32[]{:S(2)}) %all-to-all-start.1) | async-done | bytes 2359328 | tf_op jit(solution)/shard_map/all_to_all | solution.py:83
  84.4 2.4 %shard_map.69.refs_0_ = bf16[144,1024]{1,0:T(8,128)(2,1)S(1)} custom-call(bf16[1024,1152]{1,0:T(8,128)(2,1)} %bitcast.7.rows_ref, bf16[216,1152]{1,0:T(8,128)(2,1)S(1)} %bitcast.13, f32[72,2]{1,0:T(8,128)S(1)} %bitcast.15), custom_call_target="tpu_custom_call" | custom-call | flops 509607936 | bytes 2359296 | tf_op jit(solution)/shard_map/pallas_call | solution.py:147
  86.8 4.0 %shard_map.70 = bf16[4,72,256]{2,1,0:T(8,128)(2,1)} custom-call(s32[3]{0:T(128)S(1)} %bitcast.22, bf16[1024,72]{1,0:T(8,128)(2,1)S(1)} %get-tuple-element.27.query_ref, f32[1024,72]{1,0:T(8,128)S(1)} %get-tuple-element.33.own_in_ref, f32[1024,128]{1,0:T(8,128)S(1)} %shard_map.68.state_ref, bf16[144,1024]{1,0:T(8,128)(2,1)S(1)} %shard_map.69.refs_0_), custom_call_target="tpu_custom_call" | custom-call | flops 1073741824 | bytes 294912 | tf_op jit(solution)/shard_map/pallas_call | solution.py:264
  90.7 3.3 %all-to-all-start.2 = ((bf16[4,72,256]{2,1,0:T(8,128)(2,1)}), bf16[4,72,256]{2,1,0:T(8,128)(2,1)S(1)}, u32[]{:S(2)}, u32[]{:S(2)}) async-start(bf16[4,72,256]{2,1,0:T(8,128)(2,1)} %shard_map.70), calls=%async_computation.2 | async-start | bytes 294912 | tf_op jit(solution)/shard_map/all_to_all | solution.py:318
  94.1 6.0 %all-to-all-done.2.parts_ref = bf16[4,72,256]{2,1,0:T(8,128)(2,1)S(1)} async-done(((bf16[4,72,256]{2,1,0:T(8,128)(2,1)}), bf16[4,72,256]{2,1,0:T(8,128)(2,1)S(1)}, u32[]{:S(2)}, u32[]{:S(2)}) %all-to-all-start.2) | async-done | bytes 147488 | tf_op jit(solution)/shard_map/all_to_all | solution.py:318
  100.1 0.8 shard_map.71
  100.9 10.8 %all_to_all.20 = bf16[4,64,1152]{2,1,0:T(8,128)(2,1)S(1)} all-to-all(bf16[4,64,1152]{2,1,0:T(8,128)(2,1)S(1)} %shard_map.71), channel_id=1, replica_groups={{0,1,2,3},{4,5,6,7},{8,9,10,11},{12,13,14,15},{16,17,18,19},{20,21,22,2..., dimensions={0} | all-to-all | bytes 1179648 | tf_op jit(solution)/shard_map/all_to_all | solution.py:318
  111.7 0.8 reduce_sum.12
  (13 shorter events, 0.0 us)
Async XLA Ops:
  2.7 20.1 %copy-start.3 = (f32[1,2,72]{2,1,0:T(2,128)S(1)}, f32[1,2,72]{2,1,0:T(2,128)}, u32[]{:S(2)}) copy-start(f32[1,2,72]{2,1,0:T(2,128)} %param.9) | copy-start | bytes 1732
  2.7 42.6 %all-to-all-start = ((bf16[16,64,1152]{2,1,0:T(8,128)(2,1)}), bf16[16,64,1152]{2,1,0:T(8,128)(2,1)S(1)}, u32[]{:S(2)}, u32[]{:S(2)}) async-start(bf16[16,64,1152]{2,1,0:T(8,128)(2,1)} %get-tuple-element.23), calls=%async_computation | async-start | bytes 4718592 | tf_op jit(solution)/shard_map/all_to_all | solution.py:83
  9.8 16.9 %collective-permute-start = (bf16[64,1152]{1,0:T(8,128)(2,1)S(1)}, bf16[64,1152]{1,0:T(8,128)(2,1)S(1)}, u32[]{:S(2)}, u32[]{:S(2)}) collective-permute-start(bf16[64,1152]{1,0:T(8,128)(2,1)S(1)} %get-tuple-element.21), channel_id=1, source_target_pairs={{0,256},{16,272},{32,288},{48,304},{64,320},{80,336},{96,352},{112... | collective-permute-start | bytes 442376 | tf_op jit(solution)/shard_map/ppermute | solution.py:14
  45.3 4.6 %copy-start = (bf16[1,216,1152]{2,1,0:T(8,128)(2,1)S(1)}, bf16[1,216,1152]{2,1,0:T(8,128)(2,1)}, u32[]{:S(2)}) copy-start(bf16[1,216,1152]{2,1,0:T(8,128)(2,1)} %param.8) | copy-start | bytes 1492996
  45.3 39.1 %all-to-all-start.1 = ((bf16[16,64,1152]{2,1,0:T(8,128)(2,1)}), bf16[16,64,1152]{2,1,0:T(8,128)(2,1)}, u32[]{:S(2)}, u32[]{:S(2)}) async-start(bf16[16,64,1152]{2,1,0:T(8,128)(2,1)} %shard_map.65), calls=%async_computation.1 | async-start | bytes 4718592 | tf_op jit(solution)/shard_map/all_to_all | solution.py:83
  49.9 4.9 %copy-start.1 = (bf16[1,72,1152]{2,1,0:T(8,128)(2,1)S(1)}, bf16[1,72,1152]{2,1,0:T(8,128)(2,1)}, u32[]{:S(2)}) copy-start(bf16[1,72,1152]{2,1,0:T(8,128)(2,1)} %param.10) | copy-start | bytes 497668
  49.9 16.6 %copy-start.2 = (s32[3,1]{0,1:T(1,128)S(1)}, s32[3,1]{0,1:T(1,128)}, u32[]{:S(2)}) copy-start(s32[3,1]{0,1:T(1,128)} %param.11) | copy-start | bytes 40
  50.9 3.9 %collective-permute-start.1 = (bf16[144,1024]{1,0:T(8,128)(2,1)S(1)}, bf16[144,1024]{1,0:T(8,128)(2,1)S(1)}, u32[]{:S(2)}, u32[]{:S(2)}) collective-permute-start(bf16[144,1024]{1,0:T(8,128)(2,1)S(1)} %get-tuple-element.29.own_ref), channel_id=1, source_target_pairs={{0,16},{16,0},{32,48},{48,32},{64,80},{80,64},{96,112},{112,96},{1... | collective-permute-start | bytes 884744 | tf_op jit(solution)/shard_map/ppermute | solution.py:14
  52.8 18.2 %collective-permute-start.2 = (bf16[144,1024]{1,0:T(8,128)(2,1)S(1)}, bf16[144,1024]{1,0:T(8,128)(2,1)S(1)}, u32[]{:S(2)}, u32[]{:S(2)}) collective-permute-start(bf16[144,1024]{1,0:T(8,128)(2,1)S(1)} %get-tuple-element.29.own_ref), channel_id=1, source_target_pairs={{0,64},{16,80},{32,96},{48,112},{64,0},{80,16},{96,32},{112,48},{1... | collective-permute-start | bytes 884744 | tf_op jit(solution)/shard_map/ppermute | solution.py:14
  54.8 39.3 %collective-permute-start.5 = (bf16[72,1152]{1,0:T(8,128)(2,1)S(1)}, bf16[72,1152]{1,0:T(8,128)(2,1)S(1)}, u32[]{:S(2)}, u32[]{:S(2)}) collective-permute-start(bf16[72,1152]{1,0:T(8,128)(2,1)S(1)} %bitcast.16), channel_id=1, source_target_pairs={{12,0},{13,1},{14,2},{15,3},{0,4},{1,5},{2,6},{3,7},{4,8},{5,9},{6... | collective-permute-start | bytes 497672 | tf_op jit(solution)/shard_map/ppermute | solution.py:327
  58.5 35.6 %collective-permute-start.4 = (bf16[72,1152]{1,0:T(8,128)(2,1)S(1)}, bf16[72,1152]{1,0:T(8,128)(2,1)S(1)}, u32[]{:S(2)}, u32[]{:S(2)}) collective-permute-start(bf16[72,1152]{1,0:T(8,128)(2,1)S(1)} %bitcast.17), channel_id=1, source_target_pairs={{8,0},{9,1},{10,2},{11,3},{12,4},{13,5},{14,6},{15,7},{0,8},{1,9},... | collective-permute-start | bytes 497672 | tf_op jit(solution)/shard_map/ppermute | solution.py:327
  63.1 31.0 %collective-permute-start.3 = (bf16[72,1152]{1,0:T(8,128)(2,1)S(1)}, bf16[72,1152]{1,0:T(8,128)(2,1)S(1)}, u32[]{:S(2)}, u32[]{:S(2)}) collective-permute-start(bf16[72,1152]{1,0:T(8,128)(2,1)S(1)} %bitcast.18), channel_id=1, source_target_pairs={{4,0},{5,1},{6,2},{7,3},{8,4},{9,5},{10,6},{11,7},{12,8},{13,9},{1... | collective-permute-start | bytes 497672 | tf_op jit(solution)/shard_map/ppermute | solution.py:327
  90.7 9.4 %all-to-all-start.2 = ((bf16[4,72,256]{2,1,0:T(8,128)(2,1)}), bf16[4,72,256]{2,1,0:T(8,128)(2,1)S(1)}, u32[]{:S(2)}, u32[]{:S(2)}) async-start(bf16[4,72,256]{2,1,0:T(8,128)(2,1)} %shard_map.70), calls=%async_computation.2 | async-start | bytes 294912 | tf_op jit(solution)/shard_map/all_to_all | solution.py:318

commit v11 on v10

--- a/solution.py
+++ b/solution.py
@@ -95,7 +95,7 @@
         weight_ref[...], rows_ref[...], (((1,), (1,)), ((), ())), preferred_element_type=jnp.float32
     )
     flat = flat.astype(jnp.bfloat16).astype(jnp.float32)
-    query_ref[...] = rms_rows(flat[:head_dim], gain_ref[:, 0:1]).T.astype(jnp.bfloat16)
+    query_ref[...] = rms_rows(flat[:head_dim], gain_ref[:, 0:1]).astype(jnp.bfloat16)
     keys = rms_rows(flat[head_dim : 2 * head_dim], gain_ref[:, 1:2])
     pair = jnp.concatenate([keys, flat[2 * head_dim :]], axis=0)
     pair_ref[...] = pair.astype(jnp.bfloat16)
@@ -128,7 +128,7 @@
     return pl.pallas_call(
         project_kernel,
         out_shape=[
-            jax.ShapeDtypeStruct((tokens, head_dim), jnp.bfloat16),
+            jax.ShapeDtypeStruct((head_dim, tokens), jnp.bfloat16),
             jax.ShapeDtypeStruct((2 * head_dim, tokens), jnp.bfloat16),
         ],
         compiler_params=pltpu.CompilerParams(vmem_limit_bytes=16 << 20),
@@ -160,114 +160,105 @@
     )(rows, weight, gain)
 
 
-def scores_of(query, pair_ref):
-    head_dim = query.shape[1]
-    factor = math.log2(math.e) * float(head_dim) ** (-0.5)
-    keys = pair_ref[...][:head_dim]
-    return jnp.dot(query, keys, preferred_element_type=jnp.float32) * factor
+def spread_pair(pair_ref, keys_ref, values_ref):
+    head_dim = keys_ref.shape[1]
+    pair = pair_ref[...].astype(jnp.float32)
+    ones = jnp.ones((values_ref.shape[0] - head_dim, pair.shape[1]), jnp.float32)
+    keys_ref[...] = pair[:head_dim].T.astype(jnp.bfloat16)
+    values_ref[...] = jnp.concatenate([pair[head_dim:], ones], axis=0).astype(jnp.bfloat16)
+
+
+def scores_of(keys, query):
+    factor = math.log2(math.e) * float(query.shape[0]) ** (-0.5)
+    return jnp.dot(keys, query, preferred_element_type=jnp.float32) * factor
 
 
 def weighted(scores, shift, values):
     weights = jnp.exp2(scores - shift).astype(jnp.bfloat16)
-    return jnp.dot(weights, values, preferred_element_type=jnp.float32)
+    return jnp.dot(values, weights, preferred_element_type=jnp.float32)
+
+
+def cross_update(on, scores, values, best):
+    most = jnp.maximum(best, jnp.max(scores, axis=0, keepdims=True))
+    newbest = jnp.where(on, most, best)
+    shift = jnp.where(on, newbest, BLANK)
+    return newbest, jnp.exp2(best - newbest), weighted(scores, shift, values)
 
 
 def finish(acc, head_dim):
-    return acc[:, :head_dim] / jnp.maximum(acc[:, head_dim : head_dim + 1], 1.0)
-
-
-def spread_values(pair_ref, head_dim, padded):
-    part = pair_ref[...].astype(jnp.float32)[head_dim:]
-    tokens = part.shape[1]
-    lane = lax.broadcasted_iota(jnp.int32, (tokens, padded), 1)
-    filled = jnp.concatenate([part, jnp.zeros((padded - head_dim, tokens), jnp.float32)], axis=0)
-    return jnp.where(lane == head_dim, 1.0, filled.T).astype(jnp.bfloat16)
-
-
-def cross_update(active_ref, first, query, far_refs, values_ref, slot, best, acc):
-    several = [scores_of(query, ref) for ref in far_refs]
-    newbest = best
-    for n, scores in enumerate(several):
-        most = jnp.max(scores, axis=1, keepdims=True)
-        newbest = jnp.where(active_ref[first + n] > 0, jnp.maximum(newbest, most), newbest)
-    if acc is not None:
-        acc = acc * jnp.exp2(best - newbest)
-    for n, scores in enumerate(several):
-        shift = jnp.where(active_ref[first + n] > 0, newbest, BLANK)
-        term = weighted(scores, shift, values_ref[slot + n])
-        acc = term if acc is None else acc + term
-    return newbest, acc
-
-
-def near_kernel(tile, active_ref, query_ref, own_ref, *refs):
-    far_refs, own_out_ref, state_ref, values_ref = refs[:-3], refs[-3], refs[-2], refs[-1]
-    tokens, head_dim = query_ref.shape
-    padded = values_ref.shape[-1]
-    for n, ref in enumerate((own_ref,) + far_refs):
-        values_ref[n] = spread_values(ref, head_dim, padded)
-
-    def step(at, carry):
-        rows = pl.ds(pl.multiple_of(at * tile, tile), tile)
-        query = query_ref[rows, :]
-        scores = scores_of(query, own_ref)
-        acc = weighted(scores, jnp.max(scores, axis=1, keepdims=True), values_ref[0])
-        own_out_ref[rows, :] = finish(acc, head_dim)
-        start = jnp.full((tile, 1), -BLANK, jnp.float32)
-        best, acc = cross_update(active_ref, 0, query, far_refs, values_ref, 1, start, None)
-        lane = lax.broadcasted_iota(jnp.int32, (tile, padded), 1)
-        state_ref[rows, :] = jnp.where(lane == head_dim + 1, best, acc)
-        return carry
-
-    lax.fori_loop(0, tokens // tile, step, 0, unroll=True)
-
-
-def middle_kernel(tile, first, active_ref, query_ref, state_ref, *refs):
-    far_refs, out_ref, values_ref = refs[:-2], refs[-2], refs[-1]
-    tokens, head_dim = query_ref.shape
-    padded = values_ref.shape[-1]
-    for n, ref in enumerate(far_refs):
-        values_ref[n] = spread_values(ref, head_dim, padded)
-    lane = lax.broadcasted_iota(jnp.int32, (tile, padded), 1)
+    return acc[:head_dim] / jnp.maximum(acc[head_dim : head_dim + 1], 1.0)
+
+
+def near_kernel(
+    tile, active_ref, query_ref, own_ref, far_ref, own_out_ref, state_ref, best_ref, keys_ref, values_ref
+):
+    head_dim, tokens = query_ref.shape
+    for n, ref in enumerate((own_ref, far_ref)):
+        spread_pair(ref, keys_ref.at[n], values_ref.at[n])
     for at in range(tokens // tile):
-        rows = pl.ds(at * tile, tile)
-        acc = state_ref[rows, :]
-        best = acc[:, head_dim + 1 : head_dim + 2]
-        best, acc = cross_update(
-            active_ref, first, query_ref[rows, :], far_refs, values_ref, 0, best, acc
-        )
-        out_ref[rows, :] = jnp.where(lane == head_dim + 1, best, acc)
-
-
-def last_kernel(tile, first, active_ref, query_ref, own_in_ref, state_ref, *refs):
-    far_refs, out_ref, values_ref = refs[:-2], refs[-2], refs[-1]
-    tokens, head_dim = query_ref.shape
-    padded = values_ref.shape[-1]
-    for n, ref in enumerate(far_refs):
-        values_ref[n] = spread_values(ref, head_dim, padded)
-
+        columns = pl.ds(at * tile, tile)
+        query = query_ref[:, columns]
+        scores = scores_of(keys_ref[0], query)
+        acc = weighted(scores, jnp.max(scores, axis=0, keepdims=True), values_ref[0])
+        own_out_ref[:, columns] = finish(acc, head_dim)
+        start = jnp.full((1, tile), -BLANK, jnp.float32)
+        scores = scores_of(keys_ref[1], query)
+        best, _, acc = cross_update(active_ref[0] > 0, scores, values_ref[1], start)
+        state_ref[:, columns] = acc
+        best_ref[:, columns] = best
+
+
+def middle_kernel(
+    tile, which, active_ref, query_ref, state_ref, best_ref, far_ref, state_out_ref, best_out_ref,
+    keys_ref, values_ref,
+):
+    tokens = query_ref.shape[1]
+    spread_pair(far_ref, keys_ref, values_ref)
     for at in range(tokens // tile):
-        rows = pl.ds(at * tile, tile)
-        query = query_ref[rows, :]
-        acc = state_ref[rows, :]
-        best = acc[:, head_dim + 1 : head_dim + 2]
-        best, acc = cross_update(active_ref, first, query, far_refs, values_ref, 0, best, acc)
-        result = own_in_ref[rows, :] + finish(acc, head_dim)
-        out_ref[at] = result.T.astype(jnp.bfloat16)
-
-
-PADDED = 128
-
-
-def call_attend(kernel, out_shape, blocks, tokens, head_dim, arrays):
-    vmem = pl.BlockSpec(memory_space=pltpu.VMEM)
+        columns = pl.ds(at * tile, tile)
+        scores = scores_of(keys_ref[...], query_ref[:, columns])
+        on = active_ref[which] > 0
+        best, factor, term = cross_update(on, scores, values_ref[...], best_ref[:, columns])
+        state_out_ref[:, columns] = state_ref[:, columns] * factor + term
+        best_out_ref[:, columns] = best
+
+
+def last_kernel(
+    tile, which, active_ref, query_ref, own_in_ref, state_ref, best_ref, far_ref, out_ref,
+    keys_ref, values_ref,
+):
+    head_dim, tokens = query_ref.shape
+    block = out_ref.shape[-1]
+    spread_pair(far_ref, keys_ref, values_ref)
+    for at in range(tokens // tile):
+        columns = pl.ds(at * tile, tile)
+        scores = scores_of(keys_ref[...], query_ref[:, columns])
+        on = active_ref[which] > 0
+        _, factor, term = cross_update(on, scores, values_ref[...], best_ref[:, columns])
+        cross = finish(state_ref[:, columns] * factor + term, head_dim)
+        result = (own_in_ref[:, columns] + cross).astype(jnp.bfloat16)
+        for n in range(tile // block):
+            out_ref[at * (tile // block) + n] = result[:, n * block : (n + 1) * block]
+
+
+ONES = 8
+
+
+def call_attend(kernel, out_shape, blocks, arrays):
+    head_dim, tokens = arrays[1].shape
+    lead = () if blocks == 1 else (blocks,)
+    smem, vmem = pl.BlockSpec(memory_space=pltpu.SMEM), pl.BlockSpec(memory_space=pltpu.VMEM)
     several = isinstance(out_shape, list)
     return pl.pallas_call(
         kernel,
         out_shape=out_shape,
-        in_specs=[pl.BlockSpec(memory_space=pltpu.SMEM)] + [vmem] * (len(arrays) - 1),
+        in_specs=[smem] + [vmem] * (len(arrays) - 1),
         out_specs=[vmem] * len(out_shape) if several else vmem,
-        scratch_shapes=[pltpu.VMEM((blocks, tokens, PADDED), jnp.bfloat16)],
-        compiler_params=pltpu.CompilerParams(vmem_limit_bytes=20 << 20),
+        scratch_shapes=[
+            pltpu.VMEM(lead + (tokens, head_dim), jnp.bfloat16),
+            pltpu.VMEM(lead + (head_dim + ONES, tokens), jnp.bfloat16),
+        ],
+        compiler_params=pltpu.CompilerParams(vmem_limit_bytes=24 << 20),
         cost_estimate=pl.CostEstimate(
             flops=4 * blocks * tokens * tokens * 256,
             bytes_accessed=4 * blocks * tokens * head_dim,
@@ -277,34 +268,26 @@
 
 
 def attend_near(active, query, own, far):
-    tokens, head_dim = query.shape
+    head_dim, tokens = query.shape
     out_shape = [
-        jax.ShapeDtypeStruct((tokens, head_dim), jnp.float32),
-        jax.ShapeDtypeStruct((tokens, PADDED), jnp.float32),
-    ]
-    arrays = (active, query, own, *far)
-    return call_attend(
-        functools.partial(near_kernel, 256), out_shape, 1 + len(far), tokens, head_dim, arrays
-    )
-
-
-def attend_middle(active, first, query, state, far):
-    tokens, head_dim = query.shape
-    out_shape = jax.ShapeDtypeStruct((tokens, PADDED), jnp.float32)
-    arrays = (active, query, state, *far)
-    return call_attend(
-        functools.partial(middle_kernel, 256, first), out_shape, len(far), tokens, head_dim, arrays
-    )
-
-
-def attend_last(active, first, query, own_result, state, far):
-    tokens, head_dim = query.shape
+        jax.ShapeDtypeStruct((rows, tokens), jnp.float32) for rows in (head_dim, head_dim + ONES, 1)
+    ]
+    kernel = functools.partial(near_kernel, tokens // 2)
+    return call_attend(kernel, out_shape, 2, (active, query, own, far))
+
+
+def attend_middle(active, which, query, state, best, far):
+    out_shape = [jax.ShapeDtypeStruct(array.shape, jnp.float32) for array in (state, best)]
+    kernel = functools.partial(middle_kernel, query.shape[1] // 2, which)
+    return call_attend(kernel, out_shape, 1, (active, query, state, best, far))
+
+
+def attend_last(active, which, query, own_result, state, best, far):
+    head_dim, tokens = query.shape
     side = len(groups(0))
     out_shape = jax.ShapeDtypeStruct((side, head_dim, tokens // side), jnp.bfloat16)
-    arrays = (active, query, own_result, state, *far)
-    return call_attend(
-        functools.partial(last_kernel, tokens // side, first), out_shape, len(far), tokens, head_dim, arrays
-    )
+    kernel = functools.partial(last_kernel, tokens // 2, which)
+    return call_attend(kernel, out_shape, 1, (active, query, own_result, state, best, far))
 
 
 def groups(which):
@@ -381,11 +364,13 @@
     near = [partner(own, bit) for bit in bits[:-1]]
     near[0], out_rows = lax.optimization_barrier((near[0], out_weight[0]))
     out_weights = [out_weight[0]] + column_weights(out_rows)
-    own_result, state = attend_near(active, query, own, near[:1])
-    state = attend_middle(active, 1, query, state, near[1:])
-    far_every, own_result, state = lax.optimization_barrier((far_every, own_result, state))
-    far = [project_far(far_every, weight, gain)]
-    attended = attend_last(active, rounds - 1, query, own_result, state, far)
+    own_result, state, best = attend_near(active, query, own, near[0])
+    state, best = attend_middle(active, 1, query, state, best, near[1])
+    far_every, own_result, state, best = lax.optimization_barrier(
+        (far_every, own_result, state, best)
+    )
+    far = project_far(far_every, weight, gain)
+    attended = attend_last(active, rounds - 1, query, own_result, state, best, far)
     mixed = project_out(exchange(attended, 1), out_weights)
     return mixed.reshape(loc_len, view_dev, width)
 

time: 113 us -> 112 us (level)
  the two profiles are of different devices: /device:TPU:96 before, /device:TPU:448 now
where the time goes in v11:
time: 112 us
  waiting for transfers between devices  44.4 us (40%)
  starting transfers between devices  37.3 us (33%)
  Pallas kernels  17.9 us (16%)
  blocking collectives  10.8 us (10%)
    ppermute x3, waiting for transfers between devices, partner(): lax.ppermute(array, 'view', [(i, i ^ 1 << bit) for i in range(lax.axis_si...  19.8 us
    all_to_all x2, waiting for transfers between devices, gather_tokens(): lax.all_to_all(slots, 'head', split_axis=0, concat_axis=0, tiled=True)  18.6 us
    ppermute x3, starting transfers between devices, column_weights(): lax.ppermute(weight, 'head', [((head + step * side) % heads, head) for he...  11.7 us
    all_to_all x2, starting transfers between devices, gather_tokens(): lax.all_to_all(slots, 'head', split_axis=0, concat_axis=0, tiled=True)  11.6 us
    all_to_all x1, blocking collectives, exchange(): lax.all_to_all(slots, 'head', split_axis=0, concat_axis=0, tiled=True, ax...  10.8 us
    ppermute x3, starting transfers between devices, partner(): lax.ppermute(array, 'view', [(i, i ^ 1 << bit) for i in range(lax.axis_si...  10.7 us
    pallas_call x3, Pallas kernels, call_attend(): pl.pallas_call(kernel, out_shape=out_shape, in_specs=[smem] + [vmem] * (l...  9.5 us
    all_to_all x1, waiting for transfers between devices, exchange(): lax.all_to_all(slots, 'head', split_axis=0, concat_axis=0, tiled=True, ax...  5.98 us
  transfers between devices with their start and end apart: 9, of which 4 were waited for; matrix products, arithmetic and copies ran while one was open for 0% of the time, Pallas kernels for 13%

profile of v11, /device:TPU:448, one launch (start us, length us, event | category | flops | bytes accessed | tf_op | source)
XLA Modules:
  0.0 111.6 jit_solution(18196247370113697535)
XLA Ops:
  0.0 2.7 %shard_map.64 = (bf16[64,1152]{1,0:T(8,128)(2,1)S(1)}, bf16[16,64,1152]{2,1,0:T(8,128)(2,1)}) custom-call(bf16[64,1152]{1,0:T(8,128)(2,1)} %bitcast.23, f32[1152]{0:T(1024)} %gain_ref.1), custom_call_target="tpu_custom_call" | custom-call | flops 589824 | bytes 2359296 | tf_op jit(solution)/shard_map/pallas_call | solution.py:49
  2.7 7.0 %all-to-all-start = ((bf16[16,64,1152]{2,1,0:T(8,128)(2,1)}), bf16[16,64,1152]{2,1,0:T(8,128)(2,1)S(1)}, u32[]{:S(2)}, u32[]{:S(2)}) async-start(bf16[16,64,1152]{2,1,0:T(8,128)(2,1)} %get-tuple-element.27), calls=%async_computation | async-start | bytes 4718592 | tf_op jit(solution)/shard_map/all_to_all | solution.py:83
  9.8 5.4 %collective-permute-start = (bf16[64,1152]{1,0:T(8,128)(2,1)S(1)}, bf16[64,1152]{1,0:T(8,128)(2,1)S(1)}, u32[]{:S(2)}, u32[]{:S(2)}) collective-permute-start(bf16[64,1152]{1,0:T(8,128)(2,1)S(1)} %get-tuple-element.25), channel_id=1, source_target_pairs={{0,256},{16,272},{32,288},{48,304},{64,320},{80,336},{96,352},{112... | collective-permute-start | bytes 442376 | tf_op jit(solution)/shard_map/ppermute | solution.py:14
  15.2 0.1 copy.7
  15.3 19.8 %collective-permute-done.source_ref = bf16[64,1152]{1,0:T(8,128)(2,1)S(1)} collective-permute-done((bf16[64,1152]{1,0:T(8,128)(2,1)S(1)}, bf16[64,1152]{1,0:T(8,128)(2,1)S(1)}, u32[]{:S(2)}, u32[]{:S(2)}) %collective-permute-start) | collective-permute-done | bytes 147488 | tf_op jit(solution)/shard_map/ppermute | solution.py:14
  35.2 1.6 %shard_map.65 = bf16[16,64,1152]{2,1,0:T(8,128)(2,1)} custom-call(bf16[64,1152]{1,0:T(8,128)(2,1)S(1)} %collective-permute-done.source_ref), custom_call_target="tpu_custom_call" | custom-call | bytes 2359296 | tf_op jit(solution)/shard_map/pallas_call | solution.py:71
  36.7 8.5 %all-to-all-done = bf16[16,64,1152]{2,1,0:T(8,128)(2,1)S(1)} async-done(((bf16[16,64,1152]{2,1,0:T(8,128)(2,1)}), bf16[16,64,1152]{2,1,0:T(8,128)(2,1)S(1)}, u32[]{:S(2)}, u32[]{:S(2)}) %all-to-all-start) | async-done | bytes 2359328 | tf_op jit(solution)/shard_map/all_to_all | solution.py:83
  45.3 4.6 %all-to-all-start.1 = ((bf16[16,64,1152]{2,1,0:T(8,128)(2,1)}), bf16[16,64,1152]{2,1,0:T(8,128)(2,1)}, u32[]{:S(2)}, u32[]{:S(2)}) async-start(bf16[16,64,1152]{2,1,0:T(8,128)(2,1)} %shard_map.65), calls=%async_computation.1 | async-start | bytes 4718592 | tf_op jit(solution)/shard_map/all_to_all | solution.py:83
  49.9 0.9 shard_map.66
  50.8 1.9 %collective-permute-start.1 = (bf16[144,1024]{1,0:T(8,128)(2,1)S(1)}, bf16[144,1024]{1,0:T(8,128)(2,1)S(1)}, u32[]{:S(2)}, u32[]{:S(2)}) collective-permute-start(bf16[144,1024]{1,0:T(8,128)(2,1)S(1)} %get-tuple-element.33.own_ref), channel_id=1, source_target_pairs={{0,16},{16,0},{32,48},{48,32},{64,80},{80,64},{96,112},{112,96},{1... | collective-permute-start | bytes 884744 | tf_op jit(solution)/shard_map/ppermute | solution.py:14
  52.8 3.4 %collective-permute-start.2 = (bf16[144,1024]{1,0:T(8,128)(2,1)S(1)}, bf16[144,1024]{1,0:T(8,128)(2,1)S(1)}, u32[]{:S(2)}, u32[]{:S(2)}) collective-permute-start(bf16[144,1024]{1,0:T(8,128)(2,1)S(1)} %get-tuple-element.33.own_ref), channel_id=1, source_target_pairs={{0,64},{16,80},{32,96},{48,112},{64,0},{80,16},{96,32},{112,48},{1... | collective-permute-start | bytes 884744 | tf_op jit(solution)/shard_map/ppermute | solution.py:14
  56.1 3.7 %collective-permute-start.5 = (bf16[72,1152]{1,0:T(8,128)(2,1)S(1)}, bf16[72,1152]{1,0:T(8,128)(2,1)S(1)}, u32[]{:S(2)}, u32[]{:S(2)}) collective-permute-start(bf16[72,1152]{1,0:T(8,128)(2,1)S(1)} %bitcast.16), channel_id=1, source_target_pairs={{12,0},{13,1},{14,2},{15,3},{0,4},{1,5},{2,6},{3,7},{4,8},{5,9},{6... | collective-permute-start | bytes 497672 | tf_op jit(solution)/shard_map/ppermute | solution.py:310
  59.8 4.6 %collective-permute-start.4 = (bf16[72,1152]{1,0:T(8,128)(2,1)S(1)}, bf16[72,1152]{1,0:T(8,128)(2,1)S(1)}, u32[]{:S(2)}, u32[]{:S(2)}) collective-permute-start(bf16[72,1152]{1,0:T(8,128)(2,1)S(1)} %bitcast.17), channel_id=1, source_target_pairs={{8,0},{9,1},{10,2},{11,3},{12,4},{13,5},{14,6},{15,7},{0,8},{1,9},... | collective-permute-start | bytes 497672 | tf_op jit(solution)/shard_map/ppermute | solution.py:310
  64.5 3.3 %collective-permute-start.3 = (bf16[72,1152]{1,0:T(8,128)(2,1)S(1)}, bf16[72,1152]{1,0:T(8,128)(2,1)S(1)}, u32[]{:S(2)}, u32[]{:S(2)}) collective-permute-start(bf16[72,1152]{1,0:T(8,128)(2,1)S(1)} %bitcast.18), channel_id=1, source_target_pairs={{4,0},{5,1},{6,2},{7,3},{8,4},{9,5},{10,6},{11,7},{12,8},{13,9},{1... | collective-permute-start | bytes 497672 | tf_op jit(solution)/shard_map/ppermute | solution.py:310
  67.8 4.1 %shard_map.67 = (f32[72,1024]{1,0:T(8,128)S(1)}, f32[80,1024]{1,0:T(8,128)S(1)}, f32[1,1024]{1,0:T(1,128)S(1)}) custom-call(s32[3]{0:T(128)S(1)} %bitcast.20, bf16[72,1024]{1,0:T(8,128)(2,1)S(1)} %get-tuple-element.31.query_ref, bf16[144,1024]{1,0:T(8,128)(2,1)S(1)} %get-tuple-element.33.own_ref, bf16[144,1024]{1,0:T(8,128)(2,1)S(1)} %collective-permute-done.1.far_ref), custom_call_target="tpu_custom_call" | custom-call | flops 2147483648 | bytes 589824 | tf_op jit(solution)/shard_map/pallas_call | solution.py:252
  71.9 2.4 %shard_map.68 = (f32[80,1024]{1,0:T(8,128)S(1)}, f32[1,1024]{1,0:T(1,128)S(1)}) custom-call(s32[3]{0:T(128)S(1)} %bitcast.21, bf16[72,1024]{1,0:T(8,128)(2,1)S(1)} %get-tuple-element.31.query_ref, f32[80,1024]{1,0:T(8,128)S(1)} %get-tuple-element.36.state_ref, f32[1,1024]{1,0:T(1,128)S(1)} %get-tuple-element.37.best_ref, ...), custom_call_target="tpu_custom_call" | custom-call | flops 1073741824 | bytes 294912 | tf_op jit(solution)/shard_map/pallas_call | solution.py:252
  74.3 10.1 %all-to-all-done.1 = bf16[16,64,1152]{2,1,0:T(8,128)(2,1)} async-done(((bf16[16,64,1152]{2,1,0:T(8,128)(2,1)}), bf16[16,64,1152]{2,1,0:T(8,128)(2,1)}, u32[]{:S(2)}, u32[]{:S(2)}) %all-to-all-start.1) | async-done | bytes 2359328 | tf_op jit(solution)/shard_map/all_to_all | solution.py:83
  84.4 2.4 %shard_map.69.far_ref = bf16[144,1024]{1,0:T(8,128)(2,1)S(1)} custom-call(bf16[1024,1152]{1,0:T(8,128)(2,1)} %bitcast.7.rows_ref, bf16[216,1152]{1,0:T(8,128)(2,1)S(1)} %bitcast.13, f32[72,2]{1,0:T(8,128)S(1)} %bitcast.15), custom_call_target="tpu_custom_call" | custom-call | flops 509607936 | bytes 2359296 | tf_op jit(solution)/shard_map/pallas_call | solution.py:147
  86.8 3.0 %shard_map.70 = bf16[4,72,256]{2,1,0:T(8,128)(2,1)} custom-call(s32[3]{0:T(128)S(1)} %bitcast.22, bf16[72,1024]{1,0:T(8,128)(2,1)S(1)} %get-tuple-element.31.query_ref, f32[72,1024]{1,0:T(8,128)S(1)} %get-tuple-element.40.own_in_ref, f32[80,1024]{1,0:T(8,128)S(1)} %get-tuple-element.41.state_ref, f32[1,1024]{1,0:T(1,128)S(1)} %get-tuple-element.42.best_ref, ...), custom_call_target="tpu_custom_call" | custom-call | flops 1073741824 | bytes 294912 | tf_op jit(solution)/shard_map/pallas_call | solution.py:252
  89.8 3.3 %all-to-all-start.2 = ((bf16[4,72,256]{2,1,0:T(8,128)(2,1)}), bf16[4,72,256]{2,1,0:T(8,128)(2,1)S(1)}, u32[]{:S(2)}, u32[]{:S(2)}) async-start(bf16[4,72,256]{2,1,0:T(8,128)(2,1)} %shard_map.70), calls=%async_computation.2 | async-start | bytes 294912 | tf_op jit(solution)/shard_map/all_to_all | solution.py:301
  93.2 6.0 %all-to-all-done.2.parts_ref = bf16[4,72,256]{2,1,0:T(8,128)(2,1)S(1)} async-done(((bf16[4,72,256]{2,1,0:T(8,128)(2,1)}), bf16[4,72,256]{2,1,0:T(8,128)(2,1)S(1)}, u32[]{:S(2)}, u32[]{:S(2)}) %all-to-all-start.2) | async-done | bytes 147488 | tf_op jit(solution)/shard_map/all_to_all | solution.py:301
  99.2 0.8 shard_map.71
  100.0 10.8 %all_to_all.20 = bf16[4,64,1152]{2,1,0:T(8,128)(2,1)S(1)} all-to-all(bf16[4,64,1152]{2,1,0:T(8,128)(2,1)S(1)} %shard_map.71), channel_id=1, replica_groups={{0,1,2,3},{4,5,6,7},{8,9,10,11},{12,13,14,15},{16,17,18,19},{20,21,22,2..., dimensions={0} | all-to-all | bytes 1179648 | tf_op jit(solution)/shard_map/all_to_all | solution.py:301
  110.8 0.8 reduce_sum.12
  (13 shorter events, 0.0 us)
Async XLA Ops:
  2.7 12.5 %copy-start.3 = (f32[1,2,72]{2,1,0:T(2,128)S(1)}, f32[1,2,72]{2,1,0:T(2,128)}, u32[]{:S(2)}) copy-start(f32[1,2,72]{2,1,0:T(2,128)} %param.9) | copy-start | bytes 1732
  2.7 42.6 %all-to-all-start = ((bf16[16,64,1152]{2,1,0:T(8,128)(2,1)}), bf16[16,64,1152]{2,1,0:T(8,128)(2,1)S(1)}, u32[]{:S(2)}, u32[]{:S(2)}) async-start(bf16[16,64,1152]{2,1,0:T(8,128)(2,1)} %get-tuple-element.27), calls=%async_computation | async-start | bytes 4718592 | tf_op jit(solution)/shard_map/all_to_all | solution.py:83
  9.8 25.4 %collective-permute-start = (bf16[64,1152]{1,0:T(8,128)(2,1)S(1)}, bf16[64,1152]{1,0:T(8,128)(2,1)S(1)}, u32[]{:S(2)}, u32[]{:S(2)}) collective-permute-start(bf16[64,1152]{1,0:T(8,128)(2,1)S(1)} %get-tuple-element.25), channel_id=1, source_target_pairs={{0,256},{16,272},{32,288},{48,304},{64,320},{80,336},{96,352},{112... | collective-permute-start | bytes 442376 | tf_op jit(solution)/shard_map/ppermute | solution.py:14
  45.3 4.6 %copy-start = (bf16[1,216,1152]{2,1,0:T(8,128)(2,1)S(1)}, bf16[1,216,1152]{2,1,0:T(8,128)(2,1)}, u32[]{:S(2)}) copy-start(bf16[1,216,1152]{2,1,0:T(8,128)(2,1)} %param.8) | copy-start | bytes 1492996
  45.3 39.1 %all-to-all-start.1 = ((bf16[16,64,1152]{2,1,0:T(8,128)(2,1)}), bf16[16,64,1152]{2,1,0:T(8,128)(2,1)}, u32[]{:S(2)}, u32[]{:S(2)}) async-start(bf16[16,64,1152]{2,1,0:T(8,128)(2,1)} %shard_map.65), calls=%async_computation.1 | async-start | bytes 4718592 | tf_op jit(solution)/shard_map/all_to_all | solution.py:83
  49.9 6.3 %copy-start.1 = (bf16[1,72,1152]{2,1,0:T(8,128)(2,1)S(1)}, bf16[1,72,1152]{2,1,0:T(8,128)(2,1)}, u32[]{:S(2)}) copy-start(bf16[1,72,1152]{2,1,0:T(8,128)(2,1)} %param.10) | copy-start | bytes 497668
  49.9 18.0 %copy-start.2 = (s32[3,1]{0,1:T(1,128)S(1)}, s32[3,1]{0,1:T(1,128)}, u32[]{:S(2)}) copy-start(s32[3,1]{0,1:T(1,128)} %param.11) | copy-start | bytes 40
  50.8 5.3 %collective-permute-start.1 = (bf16[144,1024]{1,0:T(8,128)(2,1)S(1)}, bf16[144,1024]{1,0:T(8,128)(2,1)S(1)}, u32[]{:S(2)}, u32[]{:S(2)}) collective-permute-start(bf16[144,1024]{1,0:T(8,128)(2,1)S(1)} %get-tuple-element.33.own_ref), channel_id=1, source_target_pairs={{0,16},{16,0},{32,48},{48,32},{64,80},{80,64},{96,112},{112,96},{1... | collective-permute-start | bytes 884744 | tf_op jit(solution)/shard_map/ppermute | solution.py:14
  52.8 19.1 %collective-permute-start.2 = (bf16[144,1024]{1,0:T(8,128)(2,1)S(1)}, bf16[144,1024]{1,0:T(8,128)(2,1)S(1)}, u32[]{:S(2)}, u32[]{:S(2)}) collective-permute-start(bf16[144,1024]{1,0:T(8,128)(2,1)S(1)} %get-tuple-element.33.own_ref), channel_id=1, source_target_pairs={{0,64},{16,80},{32,96},{48,112},{64,0},{80,16},{96,32},{112,48},{1... | collective-permute-start | bytes 884744 | tf_op jit(solution)/shard_map/ppermute | solution.py:14
  56.1 37.0 %collective-permute-start.5 = (bf16[72,1152]{1,0:T(8,128)(2,1)S(1)}, bf16[72,1152]{1,0:T(8,128)(2,1)S(1)}, u32[]{:S(2)}, u32[]{:S(2)}) collective-permute-start(bf16[72,1152]{1,0:T(8,128)(2,1)S(1)} %bitcast.16), channel_id=1, source_target_pairs={{12,0},{13,1},{14,2},{15,3},{0,4},{1,5},{2,6},{3,7},{4,8},{5,9},{6... | collective-permute-start | bytes 497672 | tf_op jit(solution)/shard_map/ppermute | solution.py:310
  59.8 33.4 %collective-permute-start.4 = (bf16[72,1152]{1,0:T(8,128)(2,1)S(1)}, bf16[72,1152]{1,0:T(8,128)(2,1)S(1)}, u32[]{:S(2)}, u32[]{:S(2)}) collective-permute-start(bf16[72,1152]{1,0:T(8,128)(2,1)S(1)} %bitcast.17), channel_id=1, source_target_pairs={{8,0},{9,1},{10,2},{11,3},{12,4},{13,5},{14,6},{15,7},{0,8},{1,9},... | collective-permute-start | bytes 497672 | tf_op jit(solution)/shard_map/ppermute | solution.py:310
  64.5 28.7 %collective-permute-start.3 = (bf16[72,1152]{1,0:T(8,128)(2,1)S(1)}, bf16[72,1152]{1,0:T(8,128)(2,1)S(1)}, u32[]{:S(2)}, u32[]{:S(2)}) collective-permute-start(bf16[72,1152]{1,0:T(8,128)(2,1)S(1)} %bitcast.18), channel_id=1, source_target_pairs={{4,0},{5,1},{6,2},{7,3},{8,4},{9,5},{10,6},{11,7},{12,8},{13,9},{1... | collective-permute-start | bytes 497672 | tf_op jit(solution)/shard_map/ppermute | solution.py:310
  89.8 9.4 %all-to-all-start.2 = ((bf16[4,72,256]{2,1,0:T(8,128)(2,1)}), bf16[4,72,256]{2,1,0:T(8,128)(2,1)S(1)}, u32[]{:S(2)}, u32[]{:S(2)}) async-start(bf16[4,72,256]{2,1,0:T(8,128)(2,1)} %shard_map.70), calls=%async_computation.2 | async-start | bytes 294912 | tf_op jit(solution)/shard_map/all_to_all | solution.py:301

commit v12 on v11

v12 whole, which is shorter than its diff:
```python
import functools
import math
import jax
import jax.numpy as jnp
from jax import lax
from jax.experimental import pallas as pl
from jax.experimental.pallas import tpu as pltpu
from jax.sharding import PartitionSpec as P

BLANK = 1e30


def partner(array, bit):
    return lax.ppermute(array, "view", [(i, i ^ 1 << bit) for i in range(lax.axis_size("view"))])


def traded(array):
    views, heads = lax.axis_size("view"), lax.axis_size("head")
    pairs = []
    for view in range(views):
        for head in range(heads):
            if view % 2 != head % 2:
                pairs.append(((view ^ 1) * heads + (head ^ 1), view * heads + head))
    return lax.ppermute(array, ("view", "head"), pairs)


def beside(array):
    return lax.ppermute(array, "head", [(i, i ^ 1) for i in range(lax.axis_size("head"))])


def normalize_kernel(core_ref, rows_ref, gain_ref, keep_ref, give_ref, held_ref, held_gain_ref, read_sems):
    reads = [
        pltpu.make_async_copy(rows_ref, held_ref, read_sems.at[0]),
        pltpu.make_async_copy(gain_ref, held_gain_ref, read_sems.at[1]),
    ]
    for read in reads:
        read.start()
    for read in reads:
        read.wait()
    values = held_ref[...].astype(jnp.float32)
    mean = jnp.mean(values, axis=-1, keepdims=True)
    centred = values - mean
    var = jnp.mean(centred * centred, axis=-1, keepdims=True)
    gain = held_gain_ref[...].reshape(1, -1)
    normed = centred * lax.rsqrt(var + 1e-06) * gain
    half = normed.shape[0] // 2
    first = core_ref[0] == 0
    keep_ref[...] = jnp.where(first, normed[:half], normed[half:]).astype(jnp.bfloat16)
    give_ref[...] = jnp.where(first, normed[half:], normed[:half]).astype(jnp.bfloat16)


def normalize(core, rows, norm_gain):
    smem, vmem = pl.BlockSpec(memory_space=pltpu.SMEM), pl.BlockSpec(memory_space=pltpu.VMEM)
    hbm = pl.BlockSpec(memory_space=pltpu.HBM)
    half = jax.ShapeDtypeStruct((rows.shape[0] // 2, rows.shape[1]), jnp.bfloat16)
    rows = pltpu.with_memory_space_constraint(rows, pltpu.HBM)
    norm_gain = pltpu.with_memory_space_constraint(norm_gain, pltpu.HBM)
    return pl.pallas_call(
        normalize_kernel,
        out_shape=[half, half],
        in_specs=[smem, hbm, hbm],
        out_specs=[vmem, vmem],
        scratch_shapes=[
            pltpu.VMEM(rows.shape, rows.dtype),
            pltpu.VMEM(norm_gain.shape, norm_gain.dtype),
            pltpu.SemaphoreType.DMA((2,)),
        ],
        compiler_params=pltpu.CompilerParams(vmem_limit_bytes=16 << 20),
        cost_estimate=pl.CostEstimate(
            flops=8 * rows.size, bytes_accessed=4 * rows.size, transcendentals=0
        ),
    )(core, rows, norm_gain)


def deal_kernel(pair_ref, slots_ref, sems):
    copies = [
        pltpu.make_async_copy(pair_ref.at[n % 2], slots_ref.at[n], sems.at[n])
        for n in range(slots_ref.shape[0])
    ]
    for copy in copies:
        copy.start()
    for copy in copies:
        copy.wait()


def pair_kernel(core_ref, keep_ref, took_ref, pair_ref, slots_ref, sems):
    first = core_ref[0] == 0
    keep, took = keep_ref[...].astype(jnp.float32), took_ref[...].astype(jnp.float32)
    pair_ref[0] = jnp.where(first, keep, took).astype(jnp.bfloat16)
    pair_ref[1] = jnp.where(first, took, keep).astype(jnp.bfloat16)
    deal_kernel(pair_ref, slots_ref, sems)


def pair_up(core, keep, took, slots):
    smem, vmem = pl.BlockSpec(memory_space=pltpu.SMEM), pl.BlockSpec(memory_space=pltpu.VMEM)
    return pl.pallas_call(
        pair_kernel,
        out_shape=[
            jax.ShapeDtypeStruct((2,) + keep.shape, keep.dtype),
            pltpu.HBM((slots,) + keep.shape, keep.dtype),
        ],
        in_specs=[smem, vmem, vmem],
        out_specs=[vmem, pl.BlockSpec(memory_space=pltpu.HBM)],
        scratch_shapes=[pltpu.SemaphoreType.DMA((slots,))],
        compiler_params=pltpu.CompilerParams(vmem_limit_bytes=16 << 20),
        cost_estimate=pl.CostEstimate(flops=0, bytes_accessed=2 * slots * keep.size, transcendentals=0),
    )(core, keep, took)


def deal(pair, slots):
    return pl.pallas_call(
        deal_kernel,
        out_shape=pltpu.HBM((slots,) + pair.shape[1:], pair.dtype),
        in_specs=[pl.BlockSpec(memory_space=pltpu.VMEM)],
        out_specs=pl.BlockSpec(memory_space=pltpu.HBM),
        scratch_shapes=[pltpu.SemaphoreType.DMA((slots,))],
        compiler_params=pltpu.CompilerParams(vmem_limit_bytes=16 << 20),
        cost_estimate=pl.CostEstimate(flops=0, bytes_accessed=0, transcendentals=0),
    )(pair)


def gather_tokens(slots):
    rows = lax.all_to_all(slots, "head", split_axis=0, concat_axis=0, tiled=True)
    return rows.reshape(-1, slots.shape[-1])


def rms_rows(part, gain):
    square = jnp.mean(part * part, axis=0, keepdims=True) + 1e-06
    return part * lax.rsqrt(square) * gain


def project_kernel(mine_ref, other_ref, weight_ref, gain_ref, query_ref, pair_ref):
    head_dim = gain_ref.shape[0]
    for n, rows_ref in enumerate((mine_ref, other_ref)):
        block = rows_ref.shape[0]
        at = pl.ds(n * block, block)
        flat = lax.dot_general(
            weight_ref[...], rows_ref[...], (((1,), (1,)), ((), ())), preferred_element_type=jnp.float32
        )
        flat = flat.astype(jnp.bfloat16).astype(jnp.float32)
        query_ref[:, at] = rms_rows(flat[:head_dim], gain_ref[:, 0:1]).astype(jnp.bfloat16)
        keys = rms_rows(flat[head_dim : 2 * head_dim], gain_ref[:, 1:2])
        pair = jnp.concatenate([keys, flat[2 * head_dim :]], axis=0)
        pair_ref[:, at] = pair.astype(jnp.bfloat16)


def project_far_kernel(mine_ref, other_ref, weight_ref, gain_ref, pair_ref):
    head_dim = gain_ref.shape[0]
    skip = head_dim // 16 * 16
    for n, rows_ref in enumerate((mine_ref, other_ref)):
        block = rows_ref.shape[0]
        flat = lax.dot_general(
            weight_ref[skip:], rows_ref[...], (((1,), (1,)), ((), ())), preferred_element_type=jnp.float32
        )
        flat = flat[head_dim - skip :].astype(jnp.bfloat16).astype(jnp.float32)
        keys = rms_rows(flat[:head_dim], gain_ref[:, 1:2])
        pair = jnp.concatenate([keys, flat[head_dim:]], axis=0)
        pair_ref[:, pl.ds(n * block, block)] = pair.astype(jnp.bfloat16)


def project(mine, other, weight, gain, with_query):
    tokens, width = 2 * mine.shape[0], mine.shape[1]
    head_dim = gain.shape[0]
    pair = jax.ShapeDtypeStruct((2 * head_dim, tokens), jnp.bfloat16)
    query = jax.ShapeDtypeStruct((head_dim, tokens), jnp.bfloat16)
    return pl.pallas_call(
        project_kernel if with_query else project_far_kernel,
        out_shape=[query, pair] if with_query else pair,
        compiler_params=pltpu.CompilerParams(vmem_limit_bytes=16 << 20),
        cost_estimate=pl.CostEstimate(
            flops=(100 if with_query else 2) * tokens * width * weight.shape[0],
            bytes_accessed=2 * tokens * width,
            transcendentals=0,
        ),
    )(mine, other, weight, gain)


def spread_pair(pair_ref, keys_ref, values_ref):
    head_dim = keys_ref.shape[1]
    pair = pair_ref[...].astype(jnp.float32)
    ones = jnp.ones((values_ref.shape[0] - head_dim, pair.shape[1]), jnp.float32)
    keys_ref[...] = pair[:head_dim].T.astype(jnp.bfloat16)
    values_ref[...] = jnp.concatenate([pair[head_dim:], ones], axis=0).astype(jnp.bfloat16)


def scores_of(keys, query):
    factor = math.log2(math.e) * float(query.shape[0]) ** (-0.5)
    return jnp.dot(keys, query, preferred_element_type=jnp.float32) * factor


def weighted(scores, shift, values):
    weights = jnp.exp2(scores - shift).astype(jnp.bfloat16)
    return jnp.dot(values, weights, preferred_element_type=jnp.float32)


def cross_update(on, scores, values, best):
    most = jnp.maximum(best, jnp.max(scores, axis=0, keepdims=True))
    newbest = jnp.where(on, most, best)
    shift = jnp.where(on, newbest, BLANK)
    return newbest, jnp.exp2(best - newbest), weighted(scores, shift, values)


def finish(acc, head_dim):
    return acc[:head_dim] / jnp.maximum(acc[head_dim : head_dim + 1], 1.0)


def own_kernel(tile, query_ref, own_ref, own_out_ref, keys_ref, values_ref):
    head_dim, tokens = query_ref.shape
    spread_pair(own_ref, keys_ref, values_ref)
    for at in range(tokens // tile):
        columns = pl.ds(at * tile, tile)
        scores = scores_of(keys_ref[...], query_ref[:, columns])
        acc = weighted(scores, jnp.max(scores, axis=0, keepdims=True), values_ref[...])
        own_out_ref[:, columns] = finish(acc, head_dim)


def middle_kernel(
    tile, which, active_ref, query_ref, state_ref, best_ref, far_ref, state_out_ref, best_out_ref,
    keys_ref, values_ref,
):
    tokens = query_ref.shape[1]
    spread_pair(far_ref, keys_ref, values_ref)
    for at in range(tokens // tile):
        columns = pl.ds(at * tile, tile)
        scores = scores_of(keys_ref[...], query_ref[:, columns])
        on = active_ref[which] > 0
        best, factor, term = cross_update(on, scores, values_ref[...], best_ref[:, columns])
        state_out_ref[:, columns] = state_ref[:, columns] * factor + term
        best_out_ref[:, columns] = best


def last_kernel(
    tile, which, active_ref, query_ref, own_in_ref, state_ref, best_ref, far_ref, out_ref,
    keys_ref, values_ref,
):
    head_dim, tokens = query_ref.shape
    slots, _, block = out_ref.shape
    part = tile // slots
    spread_pair(far_ref, keys_ref, values_ref)
    for at in range(tokens // tile):
        columns = pl.ds(at * tile, tile)
        scores = scores_of(keys_ref[...], query_ref[:, columns])
        on = active_ref[which] > 0
        _, factor, term = cross_update(on, scores, values_ref[...], best_ref[:, columns])
        cross = finish(state_ref[:, columns] * factor + term, head_dim)
        result = (own_in_ref[:, columns] + cross).astype(jnp.bfloat16)
        for n in range(slots):
            out_ref[n, :, at * part : (at + 1) * part] = result[:, n * part : (n + 1) * part]


ONES = 8


def call_attend(kernel, out_shape, scalars, arrays):
    head_dim, tokens = arrays[0].shape
    smem, vmem = pl.BlockSpec(memory_space=pltpu.SMEM), pl.BlockSpec(memory_space=pltpu.VMEM)
    several = isinstance(out_shape, list)
    return pl.pallas_call(
        kernel,
        out_shape=out_shape,
        in_specs=[smem] * len(scalars) + [vmem] * len(arrays),
        out_specs=[vmem] * len(out_shape) if several else vmem,
        scratch_shapes=[
            pltpu.VMEM((tokens, head_dim), jnp.bfloat16),
            pltpu.VMEM((head_dim + ONES, tokens), jnp.bfloat16),
        ],
        compiler_params=pltpu.CompilerParams(vmem_limit_bytes=24 << 20),
        cost_estimate=pl.CostEstimate(
            flops=4 * tokens * tokens * 256,
            bytes_accessed=4 * tokens * head_dim,
            transcendentals=tokens * tokens,
        ),
    )(*scalars, *arrays)


def attend_own(query, own):
    out_shape = jax.ShapeDtypeStruct(query.shape, jnp.float32)
    return call_attend(
        functools.partial(own_kernel, query.shape[1] // 2), out_shape, (), (query, own)
    )


def attend_middle(active, which, query, state, best, far):
    out_shape = [jax.ShapeDtypeStruct(array.shape, jnp.float32) for array in (state, best)]
    kernel = functools.partial(middle_kernel, query.shape[1] // 2, which)
    return call_attend(kernel, out_shape, (active,), (query, state, best, far))


def attend_last(active, which, query, own_result, state, best, far):
    head_dim, tokens = query.shape
    side = len(groups(0))
    out_shape = jax.ShapeDtypeStruct((side, head_dim, tokens // side), jnp.bfloat16)
    kernel = functools.partial(last_kernel, tokens // 2, which)
    return call_attend(kernel, out_shape, (active,), (query, own_result, state, best, far))


def groups(which):
    heads = lax.axis_size("head")
    side = math.isqrt(heads)
    table = [[side * i + j for j in range(side)] for i in range(side)]
    return table if which == 0 else [list(column) for column in zip(*table)]


def exchange(slots, which):
    return lax.all_to_all(
        slots, "head", split_axis=0, concat_axis=0, tiled=True, axis_index_groups=groups(which)
    )


def column_weights(weight):
    heads = lax.axis_size("head")
    side = len(groups(0))
    return [
        lax.ppermute(weight, "head", [((head + step * side) % heads, head) for head in range(heads)])
        for step in range(1, side)
    ]


def project_out_kernel(line_ref, parts_ref, *refs):
    weight_refs, out_ref = refs[:-1], refs[-1]
    side = len(weight_refs)
    total = None
    for step, weight_ref in enumerate(weight_refs):
        part = parts_ref[lax.rem(line_ref[0] + step, side)]
        term = lax.dot_general(
            part, weight_ref[...], (((0,), (0,)), ((), ())), preferred_element_type=jnp.float32
        )
        total = term if total is None else total + term
    blocks, loc_len, width = out_ref.shape
    half = loc_len // 2
    for n in range(2):
        part = total[n * blocks * half : (n + 1) * blocks * half].reshape(blocks, half, width)
        place = line_ref[1] if n == 0 else 1 - line_ref[1]
        place = pl.ds(pl.multiple_of(place * half, half), half)
        out_ref[:, place, :] = part.astype(jnp.bfloat16)


def project_out(parts, weights):
    side, head_dim, tokens = parts.shape
    width = weights[0].shape[1]
    core = lax.axis_index("view") % 2
    line = jnp.stack([lax.axis_index("head") // side, core]).astype(jnp.int32)
    smem, vmem = pl.BlockSpec(memory_space=pltpu.SMEM), pl.BlockSpec(memory_space=pltpu.VMEM)
    partial = pl.pallas_call(
        project_out_kernel,
        out_shape=jax.ShapeDtypeStruct((side, tokens // side, width), jnp.bfloat16),
        in_specs=[smem] + [vmem] * (1 + len(weights)),
        out_specs=vmem,
        compiler_params=pltpu.CompilerParams(vmem_limit_bytes=16 << 20),
        cost_estimate=pl.CostEstimate(
            flops=2 * parts.size * width, bytes_accessed=2 * (side * head_dim + tokens) * width, transcendentals=0
        ),
    )(line, parts, *weights)
    partial = partial.astype(jnp.float32) + partner(partial, 0).astype(jnp.float32)
    partial = exchange(partial.astype(jnp.bfloat16), 0).astype(jnp.float32)
    first = sum(partial[n] for n in range(0, side, 2))
    second = sum(partial[n] for n in range(1, side, 2))
    return jnp.where(core == 0, first, second).astype(jnp.bfloat16)


def on_device(latents, norm_gain, qkv_weight, qk_gain, out_weight, intersection):
    loc_len, view_dev, width = latents.shape
    rows = latents.reshape(loc_len, width)
    levels = lax.axis_size("view").bit_length() - 1
    rounds = intersection.shape[0]
    bits = [step * (levels - 1) // (rounds - 1) for step in range(rounds)]
    head_dim, heads = qk_gain.shape[-1], lax.axis_size("head")
    core = lax.axis_index("view") % 2
    same = core == lax.axis_index("head") % 2
    keep, give = normalize(core.astype(jnp.int32)[None], rows, norm_gain)
    pair, slots = pair_up(core.astype(jnp.int32)[None], keep, partner(give, 0), heads)
    parts, left = [], qk_gain[0]
    for _ in range(3):
        parts.append(lax.reduce_precision(left, 8, 7))
        left = left - parts[-1]
    small = jnp.concatenate(parts + [jnp.broadcast_to(intersection, (rounds, head_dim)).astype(jnp.float32)])
    small = jnp.pad(small, ((0, 16 - small.shape[0]), (0, width - head_dim))).astype(jnp.bfloat16)
    packed = jnp.concatenate([qkv_weight[0], out_weight[0], small], axis=0)
    packed, pair = lax.optimization_barrier((packed, pair))
    came = traded(packed)
    far_slots = deal(partner(pair, bits[-1]), heads)
    mine, far_slots, came = lax.optimization_barrier((gather_tokens(slots), far_slots, came))
    weight = jnp.where(same, qkv_weight[0], came[: 3 * head_dim])
    out_rows = jnp.where(same, out_weight[0], came[3 * head_dim : 4 * head_dim])
    small = jnp.where(same, small, came[4 * head_dim :])[:, :head_dim].astype(jnp.float32)
    gain = (small[0:2] + (small[2:4] + small[4:6])).T
    active = small[6 : 6 + rounds, 0].astype(jnp.int32)
    far_mine = gather_tokens(far_slots)
    query, own = project(mine, partner(mine, 0), weight, gain, True)
    middle, near = partner(own, bits[1]), beside(own)
    own_result, out_rows = lax.optimization_barrier((attend_own(query, own), out_rows))
    out_weights = [out_rows] + column_weights(out_rows)
    state = jnp.zeros((head_dim + ONES, query.shape[1]), jnp.float32)
    best = jnp.full((1, query.shape[1]), -BLANK, jnp.float32)
    state, best = attend_middle(active, 0, query, state, best, near)
    far_mine, own_result, state, best, middle, out_weights = lax.optimization_barrier(
        (far_mine, own_result, state, best, middle, out_weights)
    )
    far = project(far_mine, partner(far_mine, 0), weight, gain, False)
    state, best = attend_middle(active, rounds - 1, query, state, best, far)
    attended = attend_last(active, 1, query, own_result, state, best, middle)
    mixed = project_out(exchange(attended, 1), out_weights)
    return mixed.reshape(loc_len, view_dev, width)


def solution(mesh):
    placed = (
        P("head", "view", None),
        P(),
        P("head", None, None),
        P("head", None, None),
        P("head", None, None),
        P(None, "view"),
    )
    return jax.shard_map(
        on_device, mesh=mesh, in_specs=placed, out_specs=P("head", "view", None), check_vma=False
    )
```

time: 112 us -> 129 us (1.15)
  the two profiles are of different devices: /device:TPU:448 before, /device:TPU:128 now
where the time goes in v12:
time: 129 us; the launch traced here: 128 us
  starting transfers between devices  64.3 us (50%)
  waiting for transfers between devices  35.4 us (27%)
  Pallas kernels  19.4 us (15%)
  other arithmetic  5.51 us (4%)
  local copies, waits for them, and re-layouts  3.3 us (3%)
    ppermute x6, starting transfers between devices, partner(): lax.ppermute(array, 'view', [(i, i ^ 1 << bit) for i in range(lax.axis_si...  25.4 us
    ppermute x6, waiting for transfers between devices, partner(): lax.ppermute(array, 'view', [(i, i ^ 1 << bit) for i in range(lax.axis_si...  18.4 us
    all_to_all x2, waiting for transfers between devices, exchange(): lax.all_to_all(slots, 'head', split_axis=0, concat_axis=0, tiled=True, ax...  16.5 us
    all_to_all x2, starting transfers between devices, gather_tokens(): lax.all_to_all(slots, 'head', split_axis=0, concat_axis=0, tiled=True)  14.4 us
    ppermute x3, starting transfers between devices, column_weights(): lax.ppermute(weight, 'head', [((head + step * side) % heads, head) for he...  11.3 us
    pallas_call x4, Pallas kernels, call_attend(): pl.pallas_call(kernel, out_shape=out_shape, in_specs=[smem] * len(scalars...  10.7 us
    all_to_all x2, starting transfers between devices, exchange(): lax.all_to_all(slots, 'head', split_axis=0, concat_axis=0, tiled=True, ax...  7.89 us
    pallas_call x2, Pallas kernels, project(): pl.pallas_call(project_kernel if with_query else project_far_kernel, out_...  3.87 us
  transfers between devices with their start and end apart: 15, of which 6 were waited for; matrix products, arithmetic and copies ran while one was open for 4% of the time, Pallas kernels for 7%

profile of v12, /device:TPU:128, one launch (start us, length us, event | category | flops | bytes accessed | tf_op | source)
XLA Modules:
  0.0 128.3 jit_solution(8913032659609878942)
XLA Ops:
  1.2 1.9 %collective-permute-start = (bf16[32,1152]{1,0:T(8,128)(2,1)S(1)}, bf16[32,1152]{1,0:T(8,128)(2,1)S(1)}, u32[]{:S(2)}, u32[]{:S(2)}) collective-permute-start(bf16[32,1152]{1,0:T(8,128)(2,1)S(1)} %get-tuple-element.32), channel_id=1, source_target_pairs={{0,16},{16,0},{32,48},{48,32},{64,80},{80,64},{96,112},{112,96},{1... | collective-permute-start | bytes 221192 | tf_op jit(solution)/shard_map/ppermute | solution.py:14
  5.8 7.2 %all-to-all-start = ((bf16[16,32,1152]{2,1,0:T(8,128)(2,1)}), bf16[16,32,1152]{2,1,0:T(8,128)(2,1)S(1)}, u32[]{:S(2)}, u32[]{:S(2)}) async-start(bf16[16,32,1152]{2,1,0:T(8,128)(2,1)} %get-tuple-element.33), calls=%async_computation | async-start | bytes 2359296 | tf_op jit(solution)/shard_map/all_to_all | solution.py:123
  14.6 10.9 %collective-permute-start.1 = (bf16[2,32,1152]{2,1,0:T(8,128)(2,1)S(1)}, bf16[2,32,1152]{2,1,0:T(8,128)(2,1)S(1)}, u32[]{:S(2)}, u32[]{:S(2)}) collective-permute-start(bf16[2,32,1152]{2,1,0:T(8,128)(2,1)S(1)} %get-tuple-element.35), channel_id=1, source_target_pairs={{0,256},{16,272},{32,288},{48,304},{64,320},{80,336},{96,352},{112... | collective-permute-start | bytes 442376 | tf_op jit(solution)/shard_map/ppermute | solution.py:14
  25.5 13.6 %collective-permute-done.1.pair_ref = bf16[2,32,1152]{2,1,0:T(8,128)(2,1)S(1)} collective-permute-done((bf16[2,32,1152]{2,1,0:T(8,128)(2,1)S(1)}, bf16[2,32,1152]{2,1,0:T(8,128)(2,1)S(1)}, u32[]{:S(2)}, u32[]{:S(2)}) %collective-permute-start.1) | collective-permute-done | bytes 147488 | tf_op jit(solution)/shard_map/ppermute | solution.py:14
  40.3 2.3 %collective-permute-start.3 = (bf16[512,1152]{1,0:T(8,128)(2,1)S(1)}, bf16[512,1152]{1,0:T(8,128)(2,1)}, u32[]{:S(2)}, u32[]{:S(2)}) collective-permute-start(bf16[512,1152]{1,0:T(8,128)(2,1)S(1)} %bitcast.24), channel_id=1, source_target_pairs={{0,16},{16,0},{32,48},{48,32},{64,80},{80,64},{96,112},{112,96},{1... | collective-permute-start | bytes 3538952 | tf_op jit(solution)/shard_map/ppermute | solution.py:14
  42.6 7.2 %all-to-all-start.1 = ((bf16[16,32,1152]{2,1,0:T(8,128)(2,1)}), bf16[16,32,1152]{2,1,0:T(8,128)(2,1)S(1)}, u32[]{:S(2)}, u32[]{:S(2)}) async-start(bf16[16,32,1152]{2,1,0:T(8,128)(2,1)} %shard_map.66), calls=%async_computation.1 | async-start | bytes 2359296 | tf_op jit(solution)/shard_map/all_to_all | solution.py:123
  51.9 2.9 %shard_map.67 = (bf16[72,1024]{1,0:T(8,128)(2,1)S(1)}, bf16[144,1024]{1,0:T(8,128)(2,1)}) custom-call(bf16[512,1152]{1,0:T(8,128)(2,1)S(1)} %bitcast.25, bf16[512,1152]{1,0:T(8,128)(2,1)} %collective-permute-done.3.other_ref, bf16[216,1152]{1,0:T(8,128)(2,1)S(1)} %slice_select_fusion.weight_ref, f32[72,2]{1,0:T(8,128)S(1)} %copy.9.gain_ref), custom_call_target="tpu_custom_call" | custom-call | flops 25480396800 | bytes 2359296 | tf_op jit(solution)/shard_map/pallas_call | solution.py:166
  54.9 3.8 %collective-permute-start.4 = (bf16[144,1024]{1,0:T(8,128)(2,1)}, bf16[144,1024]{1,0:T(8,128)(2,1)S(1)}, u32[]{:S(2)}, u32[]{:S(2)}) collective-permute-start(bf16[144,1024]{1,0:T(8,128)(2,1)} %get-tuple-element.41.own_ref), channel_id=1, source_target_pairs={{0,1},{1,0},{2,3},{3,2},{4,5},{5,4},{6,7},{7,6},{8,9},{9,8},{10,11... | collective-permute-start | bytes 884744 | tf_op jit(solution)/shard_map/ppermute | solution.py:28
  59.6 6.4 %collective-permute-start.5 = (bf16[144,1024]{1,0:T(8,128)(2,1)}, bf16[144,1024]{1,0:T(8,128)(2,1)S(1)}, u32[]{:S(2)}, u32[]{:S(2)}) collective-permute-start(bf16[144,1024]{1,0:T(8,128)(2,1)} %get-tuple-element.41.own_ref), channel_id=1, source_target_pairs={{0,64},{16,80},{32,96},{48,112},{64,0},{80,16},{96,32},{112,48},{1... | collective-permute-start | bytes 884744 | tf_op jit(solution)/shard_map/ppermute | solution.py:14
  66.1 2.8 %shard_map.68.own_in_ref = f32[72,1024]{1,0:T(8,128)S(1)} custom-call(bf16[72,1024]{1,0:T(8,128)(2,1)S(1)} %get-tuple-element.39.query_ref, bf16[144,1024]{1,0:T(8,128)(2,1)} %get-tuple-element.41.own_ref), custom_call_target="tpu_custom_call" | custom-call | flops 1073741824 | bytes 294912 | tf_op jit(solution)/shard_map/pallas_call | solution.py:258
  68.9 3.4 %collective-permute-start.8 = (bf16[72,1152]{1,0:T(8,128)(2,1)S(1)}, bf16[72,1152]{1,0:T(8,128)(2,1)S(1)}, u32[]{:S(2)}, u32[]{:S(2)}) collective-permute-start(bf16[72,1152]{1,0:T(8,128)(2,1)S(1)} %slice_select_fusion.1.refs_0_), channel_id=1, source_target_pairs={{12,0},{13,1},{14,2},{15,3},{0,4},{1,5},{2,6},{3,7},{4,8},{5,9},{6... | collective-permute-start | bytes 497672 | tf_op jit(solution)/shard_map/ppermute | solution.py:314
  72.3 4.6 %collective-permute-start.7 = (bf16[72,1152]{1,0:T(8,128)(2,1)S(1)}, bf16[72,1152]{1,0:T(8,128)(2,1)S(1)}, u32[]{:S(2)}, u32[]{:S(2)}) collective-permute-start(bf16[72,1152]{1,0:T(8,128)(2,1)S(1)} %slice_select_fusion.1.refs_0_), channel_id=1, source_target_pairs={{8,0},{9,1},{10,2},{11,3},{12,4},{13,5},{14,6},{15,7},{0,8},{1,9},... | collective-permute-start | bytes 497672 | tf_op jit(solution)/shard_map/ppermute | solution.py:314
  76.9 3.4 %collective-permute-start.6 = (bf16[72,1152]{1,0:T(8,128)(2,1)S(1)}, bf16[72,1152]{1,0:T(8,128)(2,1)S(1)}, u32[]{:S(2)}, u32[]{:S(2)}) collective-permute-start(bf16[72,1152]{1,0:T(8,128)(2,1)S(1)} %slice_select_fusion.1.refs_0_), channel_id=1, source_target_pairs={{4,0},{5,1},{6,2},{7,3},{8,4},{9,5},{10,6},{11,7},{12,8},{13,9},{1... | collective-permute-start | bytes 497672 | tf_op jit(solution)/shard_map/ppermute | solution.py:314
  80.4 2.4 %shard_map.69 = (f32[80,1024]{1,0:T(8,128)S(1)}, f32[1,1024]{1,0:T(1,128)S(1)}) custom-call(s32[3]{0:T(128)S(1)} %fusion.4.active_ref, bf16[72,1024]{1,0:T(8,128)(2,1)S(1)} %get-tuple-element.39.query_ref, f32[80,1024]{1,0:T(8,128)S(1)} %broadcast_in_dim.14.state_ref, f32[1,1024]{1,0:T(1,128)S(1)} %broadcast_in_dim.15.best_ref, ...), custom_call_target="tpu_custom_call" | custom-call | flops 1073741824 | bytes 294912 | tf_op jit(solution)/shard_map/pallas_call | solution.py:258
  84.9 1.9 %collective-permute-start.9 = (bf16[512,1152]{1,0:T(8,128)(2,1)S(1)}, bf16[512,1152]{1,0:T(8,128)(2,1)S(1)}, u32[]{:S(2)}, u32[]{:S(2)}) collective-permute-start(bf16[512,1152]{1,0:T(8,128)(2,1)S(1)} %bitcast.22), channel_id=1, source_target_pairs={{0,16},{16,0},{32,48},{48,32},{64,80},{80,64},{96,112},{112,96},{1... | collective-permute-start | bytes 3538952 | tf_op jit(solution)/shard_map/ppermute | solution.py:14
  86.8 2.8 %collective-permute-done.9.other_ref = bf16[512,1152]{1,0:T(8,128)(2,1)S(1)} collective-permute-done((bf16[512,1152]{1,0:T(8,128)(2,1)S(1)}, bf16[512,1152]{1,0:T(8,128)(2,1)S(1)}, u32[]{:S(2)}, u32[]{:S(2)}) %collective-permute-start.9) | collective-permute-done | bytes 1179680 | tf_op jit(solution)/shard_map/ppermute | solution.py:14
  91.4 2.4 %shard_map.71 = (f32[80,1024]{1,0:T(8,128)S(1)}, f32[1,1024]{1,0:T(1,128)S(1)}) custom-call(s32[3]{0:T(128)S(1)} %fusion.4.active_ref, bf16[72,1024]{1,0:T(8,128)(2,1)S(1)} %copy-done.9, f32[80,1024]{1,0:T(8,128)S(1)} %copy-done.7, f32[1,1024]{1,0:T(1,128)S(1)} %get-tuple-element.48.best_ref, bf16[144,1024]{1,0:T(8,128)(2,1)S(1)} %shard_map.70.far_ref), custom_call_target="tpu_custom_call" | custom-call | flops 1073741824 | bytes 294912 | tf_op jit(solution)/shard_map/pallas_call | solution.py:258
  93.8 3.0 %shard_map.72 = bf16[4,72,256]{2,1,0:T(8,128)(2,1)} custom-call(s32[3]{0:T(128)S(1)} %fusion.4.active_ref, bf16[72,1024]{1,0:T(8,128)(2,1)S(1)} %copy-done.9, f32[72,1024]{1,0:T(8,128)S(1)} %copy-done.5, f32[80,1024]{1,0:T(8,128)S(1)} %get-tuple-element.50.state_ref, f32[1,1024]{1,0:T(1,128)S(1)} %get-tuple-element.51.best_ref, bf16[144,1024]{1,0:T(8,128)(2,1)S(1)} %copy-done.3), custom_call_target="tpu_custom_call" | custom-call | flops 1073741824 | bytes 294912 | tf_op jit(solution)/shard_map/pallas_call | solution.py:258
  96.8 3.9 %all-to-all-start.2 = ((bf16[4,72,256]{2,1,0:T(8,128)(2,1)}), bf16[4,72,256]{2,1,0:T(8,128)(2,1)S(1)}, u32[]{:S(2)}, u32[]{:S(2)}) async-start(bf16[4,72,256]{2,1,0:T(8,128)(2,1)} %shard_map.72), calls=%async_computation.2 | async-start | bytes 294912 | tf_op jit(solution)/shard_map/all_to_all | solution.py:305
  100.9 6.0 %all-to-all-done.2.parts_ref = bf16[4,72,256]{2,1,0:T(8,128)(2,1)S(1)} async-done(((bf16[4,72,256]{2,1,0:T(8,128)(2,1)}), bf16[4,72,256]{2,1,0:T(8,128)(2,1)S(1)}, u32[]{:S(2)}, u32[]{:S(2)}) %all-to-all-start.2) | async-done | bytes 147488 | tf_op jit(solution)/shard_map/all_to_all | solution.py:305
  108.2 1.9 %collective-permute-start.10 = (bf16[4,64,1152]{2,1,0:T(8,128)(2,1)S(1)}, bf16[4,64,1152]{2,1,0:T(8,128)(2,1)S(1)}, u32[]{:S(2)}, u32[]{:S(2)}) collective-permute-start(bf16[4,64,1152]{2,1,0:T(8,128)(2,1)S(1)} %shard_map.73), channel_id=1, source_target_pairs={{0,16},{16,0},{32,48},{48,32},{64,80},{80,64},{96,112},{112,96},{1... | collective-permute-start | bytes 1769480 | tf_op jit(solution)/shard_map/ppermute | solution.py:14
  110.1 2.0 %collective-permute-done.10 = bf16[4,64,1152]{2,1,0:T(8,128)(2,1)S(1)} collective-permute-done((bf16[4,64,1152]{2,1,0:T(8,128)(2,1)S(1)}, bf16[4,64,1152]{2,1,0:T(8,128)(2,1)S(1)}, u32[]{:S(2)}, u32[]{:S(2)}) %collective-permute-start.10) | collective-permute-done | bytes 589856 | tf_op jit(solution)/shard_map/ppermute | solution.py:14
  113.1 3.9 %all-to-all-start.3 = ((bf16[4,64,1152]{2,1,0:T(8,128)(2,1)}), bf16[4,64,1152]{2,1,0:T(8,128)(2,1)S(1)}, u32[]{:S(2)}, u32[]{:S(2)}) async-start(bf16[4,64,1152]{2,1,0:T(8,128)(2,1)} %add_convert_fusion), calls=%async_computation.3 | async-start | bytes 1179648 | tf_op jit(solution)/shard_map/all_to_all | solution.py:305
  117.0 10.5 %all-to-all-done.3 = bf16[4,64,1152]{2,1,0:T(8,128)(2,1)S(1)} async-done(((bf16[4,64,1152]{2,1,0:T(8,128)(2,1)}), bf16[4,64,1152]{2,1,0:T(8,128)(2,1)S(1)}, u32[]{:S(2)}, u32[]{:S(2)}) %all-to-all-start.3) | async-done | bytes 589856 | tf_op jit(solution)/shard_map/all_to_all | solution.py:305
  (61 shorter events, 16.7 us)
Async XLA Ops:
  1.2 3.4 %collective-permute-start = (bf16[32,1152]{1,0:T(8,128)(2,1)S(1)}, bf16[32,1152]{1,0:T(8,128)(2,1)S(1)}, u32[]{:S(2)}, u32[]{:S(2)}) collective-permute-start(bf16[32,1152]{1,0:T(8,128)(2,1)S(1)} %get-tuple-element.32), channel_id=1, source_target_pairs={{0,16},{16,0},{32,48},{48,32},{64,80},{80,64},{96,112},{112,96},{1... | collective-permute-start | bytes 221192 | tf_op jit(solution)/shard_map/ppermute | solution.py:14
  5.7 7.3 %copy-start.10 = (bf16[1,216,1152]{2,1,0:T(8,128)(2,1)S(1)}, bf16[1,216,1152]{2,1,0:T(8,128)(2,1)}, u32[]{:S(2)}) copy-start(bf16[1,216,1152]{2,1,0:T(8,128)(2,1)} %param.8) | copy-start | bytes 1492996
  5.7 7.3 %copy-start.11 = (bf16[1,72,1152]{2,1,0:T(8,128)(2,1)S(1)}, bf16[1,72,1152]{2,1,0:T(8,128)(2,1)}, u32[]{:S(2)}) copy-start(bf16[1,72,1152]{2,1,0:T(8,128)(2,1)} %param.10) | copy-start | bytes 497668
  5.8 34.6 %all-to-all-start = ((bf16[16,32,1152]{2,1,0:T(8,128)(2,1)}), bf16[16,32,1152]{2,1,0:T(8,128)(2,1)S(1)}, u32[]{:S(2)}, u32[]{:S(2)}) async-start(bf16[16,32,1152]{2,1,0:T(8,128)(2,1)} %get-tuple-element.33), calls=%async_computation | async-start | bytes 2359296 | tf_op jit(solution)/shard_map/all_to_all | solution.py:123
  13.1 27.2 %collective-permute-start.2 = (bf16[304,1152]{1,0:T(8,128)(2,1)S(1)}, bf16[304,1152]{1,0:T(8,128)(2,1)}, u32[]{:S(2)}, u32[]{:S(2)}) collective-permute-start(bf16[304,1152]{1,0:T(8,128)(2,1)S(1)} %pad_maximum_fusion), channel_id=1, source_target_pairs={{16,1},{18,3},{20,5},{22,7},{24,9},{26,11},{28,13},{30,15},{1,16},... | collective-permute-start | bytes 2101256 | tf_op jit(solution)/shard_map/ppermute | solution.py:24
  14.6 24.5 %collective-permute-start.1 = (bf16[2,32,1152]{2,1,0:T(8,128)(2,1)S(1)}, bf16[2,32,1152]{2,1,0:T(8,128)(2,1)S(1)}, u32[]{:S(2)}, u32[]{:S(2)}) collective-permute-start(bf16[2,32,1152]{2,1,0:T(8,128)(2,1)S(1)} %get-tuple-element.35), channel_id=1, source_target_pairs={{0,256},{16,272},{32,288},{48,304},{64,320},{80,336},{96,352},{112... | collective-permute-start | bytes 442376 | tf_op jit(solution)/shard_map/ppermute | solution.py:14
  40.3 11.6 %collective-permute-start.3 = (bf16[512,1152]{1,0:T(8,128)(2,1)S(1)}, bf16[512,1152]{1,0:T(8,128)(2,1)}, u32[]{:S(2)}, u32[]{:S(2)}) collective-permute-start(bf16[512,1152]{1,0:T(8,128)(2,1)S(1)} %bitcast.24), channel_id=1, source_target_pairs={{0,16},{16,0},{32,48},{48,32},{64,80},{80,64},{96,112},{112,96},{1... | collective-permute-start | bytes 3538952 | tf_op jit(solution)/shard_map/ppermute | solution.py:14
  42.6 41.0 %all-to-all-start.1 = ((bf16[16,32,1152]{2,1,0:T(8,128)(2,1)}), bf16[16,32,1152]{2,1,0:T(8,128)(2,1)S(1)}, u32[]{:S(2)}, u32[]{:S(2)}) async-start(bf16[16,32,1152]{2,1,0:T(8,128)(2,1)} %shard_map.66), calls=%async_computation.1 | async-start | bytes 2359296 | tf_op jit(solution)/shard_map/all_to_all | solution.py:123
  50.8 4.1 %copy-start = (f32[72,2]{1,0:T(8,128)}, f32[72,2]{1,0:T(8,128)S(1)}, u32[]{:S(2)}) copy-start(f32[72,2]{1,0:T(8,128)S(1)} %copy.9.gain_ref) | copy-start | bytes 1732
  51.9 6.8 %copy-start.12 = (bf16[1,72,1152]{2,1,0:T(8,128)(2,1)S(1)}, bf16[1,72,1152]{2,1,0:T(8,128)(2,1)}, u32[]{:S(2)}) copy-start(bf16[1,72,1152]{2,1,0:T(8,128)(2,1)} %param.10) | copy-start | bytes 497668
  54.9 25.6 %copy-start.8 = (bf16[72,1024]{1,0:T(8,128)(2,1)}, bf16[72,1024]{1,0:T(8,128)(2,1)S(1)}, u32[]{:S(2)}) copy-start(bf16[72,1024]{1,0:T(8,128)(2,1)S(1)} %get-tuple-element.39.query_ref) | copy-start | bytes 442372
  54.9 25.5 %collective-permute-start.4 = (bf16[144,1024]{1,0:T(8,128)(2,1)}, bf16[144,1024]{1,0:T(8,128)(2,1)S(1)}, u32[]{:S(2)}, u32[]{:S(2)}) collective-permute-start(bf16[144,1024]{1,0:T(8,128)(2,1)} %get-tuple-element.41.own_ref), channel_id=1, source_target_pairs={{0,1},{1,0},{2,3},{3,2},{4,5},{5,4},{6,7},{7,6},{8,9},{9,8},{10,11... | collective-permute-start | bytes 884744 | tf_op jit(solution)/shard_map/ppermute | solution.py:28
  59.6 24.5 %collective-permute-start.5 = (bf16[144,1024]{1,0:T(8,128)(2,1)}, bf16[144,1024]{1,0:T(8,128)(2,1)S(1)}, u32[]{:S(2)}, u32[]{:S(2)}) collective-permute-start(bf16[144,1024]{1,0:T(8,128)(2,1)} %get-tuple-element.41.own_ref), channel_id=1, source_target_pairs={{0,64},{16,80},{32,96},{48,112},{64,0},{80,16},{96,32},{112,48},{1... | collective-permute-start | bytes 884744 | tf_op jit(solution)/shard_map/ppermute | solution.py:14
  68.9 13.9 %copy-start.4 = (f32[72,1024]{1,0:T(8,128)}, f32[72,1024]{1,0:T(8,128)S(1)}, u32[]{:S(2)}) copy-start(f32[72,1024]{1,0:T(8,128)S(1)} %shard_map.68.own_in_ref) | copy-start | bytes 884740
  68.9 14.7 %collective-permute-start.8 = (bf16[72,1152]{1,0:T(8,128)(2,1)S(1)}, bf16[72,1152]{1,0:T(8,128)(2,1)S(1)}, u32[]{:S(2)}, u32[]{:S(2)}) collective-permute-start(bf16[72,1152]{1,0:T(8,128)(2,1)S(1)} %slice_select_fusion.1.refs_0_), channel_id=1, source_target_pairs={{12,0},{13,1},{14,2},{15,3},{0,4},{1,5},{2,6},{3,7},{4,8},{5,9},{6... | collective-permute-start | bytes 497672 | tf_op jit(solution)/shard_map/ppermute | solution.py:314
  72.3 11.3 %collective-permute-start.7 = (bf16[72,1152]{1,0:T(8,128)(2,1)S(1)}, bf16[72,1152]{1,0:T(8,128)(2,1)S(1)}, u32[]{:S(2)}, u32[]{:S(2)}) collective-permute-start(bf16[72,1152]{1,0:T(8,128)(2,1)S(1)} %slice_select_fusion.1.refs_0_), channel_id=1, source_target_pairs={{8,0},{9,1},{10,2},{11,3},{12,4},{13,5},{14,6},{15,7},{0,8},{1,9},... | collective-permute-start | bytes 497672 | tf_op jit(solution)/shard_map/ppermute | solution.py:314
  76.9 7.2 %collective-permute-start.6 = (bf16[72,1152]{1,0:T(8,128)(2,1)S(1)}, bf16[72,1152]{1,0:T(8,128)(2,1)S(1)}, u32[]{:S(2)}, u32[]{:S(2)}) collective-permute-start(bf16[72,1152]{1,0:T(8,128)(2,1)S(1)} %slice_select_fusion.1.refs_0_), channel_id=1, source_target_pairs={{4,0},{5,1},{6,2},{7,3},{8,4},{9,5},{10,6},{11,7},{12,8},{13,9},{1... | collective-permute-start | bytes 497672 | tf_op jit(solution)/shard_map/ppermute | solution.py:314
  84.9 4.7 %collective-permute-start.9 = (bf16[512,1152]{1,0:T(8,128)(2,1)S(1)}, bf16[512,1152]{1,0:T(8,128)(2,1)S(1)}, u32[]{:S(2)}, u32[]{:S(2)}) collective-permute-start(bf16[512,1152]{1,0:T(8,128)(2,1)S(1)} %bitcast.22), channel_id=1, source_target_pairs={{0,16},{16,0},{32,48},{48,32},{64,80},{80,64},{96,112},{112,96},{1... | collective-permute-start | bytes 3538952 | tf_op jit(solution)/shard_map/ppermute | solution.py:14
  90.4 1.0 copy-start.9
  91.4 2.4 %copy-start.3 = (bf16[144,1024]{1,0:T(8,128)(2,1)S(1)}, bf16[144,1024]{1,0:T(8,128)(2,1)}, u32[]{:S(2)}) copy-start(bf16[144,1024]{1,0:T(8,128)(2,1)} %copy-done.2) | copy-start | bytes 884740
  91.4 2.4 %copy-start.5 = (f32[72,1024]{1,0:T(8,128)S(1)}, f32[72,1024]{1,0:T(8,128)}, u32[]{:S(2)}) copy-start(f32[72,1024]{1,0:T(8,128)} %copy-done.4) | copy-start | bytes 884740
  96.8 10.0 %all-to-all-start.2 = ((bf16[4,72,256]{2,1,0:T(8,128)(2,1)}), bf16[4,72,256]{2,1,0:T(8,128)(2,1)S(1)}, u32[]{:S(2)}, u32[]{:S(2)}) async-start(bf16[4,72,256]{2,1,0:T(8,128)(2,1)} %shard_map.72), calls=%async_computation.2 | async-start | bytes 294912 | tf_op jit(solution)/shard_map/all_to_all | solution.py:305
  108.2 3.9 %collective-permute-start.10 = (bf16[4,64,1152]{2,1,0:T(8,128)(2,1)S(1)}, bf16[4,64,1152]{2,1,0:T(8,128)(2,1)S(1)}, u32[]{:S(2)}, u32[]{:S(2)}) collective-permute-start(bf16[4,64,1152]{2,1,0:T(8,128)(2,1)S(1)} %shard_map.73), channel_id=1, source_target_pairs={{0,16},{16,0},{32,48},{48,32},{64,80},{80,64},{96,112},{112,96},{1... | collective-permute-start | bytes 1769480 | tf_op jit(solution)/shard_map/ppermute | solution.py:14
  113.1 14.4 %all-to-all-start.3 = ((bf16[4,64,1152]{2,1,0:T(8,128)(2,1)}), bf16[4,64,1152]{2,1,0:T(8,128)(2,1)S(1)}, u32[]{:S(2)}, u32[]{:S(2)}) async-start(bf16[4,64,1152]{2,1,0:T(8,128)(2,1)} %add_convert_fusion), calls=%async_computation.3 | async-start | bytes 1179648 | tf_op jit(solution)/shard_map/all_to_all | solution.py:305
  (4 other events, 3.2 us)

commit v13 on v11

--- a/solution.py
+++ b/solution.py
@@ -101,27 +101,6 @@
     pair_ref[...] = pair.astype(jnp.bfloat16)
 
 
-def project_far_kernel(rows_ref, weight_ref, gain_ref, pair_ref, held_ref, sems):
-    head_dim = gain_ref.shape[0]
-    skip = head_dim // 16 * 16
-    blocks, block = held_ref.shape[:2]
-    copies = [
-        pltpu.make_async_copy(rows_ref.at[pl.ds(n * block, block)], held_ref.at[n], sems.at[n])
-        for n in range(blocks)
-    ]
-    for copy in copies:
-        copy.start()
-    for n in range(blocks):
-        copies[n].wait()
-        flat = lax.dot_general(
-            weight_ref[skip:], held_ref[n], (((1,), (1,)), ((), ())), preferred_element_type=jnp.float32
-        )
-        flat = flat[head_dim - skip :].astype(jnp.bfloat16).astype(jnp.float32)
-        keys = rms_rows(flat[:head_dim], gain_ref[:, 1:2])
-        pair = jnp.concatenate([keys, flat[head_dim:]], axis=0)
-        pair_ref[:, pl.ds(n * block, block)] = pair.astype(jnp.bfloat16)
-
-
 def project(rows, weight, gain):
     tokens, width = rows.shape
     head_dim = gain.shape[0]
@@ -138,26 +117,67 @@
     )(rows, weight, gain)
 
 
-def project_far(rows, weight, gain):
-    tokens, width = rows.shape
-    head_dim = gain.shape[0]
-    blocks = 2
-    vmem = pl.BlockSpec(memory_space=pltpu.VMEM)
-    rows = pltpu.with_memory_space_constraint(rows, pltpu.HBM)
+def project_far_kernel(place_ref, rows_ref, weight_ref, mine_ref, other_ref, out_ref):
+    tokens = rows_ref[...]
+    wide = out_ref.shape[1]
+    size = mine_ref.shape[0] - COLUMN
+    start = weight_ref.shape[0] - wide
+    even = start // 16 * 16
+
+    def product(rows):
+        return lax.dot_general(
+            rows, tokens, (((1,), (1,)), ((), ())), preferred_element_type=jnp.float32
+        )
+
+    own = product(weight_ref[even:])[start - even :]
+    skip = size - PAD - wide
+    mine, other = product(mine_ref[COLUMN - size : COLUMN]), product(other_ref[COLUMN - size : COLUMN])
+    first, second = product(mine_ref[COLUMN:]), product(other_ref[COLUMN:])
+    far = jnp.where(place_ref[4] == 0, second, first)
+    out_ref[place_ref[0]] = own.astype(jnp.bfloat16)
+    for n, flat in enumerate((mine, other, far)):
+        out_ref[place_ref[1 + n]] = flat[skip : skip + wide].astype(jnp.bfloat16)
+
+
+PAD = 8
+COLUMN = 304
+
+
+def project_far(place, rows, weight, mine, other, head_dim):
+    side = len(groups(0))
+    smem, vmem = pl.BlockSpec(memory_space=pltpu.SMEM), pl.BlockSpec(memory_space=pltpu.VMEM)
     return pl.pallas_call(
         project_far_kernel,
-        out_shape=jax.ShapeDtypeStruct((2 * head_dim, tokens), jnp.bfloat16),
-        in_specs=[pl.BlockSpec(memory_space=pltpu.HBM), vmem, vmem],
+        out_shape=jax.ShapeDtypeStruct((side, 2 * head_dim, rows.shape[0]), jnp.bfloat16),
+        in_specs=[smem] + [vmem] * 4,
         out_specs=vmem,
-        scratch_shapes=[
-            pltpu.VMEM((blocks, tokens // blocks, width), jnp.bfloat16),
-            pltpu.SemaphoreType.DMA((blocks,)),
-        ],
-        compiler_params=pltpu.CompilerParams(vmem_limit_bytes=20 << 20),
-        cost_estimate=pl.CostEstimate(
-            flops=2 * tokens * width * weight.shape[0], bytes_accessed=2 * tokens * width, transcendentals=0
-        ),
-    )(rows, weight, gain)
+        compiler_params=pltpu.CompilerParams(vmem_limit_bytes=16 << 20),
+        cost_estimate=pl.CostEstimate(
+            flops=2 * side * rows.size * weight.shape[0], bytes_accessed=4 * rows.size, transcendentals=0
+        ),
+    )(place, rows, weight, mine, other)
+
+
+def settle_kernel(parts_ref, gain_ref, pair_ref):
+    head_dim = gain_ref.shape[0]
+    blocks, _, tokens = parts_ref.shape
+    for n in range(blocks):
+        flat = parts_ref[n].astype(jnp.float32)
+        keys = rms_rows(flat[:head_dim], gain_ref[:, 1:2])
+        pair = jnp.concatenate([keys, flat[head_dim:]], axis=0)
+        pair_ref[:, pl.ds(n * tokens, tokens)] = pair.astype(jnp.bfloat16)
+
+
+def settle(parts, gain):
+    blocks, wide, tokens = parts.shape
+    return pl.pallas_call(
+        settle_kernel,
+        out_shape=jax.ShapeDtypeStruct((wide, blocks * tokens), jnp.bfloat16),
+        compiler_params=pltpu.CompilerParams(vmem_limit_bytes=16 << 20),
+        cost_estimate=pl.CostEstimate(
+            flops=8 * parts.size, bytes_accessed=4 * parts.size, transcendentals=0
+        ),
+    )(parts, gain)
 
 
 def spread_pair(pair_ref, keys_ref, values_ref):
@@ -303,43 +323,56 @@
     )
 
 
-def column_weights(weight):
-    heads = lax.axis_size("head")
+def column_weights(weight, out_weight):
+    views, heads = lax.axis_size("view"), lax.axis_size("head")
     side = len(groups(0))
-    return [
-        lax.ppermute(weight, "head", [((head + step * side) % heads, head) for head in range(heads)])
-        for step in range(1, side)
-    ]
-
-
-def project_out_kernel(line_ref, parts_ref, *refs):
-    weight_refs, out_ref = refs[:-1], refs[-1]
-    side = len(weight_refs)
+    core = lax.axis_index("view") % 2
+    blank = jnp.zeros((PAD, weight.shape[1]), weight.dtype)
+    packed = jnp.concatenate([out_weight, blank, weight, blank], axis=0)
+    part = (COLUMN // 2 + 15) // 16 * 16
+    pairs = []
+    for view in range(views):
+        step = side if view % 2 == 0 else -side
+        for head in range(heads):
+            pairs.append((view * heads + (head + step) % heads, view * heads + head))
+    beside = lax.ppermute(packed, ("view", "head"), pairs)
+    sent = jnp.where(core == 0, packed[:part], packed[COLUMN - part :])
+    across = [(head, (head + heads // 2) % heads) for head in range(heads)]
+    return jnp.concatenate([beside, lax.ppermute(sent, "head", across)], axis=0)
+
+
+def project_out_kernel(place_ref, parts_ref, weight_ref, mine_ref, other_ref, out_ref):
+    head_dim = weight_ref.shape[0]
+
+    def rows_at(ref, start):
+        return ref[start : start + head_dim + PAD].astype(jnp.float32)[:head_dim]
+
+    first, second = rows_at(mine_ref, COLUMN), rows_at(other_ref, COLUMN)
+    far = jnp.where(place_ref[4] == 0, first, second)
+    weights = [rows_at(mine_ref, 0), rows_at(other_ref, 0), far]
     total = None
-    for step, weight_ref in enumerate(weight_refs):
-        part = parts_ref[lax.rem(line_ref[0] + step, side)]
+    for n, weight in enumerate([weight_ref[...]] + [rows.astype(jnp.bfloat16) for rows in weights]):
         term = lax.dot_general(
-            part, weight_ref[...], (((0,), (0,)), ((), ())), preferred_element_type=jnp.float32
+            parts_ref[place_ref[n]], weight, (((0,), (0,)), ((), ())), preferred_element_type=jnp.float32
         )
         total = term if total is None else total + term
     out_ref[...] = total.reshape(out_ref.shape).astype(jnp.bfloat16)
 
 
-def project_out(parts, weights):
+def project_out(place, parts, weight, mine, other):
     side, head_dim, tokens = parts.shape
-    width = weights[0].shape[1]
-    line = (lax.axis_index("head") // side).astype(jnp.int32)[None]
+    width = weight.shape[1]
     smem, vmem = pl.BlockSpec(memory_space=pltpu.SMEM), pl.BlockSpec(memory_space=pltpu.VMEM)
     partial = pl.pallas_call(
         project_out_kernel,
         out_shape=jax.ShapeDtypeStruct((side, tokens // side, width), jnp.bfloat16),
-        in_specs=[smem] + [vmem] * (1 + len(weights)),
+        in_specs=[smem] + [vmem] * 4,
         out_specs=vmem,
         compiler_params=pltpu.CompilerParams(vmem_limit_bytes=16 << 20),
         cost_estimate=pl.CostEstimate(
             flops=2 * parts.size * width, bytes_accessed=2 * (side * head_dim + tokens) * width, transcendentals=0
         ),
-    )(line, parts, *weights)
+    )(place, parts, weight, mine, other)
     partial = exchange(partial, 0)
     return jnp.sum(partial.astype(jnp.float32), axis=0).astype(jnp.bfloat16)
 
@@ -356,22 +389,29 @@
     active = intersection[:, 0]
     heads = lax.axis_size("head")
     normed, slots = normalize(rows, norm_gain, heads)
-    far_normed, gain, active = lax.optimization_barrier((partner(normed, bits[-1]), gain, active))
-    far_slots = copies_of(far_normed, heads)
+    core, side = lax.axis_index("view") % 2, len(groups(0))
+    line = lax.axis_index("head") // side
+    turn = jnp.where(core == 0, 1, side - 1)
+    place = jnp.stack([line, line + turn, line + side - turn, line + side // 2]) % side
+    place = jnp.concatenate([place, core[None]]).astype(jnp.int32)
+    far_normed, mine, gain, active = lax.optimization_barrier(
+        (partner(normed, bits[-1]), column_weights(weight, out_weight[0]), gain, active)
+    )
+    far_slots = copies_of(far_normed, side)
     every, far_slots = lax.optimization_barrier((gather_tokens(slots), far_slots))
-    far_every = gather_tokens(far_slots)
+    far_tokens = exchange(far_slots, 0).reshape(-1, width)
     query, own = project(every, weight, gain)
     near = [partner(own, bit) for bit in bits[:-1]]
-    near[0], out_rows = lax.optimization_barrier((near[0], out_weight[0]))
-    out_weights = [out_weight[0]] + column_weights(out_rows)
+    other = partner(mine, 0)
+    far_parts = project_far(place, far_tokens, weight, mine, other, head_dim)
+    far_parts = exchange(far_parts, 1)
     own_result, state, best = attend_near(active, query, own, near[0])
-    state, best = attend_middle(active, 1, query, state, best, near[1])
-    far_every, own_result, state, best = lax.optimization_barrier(
-        (far_every, own_result, state, best)
-    )
-    far = project_far(far_every, weight, gain)
-    attended = attend_last(active, rounds - 1, query, own_result, state, best, far)
-    mixed = project_out(exchange(attended, 1), out_weights)
+    far_parts, own_result, state, best, near[1] = lax.optimization_barrier(
+        (far_parts, own_result, state, best, near[1])
+    )
+    state, best = attend_middle(active, rounds - 1, query, state, best, settle(far_parts, gain))
+    attended = attend_last(active, 1, query, own_result, state, best, near[1])
+    mixed = project_out(place, exchange(attended, 1), out_weight[0], mine, other)
     return mixed.reshape(loc_len, view_dev, width)
 
 

time: 112 us -> 121 us (1.080)
  the two profiles are of different devices: /device:TPU:448 before, /device:TPU:32 now
where the time goes in v13:
time: 121 us; the launch traced here: 120 us
  starting transfers between devices  52.6 us (43%)
  blocking collectives  21.6 us (18%)
  Pallas kernels  21.4 us (18%)
  waiting for transfers between devices  17.7 us (15%)
  local copies, waits for them, and re-layouts  3.6 us (3%)
  other arithmetic  3.23 us (3%)
    ppermute x4, starting transfers between devices, partner(): lax.ppermute(array, 'view', [(i, i ^ 1 << bit) for i in range(lax.axis_si...  29.7 us
    all_to_all x2, blocking collectives, exchange(): lax.all_to_all(slots, 'head', split_axis=0, concat_axis=0, tiled=True, ax...  21.6 us
    ppermute x1, waiting for transfers between devices, column_weights(): return jnp.concatenate([beside, lax.ppermute(sent, 'head', across)], axis=0)  14.6 us
    pallas_call x3, Pallas kernels, call_attend(): pl.pallas_call(kernel, out_shape=out_shape, in_specs=[smem] + [vmem] * (l...  9.27 us
    all_to_all x2, starting transfers between devices, exchange(): lax.all_to_all(slots, 'head', split_axis=0, concat_axis=0, tiled=True, ax...  7.92 us
    all_to_all x1, starting transfers between devices, gather_tokens(): lax.all_to_all(slots, 'head', split_axis=0, concat_axis=0, tiled=True)  7.18 us
    ppermute x1, starting transfers between devices, column_weights(): beside = lax.ppermute(packed, ('view', 'head'), pairs)  5.03 us
    unnamed x21, local copies, waits for them, and re-layouts  3.6 us
  transfers between devices with their start and end apart: 9, of which 3 were waited for; matrix products, arithmetic and copies ran while one was open for 2% of the time, Pallas kernels for 9%

profile of v13, /device:TPU:32, one launch (start us, length us, event | category | flops | bytes accessed | tf_op | source)
XLA Modules:
  0.0 120.4 jit_solution(7889588550486711732)
XLA Ops:
  0.0 3.4 %shard_map.64 = (bf16[64,1152]{1,0:T(8,128)(2,1)}, bf16[16,64,1152]{2,1,0:T(8,128)(2,1)}) custom-call(bf16[64,1152]{1,0:T(8,128)(2,1)} %bitcast.28, f32[1152]{0:T(1024)} %gain_ref.1), custom_call_target="tpu_custom_call" | custom-call | flops 589824 | bytes 2359296 | tf_op jit(solution)/shard_map/pallas_call | solution.py:49
  3.4 7.2 %all-to-all-start = ((bf16[16,64,1152]{2,1,0:T(8,128)(2,1)}), bf16[16,64,1152]{2,1,0:T(8,128)(2,1)S(1)}, u32[]{:S(2)}, u32[]{:S(2)}) async-start(bf16[16,64,1152]{2,1,0:T(8,128)(2,1)} %get-tuple-element.27), calls=%async_computation | async-start | bytes 4718592 | tf_op jit(solution)/shard_map/all_to_all | solution.py:83
  11.6 5.0 %collective-permute-start.1 = (bf16[304,1152]{1,0:T(8,128)(2,1)}, bf16[304,1152]{1,0:T(8,128)(2,1)}, u32[]{:S(2)}, u32[]{:S(2)}) collective-permute-start(bf16[304,1152]{1,0:T(8,128)(2,1)} %pad_maximum_fusion.1), channel_id=1, source_target_pairs={{4,0},{5,1},{6,2},{7,3},{8,4},{9,5},{10,6},{11,7},{12,8},{13,9},{1... | collective-permute-start | bytes 2101256 | tf_op jit(solution)/shard_map/ppermute | solution.py:338
  16.7 2.8 %collective-permute-start.2 = (bf16[160,1152]{1,0:T(8,128)(2,1)S(1)}, bf16[160,1152]{1,0:T(8,128)(2,1)S(1)}, u32[]{:S(2)}, u32[]{:S(2)}) collective-permute-start(bf16[160,1152]{1,0:T(8,128)(2,1)S(1)} %fusion), channel_id=1, source_target_pairs={{0,8},{1,9},{2,10},{3,11},{4,12},{5,13},{6,14},{7,15},{8,0},{9,1},... | collective-permute-start | bytes 1105928 | tf_op jit(solution)/shard_map/ppermute | solution.py:341
  19.5 14.8 %collective-permute-start = (bf16[64,1152]{1,0:T(8,128)(2,1)}, bf16[64,1152]{1,0:T(8,128)(2,1)}, u32[]{:S(2)}, u32[]{:S(2)}) collective-permute-start(bf16[64,1152]{1,0:T(8,128)(2,1)} %get-tuple-element.25), channel_id=1, source_target_pairs={{0,256},{16,272},{32,288},{48,304},{64,320},{80,336},{96,352},{112... | collective-permute-start | bytes 442376 | tf_op jit(solution)/shard_map/ppermute | solution.py:14
  34.4 14.6 %collective-permute-done.2 = bf16[160,1152]{1,0:T(8,128)(2,1)S(1)} collective-permute-done((bf16[160,1152]{1,0:T(8,128)(2,1)S(1)}, bf16[160,1152]{1,0:T(8,128)(2,1)S(1)}, u32[]{:S(2)}, u32[]{:S(2)}) %collective-permute-start.2) | collective-permute-done | bytes 368672 | tf_op jit(solution)/shard_map/ppermute | solution.py:341
  49.8 1.3 %pad_maximum_fusion.mine_ref = bf16[464,1152]{1,0:T(8,128)(2,1)S(1)} fusion(bf16[160,1152]{1,0:T(8,128)(2,1)} %copy-done.8, bf16[304,1152]{1,0:T(8,128)(2,1)} %collective-permute-done.1), kind=kLoop, calls=%fused_computation | loop fusion | flops 2138112 | bytes 2138112 | tf_op jit(solution)/shard_map/concatenate | solution.py:341
  51.1 7.8 %collective-permute-start.3 = (bf16[464,1152]{1,0:T(8,128)(2,1)S(1)}, bf16[464,1152]{1,0:T(8,128)(2,1)}, u32[]{:S(2)}, u32[]{:S(2)}) collective-permute-start(bf16[464,1152]{1,0:T(8,128)(2,1)S(1)} %pad_maximum_fusion.mine_ref), channel_id=1, source_target_pairs={{0,16},{16,0},{32,48},{48,32},{64,80},{80,64},{96,112},{112,96},{1... | collective-permute-start | bytes 3207176 | tf_op jit(solution)/shard_map/ppermute | solution.py:14
  58.9 1.8 %shard_map.65 = bf16[4,64,1152]{2,1,0:T(8,128)(2,1)} custom-call(bf16[64,1152]{1,0:T(8,128)(2,1)} %collective-permute-done.source_ref), custom_call_target="tpu_custom_call" | custom-call | bytes 589824 | tf_op jit(solution)/shard_map/pallas_call | solution.py:71
  60.6 4.5 %all-to-all-start.1 = ((bf16[4,64,1152]{2,1,0:T(8,128)(2,1)}), bf16[4,64,1152]{2,1,0:T(8,128)(2,1)}, u32[]{:S(2)}, u32[]{:S(2)}) async-start(bf16[4,64,1152]{2,1,0:T(8,128)(2,1)} %shard_map.65), calls=%async_computation.1 | async-start | bytes 1179648 | tf_op jit(solution)/shard_map/all_to_all | solution.py:321
  65.1 1.0 copy-done.1
  66.1 1.7 %shard_map.66 = (bf16[72,1024]{1,0:T(8,128)(2,1)S(1)}, bf16[144,1024]{1,0:T(8,128)(2,1)}) custom-call(bf16[1024,1152]{1,0:T(8,128)(2,1)S(1)} %bitcast.15, bf16[216,1152]{1,0:T(8,128)(2,1)S(1)} %bitcast.18, f32[72,2]{1,0:T(8,128)S(1)} %bitcast.23), custom_call_target="tpu_custom_call" | custom-call | flops 509607936 | bytes 2359296 | tf_op jit(solution)/shard_map/pallas_call | solution.py:107
  68.4 1.9 %collective-permute-start.4 = (bf16[144,1024]{1,0:T(8,128)(2,1)}, bf16[144,1024]{1,0:T(8,128)(2,1)S(1)}, u32[]{:S(2)}, u32[]{:S(2)}) collective-permute-start(bf16[144,1024]{1,0:T(8,128)(2,1)} %get-tuple-element.34.own_ref), channel_id=1, source_target_pairs={{0,16},{16,0},{32,48},{48,32},{64,80},{80,64},{96,112},{112,96},{1... | collective-permute-start | bytes 884744 | tf_op jit(solution)/shard_map/ppermute | solution.py:14
  70.5 5.2 %collective-permute-start.5 = (bf16[144,1024]{1,0:T(8,128)(2,1)}, bf16[144,1024]{1,0:T(8,128)(2,1)S(1)}, u32[]{:S(2)}, u32[]{:S(2)}) collective-permute-start(bf16[144,1024]{1,0:T(8,128)(2,1)} %get-tuple-element.34.own_ref), channel_id=1, source_target_pairs={{0,64},{16,80},{32,96},{48,112},{64,0},{80,16},{96,32},{112,48},{1... | collective-permute-start | bytes 884744 | tf_op jit(solution)/shard_map/ppermute | solution.py:14
  75.7 1.0 copy-done.2
  76.8 3.2 %shard_map.67 = bf16[4,144,256]{2,1,0:T(8,128)(2,1)} custom-call(s32[5]{0:T(128)S(1)} %pad_add_fusion.place_ref, bf16[256,1152]{1,0:T(8,128)(2,1)} %bitcast.12.rows_ref, bf16[216,1152]{1,0:T(8,128)(2,1)S(1)} %bitcast.19, bf16[464,1152]{1,0:T(8,128)(2,1)S(1)} %pad_maximum_fusion.mine_ref, bf16[464,1152]{1,0:T(8,128)(2,1)} %collective-permute-done.3.other_ref), custom_call_target="tpu_custom_call" | custom-call | flops 509607936 | bytes 1179648 | tf_op jit(solution)/shard_map/pallas_call | solution.py:149
  80.0 3.5 %all-to-all-start.2 = ((bf16[4,144,256]{2,1,0:T(8,128)(2,1)}), bf16[4,144,256]{2,1,0:T(8,128)(2,1)S(1)}, u32[]{:S(2)}, u32[]{:S(2)}) async-start(bf16[4,144,256]{2,1,0:T(8,128)(2,1)} %shard_map.67), calls=%async_computation.2 | async-start | bytes 589824 | tf_op jit(solution)/shard_map/all_to_all | solution.py:321
  83.4 4.5 %shard_map.68 = (f32[72,1024]{1,0:T(8,128)S(1)}, f32[80,1024]{1,0:T(8,128)S(1)}, f32[1,1024]{1,0:T(1,128)S(1)}) custom-call(s32[3]{0:T(128)S(1)} %bitcast.25, bf16[72,1024]{1,0:T(8,128)(2,1)S(1)} %copy-done.6, bf16[144,1024]{1,0:T(8,128)(2,1)} %get-tuple-element.34.own_ref, bf16[144,1024]{1,0:T(8,128)(2,1)S(1)} %collective-permute-done.4.far_ref), custom_call_target="tpu_custom_call" | custom-call | flops 2147483648 | bytes 589824 | tf_op jit(solution)/shard_map/pallas_call | solution.py:272
  88.7 2.3 %all-to-all-done.2.parts_ref = bf16[4,144,256]{2,1,0:T(8,128)(2,1)S(1)} async-done(((bf16[4,144,256]{2,1,0:T(8,128)(2,1)}), bf16[4,144,256]{2,1,0:T(8,128)(2,1)S(1)}, u32[]{:S(2)}, u32[]{:S(2)}) %all-to-all-start.2) | async-done | bytes 294944 | tf_op jit(solution)/shard_map/all_to_all | solution.py:321
  91.2 2.4 %shard_map.70 = (f32[80,1024]{1,0:T(8,128)S(1)}, f32[1,1024]{1,0:T(1,128)S(1)}) custom-call(s32[3]{0:T(128)S(1)} %bitcast.26, bf16[72,1024]{1,0:T(8,128)(2,1)S(1)} %copy-done.6, f32[80,1024]{1,0:T(8,128)S(1)} %get-tuple-element.39.state_ref, f32[1,1024]{1,0:T(1,128)S(1)} %get-tuple-element.40.best_ref, bf16[144,1024]{1,0:T(8,128)(2,1)S(1)} %shard_map.69.far_ref), custom_call_target="tpu_custom_call" | custom-call | flops 1073741824 | bytes 294912 | tf_op jit(solution)/shard_map/pallas_call | solution.py:272
  93.6 2.4 %shard_map.71 = bf16[4,72,256]{2,1,0:T(8,128)(2,1)S(1)} custom-call(s32[3]{0:T(128)S(1)} %bitcast.27, bf16[72,1024]{1,0:T(8,128)(2,1)S(1)} %copy-done.6, f32[72,1024]{1,0:T(8,128)S(1)} %get-tuple-element.38.own_in_ref, f32[80,1024]{1,0:T(8,128)S(1)} %get-tuple-element.42.state_ref, f32[1,1024]{1,0:T(1,128)S(1)} %get-tuple-element.43.best_ref, ...), custom_call_target="tpu_custom_call" | custom-call | flops 1073741824 | bytes 294912 | tf_op jit(solution)/shard_map/pallas_call | solution.py:272
  96.0 8.4 %all_to_all.25.parts_ref = bf16[4,72,256]{2,1,0:T(8,128)(2,1)S(1)} all-to-all(bf16[4,72,256]{2,1,0:T(8,128)(2,1)S(1)} %shard_map.71), channel_id=1, replica_groups={{0,4,8,12},{1,5,9,13},{2,6,10,14},{3,7,11,15},{16,20,24,28},{17,21,25,2..., dimensions={0} | all-to-all | bytes 294912 | tf_op jit(solution)/shard_map/all_to_all | solution.py:321
  104.4 2.0 %shard_map.72 = bf16[4,64,1152]{2,1,0:T(8,128)(2,1)S(1)} custom-call(s32[5]{0:T(128)S(1)} %pad_add_fusion.place_ref, bf16[4,72,256]{2,1,0:T(8,128)(2,1)S(1)} %all_to_all.25.parts_ref, bf16[72,1152]{1,0:T(8,128)(2,1)S(1)} %bitcast.22, bf16[464,1152]{1,0:T(8,128)(2,1)S(1)} %pad_maximum_fusion.mine_ref, bf16[464,1152]{1,0:T(8,128)(2,1)} %collective-permute-done.3.other_ref), custom_call_target="tpu_custom_call" | custom-call | flops 169869312 | bytes 1253376 | tf_op jit(solution)/shard_map/pallas_call | solution.py:366
  106.4 13.2 %all_to_all.26 = bf16[4,64,1152]{2,1,0:T(8,128)(2,1)S(1)} all-to-all(bf16[4,64,1152]{2,1,0:T(8,128)(2,1)S(1)} %shard_map.72), channel_id=1, replica_groups={{0,1,2,3},{4,5,6,7},{8,9,10,11},{12,13,14,15},{16,17,18,19},{20,21,22,2..., dimensions={0} | all-to-all | bytes 1179648 | tf_op jit(solution)/shard_map/all_to_all | solution.py:321
  (33 shorter events, 4.4 us)
Async XLA Ops:
  3.4 7.2 %copy-start = (bf16[1,216,1152]{2,1,0:T(8,128)(2,1)S(1)}, bf16[1,216,1152]{2,1,0:T(8,128)(2,1)}, u32[]{:S(2)}) copy-start(bf16[1,216,1152]{2,1,0:T(8,128)(2,1)} %param.8) | copy-start | bytes 1492996
  3.4 7.2 %copy-start.3 = (bf16[1,72,1152]{2,1,0:T(8,128)(2,1)S(1)}, bf16[1,72,1152]{2,1,0:T(8,128)(2,1)}, u32[]{:S(2)}) copy-start(bf16[1,72,1152]{2,1,0:T(8,128)(2,1)} %param.10) | copy-start | bytes 497668
  3.4 57.2 %all-to-all-start = ((bf16[16,64,1152]{2,1,0:T(8,128)(2,1)}), bf16[16,64,1152]{2,1,0:T(8,128)(2,1)S(1)}, u32[]{:S(2)}, u32[]{:S(2)}) async-start(bf16[16,64,1152]{2,1,0:T(8,128)(2,1)} %get-tuple-element.27), calls=%async_computation | async-start | bytes 4718592 | tf_op jit(solution)/shard_map/all_to_all | solution.py:83
  10.6 23.7 %copy-start.9 = (f32[1,2,72]{2,1,0:T(2,128)S(1)}, f32[1,2,72]{2,1,0:T(2,128)}, u32[]{:S(2)}) copy-start(f32[1,2,72]{2,1,0:T(2,128)} %param.9) | copy-start | bytes 1732
  11.6 38.2 %collective-permute-start.1 = (bf16[304,1152]{1,0:T(8,128)(2,1)}, bf16[304,1152]{1,0:T(8,128)(2,1)}, u32[]{:S(2)}, u32[]{:S(2)}) collective-permute-start(bf16[304,1152]{1,0:T(8,128)(2,1)} %pad_maximum_fusion.1), channel_id=1, source_target_pairs={{4,0},{5,1},{6,2},{7,3},{8,4},{9,5},{10,6},{11,7},{12,8},{13,9},{1... | collective-permute-start | bytes 2101256 | tf_op jit(solution)/shard_map/ppermute | solution.py:338
  16.7 32.3 %collective-permute-start.2 = (bf16[160,1152]{1,0:T(8,128)(2,1)S(1)}, bf16[160,1152]{1,0:T(8,128)(2,1)S(1)}, u32[]{:S(2)}, u32[]{:S(2)}) collective-permute-start(bf16[160,1152]{1,0:T(8,128)(2,1)S(1)} %fusion), channel_id=1, source_target_pairs={{0,8},{1,9},{2,10},{3,11},{4,12},{5,13},{6,14},{7,15},{8,0},{9,1},... | collective-permute-start | bytes 1105928 | tf_op jit(solution)/shard_map/ppermute | solution.py:341
  19.5 31.6 %collective-permute-start = (bf16[64,1152]{1,0:T(8,128)(2,1)}, bf16[64,1152]{1,0:T(8,128)(2,1)}, u32[]{:S(2)}, u32[]{:S(2)}) collective-permute-start(bf16[64,1152]{1,0:T(8,128)(2,1)} %get-tuple-element.25), channel_id=1, source_target_pairs={{0,256},{16,272},{32,288},{48,304},{64,320},{80,336},{96,352},{112... | collective-permute-start | bytes 442376 | tf_op jit(solution)/shard_map/ppermute | solution.py:14
  49.0 0.7 copy-start.8
  51.1 24.6 %collective-permute-start.3 = (bf16[464,1152]{1,0:T(8,128)(2,1)S(1)}, bf16[464,1152]{1,0:T(8,128)(2,1)}, u32[]{:S(2)}, u32[]{:S(2)}) collective-permute-start(bf16[464,1152]{1,0:T(8,128)(2,1)S(1)} %pad_maximum_fusion.mine_ref), channel_id=1, source_target_pairs={{0,16},{16,0},{32,48},{48,32},{64,80},{80,64},{96,112},{112,96},{1... | collective-permute-start | bytes 3207176 | tf_op jit(solution)/shard_map/ppermute | solution.py:14
  60.6 15.1 %all-to-all-start.1 = ((bf16[4,64,1152]{2,1,0:T(8,128)(2,1)}), bf16[4,64,1152]{2,1,0:T(8,128)(2,1)}, u32[]{:S(2)}, u32[]{:S(2)}) async-start(bf16[4,64,1152]{2,1,0:T(8,128)(2,1)} %shard_map.65), calls=%async_computation.1 | async-start | bytes 1179648 | tf_op jit(solution)/shard_map/all_to_all | solution.py:321
  65.1 1.0 copy-start.1
  67.8 0.7 copy-start.5
  68.4 15.0 %collective-permute-start.4 = (bf16[144,1024]{1,0:T(8,128)(2,1)}, bf16[144,1024]{1,0:T(8,128)(2,1)S(1)}, u32[]{:S(2)}, u32[]{:S(2)}) collective-permute-start(bf16[144,1024]{1,0:T(8,128)(2,1)} %get-tuple-element.34.own_ref), channel_id=1, source_target_pairs={{0,16},{16,0},{32,48},{48,32},{64,80},{80,64},{96,112},{112,96},{1... | collective-permute-start | bytes 884744 | tf_op jit(solution)/shard_map/ppermute | solution.py:14
  70.5 18.3 %collective-permute-start.5 = (bf16[144,1024]{1,0:T(8,128)(2,1)}, bf16[144,1024]{1,0:T(8,128)(2,1)S(1)}, u32[]{:S(2)}, u32[]{:S(2)}) collective-permute-start(bf16[144,1024]{1,0:T(8,128)(2,1)} %get-tuple-element.34.own_ref), channel_id=1, source_target_pairs={{0,64},{16,80},{32,96},{48,112},{64,0},{80,16},{96,32},{112,48},{1... | collective-permute-start | bytes 884744 | tf_op jit(solution)/shard_map/ppermute | solution.py:14
  75.7 1.0 copy-start.2
  76.8 6.7 %copy-start.6 = (bf16[72,1024]{1,0:T(8,128)(2,1)S(1)}, bf16[72,1024]{1,0:T(8,128)(2,1)}, u32[]{:S(2)}) copy-start(bf16[72,1024]{1,0:T(8,128)(2,1)} %copy-done.5) | copy-start | bytes 442372
  76.8 6.7 %copy-start.7 = (s32[3,1]{0,1:T(1,128)S(1)}, s32[3,1]{0,1:T(1,128)}, u32[]{:S(2)}) copy-start(s32[3,1]{0,1:T(1,128)} %param.11) | copy-start | bytes 40
  80.0 11.1 %all-to-all-start.2 = ((bf16[4,144,256]{2,1,0:T(8,128)(2,1)}), bf16[4,144,256]{2,1,0:T(8,128)(2,1)S(1)}, u32[]{:S(2)}, u32[]{:S(2)}) async-start(bf16[4,144,256]{2,1,0:T(8,128)(2,1)} %shard_map.67), calls=%async_computation.2 | async-start | bytes 589824 | tf_op jit(solution)/shard_map/all_to_all | solution.py:321
  93.6 10.8 %copy-start.4 = (bf16[1,72,1152]{2,1,0:T(8,128)(2,1)S(1)}, bf16[1,72,1152]{2,1,0:T(8,128)(2,1)}, u32[]{:S(2)}) copy-start(bf16[1,72,1152]{2,1,0:T(8,128)(2,1)} %param.10) | copy-start | bytes 497668

commit v14 on v13

--- a/solution.py
+++ b/solution.py
@@ -120,7 +120,7 @@
 def project_far_kernel(place_ref, rows_ref, weight_ref, mine_ref, other_ref, out_ref):
     tokens = rows_ref[...]
     wide = out_ref.shape[1]
-    size = mine_ref.shape[0] - COLUMN
+    column = weight_ref.shape[0] // 3 + PAD + wide
     start = weight_ref.shape[0] - wide
     even = start // 16 * 16
 
@@ -130,17 +130,16 @@
         )
 
     own = product(weight_ref[even:])[start - even :]
-    skip = size - PAD - wide
-    mine, other = product(mine_ref[COLUMN - size : COLUMN]), product(other_ref[COLUMN - size : COLUMN])
-    first, second = product(mine_ref[COLUMN:]), product(other_ref[COLUMN:])
-    far = jnp.where(place_ref[4] == 0, second, first)
-    out_ref[place_ref[0]] = own.astype(jnp.bfloat16)
-    for n, flat in enumerate((mine, other, far)):
-        out_ref[place_ref[1 + n]] = flat[skip : skip + wide].astype(jnp.bfloat16)
+    mine, other = product(mine_ref[column - wide : column]), product(other_ref[column - wide : column])
+    first, second = product(mine_ref[column:]), product(other_ref[column:])
+    low = jnp.where(place_ref[4] == 0, first, second)
+    high = jnp.where(place_ref[4] == 0, second, first)
+    far = jnp.concatenate([low[column - wide :], high], axis=0)
+    for n, flat in enumerate((own, mine, other, far)):
+        out_ref[place_ref[n]] = flat.astype(jnp.bfloat16)
 
 
 PAD = 8
-COLUMN = 304
 
 
 def project_far(place, rows, weight, mine, other, head_dim):
@@ -328,15 +327,15 @@
     side = len(groups(0))
     core = lax.axis_index("view") % 2
     blank = jnp.zeros((PAD, weight.shape[1]), weight.dtype)
-    packed = jnp.concatenate([out_weight, blank, weight, blank], axis=0)
-    part = (COLUMN // 2 + 15) // 16 * 16
+    packed = jnp.concatenate([out_weight, blank, weight[out_weight.shape[0] :]], axis=0)
+    part = packed.shape[0] // 2
     pairs = []
     for view in range(views):
         step = side if view % 2 == 0 else -side
         for head in range(heads):
             pairs.append((view * heads + (head + step) % heads, view * heads + head))
     beside = lax.ppermute(packed, ("view", "head"), pairs)
-    sent = jnp.where(core == 0, packed[:part], packed[COLUMN - part :])
+    sent = jnp.where(core == 0, packed[:part], packed[part:])
     across = [(head, (head + heads // 2) % heads) for head in range(heads)]
     return jnp.concatenate([beside, lax.ppermute(sent, "head", across)], axis=0)
 
@@ -347,7 +346,8 @@
     def rows_at(ref, start):
         return ref[start : start + head_dim + PAD].astype(jnp.float32)[:head_dim]
 
-    first, second = rows_at(mine_ref, COLUMN), rows_at(other_ref, COLUMN)
+    column = 3 * head_dim + PAD
+    first, second = rows_at(mine_ref, column), rows_at(other_ref, column)
     far = jnp.where(place_ref[4] == 0, first, second)
     weights = [rows_at(mine_ref, 0), rows_at(other_ref, 0), far]
     total = None
@@ -394,11 +394,11 @@
     turn = jnp.where(core == 0, 1, side - 1)
     place = jnp.stack([line, line + turn, line + side - turn, line + side // 2]) % side
     place = jnp.concatenate([place, core[None]]).astype(jnp.int32)
-    far_normed, mine, gain, active = lax.optimization_barrier(
-        (partner(normed, bits[-1]), column_weights(weight, out_weight[0]), gain, active)
-    )
+    far_normed, gain, active = lax.optimization_barrier((partner(normed, bits[-1]), gain, active))
     far_slots = copies_of(far_normed, side)
-    every, far_slots = lax.optimization_barrier((gather_tokens(slots), far_slots))
+    every, far_slots, mine = lax.optimization_barrier(
+        (gather_tokens(slots), far_slots, column_weights(weight, out_weight[0]))
+    )
     far_tokens = exchange(far_slots, 0).reshape(-1, width)
     query, own = project(every, weight, gain)
     near = [partner(own, bit) for bit in bits[:-1]]

time: 121 us -> 113 us (0.934)
  starting transfers between devices: 52.6 us -> 48.4 us
  waiting for transfers between devices: 17.7 us -> 15.7 us
  Pallas kernels: 21.4 us -> 19.5 us
    ppermute x1, waiting for transfers between devices: 14.6 us -> 0.01 us  [column_weights(): return jnp.concatenate([beside, lax.ppermute(sent, 'head', across)], axis=0)]
    ppermute x4, waiting for transfers between devices: 0.8 us -> 13 us  [partner(): lax.ppermute(array, 'view', [(i, i ^ 1 << bit) for i in range(lax.axis_si...]
    ppermute x4, starting transfers between devices: 29.7 us -> 25.5 us  [partner(): lax.ppermute(array, 'view', [(i, i ^ 1 << bit) for i in range(lax.axis_si...]
    unnamed x21 -> x15, local copies, waits for them, and re-layouts: 3.6 us -> 2.88 us
  transfers between devices with their start and end apart: 9 -> 9, of which waited for: 3 -> 4; matrix products, arithmetic and copies ran while one was open for 2% -> 3% of each run, Pallas kernels for 9% -> 9%
where the time goes in v14:
time: 113 us
  starting transfers between devices  48.4 us (43%)
  blocking collectives  21.6 us (19%)
  Pallas kernels  19.5 us (17%)
  waiting for transfers between devices  15.7 us (14%)
  other arithmetic  4.13 us (4%)
  local copies, waits for them, and re-layouts  2.98 us (3%)
    ppermute x4, starting transfers between devices, partner(): lax.ppermute(array, 'view', [(i, i ^ 1 << bit) for i in range(lax.axis_si...  25.5 us
    all_to_all x2, blocking collectives, exchange(): lax.all_to_all(slots, 'head', split_axis=0, concat_axis=0, tiled=True, ax...  21.6 us
    ppermute x4, waiting for transfers between devices, partner(): lax.ppermute(array, 'view', [(i, i ^ 1 << bit) for i in range(lax.axis_si...  13 us
    pallas_call x3, Pallas kernels, call_attend(): pl.pallas_call(kernel, out_shape=out_shape, in_specs=[smem] + [vmem] * (l...  9.25 us
    all_to_all x2, starting transfers between devices, exchange(): lax.all_to_all(slots, 'head', split_axis=0, concat_axis=0, tiled=True, ax...  7.92 us
    all_to_all x1, starting transfers between devices, gather_tokens(): lax.all_to_all(slots, 'head', split_axis=0, concat_axis=0, tiled=True)  7.18 us
    ppermute x1, starting transfers between devices, column_weights(): beside = lax.ppermute(packed, ('view', 'head'), pairs)  5.03 us
    pallas_call x1, Pallas kernels, project_far(): pl.pallas_call(project_far_kernel, out_shape=jax.ShapeDtypeStruct((side,...  3.03 us
  transfers between devices with their start and end apart: 9, of which 4 were waited for; matrix products, arithmetic and copies ran while one was open for 3% of the time, Pallas kernels for 9%

profile of v14, /device:TPU:32, one launch (start us, length us, event | category | flops | bytes accessed | tf_op | source)
XLA Modules:
  0.0 112.5 jit_solution(12292540534744178920)
XLA Ops:
  0.0 2.7 %shard_map.64 = (bf16[64,1152]{1,0:T(8,128)(2,1)S(1)}, bf16[16,64,1152]{2,1,0:T(8,128)(2,1)}) custom-call(bf16[64,1152]{1,0:T(8,128)(2,1)} %bitcast.29, f32[1152]{0:T(1024)} %gain_ref.1), custom_call_target="tpu_custom_call" | custom-call | flops 589824 | bytes 2359296 | tf_op jit(solution)/shard_map/pallas_call | solution.py:49
  2.7 7.2 %all-to-all-start = ((bf16[16,64,1152]{2,1,0:T(8,128)(2,1)}), bf16[16,64,1152]{2,1,0:T(8,128)(2,1)S(1)}, u32[]{:S(2)}, u32[]{:S(2)}) async-start(bf16[16,64,1152]{2,1,0:T(8,128)(2,1)} %get-tuple-element.27), calls=%async_computation | async-start | bytes 4718592 | tf_op jit(solution)/shard_map/all_to_all | solution.py:83
  11.0 5.0 %collective-permute-start.1 = (bf16[224,1152]{1,0:T(8,128)(2,1)}, bf16[224,1152]{1,0:T(8,128)(2,1)}, u32[]{:S(2)}, u32[]{:S(2)}) collective-permute-start(bf16[224,1152]{1,0:T(8,128)(2,1)} %pad_maximum_fusion.1), channel_id=1, source_target_pairs={{4,0},{5,1},{6,2},{7,3},{8,4},{9,5},{10,6},{11,7},{12,8},{13,9},{1... | collective-permute-start | bytes 1548296 | tf_op jit(solution)/shard_map/ppermute | solution.py:337
  16.1 1.0 slice_select_fusion
  17.1 2.8 %collective-permute-start.2 = (bf16[112,1152]{1,0:T(8,128)(2,1)S(1)}, bf16[112,1152]{1,0:T(8,128)(2,1)S(1)}, u32[]{:S(2)}, u32[]{:S(2)}) collective-permute-start(bf16[112,1152]{1,0:T(8,128)(2,1)S(1)} %slice_select_fusion), channel_id=1, source_target_pairs={{0,8},{1,9},{2,10},{3,11},{4,12},{5,13},{6,14},{7,15},{8,0},{9,1},... | collective-permute-start | bytes 774152 | tf_op jit(solution)/shard_map/ppermute | solution.py:340
  19.9 14.8 %collective-permute-start = (bf16[64,1152]{1,0:T(8,128)(2,1)S(1)}, bf16[64,1152]{1,0:T(8,128)(2,1)S(1)}, u32[]{:S(2)}, u32[]{:S(2)}) collective-permute-start(bf16[64,1152]{1,0:T(8,128)(2,1)S(1)} %get-tuple-element.25), channel_id=1, source_target_pairs={{0,256},{16,272},{32,288},{48,304},{64,320},{80,336},{96,352},{112... | collective-permute-start | bytes 442376 | tf_op jit(solution)/shard_map/ppermute | solution.py:14
  34.8 12.5 %collective-permute-done.source_ref = bf16[64,1152]{1,0:T(8,128)(2,1)S(1)} collective-permute-done((bf16[64,1152]{1,0:T(8,128)(2,1)S(1)}, bf16[64,1152]{1,0:T(8,128)(2,1)S(1)}, u32[]{:S(2)}, u32[]{:S(2)}) %collective-permute-start) | collective-permute-done | bytes 147488 | tf_op jit(solution)/shard_map/ppermute | solution.py:14
  48.9 1.2 %pad_maximum_fusion.mine_ref = bf16[336,1152]{1,0:T(8,128)(2,1)S(1)} fusion(bf16[112,1152]{1,0:T(8,128)(2,1)} %copy-done.5, bf16[224,1152]{1,0:T(8,128)(2,1)} %collective-permute-done.1), kind=kLoop, calls=%fused_computation | loop fusion | flops 1548288 | bytes 1548288 | tf_op jit(solution)/shard_map/concatenate | solution.py:340
  50.1 3.6 %collective-permute-start.3 = (bf16[336,1152]{1,0:T(8,128)(2,1)S(1)}, bf16[336,1152]{1,0:T(8,128)(2,1)}, u32[]{:S(2)}, u32[]{:S(2)}) collective-permute-start(bf16[336,1152]{1,0:T(8,128)(2,1)S(1)} %pad_maximum_fusion.mine_ref), channel_id=1, source_target_pairs={{0,16},{16,0},{32,48},{48,32},{64,80},{80,64},{96,112},{112,96},{1... | collective-permute-start | bytes 2322440 | tf_op jit(solution)/shard_map/ppermute | solution.py:14
  53.7 4.5 %all-to-all-start.1 = ((bf16[4,64,1152]{2,1,0:T(8,128)(2,1)}), bf16[4,64,1152]{2,1,0:T(8,128)(2,1)}, u32[]{:S(2)}, u32[]{:S(2)}) async-start(bf16[4,64,1152]{2,1,0:T(8,128)(2,1)} %shard_map.65), calls=%async_computation.1 | async-start | bytes 1179648 | tf_op jit(solution)/shard_map/all_to_all | solution.py:320
  58.2 1.0 copy-done.1
  59.2 1.6 %shard_map.66 = (bf16[72,1024]{1,0:T(8,128)(2,1)S(1)}, bf16[144,1024]{1,0:T(8,128)(2,1)}) custom-call(bf16[1024,1152]{1,0:T(8,128)(2,1)S(1)} %bitcast.19, bf16[216,1152]{1,0:T(8,128)(2,1)S(1)} %bitcast.20, f32[72,2]{1,0:T(8,128)S(1)} %bitcast.24), custom_call_target="tpu_custom_call" | custom-call | flops 509607936 | bytes 2359296 | tf_op jit(solution)/shard_map/pallas_call | solution.py:107
  60.9 1.9 %collective-permute-start.4 = (bf16[144,1024]{1,0:T(8,128)(2,1)}, bf16[144,1024]{1,0:T(8,128)(2,1)S(1)}, u32[]{:S(2)}, u32[]{:S(2)}) collective-permute-start(bf16[144,1024]{1,0:T(8,128)(2,1)} %get-tuple-element.34.own_ref), channel_id=1, source_target_pairs={{0,16},{16,0},{32,48},{48,32},{64,80},{80,64},{96,112},{112,96},{1... | collective-permute-start | bytes 884744 | tf_op jit(solution)/shard_map/ppermute | solution.py:14
  62.9 5.2 %collective-permute-start.5 = (bf16[144,1024]{1,0:T(8,128)(2,1)}, bf16[144,1024]{1,0:T(8,128)(2,1)S(1)}, u32[]{:S(2)}, u32[]{:S(2)}) collective-permute-start(bf16[144,1024]{1,0:T(8,128)(2,1)} %get-tuple-element.34.own_ref), channel_id=1, source_target_pairs={{0,64},{16,80},{32,96},{48,112},{64,0},{80,16},{96,32},{112,48},{1... | collective-permute-start | bytes 884744 | tf_op jit(solution)/shard_map/ppermute | solution.py:14
  68.7 1.0 copy-done.2
  69.7 3.0 %shard_map.67 = bf16[4,144,256]{2,1,0:T(8,128)(2,1)} custom-call(s32[5]{0:T(128)S(1)} %pad_add_fusion.place_ref, bf16[256,1152]{1,0:T(8,128)(2,1)} %bitcast.14.rows_ref, bf16[216,1152]{1,0:T(8,128)(2,1)S(1)} %bitcast.21, bf16[336,1152]{1,0:T(8,128)(2,1)S(1)} %pad_maximum_fusion.mine_ref, bf16[336,1152]{1,0:T(8,128)(2,1)} %collective-permute-done.3.other_ref), custom_call_target="tpu_custom_call" | custom-call | flops 509607936 | bytes 1179648 | tf_op jit(solution)/shard_map/pallas_call | solution.py:148
  72.7 3.5 %all-to-all-start.2 = ((bf16[4,144,256]{2,1,0:T(8,128)(2,1)}), bf16[4,144,256]{2,1,0:T(8,128)(2,1)S(1)}, u32[]{:S(2)}, u32[]{:S(2)}) async-start(bf16[4,144,256]{2,1,0:T(8,128)(2,1)} %shard_map.67), calls=%async_computation.2 | async-start | bytes 589824 | tf_op jit(solution)/shard_map/all_to_all | solution.py:320
  76.2 4.5 %shard_map.68 = (f32[72,1024]{1,0:T(8,128)S(1)}, f32[80,1024]{1,0:T(8,128)S(1)}, f32[1,1024]{1,0:T(1,128)S(1)}) custom-call(s32[3]{0:T(128)S(1)} %bitcast.26, bf16[72,1024]{1,0:T(8,128)(2,1)S(1)} %get-tuple-element.31.query_ref, bf16[144,1024]{1,0:T(8,128)(2,1)} %get-tuple-element.34.own_ref, bf16[144,1024]{1,0:T(8,128)(2,1)S(1)} %collective-permute-done.4.far_ref), custom_call_target="tpu_custom_call" | custom-call | flops 2147483648 | bytes 589824 | tf_op jit(solution)/shard_map/pallas_call | solution.py:271
  81.2 2.2 %all-to-all-done.2.parts_ref = bf16[4,144,256]{2,1,0:T(8,128)(2,1)S(1)} async-done(((bf16[4,144,256]{2,1,0:T(8,128)(2,1)}), bf16[4,144,256]{2,1,0:T(8,128)(2,1)S(1)}, u32[]{:S(2)}, u32[]{:S(2)}) %all-to-all-start.2) | async-done | bytes 294944 | tf_op jit(solution)/shard_map/all_to_all | solution.py:320
  83.4 2.4 %shard_map.70 = (f32[80,1024]{1,0:T(8,128)S(1)}, f32[1,1024]{1,0:T(1,128)S(1)}) custom-call(s32[3]{0:T(128)S(1)} %bitcast.27, bf16[72,1024]{1,0:T(8,128)(2,1)S(1)} %get-tuple-element.31.query_ref, f32[80,1024]{1,0:T(8,128)S(1)} %get-tuple-element.39.state_ref, f32[1,1024]{1,0:T(1,128)S(1)} %get-tuple-element.40.best_ref, bf16[144,1024]{1,0:T(8,128)(2,1)S(1)} %shard_map.69.far_ref), custom_call_target="tpu_custom_call" | custom-call | flops 1073741824 | bytes 294912 | tf_op jit(solution)/shard_map/pallas_call | solution.py:271
  85.8 2.4 %shard_map.71 = bf16[4,72,256]{2,1,0:T(8,128)(2,1)S(1)} custom-call(s32[3]{0:T(128)S(1)} %bitcast.28, bf16[72,1024]{1,0:T(8,128)(2,1)S(1)} %get-tuple-element.31.query_ref, f32[72,1024]{1,0:T(8,128)S(1)} %get-tuple-element.38.own_in_ref, f32[80,1024]{1,0:T(8,128)S(1)} %get-tuple-element.42.state_ref, f32[1,1024]{1,0:T(1,128)S(1)} %get-tuple-element.43.best_ref, ...), custom_call_target="tpu_custom_call" | custom-call | flops 1073741824 | bytes 294912 | tf_op jit(solution)/shard_map/pallas_call | solution.py:271
  88.2 8.4 %all_to_all.25.parts_ref = bf16[4,72,256]{2,1,0:T(8,128)(2,1)S(1)} all-to-all(bf16[4,72,256]{2,1,0:T(8,128)(2,1)S(1)} %shard_map.71), channel_id=1, replica_groups={{0,4,8,12},{1,5,9,13},{2,6,10,14},{3,7,11,15},{16,20,24,28},{17,21,25,2..., dimensions={0} | all-to-all | bytes 294912 | tf_op jit(solution)/shard_map/all_to_all | solution.py:320
  96.6 1.9 %shard_map.72 = bf16[4,64,1152]{2,1,0:T(8,128)(2,1)S(1)} custom-call(s32[5]{0:T(128)S(1)} %pad_add_fusion.place_ref, bf16[4,72,256]{2,1,0:T(8,128)(2,1)S(1)} %all_to_all.25.parts_ref, bf16[72,1152]{1,0:T(8,128)(2,1)S(1)} %bitcast.23, bf16[336,1152]{1,0:T(8,128)(2,1)S(1)} %pad_maximum_fusion.mine_ref, bf16[336,1152]{1,0:T(8,128)(2,1)} %collective-permute-done.3.other_ref), custom_call_target="tpu_custom_call" | custom-call | flops 169869312 | bytes 1253376 | tf_op jit(solution)/shard_map/pallas_call | solution.py:366
  98.6 13.2 %all_to_all.26 = bf16[4,64,1152]{2,1,0:T(8,128)(2,1)S(1)} all-to-all(bf16[4,64,1152]{2,1,0:T(8,128)(2,1)S(1)} %shard_map.72), channel_id=1, replica_groups={{0,1,2,3},{4,5,6,7},{8,9,10,11},{12,13,14,15},{16,17,18,19},{20,21,22,2..., dimensions={0} | all-to-all | bytes 1179648 | tf_op jit(solution)/shard_map/all_to_all | solution.py:320
  (29 shorter events, 4.7 us)
Async XLA Ops:
  2.7 7.3 %copy-start = (bf16[1,216,1152]{2,1,0:T(8,128)(2,1)S(1)}, bf16[1,216,1152]{2,1,0:T(8,128)(2,1)}, u32[]{:S(2)}) copy-start(bf16[1,216,1152]{2,1,0:T(8,128)(2,1)} %param.8) | copy-start | bytes 1492996
  2.7 7.3 %copy-start.3 = (bf16[1,72,1152]{2,1,0:T(8,128)(2,1)S(1)}, bf16[1,72,1152]{2,1,0:T(8,128)(2,1)}, u32[]{:S(2)}) copy-start(bf16[1,72,1152]{2,1,0:T(8,128)(2,1)} %param.10) | copy-start | bytes 497668
  2.7 47.4 %all-to-all-start = ((bf16[16,64,1152]{2,1,0:T(8,128)(2,1)}), bf16[16,64,1152]{2,1,0:T(8,128)(2,1)S(1)}, u32[]{:S(2)}, u32[]{:S(2)}) async-start(bf16[16,64,1152]{2,1,0:T(8,128)(2,1)} %get-tuple-element.27), calls=%async_computation | async-start | bytes 4718592 | tf_op jit(solution)/shard_map/all_to_all | solution.py:83
  9.9 24.8 %copy-start.6 = (f32[1,2,72]{2,1,0:T(2,128)S(1)}, f32[1,2,72]{2,1,0:T(2,128)}, u32[]{:S(2)}) copy-start(f32[1,2,72]{2,1,0:T(2,128)} %param.9) | copy-start | bytes 1732
  11.0 37.9 %collective-permute-start.1 = (bf16[224,1152]{1,0:T(8,128)(2,1)}, bf16[224,1152]{1,0:T(8,128)(2,1)}, u32[]{:S(2)}, u32[]{:S(2)}) collective-permute-start(bf16[224,1152]{1,0:T(8,128)(2,1)} %pad_maximum_fusion.1), channel_id=1, source_target_pairs={{4,0},{5,1},{6,2},{7,3},{8,4},{9,5},{10,6},{11,7},{12,8},{13,9},{1... | collective-permute-start | bytes 1548296 | tf_op jit(solution)/shard_map/ppermute | solution.py:337
  17.1 31.1 %collective-permute-start.2 = (bf16[112,1152]{1,0:T(8,128)(2,1)S(1)}, bf16[112,1152]{1,0:T(8,128)(2,1)S(1)}, u32[]{:S(2)}, u32[]{:S(2)}) collective-permute-start(bf16[112,1152]{1,0:T(8,128)(2,1)S(1)} %slice_select_fusion), channel_id=1, source_target_pairs={{0,8},{1,9},{2,10},{3,11},{4,12},{5,13},{6,14},{7,15},{8,0},{9,1},... | collective-permute-start | bytes 774152 | tf_op jit(solution)/shard_map/ppermute | solution.py:340
  19.9 27.5 %collective-permute-start = (bf16[64,1152]{1,0:T(8,128)(2,1)S(1)}, bf16[64,1152]{1,0:T(8,128)(2,1)S(1)}, u32[]{:S(2)}, u32[]{:S(2)}) collective-permute-start(bf16[64,1152]{1,0:T(8,128)(2,1)S(1)} %get-tuple-element.25), channel_id=1, source_target_pairs={{0,256},{16,272},{32,288},{48,304},{64,320},{80,336},{96,352},{112... | collective-permute-start | bytes 442376 | tf_op jit(solution)/shard_map/ppermute | solution.py:14
  48.2 0.7 copy-start.5
  50.1 18.5 %collective-permute-start.3 = (bf16[336,1152]{1,0:T(8,128)(2,1)S(1)}, bf16[336,1152]{1,0:T(8,128)(2,1)}, u32[]{:S(2)}, u32[]{:S(2)}) collective-permute-start(bf16[336,1152]{1,0:T(8,128)(2,1)S(1)} %pad_maximum_fusion.mine_ref), channel_id=1, source_target_pairs={{0,16},{16,0},{32,48},{48,32},{64,80},{80,64},{96,112},{112,96},{1... | collective-permute-start | bytes 2322440 | tf_op jit(solution)/shard_map/ppermute | solution.py:14
  53.7 14.9 %all-to-all-start.1 = ((bf16[4,64,1152]{2,1,0:T(8,128)(2,1)}), bf16[4,64,1152]{2,1,0:T(8,128)(2,1)}, u32[]{:S(2)}, u32[]{:S(2)}) async-start(bf16[4,64,1152]{2,1,0:T(8,128)(2,1)} %shard_map.65), calls=%async_computation.1 | async-start | bytes 1179648 | tf_op jit(solution)/shard_map/all_to_all | solution.py:320
  58.2 1.0 copy-start.1
  60.9 15.3 %collective-permute-start.4 = (bf16[144,1024]{1,0:T(8,128)(2,1)}, bf16[144,1024]{1,0:T(8,128)(2,1)S(1)}, u32[]{:S(2)}, u32[]{:S(2)}) collective-permute-start(bf16[144,1024]{1,0:T(8,128)(2,1)} %get-tuple-element.34.own_ref), channel_id=1, source_target_pairs={{0,16},{16,0},{32,48},{48,32},{64,80},{80,64},{96,112},{112,96},{1... | collective-permute-start | bytes 884744 | tf_op jit(solution)/shard_map/ppermute | solution.py:14
  62.9 18.3 %collective-permute-start.5 = (bf16[144,1024]{1,0:T(8,128)(2,1)}, bf16[144,1024]{1,0:T(8,128)(2,1)S(1)}, u32[]{:S(2)}, u32[]{:S(2)}) collective-permute-start(bf16[144,1024]{1,0:T(8,128)(2,1)} %get-tuple-element.34.own_ref), channel_id=1, source_target_pairs={{0,64},{16,80},{32,96},{48,112},{64,0},{80,16},{96,32},{112,48},{1... | collective-permute-start | bytes 884744 | tf_op jit(solution)/shard_map/ppermute | solution.py:14
  68.6 1.0 copy-start.2
  69.7 6.5 %copy-start.4 = (s32[3,1]{0,1:T(1,128)S(1)}, s32[3,1]{0,1:T(1,128)}, u32[]{:S(2)}) copy-start(s32[3,1]{0,1:T(1,128)} %param.11) | copy-start | bytes 40
  72.7 10.6 %all-to-all-start.2 = ((bf16[4,144,256]{2,1,0:T(8,128)(2,1)}), bf16[4,144,256]{2,1,0:T(8,128)(2,1)S(1)}, u32[]{:S(2)}, u32[]{:S(2)}) async-start(bf16[4,144,256]{2,1,0:T(8,128)(2,1)} %shard_map.67), calls=%async_computation.2 | async-start | bytes 589824 | tf_op jit(solution)/shard_map/all_to_all | solution.py:320

commit v15 on v14

--- a/solution.py
+++ b/solution.py
@@ -117,44 +117,52 @@
     )(rows, weight, gain)
 
 
-def project_far_kernel(place_ref, rows_ref, weight_ref, mine_ref, other_ref, out_ref):
-    tokens = rows_ref[...]
+def project_far_kernel(
+    place_ref, rows_ref, weight_ref, mine_ref, other_ref, mine_half_ref, other_half_ref, out_ref
+):
     wide = out_ref.shape[1]
-    column = weight_ref.shape[0] // 3 + PAD + wide
+    column, part = mine_ref.shape[0], mine_half_ref.shape[0]
     start = weight_ref.shape[0] - wide
     even = start // 16 * 16
-
-    def product(rows):
-        return lax.dot_general(
-            rows, tokens, (((1,), (1,)), ((), ())), preferred_element_type=jnp.float32
-        )
-
-    own = product(weight_ref[even:])[start - even :]
-    mine, other = product(mine_ref[column - wide : column]), product(other_ref[column - wide : column])
-    first, second = product(mine_ref[column:]), product(other_ref[column:])
+    stacked = jnp.concatenate(
+        [
+            mine_ref[column - wide :],
+            other_ref[column - wide :],
+            mine_half_ref[...],
+            other_half_ref[...],
+            weight_ref[even:],
+        ],
+        axis=0,
+    )
+    flat = lax.dot_general(
+        stacked, rows_ref[...], (((1,), (1,)), ((), ())), preferred_element_type=jnp.float32
+    )
+    mine, other = flat[:wide], flat[wide : 2 * wide]
+    first, second = flat[2 * wide : 2 * wide + part], flat[2 * wide + part : 2 * wide + 2 * part]
+    own = flat[2 * wide + 2 * part + start - even :]
     low = jnp.where(place_ref[4] == 0, first, second)
     high = jnp.where(place_ref[4] == 0, second, first)
     far = jnp.concatenate([low[column - wide :], high], axis=0)
-    for n, flat in enumerate((own, mine, other, far)):
-        out_ref[place_ref[n]] = flat.astype(jnp.bfloat16)
+    for n, rows in enumerate((own, mine, other, far)):
+        out_ref[place_ref[n]] = rows.astype(jnp.bfloat16)
 
 
 PAD = 8
 
 
-def project_far(place, rows, weight, mine, other, head_dim):
+def project_far(place, rows, weight, column, head_dim):
     side = len(groups(0))
     smem, vmem = pl.BlockSpec(memory_space=pltpu.SMEM), pl.BlockSpec(memory_space=pltpu.VMEM)
     return pl.pallas_call(
         project_far_kernel,
         out_shape=jax.ShapeDtypeStruct((side, 2 * head_dim, rows.shape[0]), jnp.bfloat16),
-        in_specs=[smem] + [vmem] * 4,
+        in_specs=[smem] + [vmem] * (2 + len(column)),
         out_specs=vmem,
         compiler_params=pltpu.CompilerParams(vmem_limit_bytes=16 << 20),
         cost_estimate=pl.CostEstimate(
             flops=2 * side * rows.size * weight.shape[0], bytes_accessed=4 * rows.size, transcendentals=0
         ),
-    )(place, rows, weight, mine, other)
+    )(place, rows, weight, *column)
 
 
 def settle_kernel(parts_ref, gain_ref, pair_ref):
@@ -337,19 +345,20 @@
     beside = lax.ppermute(packed, ("view", "head"), pairs)
     sent = jnp.where(core == 0, packed[:part], packed[part:])
     across = [(head, (head + heads // 2) % heads) for head in range(heads)]
-    return jnp.concatenate([beside, lax.ppermute(sent, "head", across)], axis=0)
-
-
-def project_out_kernel(place_ref, parts_ref, weight_ref, mine_ref, other_ref, out_ref):
+    return beside, lax.ppermute(sent, "head", across)
+
+
+def project_out_kernel(
+    place_ref, parts_ref, weight_ref, mine_ref, other_ref, mine_half_ref, other_half_ref, out_ref
+):
     head_dim = weight_ref.shape[0]
 
-    def rows_at(ref, start):
-        return ref[start : start + head_dim + PAD].astype(jnp.float32)[:head_dim]
-
-    column = 3 * head_dim + PAD
-    first, second = rows_at(mine_ref, column), rows_at(other_ref, column)
+    def rows_at(ref):
+        return ref[: head_dim + PAD].astype(jnp.float32)[:head_dim]
+
+    first, second = rows_at(mine_half_ref), rows_at(other_half_ref)
     far = jnp.where(place_ref[4] == 0, first, second)
-    weights = [rows_at(mine_ref, 0), rows_at(other_ref, 0), far]
+    weights = [rows_at(mine_ref), rows_at(other_ref), far]
     total = None
     for n, weight in enumerate([weight_ref[...]] + [rows.astype(jnp.bfloat16) for rows in weights]):
         term = lax.dot_general(
@@ -359,20 +368,20 @@
     out_ref[...] = total.reshape(out_ref.shape).astype(jnp.bfloat16)
 
 
-def project_out(place, parts, weight, mine, other):
+def project_out(place, parts, weight, column):
     side, head_dim, tokens = parts.shape
     width = weight.shape[1]
     smem, vmem = pl.BlockSpec(memory_space=pltpu.SMEM), pl.BlockSpec(memory_space=pltpu.VMEM)
     partial = pl.pallas_call(
         project_out_kernel,
         out_shape=jax.ShapeDtypeStruct((side, tokens // side, width), jnp.bfloat16),
-        in_specs=[smem] + [vmem] * 4,
+        in_specs=[smem] + [vmem] * (2 + len(column)),
         out_specs=vmem,
         compiler_params=pltpu.CompilerParams(vmem_limit_bytes=16 << 20),
         cost_estimate=pl.CostEstimate(
             flops=2 * parts.size * width, bytes_accessed=2 * (side * head_dim + tokens) * width, transcendentals=0
         ),
-    )(place, parts, weight, mine, other)
+    )(place, parts, weight, *column)
     partial = exchange(partial, 0)
     return jnp.sum(partial.astype(jnp.float32), axis=0).astype(jnp.bfloat16)
 
@@ -396,14 +405,13 @@
     place = jnp.concatenate([place, core[None]]).astype(jnp.int32)
     far_normed, gain, active = lax.optimization_barrier((partner(normed, bits[-1]), gain, active))
     far_slots = copies_of(far_normed, side)
-    every, far_slots, mine = lax.optimization_barrier(
-        (gather_tokens(slots), far_slots, column_weights(weight, out_weight[0]))
-    )
+    whole, half = column_weights(weight, out_weight[0])
+    every, far_slots, whole = lax.optimization_barrier((gather_tokens(slots), far_slots, whole))
     far_tokens = exchange(far_slots, 0).reshape(-1, width)
     query, own = project(every, weight, gain)
     near = [partner(own, bit) for bit in bits[:-1]]
-    other = partner(mine, 0)
-    far_parts = project_far(place, far_tokens, weight, mine, other, head_dim)
+    column = [whole, partner(whole, 0), half, partner(half, 0)]
+    far_parts = project_far(place, far_tokens, weight, column, head_dim)
     far_parts = exchange(far_parts, 1)
     own_result, state, best = attend_near(active, query, own, near[0])
     far_parts, own_result, state, best, near[1] = lax.optimization_barrier(
@@ -411,7 +419,7 @@
     )
     state, best = attend_middle(active, rounds - 1, query, state, best, settle(far_parts, gain))
     attended = attend_last(active, 1, query, own_result, state, best, near[1])
-    mixed = project_out(place, exchange(attended, 1), out_weight[0], mine, other)
+    mixed = project_out(place, exchange(attended, 1), out_weight[0], column)
     return mixed.reshape(loc_len, view_dev, width)
 
 

time: 113 us -> 111 us (0.982)
  the two profiles are of different devices: /device:TPU:32 before, /device:TPU:128 now
where the time goes in v15:
time: 111 us; the launch traced here: 110 us
  starting transfers between devices  47.5 us (43%)
  blocking collectives  22.9 us (21%)
  Pallas kernels  19.4 us (17%)
  waiting for transfers between devices  15.9 us (14%)
  other arithmetic  3.57 us (3%)
    ppermute x5, starting transfers between devices, partner(): lax.ppermute(array, 'view', [(i, i ^ 1 << bit) for i in range(lax.axis_si...  23.4 us
    all_to_all x2, blocking collectives, exchange(): lax.all_to_all(slots, 'head', split_axis=0, concat_axis=0, tiled=True, ax...  22.9 us
    pallas_call x3, Pallas kernels, call_attend(): pl.pallas_call(kernel, out_shape=out_shape, in_specs=[smem] + [vmem] * (l...  9.23 us
    all_to_all x2, starting transfers between devices, exchange(): lax.all_to_all(slots, 'head', split_axis=0, concat_axis=0, tiled=True, ax...  9.13 us
    ppermute x5, waiting for transfers between devices, partner(): lax.ppermute(array, 'view', [(i, i ^ 1 << bit) for i in range(lax.axis_si...  8.14 us
    all_to_all x1, starting transfers between devices, gather_tokens(): lax.all_to_all(slots, 'head', split_axis=0, concat_axis=0, tiled=True)  7.18 us
    ppermute x1, waiting for transfers between devices, column_weights(): beside = lax.ppermute(packed, ('view', 'head'), pairs)  6.85 us
    ppermute x1, starting transfers between devices, column_weights(): beside = lax.ppermute(packed, ('view', 'head'), pairs)  5.03 us
  transfers between devices with their start and end apart: 10, of which 4 were waited for; matrix products, arithmetic and copies ran while one was open for 3% of the time, Pallas kernels for 9%

profile of v15, /device:TPU:128, one launch (start us, length us, event | category | flops | bytes accessed | tf_op | source)
XLA Modules:
  0.0 110.4 jit_solution(16711094434942325861)
XLA Ops:
  0.0 2.7 %shard_map.64 = (bf16[64,1152]{1,0:T(8,128)(2,1)S(1)}, bf16[16,64,1152]{2,1,0:T(8,128)(2,1)}) custom-call(bf16[64,1152]{1,0:T(8,128)(2,1)} %bitcast.30, f32[1152]{0:T(1024)} %gain_ref.1), custom_call_target="tpu_custom_call" | custom-call | flops 589824 | bytes 2359296 | tf_op jit(solution)/shard_map/pallas_call | solution.py:49
  2.7 7.2 %all-to-all-start = ((bf16[16,64,1152]{2,1,0:T(8,128)(2,1)}), bf16[16,64,1152]{2,1,0:T(8,128)(2,1)S(1)}, u32[]{:S(2)}, u32[]{:S(2)}) async-start(bf16[16,64,1152]{2,1,0:T(8,128)(2,1)} %get-tuple-element.27), calls=%async_computation | async-start | bytes 4718592 | tf_op jit(solution)/shard_map/all_to_all | solution.py:83
  10.1 0.9 pad_maximum_fusion
  11.0 5.0 %collective-permute-start.1 = (bf16[224,1152]{1,0:T(8,128)(2,1)}, bf16[224,1152]{1,0:T(8,128)(2,1)}, u32[]{:S(2)}, u32[]{:S(2)}) collective-permute-start(bf16[224,1152]{1,0:T(8,128)(2,1)} %pad_maximum_fusion), channel_id=1, source_target_pairs={{4,0},{5,1},{6,2},{7,3},{8,4},{9,5},{10,6},{11,7},{12,8},{13,9},{1... | collective-permute-start | bytes 1548296 | tf_op jit(solution)/shard_map/ppermute | solution.py:345
  16.1 10.9 %collective-permute-start = (bf16[64,1152]{1,0:T(8,128)(2,1)S(1)}, bf16[64,1152]{1,0:T(8,128)(2,1)S(1)}, u32[]{:S(2)}, u32[]{:S(2)}) collective-permute-start(bf16[64,1152]{1,0:T(8,128)(2,1)S(1)} %get-tuple-element.25), channel_id=1, source_target_pairs={{0,256},{16,272},{32,288},{48,304},{64,320},{80,336},{96,352},{112... | collective-permute-start | bytes 442376 | tf_op jit(solution)/shard_map/ppermute | solution.py:14
  27.0 1.7 %slice_select_fusion = bf16[112,1152]{1,0:T(8,128)(2,1)} fusion(bf16[224,1152]{1,0:T(8,128)(2,1)} %pad_maximum_fusion, bf16[1,216,1152]{2,1,0:T(8,128)(2,1)S(1)} %copy-done, pred[]{:T(512)S(6)} %eq.9), kind=kLoop, calls=%fused_computation.2 | loop fusion | flops 129024 | bytes 774145 | tf_op jit(solution)/shard_map/jit(_where)/select_n | solution.py:346
  28.7 2.8 %collective-permute-start.3 = (bf16[112,1152]{1,0:T(8,128)(2,1)}, bf16[112,1152]{1,0:T(8,128)(2,1)}, u32[]{:S(2)}, u32[]{:S(2)}) collective-permute-start(bf16[112,1152]{1,0:T(8,128)(2,1)} %slice_select_fusion), channel_id=1, source_target_pairs={{0,8},{1,9},{2,10},{3,11},{4,12},{5,13},{6,14},{7,15},{8,0},{9,1},... | collective-permute-start | bytes 774152 | tf_op jit(solution)/shard_map/ppermute | solution.py:348
  31.6 6.6 %collective-permute-done.source_ref = bf16[64,1152]{1,0:T(8,128)(2,1)S(1)} collective-permute-done((bf16[64,1152]{1,0:T(8,128)(2,1)S(1)}, bf16[64,1152]{1,0:T(8,128)(2,1)S(1)}, u32[]{:S(2)}, u32[]{:S(2)}) %collective-permute-start) | collective-permute-done | bytes 147488 | tf_op jit(solution)/shard_map/ppermute | solution.py:14
  39.1 6.8 %collective-permute-done.1.mine_ref = bf16[224,1152]{1,0:T(8,128)(2,1)} collective-permute-done((bf16[224,1152]{1,0:T(8,128)(2,1)}, bf16[224,1152]{1,0:T(8,128)(2,1)}, u32[]{:S(2)}, u32[]{:S(2)}) %collective-permute-start.1) | collective-permute-done | bytes 516128 | tf_op jit(solution)/shard_map/ppermute | solution.py:345
  45.9 2.9 %collective-permute-start.2 = (bf16[224,1152]{1,0:T(8,128)(2,1)}, bf16[224,1152]{1,0:T(8,128)(2,1)}, u32[]{:S(2)}, u32[]{:S(2)}) collective-permute-start(bf16[224,1152]{1,0:T(8,128)(2,1)} %collective-permute-done.1.mine_ref), channel_id=1, source_target_pairs={{0,16},{16,0},{32,48},{48,32},{64,80},{80,64},{96,112},{112,96},{1... | collective-permute-start | bytes 1548296 | tf_op jit(solution)/shard_map/ppermute | solution.py:14
  48.8 4.2 %all-to-all-start.1 = ((bf16[4,64,1152]{2,1,0:T(8,128)(2,1)}), bf16[4,64,1152]{2,1,0:T(8,128)(2,1)S(1)}, u32[]{:S(2)}, u32[]{:S(2)}) async-start(bf16[4,64,1152]{2,1,0:T(8,128)(2,1)} %shard_map.65), calls=%async_computation.1 | async-start | bytes 1179648 | tf_op jit(solution)/shard_map/all_to_all | solution.py:328
  53.1 1.9 %collective-permute-start.4 = (bf16[112,1152]{1,0:T(8,128)(2,1)}, bf16[112,1152]{1,0:T(8,128)(2,1)}, u32[]{:S(2)}, u32[]{:S(2)}) collective-permute-start(bf16[112,1152]{1,0:T(8,128)(2,1)} %collective-permute-done.3.mine_half_ref), channel_id=1, source_target_pairs={{0,16},{16,0},{32,48},{48,32},{64,80},{80,64},{96,112},{112,96},{1... | collective-permute-start | bytes 774152 | tf_op jit(solution)/shard_map/ppermute | solution.py:14
  55.0 1.7 %shard_map.66 = (bf16[72,1024]{1,0:T(8,128)(2,1)S(1)}, bf16[144,1024]{1,0:T(8,128)(2,1)}) custom-call(bf16[1024,1152]{1,0:T(8,128)(2,1)S(1)} %bitcast.19, bf16[216,1152]{1,0:T(8,128)(2,1)S(1)} %bitcast.20, f32[72,2]{1,0:T(8,128)S(1)} %bitcast.25), custom_call_target="tpu_custom_call" | custom-call | flops 509607936 | bytes 2359296 | tf_op jit(solution)/shard_map/pallas_call | solution.py:107
  57.3 2.5 %collective-permute-start.5 = (bf16[144,1024]{1,0:T(8,128)(2,1)}, bf16[144,1024]{1,0:T(8,128)(2,1)S(1)}, u32[]{:S(2)}, u32[]{:S(2)}) collective-permute-start(bf16[144,1024]{1,0:T(8,128)(2,1)} %get-tuple-element.34.own_ref), channel_id=1, source_target_pairs={{0,16},{16,0},{32,48},{48,32},{64,80},{80,64},{96,112},{112,96},{1... | collective-permute-start | bytes 884744 | tf_op jit(solution)/shard_map/ppermute | solution.py:14
  60.0 5.2 %collective-permute-start.6 = (bf16[144,1024]{1,0:T(8,128)(2,1)}, bf16[144,1024]{1,0:T(8,128)(2,1)S(1)}, u32[]{:S(2)}, u32[]{:S(2)}) collective-permute-start(bf16[144,1024]{1,0:T(8,128)(2,1)} %get-tuple-element.34.own_ref), channel_id=1, source_target_pairs={{0,64},{16,80},{32,96},{48,112},{64,0},{80,16},{96,32},{112,48},{1... | collective-permute-start | bytes 884744 | tf_op jit(solution)/shard_map/ppermute | solution.py:14
  65.2 2.7 %shard_map.67 = bf16[4,144,256]{2,1,0:T(8,128)(2,1)} custom-call(s32[5]{0:T(128)S(1)} %pad_add_fusion.place_ref, bf16[256,1152]{1,0:T(8,128)(2,1)S(1)} %bitcast.22, bf16[216,1152]{1,0:T(8,128)(2,1)S(1)} %bitcast.21, bf16[224,1152]{1,0:T(8,128)(2,1)} %collective-permute-done.1.mine_ref, bf16[224,1152]{1,0:T(8,128)(2,1)} %collective-permute-done.2.other_ref, ...), custom_call_target="tpu_custom_call" | custom-call | flops 509607936 | bytes 1179648 | tf_op jit(solution)/shard_map/pallas_call | solution.py:156
  68.0 4.9 %all-to-all-start.2 = ((bf16[4,144,256]{2,1,0:T(8,128)(2,1)}), bf16[4,144,256]{2,1,0:T(8,128)(2,1)S(1)}, u32[]{:S(2)}, u32[]{:S(2)}) async-start(bf16[4,144,256]{2,1,0:T(8,128)(2,1)} %shard_map.67), calls=%async_computation.2 | async-start | bytes 589824 | tf_op jit(solution)/shard_map/all_to_all | solution.py:328
  72.9 4.5 %shard_map.68 = (f32[72,1024]{1,0:T(8,128)S(1)}, f32[80,1024]{1,0:T(8,128)S(1)}, f32[1,1024]{1,0:T(1,128)S(1)}) custom-call(s32[3]{0:T(128)S(1)} %bitcast.27, bf16[72,1024]{1,0:T(8,128)(2,1)S(1)} %copy-done.4, bf16[144,1024]{1,0:T(8,128)(2,1)} %get-tuple-element.34.own_ref, bf16[144,1024]{1,0:T(8,128)(2,1)S(1)} %collective-permute-done.5.far_ref), custom_call_target="tpu_custom_call" | custom-call | flops 2147483648 | bytes 589824 | tf_op jit(solution)/shard_map/pallas_call | solution.py:279
  77.3 1.5 %collective-permute-done.6.far_ref = bf16[144,1024]{1,0:T(8,128)(2,1)S(1)} collective-permute-done((bf16[144,1024]{1,0:T(8,128)(2,1)}, bf16[144,1024]{1,0:T(8,128)(2,1)S(1)}, u32[]{:S(2)}, u32[]{:S(2)}) %collective-permute-start.6) | collective-permute-done | bytes 294944 | tf_op jit(solution)/shard_map/ppermute | solution.py:14
  79.9 2.4 %shard_map.70 = (f32[80,1024]{1,0:T(8,128)S(1)}, f32[1,1024]{1,0:T(1,128)S(1)}) custom-call(s32[3]{0:T(128)S(1)} %bitcast.28, bf16[72,1024]{1,0:T(8,128)(2,1)S(1)} %copy-done.4, f32[80,1024]{1,0:T(8,128)S(1)} %get-tuple-element.39.state_ref, f32[1,1024]{1,0:T(1,128)S(1)} %get-tuple-element.40.best_ref, bf16[144,1024]{1,0:T(8,128)(2,1)S(1)} %shard_map.69.far_ref), custom_call_target="tpu_custom_call" | custom-call | flops 1073741824 | bytes 294912 | tf_op jit(solution)/shard_map/pallas_call | solution.py:279
  82.3 2.4 %shard_map.71 = bf16[4,72,256]{2,1,0:T(8,128)(2,1)S(1)} custom-call(s32[3]{0:T(128)S(1)} %bitcast.29, bf16[72,1024]{1,0:T(8,128)(2,1)S(1)} %copy-done.4, f32[72,1024]{1,0:T(8,128)S(1)} %get-tuple-element.38.own_in_ref, f32[80,1024]{1,0:T(8,128)S(1)} %get-tuple-element.42.state_ref, f32[1,1024]{1,0:T(1,128)S(1)} %get-tuple-element.43.best_ref, ...), custom_call_target="tpu_custom_call" | custom-call | flops 1073741824 | bytes 294912 | tf_op jit(solution)/shard_map/pallas_call | solution.py:279
  84.6 9.8 %all_to_all.25.parts_ref = bf16[4,72,256]{2,1,0:T(8,128)(2,1)S(1)} all-to-all(bf16[4,72,256]{2,1,0:T(8,128)(2,1)S(1)} %shard_map.71), channel_id=1, replica_groups={{0,4,8,12},{1,5,9,13},{2,6,10,14},{3,7,11,15},{16,20,24,28},{17,21,25,2..., dimensions={0} | all-to-all | bytes 294912 | tf_op jit(solution)/shard_map/all_to_all | solution.py:328
  94.5 2.1 %shard_map.72 = bf16[4,64,1152]{2,1,0:T(8,128)(2,1)S(1)} custom-call(s32[5]{0:T(128)S(1)} %pad_add_fusion.place_ref, bf16[4,72,256]{2,1,0:T(8,128)(2,1)S(1)} %all_to_all.25.parts_ref, bf16[72,1152]{1,0:T(8,128)(2,1)S(1)} %bitcast.24, bf16[224,1152]{1,0:T(8,128)(2,1)} %collective-permute-done.1.mine_ref, bf16[224,1152]{1,0:T(8,128)(2,1)} %collective-permute-done.2.other_ref, ...), custom_call_target="tpu_custom_call" | custom-call | flops 169869312 | bytes 1253376 | tf_op jit(solution)/shard_map/pallas_call | solution.py:375
  96.6 13.0 %all_to_all.26 = bf16[4,64,1152]{2,1,0:T(8,128)(2,1)S(1)} all-to-all(bf16[4,64,1152]{2,1,0:T(8,128)(2,1)S(1)} %shard_map.72), channel_id=1, replica_groups={{0,1,2,3},{4,5,6,7},{8,9,10,11},{12,13,14,15},{16,17,18,19},{20,21,22,2..., dimensions={0} | all-to-all | bytes 1179648 | tf_op jit(solution)/shard_map/all_to_all | solution.py:328
  (30 shorter events, 3.7 us)
Async XLA Ops:
  2.7 7.3 %copy-start = (bf16[1,216,1152]{2,1,0:T(8,128)(2,1)S(1)}, bf16[1,216,1152]{2,1,0:T(8,128)(2,1)}, u32[]{:S(2)}) copy-start(bf16[1,216,1152]{2,1,0:T(8,128)(2,1)} %param.8) | copy-start | bytes 1492996
  2.7 7.3 %copy-start.1 = (bf16[1,72,1152]{2,1,0:T(8,128)(2,1)S(1)}, bf16[1,72,1152]{2,1,0:T(8,128)(2,1)}, u32[]{:S(2)}) copy-start(bf16[1,72,1152]{2,1,0:T(8,128)(2,1)} %param.10) | copy-start | bytes 497668
  2.7 43.2 %all-to-all-start = ((bf16[16,64,1152]{2,1,0:T(8,128)(2,1)}), bf16[16,64,1152]{2,1,0:T(8,128)(2,1)S(1)}, u32[]{:S(2)}, u32[]{:S(2)}) async-start(bf16[16,64,1152]{2,1,0:T(8,128)(2,1)} %get-tuple-element.27), calls=%async_computation | async-start | bytes 4718592 | tf_op jit(solution)/shard_map/all_to_all | solution.py:83
  9.9 21.5 %copy-start.6 = (f32[1,2,72]{2,1,0:T(2,128)S(1)}, f32[1,2,72]{2,1,0:T(2,128)}, u32[]{:S(2)}) copy-start(f32[1,2,72]{2,1,0:T(2,128)} %param.9) | copy-start | bytes 1732
  11.0 34.9 %collective-permute-start.1 = (bf16[224,1152]{1,0:T(8,128)(2,1)}, bf16[224,1152]{1,0:T(8,128)(2,1)}, u32[]{:S(2)}, u32[]{:S(2)}) collective-permute-start(bf16[224,1152]{1,0:T(8,128)(2,1)} %pad_maximum_fusion), channel_id=1, source_target_pairs={{4,0},{5,1},{6,2},{7,3},{8,4},{9,5},{10,6},{11,7},{12,8},{13,9},{1... | collective-permute-start | bytes 1548296 | tf_op jit(solution)/shard_map/ppermute | solution.py:345
  16.1 22.1 %collective-permute-start = (bf16[64,1152]{1,0:T(8,128)(2,1)S(1)}, bf16[64,1152]{1,0:T(8,128)(2,1)S(1)}, u32[]{:S(2)}, u32[]{:S(2)}) collective-permute-start(bf16[64,1152]{1,0:T(8,128)(2,1)S(1)} %get-tuple-element.25), channel_id=1, source_target_pairs={{0,256},{16,272},{32,288},{48,304},{64,320},{80,336},{96,352},{112... | collective-permute-start | bytes 442376 | tf_op jit(solution)/shard_map/ppermute | solution.py:14
  28.7 24.4 %collective-permute-start.3 = (bf16[112,1152]{1,0:T(8,128)(2,1)}, bf16[112,1152]{1,0:T(8,128)(2,1)}, u32[]{:S(2)}, u32[]{:S(2)}) collective-permute-start(bf16[112,1152]{1,0:T(8,128)(2,1)} %slice_select_fusion), channel_id=1, source_target_pairs={{0,8},{1,9},{2,10},{3,11},{4,12},{5,13},{6,14},{7,15},{8,0},{9,1},... | collective-permute-start | bytes 774152 | tf_op jit(solution)/shard_map/ppermute | solution.py:348
  45.9 19.3 %collective-permute-start.2 = (bf16[224,1152]{1,0:T(8,128)(2,1)}, bf16[224,1152]{1,0:T(8,128)(2,1)}, u32[]{:S(2)}, u32[]{:S(2)}) collective-permute-start(bf16[224,1152]{1,0:T(8,128)(2,1)} %collective-permute-done.1.mine_ref), channel_id=1, source_target_pairs={{0,16},{16,0},{32,48},{48,32},{64,80},{80,64},{96,112},{112,96},{1... | collective-permute-start | bytes 1548296 | tf_op jit(solution)/shard_map/ppermute | solution.py:14
  48.8 16.4 %all-to-all-start.1 = ((bf16[4,64,1152]{2,1,0:T(8,128)(2,1)}), bf16[4,64,1152]{2,1,0:T(8,128)(2,1)S(1)}, u32[]{:S(2)}, u32[]{:S(2)}) async-start(bf16[4,64,1152]{2,1,0:T(8,128)(2,1)} %shard_map.65), calls=%async_computation.1 | async-start | bytes 1179648 | tf_op jit(solution)/shard_map/all_to_all | solution.py:328
  53.1 12.2 %collective-permute-start.4 = (bf16[112,1152]{1,0:T(8,128)(2,1)}, bf16[112,1152]{1,0:T(8,128)(2,1)}, u32[]{:S(2)}, u32[]{:S(2)}) collective-permute-start(bf16[112,1152]{1,0:T(8,128)(2,1)} %collective-permute-done.3.mine_half_ref), channel_id=1, source_target_pairs={{0,16},{16,0},{32,48},{48,32},{64,80},{80,64},{96,112},{112,96},{1... | collective-permute-start | bytes 774152 | tf_op jit(solution)/shard_map/ppermute | solution.py:14
  56.6 0.7 copy-start.3
  57.3 15.5 %copy-start.5 = (s32[3,1]{0,1:T(1,128)S(1)}, s32[3,1]{0,1:T(1,128)}, u32[]{:S(2)}) copy-start(s32[3,1]{0,1:T(1,128)} %param.11) | copy-start | bytes 40
  57.3 15.5 %copy-start.4 = (bf16[72,1024]{1,0:T(8,128)(2,1)S(1)}, bf16[72,1024]{1,0:T(8,128)(2,1)}, u32[]{:S(2)}) copy-start(bf16[72,1024]{1,0:T(8,128)(2,1)} %copy-done.3) | copy-start | bytes 442372
  57.3 15.5 %collective-permute-start.5 = (bf16[144,1024]{1,0:T(8,128)(2,1)}, bf16[144,1024]{1,0:T(8,128)(2,1)S(1)}, u32[]{:S(2)}, u32[]{:S(2)}) collective-permute-start(bf16[144,1024]{1,0:T(8,128)(2,1)} %get-tuple-element.34.own_ref), channel_id=1, source_target_pairs={{0,16},{16,0},{32,48},{48,32},{64,80},{80,64},{96,112},{112,96},{1... | collective-permute-start | bytes 884744 | tf_op jit(solution)/shard_map/ppermute | solution.py:14
  60.0 18.9 %collective-permute-start.6 = (bf16[144,1024]{1,0:T(8,128)(2,1)}, bf16[144,1024]{1,0:T(8,128)(2,1)S(1)}, u32[]{:S(2)}, u32[]{:S(2)}) collective-permute-start(bf16[144,1024]{1,0:T(8,128)(2,1)} %get-tuple-element.34.own_ref), channel_id=1, source_target_pairs={{0,64},{16,80},{32,96},{48,112},{64,0},{80,16},{96,32},{112,48},{1... | collective-permute-start | bytes 884744 | tf_op jit(solution)/shard_map/ppermute | solution.py:14
  68.0 11.8 %all-to-all-start.2 = ((bf16[4,144,256]{2,1,0:T(8,128)(2,1)}), bf16[4,144,256]{2,1,0:T(8,128)(2,1)S(1)}, u32[]{:S(2)}, u32[]{:S(2)}) async-start(bf16[4,144,256]{2,1,0:T(8,128)(2,1)} %shard_map.67), calls=%async_computation.2 | async-start | bytes 589824 | tf_op jit(solution)/shard_map/all_to_all | solution.py:328
  82.3 12.2 %copy-start.2 = (bf16[1,72,1152]{2,1,0:T(8,128)(2,1)S(1)}, bf16[1,72,1152]{2,1,0:T(8,128)(2,1)}, u32[]{:S(2)}) copy-start(bf16[1,72,1152]{2,1,0:T(8,128)(2,1)} %param.10) | copy-start | bytes 497668

commit v16 on v15

--- a/solution.py
+++ b/solution.py
@@ -263,7 +263,8 @@
         on = active_ref[which] > 0
         _, factor, term = cross_update(on, scores, values_ref[...], best_ref[:, columns])
         cross = finish(state_ref[:, columns] * factor + term, head_dim)
-        result = (own_in_ref[:, columns] + cross).astype(jnp.bfloat16)
+        blank = jnp.zeros((out_ref.shape[1] - head_dim, tile), jnp.float32)
+        result = jnp.concatenate([own_in_ref[:, columns] + cross, blank], axis=0).astype(jnp.bfloat16)
         for n in range(tile // block):
             out_ref[at * (tile // block) + n] = result[:, n * block : (n + 1) * block]
 
@@ -312,7 +313,7 @@
 def attend_last(active, which, query, own_result, state, best, far):
     head_dim, tokens = query.shape
     side = len(groups(0))
-    out_shape = jax.ShapeDtypeStruct((side, head_dim, tokens // side), jnp.bfloat16)
+    out_shape = jax.ShapeDtypeStruct((side, head_dim + PAD, tokens // side), jnp.bfloat16)
     kernel = functools.partial(last_kernel, tokens // 2, which)
     return call_attend(kernel, out_shape, 1, (active, query, own_result, state, best, far))
 
@@ -345,43 +346,46 @@
     beside = lax.ppermute(packed, ("view", "head"), pairs)
     sent = jnp.where(core == 0, packed[:part], packed[part:])
     across = [(head, (head + heads // 2) % heads) for head in range(heads)]
-    return beside, lax.ppermute(sent, "head", across)
+    return packed, beside, lax.ppermute(sent, "head", across)
 
 
 def project_out_kernel(
     place_ref, parts_ref, weight_ref, mine_ref, other_ref, mine_half_ref, other_half_ref, out_ref
 ):
-    head_dim = weight_ref.shape[0]
-
-    def rows_at(ref):
-        return ref[: head_dim + PAD].astype(jnp.float32)[:head_dim]
-
-    first, second = rows_at(mine_half_ref), rows_at(other_half_ref)
-    far = jnp.where(place_ref[4] == 0, first, second)
-    weights = [rows_at(mine_ref), rows_at(other_ref), far]
+    wide = parts_ref.shape[1]
+    far = parts_ref[place_ref[3]].astype(jnp.float32)
+    blank = jnp.zeros_like(far)
+    first = jnp.where(place_ref[4] == 0, far, blank).astype(jnp.bfloat16)
+    second = jnp.where(place_ref[4] == 0, blank, far).astype(jnp.bfloat16)
     total = None
-    for n, weight in enumerate([weight_ref[...]] + [rows.astype(jnp.bfloat16) for rows in weights]):
+    for part, rows_ref in (
+        (parts_ref[place_ref[0]], weight_ref),
+        (parts_ref[place_ref[1]], mine_ref),
+        (parts_ref[place_ref[2]], other_ref),
+        (first, mine_half_ref),
+        (second, other_half_ref),
+    ):
         term = lax.dot_general(
-            parts_ref[place_ref[n]], weight, (((0,), (0,)), ((), ())), preferred_element_type=jnp.float32
+            part, rows_ref[:wide], (((0,), (0,)), ((), ())), preferred_element_type=jnp.float32
         )
         total = term if total is None else total + term
     out_ref[...] = total.reshape(out_ref.shape).astype(jnp.bfloat16)
 
 
-def project_out(place, parts, weight, column):
-    side, head_dim, tokens = parts.shape
-    width = weight.shape[1]
+def project_out(place, parts, column):
+    side, wide, tokens = parts.shape
+    width = column[0].shape[1]
     smem, vmem = pl.BlockSpec(memory_space=pltpu.SMEM), pl.BlockSpec(memory_space=pltpu.VMEM)
     partial = pl.pallas_call(
         project_out_kernel,
         out_shape=jax.ShapeDtypeStruct((side, tokens // side, width), jnp.bfloat16),
-        in_specs=[smem] + [vmem] * (2 + len(column)),
+        in_specs=[smem] + [vmem] * (1 + len(column)),
         out_specs=vmem,
         compiler_params=pltpu.CompilerParams(vmem_limit_bytes=16 << 20),
         cost_estimate=pl.CostEstimate(
-            flops=2 * parts.size * width, bytes_accessed=2 * (side * head_dim + tokens) * width, transcendentals=0
-        ),
-    )(place, parts, weight, *column)
+            flops=2 * parts.size * width, bytes_accessed=2 * (side * wide + tokens) * width, transcendentals=0
+        ),
+    )(place, parts, *column)
     partial = exchange(partial, 0)
     return jnp.sum(partial.astype(jnp.float32), axis=0).astype(jnp.bfloat16)
 
@@ -405,7 +409,7 @@
     place = jnp.concatenate([place, core[None]]).astype(jnp.int32)
     far_normed, gain, active = lax.optimization_barrier((partner(normed, bits[-1]), gain, active))
     far_slots = copies_of(far_normed, side)
-    whole, half = column_weights(weight, out_weight[0])
+    packed, whole, half = column_weights(weight, out_weight[0])
     every, far_slots, whole = lax.optimization_barrier((gather_tokens(slots), far_slots, whole))
     far_tokens = exchange(far_slots, 0).reshape(-1, width)
     query, own = project(every, weight, gain)
@@ -419,7 +423,7 @@
     )
     state, best = attend_middle(active, rounds - 1, query, state, best, settle(far_parts, gain))
     attended = attend_last(active, 1, query, own_result, state, best, near[1])
-    mixed = project_out(place, exchange(attended, 1), out_weight[0], column)
+    mixed = project_out(place, exchange(attended, 1), [packed] + column)
     return mixed.reshape(loc_len, view_dev, width)
 
 

time: 111 us -> 112 us (level)
  Pallas kernels: 19.4 us -> 21.4 us
    ppermute x1, waiting for transfers between devices: 6.85 us -> 5.48 us  [column_weights(): beside = lax.ppermute(packed, ('view', 'head'), pairs)]
  transfers between devices with their start and end apart: 10 -> 10, of which waited for: 4 -> 4; matrix products, arithmetic and copies ran while one was open for 3% -> 2% of each run, Pallas kernels for 9% -> 10%
where the time goes in v16:
time: 112 us; the launch traced here: 111 us
  starting transfers between devices  47.5 us (42%)
  blocking collectives  22.8 us (20%)
  Pallas kernels  21.4 us (19%)
  waiting for transfers between devices  15.8 us (14%)
  other arithmetic  2.74 us (2%)
    ppermute x5, starting transfers between devices, partner(): lax.ppermute(array, 'view', [(i, i ^ 1 << bit) for i in range(lax.axis_si...  23.4 us
    all_to_all x2, blocking collectives, exchange(): lax.all_to_all(slots, 'head', split_axis=0, concat_axis=0, tiled=True, ax...  22.8 us
    pallas_call x3, Pallas kernels, call_attend(): pl.pallas_call(kernel, out_shape=out_shape, in_specs=[smem] + [vmem] * (l...  9.24 us
    ppermute x5, waiting for transfers between devices, partner(): lax.ppermute(array, 'view', [(i, i ^ 1 << bit) for i in range(lax.axis_si...  9.18 us
    all_to_all x2, starting transfers between devices, exchange(): lax.all_to_all(slots, 'head', split_axis=0, concat_axis=0, tiled=True, ax...  9.13 us
    all_to_all x1, starting transfers between devices, gather_tokens(): lax.all_to_all(slots, 'head', split_axis=0, concat_axis=0, tiled=True)  7.18 us
    ppermute x1, waiting for transfers between devices, column_weights(): beside = lax.ppermute(packed, ('view', 'head'), pairs)  5.48 us
    ppermute x1, starting transfers between devices, column_weights(): beside = lax.ppermute(packed, ('view', 'head'), pairs)  5.05 us
  transfers between devices with their start and end apart: 10, of which 4 were waited for; matrix products, arithmetic and copies ran while one was open for 2% of the time, Pallas kernels for 10%

profile of v16, /device:TPU:128, one launch (start us, length us, event | category | flops | bytes accessed | tf_op | source)
XLA Modules:
  0.0 111.3 jit_solution(829801396884001262)
XLA Ops:
  0.0 3.4 %shard_map.64 = (bf16[64,1152]{1,0:T(8,128)(2,1)}, bf16[16,64,1152]{2,1,0:T(8,128)(2,1)}) custom-call(bf16[64,1152]{1,0:T(8,128)(2,1)} %bitcast.28, f32[1152]{0:T(1024)} %gain_ref.1), custom_call_target="tpu_custom_call" | custom-call | flops 589824 | bytes 2359296 | tf_op jit(solution)/shard_map/pallas_call | solution.py:49
  3.4 7.2 %all-to-all-start = ((bf16[16,64,1152]{2,1,0:T(8,128)(2,1)}), bf16[16,64,1152]{2,1,0:T(8,128)(2,1)S(1)}, u32[]{:S(2)}, u32[]{:S(2)}) async-start(bf16[16,64,1152]{2,1,0:T(8,128)(2,1)} %get-tuple-element.27), calls=%async_computation | async-start | bytes 4718592 | tf_op jit(solution)/shard_map/all_to_all | solution.py:83
  11.8 5.0 %collective-permute-start.1 = (bf16[224,1152]{1,0:T(8,128)(2,1)S(1)}, bf16[224,1152]{1,0:T(8,128)(2,1)}, u32[]{:S(2)}, u32[]{:S(2)}) collective-permute-start(bf16[224,1152]{1,0:T(8,128)(2,1)S(1)} %pad_maximum_fusion.weight_ref), channel_id=1, source_target_pairs={{4,0},{5,1},{6,2},{7,3},{8,4},{9,5},{10,6},{11,7},{12,8},{13,9},{1... | collective-permute-start | bytes 1548296 | tf_op jit(solution)/shard_map/ppermute | solution.py:346
  16.8 10.9 %collective-permute-start = (bf16[64,1152]{1,0:T(8,128)(2,1)}, bf16[64,1152]{1,0:T(8,128)(2,1)}, u32[]{:S(2)}, u32[]{:S(2)}) collective-permute-start(bf16[64,1152]{1,0:T(8,128)(2,1)} %get-tuple-element.25), channel_id=1, source_target_pairs={{0,256},{16,272},{32,288},{48,304},{64,320},{80,336},{96,352},{112... | collective-permute-start | bytes 442376 | tf_op jit(solution)/shard_map/ppermute | solution.py:14
  28.5 2.8 %collective-permute-start.3 = (bf16[112,1152]{1,0:T(8,128)(2,1)}, bf16[112,1152]{1,0:T(8,128)(2,1)}, u32[]{:S(2)}, u32[]{:S(2)}) collective-permute-start(bf16[112,1152]{1,0:T(8,128)(2,1)} %slice_select_fusion), channel_id=1, source_target_pairs={{0,8},{1,9},{2,10},{3,11},{4,12},{5,13},{6,14},{7,15},{8,0},{9,1},... | collective-permute-start | bytes 774152 | tf_op jit(solution)/shard_map/ppermute | solution.py:349
  31.4 7.9 %collective-permute-done.source_ref = bf16[64,1152]{1,0:T(8,128)(2,1)} collective-permute-done((bf16[64,1152]{1,0:T(8,128)(2,1)}, bf16[64,1152]{1,0:T(8,128)(2,1)}, u32[]{:S(2)}, u32[]{:S(2)}) %collective-permute-start) | collective-permute-done | bytes 147488 | tf_op jit(solution)/shard_map/ppermute | solution.py:14
  39.3 1.8 %shard_map.65 = bf16[4,64,1152]{2,1,0:T(8,128)(2,1)} custom-call(bf16[64,1152]{1,0:T(8,128)(2,1)} %collective-permute-done.source_ref), custom_call_target="tpu_custom_call" | custom-call | bytes 589824 | tf_op jit(solution)/shard_map/pallas_call | solution.py:71
  41.1 5.5 %collective-permute-done.1.mine_ref = bf16[224,1152]{1,0:T(8,128)(2,1)} collective-permute-done((bf16[224,1152]{1,0:T(8,128)(2,1)S(1)}, bf16[224,1152]{1,0:T(8,128)(2,1)}, u32[]{:S(2)}, u32[]{:S(2)}) %collective-permute-start.1) | collective-permute-done | bytes 516128 | tf_op jit(solution)/shard_map/ppermute | solution.py:346
  46.6 2.9 %collective-permute-start.2 = (bf16[224,1152]{1,0:T(8,128)(2,1)}, bf16[224,1152]{1,0:T(8,128)(2,1)}, u32[]{:S(2)}, u32[]{:S(2)}) collective-permute-start(bf16[224,1152]{1,0:T(8,128)(2,1)} %collective-permute-done.1.mine_ref), channel_id=1, source_target_pairs={{0,16},{16,0},{32,48},{48,32},{64,80},{80,64},{96,112},{112,96},{1... | collective-permute-start | bytes 1548296 | tf_op jit(solution)/shard_map/ppermute | solution.py:14
  49.5 4.2 %all-to-all-start.1 = ((bf16[4,64,1152]{2,1,0:T(8,128)(2,1)}), bf16[4,64,1152]{2,1,0:T(8,128)(2,1)}, u32[]{:S(2)}, u32[]{:S(2)}) async-start(bf16[4,64,1152]{2,1,0:T(8,128)(2,1)} %shard_map.65), calls=%async_computation.1 | async-start | bytes 1179648 | tf_op jit(solution)/shard_map/all_to_all | solution.py:329
  53.7 1.9 %collective-permute-start.4 = (bf16[112,1152]{1,0:T(8,128)(2,1)}, bf16[112,1152]{1,0:T(8,128)(2,1)}, u32[]{:S(2)}, u32[]{:S(2)}) collective-permute-start(bf16[112,1152]{1,0:T(8,128)(2,1)} %collective-permute-done.3.mine_half_ref), channel_id=1, source_target_pairs={{0,16},{16,0},{32,48},{48,32},{64,80},{80,64},{96,112},{112,96},{1... | collective-permute-start | bytes 774152 | tf_op jit(solution)/shard_map/ppermute | solution.py:14
  55.6 1.7 %shard_map.66 = (bf16[72,1024]{1,0:T(8,128)(2,1)S(1)}, bf16[144,1024]{1,0:T(8,128)(2,1)}) custom-call(bf16[1024,1152]{1,0:T(8,128)(2,1)S(1)} %bitcast.19, bf16[216,1152]{1,0:T(8,128)(2,1)S(1)} %bitcast.20, f32[72,2]{1,0:T(8,128)S(1)} %bitcast.22), custom_call_target="tpu_custom_call" | custom-call | flops 509607936 | bytes 2359296 | tf_op jit(solution)/shard_map/pallas_call | solution.py:107
  58.0 2.5 %collective-permute-start.5 = (bf16[144,1024]{1,0:T(8,128)(2,1)}, bf16[144,1024]{1,0:T(8,128)(2,1)S(1)}, u32[]{:S(2)}, u32[]{:S(2)}) collective-permute-start(bf16[144,1024]{1,0:T(8,128)(2,1)} %get-tuple-element.34.own_ref), channel_id=1, source_target_pairs={{0,16},{16,0},{32,48},{48,32},{64,80},{80,64},{96,112},{112,96},{1... | collective-permute-start | bytes 884744 | tf_op jit(solution)/shard_map/ppermute | solution.py:14
  60.6 5.2 %collective-permute-start.6 = (bf16[144,1024]{1,0:T(8,128)(2,1)}, bf16[144,1024]{1,0:T(8,128)(2,1)S(1)}, u32[]{:S(2)}, u32[]{:S(2)}) collective-permute-start(bf16[144,1024]{1,0:T(8,128)(2,1)} %get-tuple-element.34.own_ref), channel_id=1, source_target_pairs={{0,64},{16,80},{32,96},{48,112},{64,0},{80,16},{96,32},{112,48},{1... | collective-permute-start | bytes 884744 | tf_op jit(solution)/shard_map/ppermute | solution.py:14
  65.9 2.9 %shard_map.67 = bf16[4,144,256]{2,1,0:T(8,128)(2,1)} custom-call(s32[5]{0:T(128)S(1)} %pad_add_fusion.place_ref, bf16[256,1152]{1,0:T(8,128)(2,1)} %bitcast.13.rows_ref, bf16[216,1152]{1,0:T(8,128)(2,1)S(1)} %bitcast.21, bf16[224,1152]{1,0:T(8,128)(2,1)} %collective-permute-done.1.mine_ref, bf16[224,1152]{1,0:T(8,128)(2,1)} %collective-permute-done.2.other_ref, ...), custom_call_target="tpu_custom_call" | custom-call | flops 509607936 | bytes 1179648 | tf_op jit(solution)/shard_map/pallas_call | solution.py:156
  68.8 4.9 %all-to-all-start.2 = ((bf16[4,144,256]{2,1,0:T(8,128)(2,1)}), bf16[4,144,256]{2,1,0:T(8,128)(2,1)S(1)}, u32[]{:S(2)}, u32[]{:S(2)}) async-start(bf16[4,144,256]{2,1,0:T(8,128)(2,1)} %shard_map.67), calls=%async_computation.2 | async-start | bytes 589824 | tf_op jit(solution)/shard_map/all_to_all | solution.py:329
  73.7 4.5 %shard_map.68 = (f32[72,1024]{1,0:T(8,128)S(1)}, f32[80,1024]{1,0:T(8,128)S(1)}, f32[1,1024]{1,0:T(1,128)S(1)}) custom-call(s32[3]{0:T(128)S(1)} %bitcast.24, bf16[72,1024]{1,0:T(8,128)(2,1)S(1)} %copy-done.2, bf16[144,1024]{1,0:T(8,128)(2,1)} %get-tuple-element.34.own_ref, bf16[144,1024]{1,0:T(8,128)(2,1)S(1)} %collective-permute-done.5.far_ref), custom_call_target="tpu_custom_call" | custom-call | flops 2147483648 | bytes 589824 | tf_op jit(solution)/shard_map/pallas_call | solution.py:280
  78.2 1.3 %collective-permute-done.6.far_ref = bf16[144,1024]{1,0:T(8,128)(2,1)S(1)} collective-permute-done((bf16[144,1024]{1,0:T(8,128)(2,1)}, bf16[144,1024]{1,0:T(8,128)(2,1)S(1)}, u32[]{:S(2)}, u32[]{:S(2)}) %collective-permute-start.6) | collective-permute-done | bytes 294944 | tf_op jit(solution)/shard_map/ppermute | solution.py:14
  79.5 1.1 %all-to-all-done.2.parts_ref = bf16[4,144,256]{2,1,0:T(8,128)(2,1)S(1)} async-done(((bf16[4,144,256]{2,1,0:T(8,128)(2,1)}), bf16[4,144,256]{2,1,0:T(8,128)(2,1)S(1)}, u32[]{:S(2)}, u32[]{:S(2)}) %all-to-all-start.2) | async-done | bytes 294944 | tf_op jit(solution)/shard_map/all_to_all | solution.py:329
  80.7 2.4 %shard_map.70 = (f32[80,1024]{1,0:T(8,128)S(1)}, f32[1,1024]{1,0:T(1,128)S(1)}) custom-call(s32[3]{0:T(128)S(1)} %bitcast.25, bf16[72,1024]{1,0:T(8,128)(2,1)S(1)} %copy-done.2, f32[80,1024]{1,0:T(8,128)S(1)} %get-tuple-element.39.state_ref, f32[1,1024]{1,0:T(1,128)S(1)} %get-tuple-element.40.best_ref, bf16[144,1024]{1,0:T(8,128)(2,1)S(1)} %shard_map.69.far_ref), custom_call_target="tpu_custom_call" | custom-call | flops 1073741824 | bytes 294912 | tf_op jit(solution)/shard_map/pallas_call | solution.py:280
  83.1 2.4 %shard_map.71 = bf16[4,80,256]{2,1,0:T(8,128)(2,1)S(1)} custom-call(s32[3]{0:T(128)S(1)} %bitcast.26, bf16[72,1024]{1,0:T(8,128)(2,1)S(1)} %copy-done.2, f32[72,1024]{1,0:T(8,128)S(1)} %get-tuple-element.38.own_in_ref, f32[80,1024]{1,0:T(8,128)S(1)} %get-tuple-element.42.state_ref, f32[1,1024]{1,0:T(1,128)S(1)} %get-tuple-element.43.best_ref, ...), custom_call_target="tpu_custom_call" | custom-call | flops 1073741824 | bytes 294912 | tf_op jit(solution)/shard_map/pallas_call | solution.py:280
  85.5 9.7 %all_to_all.25.parts_ref = bf16[4,80,256]{2,1,0:T(8,128)(2,1)S(1)} all-to-all(bf16[4,80,256]{2,1,0:T(8,128)(2,1)S(1)} %shard_map.71), channel_id=1, replica_groups={{0,4,8,12},{1,5,9,13},{2,6,10,14},{3,7,11,15},{16,20,24,28},{17,21,25,2..., dimensions={0} | all-to-all | bytes 327680 | tf_op jit(solution)/shard_map/all_to_all | solution.py:329
  95.2 2.3 %shard_map.72 = bf16[4,64,1152]{2,1,0:T(8,128)(2,1)S(1)} custom-call(s32[5]{0:T(128)S(1)} %pad_add_fusion.place_ref, bf16[4,80,256]{2,1,0:T(8,128)(2,1)S(1)} %all_to_all.25.parts_ref, bf16[224,1152]{1,0:T(8,128)(2,1)S(1)} %pad_maximum_fusion.weight_ref, bf16[224,1152]{1,0:T(8,128)(2,1)} %collective-permute-done.1.mine_ref, ...), custom_call_target="tpu_custom_call" | custom-call | flops 188743680 | bytes 1327104 | tf_op jit(solution)/shard_map/pallas_call | solution.py:379
  97.5 13.0 %all_to_all.26 = bf16[4,64,1152]{2,1,0:T(8,128)(2,1)S(1)} all-to-all(bf16[4,64,1152]{2,1,0:T(8,128)(2,1)S(1)} %shard_map.72), channel_id=1, replica_groups={{0,1,2,3},{4,5,6,7},{8,9,10,11},{12,13,14,15},{16,17,18,19},{20,21,22,2..., dimensions={0} | all-to-all | bytes 1179648 | tf_op jit(solution)/shard_map/all_to_all | solution.py:329
  (26 shorter events, 3.7 us)
Async XLA Ops:
  3.4 7.3 %copy-start = (bf16[1,216,1152]{2,1,0:T(8,128)(2,1)S(1)}, bf16[1,216,1152]{2,1,0:T(8,128)(2,1)}, u32[]{:S(2)}) copy-start(bf16[1,216,1152]{2,1,0:T(8,128)(2,1)} %param.8) | copy-start | bytes 1492996
  3.4 43.2 %all-to-all-start = ((bf16[16,64,1152]{2,1,0:T(8,128)(2,1)}), bf16[16,64,1152]{2,1,0:T(8,128)(2,1)S(1)}, u32[]{:S(2)}, u32[]{:S(2)}) async-start(bf16[16,64,1152]{2,1,0:T(8,128)(2,1)} %get-tuple-element.27), calls=%async_computation | async-start | bytes 4718592 | tf_op jit(solution)/shard_map/all_to_all | solution.py:83
  10.6 20.7 %copy-start.4 = (f32[1,2,72]{2,1,0:T(2,128)S(1)}, f32[1,2,72]{2,1,0:T(2,128)}, u32[]{:S(2)}) copy-start(f32[1,2,72]{2,1,0:T(2,128)} %param.9) | copy-start | bytes 1732
  11.8 34.8 %collective-permute-start.1 = (bf16[224,1152]{1,0:T(8,128)(2,1)S(1)}, bf16[224,1152]{1,0:T(8,128)(2,1)}, u32[]{:S(2)}, u32[]{:S(2)}) collective-permute-start(bf16[224,1152]{1,0:T(8,128)(2,1)S(1)} %pad_maximum_fusion.weight_ref), channel_id=1, source_target_pairs={{4,0},{5,1},{6,2},{7,3},{8,4},{9,5},{10,6},{11,7},{12,8},{13,9},{1... | collective-permute-start | bytes 1548296 | tf_op jit(solution)/shard_map/ppermute | solution.py:346
  16.8 22.5 %collective-permute-start = (bf16[64,1152]{1,0:T(8,128)(2,1)}, bf16[64,1152]{1,0:T(8,128)(2,1)}, u32[]{:S(2)}, u32[]{:S(2)}) collective-permute-start(bf16[64,1152]{1,0:T(8,128)(2,1)} %get-tuple-element.25), channel_id=1, source_target_pairs={{0,256},{16,272},{32,288},{48,304},{64,320},{80,336},{96,352},{112... | collective-permute-start | bytes 442376 | tf_op jit(solution)/shard_map/ppermute | solution.py:14
  28.5 25.2 %collective-permute-start.3 = (bf16[112,1152]{1,0:T(8,128)(2,1)}, bf16[112,1152]{1,0:T(8,128)(2,1)}, u32[]{:S(2)}, u32[]{:S(2)}) collective-permute-start(bf16[112,1152]{1,0:T(8,128)(2,1)} %slice_select_fusion), channel_id=1, source_target_pairs={{0,8},{1,9},{2,10},{3,11},{4,12},{5,13},{6,14},{7,15},{8,0},{9,1},... | collective-permute-start | bytes 774152 | tf_op jit(solution)/shard_map/ppermute | solution.py:349
  46.6 19.3 %collective-permute-start.2 = (bf16[224,1152]{1,0:T(8,128)(2,1)}, bf16[224,1152]{1,0:T(8,128)(2,1)}, u32[]{:S(2)}, u32[]{:S(2)}) collective-permute-start(bf16[224,1152]{1,0:T(8,128)(2,1)} %collective-permute-done.1.mine_ref), channel_id=1, source_target_pairs={{0,16},{16,0},{32,48},{48,32},{64,80},{80,64},{96,112},{112,96},{1... | collective-permute-start | bytes 1548296 | tf_op jit(solution)/shard_map/ppermute | solution.py:14
  49.5 16.4 %all-to-all-start.1 = ((bf16[4,64,1152]{2,1,0:T(8,128)(2,1)}), bf16[4,64,1152]{2,1,0:T(8,128)(2,1)}, u32[]{:S(2)}, u32[]{:S(2)}) async-start(bf16[4,64,1152]{2,1,0:T(8,128)(2,1)} %shard_map.65), calls=%async_computation.1 | async-start | bytes 1179648 | tf_op jit(solution)/shard_map/all_to_all | solution.py:329
  53.7 12.2 %collective-permute-start.4 = (bf16[112,1152]{1,0:T(8,128)(2,1)}, bf16[112,1152]{1,0:T(8,128)(2,1)}, u32[]{:S(2)}, u32[]{:S(2)}) collective-permute-start(bf16[112,1152]{1,0:T(8,128)(2,1)} %collective-permute-done.3.mine_half_ref), channel_id=1, source_target_pairs={{0,16},{16,0},{32,48},{48,32},{64,80},{80,64},{96,112},{112,96},{1... | collective-permute-start | bytes 774152 | tf_op jit(solution)/shard_map/ppermute | solution.py:14
  57.3 0.7 copy-start.1
  58.0 15.8 %copy-start.3 = (s32[3,1]{0,1:T(1,128)S(1)}, s32[3,1]{0,1:T(1,128)}, u32[]{:S(2)}) copy-start(s32[3,1]{0,1:T(1,128)} %param.11) | copy-start | bytes 40
  58.0 15.8 %copy-start.2 = (bf16[72,1024]{1,0:T(8,128)(2,1)S(1)}, bf16[72,1024]{1,0:T(8,128)(2,1)}, u32[]{:S(2)}) copy-start(bf16[72,1024]{1,0:T(8,128)(2,1)} %copy-done.1) | copy-start | bytes 442372
  58.0 15.7 %collective-permute-start.5 = (bf16[144,1024]{1,0:T(8,128)(2,1)}, bf16[144,1024]{1,0:T(8,128)(2,1)S(1)}, u32[]{:S(2)}, u32[]{:S(2)}) collective-permute-start(bf16[144,1024]{1,0:T(8,128)(2,1)} %get-tuple-element.34.own_ref), channel_id=1, source_target_pairs={{0,16},{16,0},{32,48},{48,32},{64,80},{80,64},{96,112},{112,96},{1... | collective-permute-start | bytes 884744 | tf_op jit(solution)/shard_map/ppermute | solution.py:14
  60.6 18.9 %collective-permute-start.6 = (bf16[144,1024]{1,0:T(8,128)(2,1)}, bf16[144,1024]{1,0:T(8,128)(2,1)S(1)}, u32[]{:S(2)}, u32[]{:S(2)}) collective-permute-start(bf16[144,1024]{1,0:T(8,128)(2,1)} %get-tuple-element.34.own_ref), channel_id=1, source_target_pairs={{0,64},{16,80},{32,96},{48,112},{64,0},{80,16},{96,32},{112,48},{1... | collective-permute-start | bytes 884744 | tf_op jit(solution)/shard_map/ppermute | solution.py:14
  68.8 11.8 %all-to-all-start.2 = ((bf16[4,144,256]{2,1,0:T(8,128)(2,1)}), bf16[4,144,256]{2,1,0:T(8,128)(2,1)S(1)}, u32[]{:S(2)}, u32[]{:S(2)}) async-start(bf16[4,144,256]{2,1,0:T(8,128)(2,1)} %shard_map.67), calls=%async_computation.2 | async-start | bytes 589824 | tf_op jit(solution)/shard_map/all_to_all | solution.py:329

commit v17 on v16

--- a/solution.py
+++ b/solution.py
@@ -379,7 +379,8 @@
     partial = pl.pallas_call(
         project_out_kernel,
         out_shape=jax.ShapeDtypeStruct((side, tokens // side, width), jnp.bfloat16),
-        in_specs=[smem] + [vmem] * (1 + len(column)),
+        grid=(1,),
+        in_specs=[smem, vmem] + [pl.BlockSpec((wide, width), lambda n: (0, 0))] * len(column),
         out_specs=vmem,
         compiler_params=pltpu.CompilerParams(vmem_limit_bytes=16 << 20),
         cost_estimate=pl.CostEstimate(

time: 112 us -> 112 us (level)
  no operation moved by 1% of the time
where the time goes in v17:
time: 112 us; the launch traced here: 111 us
  starting transfers between devices  47.5 us (42%)
  blocking collectives  22.8 us (20%)
  Pallas kernels  21.3 us (19%)
  waiting for transfers between devices  15.8 us (14%)
  other arithmetic  2.74 us (2%)
    ppermute x5, starting transfers between devices, partner(): lax.ppermute(array, 'view', [(i, i ^ 1 << bit) for i in range(lax.axis_si...  23.4 us
    all_to_all x2, blocking collectives, exchange(): lax.all_to_all(slots, 'head', split_axis=0, concat_axis=0, tiled=True, ax...  22.8 us
    pallas_call x3, Pallas kernels, call_attend(): pl.pallas_call(kernel, out_shape=out_shape, in_specs=[smem] + [vmem] * (l...  9.24 us
    ppermute x5, waiting for transfers between devices, partner(): lax.ppermute(array, 'view', [(i, i ^ 1 << bit) for i in range(lax.axis_si...  9.18 us
    all_to_all x2, starting transfers between devices, exchange(): lax.all_to_all(slots, 'head', split_axis=0, concat_axis=0, tiled=True, ax...  9.13 us
    all_to_all x1, starting transfers between devices, gather_tokens(): lax.all_to_all(slots, 'head', split_axis=0, concat_axis=0, tiled=True)  7.18 us
    ppermute x1, waiting for transfers between devices, column_weights(): beside = lax.ppermute(packed, ('view', 'head'), pairs)  5.48 us
    ppermute x1, starting transfers between devices, column_weights(): beside = lax.ppermute(packed, ('view', 'head'), pairs)  5.05 us
  transfers between devices with their start and end apart: 10, of which 4 were waited for; matrix products, arithmetic and copies ran while one was open for 2% of the time, Pallas kernels for 10%

profile of v17, /device:TPU:128, one launch (start us, length us, event | category | flops | bytes accessed | tf_op | source)
XLA Modules:
  0.0 111.2 jit_solution(266756033027432876)
XLA Ops:
  0.0 3.4 %shard_map.64 = (bf16[64,1152]{1,0:T(8,128)(2,1)}, bf16[16,64,1152]{2,1,0:T(8,128)(2,1)}) custom-call(bf16[64,1152]{1,0:T(8,128)(2,1)} %bitcast.28, f32[1152]{0:T(1024)} %gain_ref.1), custom_call_target="tpu_custom_call" | custom-call | flops 589824 | bytes 2359296 | tf_op jit(solution)/shard_map/pallas_call | solution.py:49
  3.4 7.2 %all-to-all-start = ((bf16[16,64,1152]{2,1,0:T(8,128)(2,1)}), bf16[16,64,1152]{2,1,0:T(8,128)(2,1)S(1)}, u32[]{:S(2)}, u32[]{:S(2)}) async-start(bf16[16,64,1152]{2,1,0:T(8,128)(2,1)} %get-tuple-element.27), calls=%async_computation | async-start | bytes 4718592 | tf_op jit(solution)/shard_map/all_to_all | solution.py:83
  11.8 5.0 %collective-permute-start.1 = (bf16[224,1152]{1,0:T(8,128)(2,1)S(1)}, bf16[224,1152]{1,0:T(8,128)(2,1)}, u32[]{:S(2)}, u32[]{:S(2)}) collective-permute-start(bf16[224,1152]{1,0:T(8,128)(2,1)S(1)} %pad_maximum_fusion.weight_ref), channel_id=1, source_target_pairs={{4,0},{5,1},{6,2},{7,3},{8,4},{9,5},{10,6},{11,7},{12,8},{13,9},{1... | collective-permute-start | bytes 1548296 | tf_op jit(solution)/shard_map/ppermute | solution.py:346
  16.8 10.9 %collective-permute-start = (bf16[64,1152]{1,0:T(8,128)(2,1)}, bf16[64,1152]{1,0:T(8,128)(2,1)}, u32[]{:S(2)}, u32[]{:S(2)}) collective-permute-start(bf16[64,1152]{1,0:T(8,128)(2,1)} %get-tuple-element.25), channel_id=1, source_target_pairs={{0,256},{16,272},{32,288},{48,304},{64,320},{80,336},{96,352},{112... | collective-permute-start | bytes 442376 | tf_op jit(solution)/shard_map/ppermute | solution.py:14
  28.5 2.8 %collective-permute-start.3 = (bf16[112,1152]{1,0:T(8,128)(2,1)}, bf16[112,1152]{1,0:T(8,128)(2,1)}, u32[]{:S(2)}, u32[]{:S(2)}) collective-permute-start(bf16[112,1152]{1,0:T(8,128)(2,1)} %slice_select_fusion), channel_id=1, source_target_pairs={{0,8},{1,9},{2,10},{3,11},{4,12},{5,13},{6,14},{7,15},{8,0},{9,1},... | collective-permute-start | bytes 774152 | tf_op jit(solution)/shard_map/ppermute | solution.py:349
  31.4 7.9 %collective-permute-done.source_ref = bf16[64,1152]{1,0:T(8,128)(2,1)} collective-permute-done((bf16[64,1152]{1,0:T(8,128)(2,1)}, bf16[64,1152]{1,0:T(8,128)(2,1)}, u32[]{:S(2)}, u32[]{:S(2)}) %collective-permute-start) | collective-permute-done | bytes 147488 | tf_op jit(solution)/shard_map/ppermute | solution.py:14
  39.3 1.8 %shard_map.65 = bf16[4,64,1152]{2,1,0:T(8,128)(2,1)} custom-call(bf16[64,1152]{1,0:T(8,128)(2,1)} %collective-permute-done.source_ref), custom_call_target="tpu_custom_call" | custom-call | bytes 589824 | tf_op jit(solution)/shard_map/pallas_call | solution.py:71
  41.1 5.5 %collective-permute-done.1.mine_ref = bf16[224,1152]{1,0:T(8,128)(2,1)} collective-permute-done((bf16[224,1152]{1,0:T(8,128)(2,1)S(1)}, bf16[224,1152]{1,0:T(8,128)(2,1)}, u32[]{:S(2)}, u32[]{:S(2)}) %collective-permute-start.1) | collective-permute-done | bytes 516128 | tf_op jit(solution)/shard_map/ppermute | solution.py:346
  46.6 2.9 %collective-permute-start.2 = (bf16[224,1152]{1,0:T(8,128)(2,1)}, bf16[224,1152]{1,0:T(8,128)(2,1)}, u32[]{:S(2)}, u32[]{:S(2)}) collective-permute-start(bf16[224,1152]{1,0:T(8,128)(2,1)} %collective-permute-done.1.mine_ref), channel_id=1, source_target_pairs={{0,16},{16,0},{32,48},{48,32},{64,80},{80,64},{96,112},{112,96},{1... | collective-permute-start | bytes 1548296 | tf_op jit(solution)/shard_map/ppermute | solution.py:14
  49.5 4.2 %all-to-all-start.1 = ((bf16[4,64,1152]{2,1,0:T(8,128)(2,1)}), bf16[4,64,1152]{2,1,0:T(8,128)(2,1)}, u32[]{:S(2)}, u32[]{:S(2)}) async-start(bf16[4,64,1152]{2,1,0:T(8,128)(2,1)} %shard_map.65), calls=%async_computation.1 | async-start | bytes 1179648 | tf_op jit(solution)/shard_map/all_to_all | solution.py:329
  53.7 1.9 %collective-permute-start.4 = (bf16[112,1152]{1,0:T(8,128)(2,1)}, bf16[112,1152]{1,0:T(8,128)(2,1)}, u32[]{:S(2)}, u32[]{:S(2)}) collective-permute-start(bf16[112,1152]{1,0:T(8,128)(2,1)} %collective-permute-done.3.mine_half_ref), channel_id=1, source_target_pairs={{0,16},{16,0},{32,48},{48,32},{64,80},{80,64},{96,112},{112,96},{1... | collective-permute-start | bytes 774152 | tf_op jit(solution)/shard_map/ppermute | solution.py:14
  55.6 1.7 %shard_map.66 = (bf16[72,1024]{1,0:T(8,128)(2,1)S(1)}, bf16[144,1024]{1,0:T(8,128)(2,1)}) custom-call(bf16[1024,1152]{1,0:T(8,128)(2,1)S(1)} %bitcast.19, bf16[216,1152]{1,0:T(8,128)(2,1)S(1)} %bitcast.20, f32[72,2]{1,0:T(8,128)S(1)} %bitcast.22), custom_call_target="tpu_custom_call" | custom-call | flops 509607936 | bytes 2359296 | tf_op jit(solution)/shard_map/pallas_call | solution.py:107
  58.0 2.5 %collective-permute-start.5 = (bf16[144,1024]{1,0:T(8,128)(2,1)}, bf16[144,1024]{1,0:T(8,128)(2,1)S(1)}, u32[]{:S(2)}, u32[]{:S(2)}) collective-permute-start(bf16[144,1024]{1,0:T(8,128)(2,1)} %get-tuple-element.34.own_ref), channel_id=1, source_target_pairs={{0,16},{16,0},{32,48},{48,32},{64,80},{80,64},{96,112},{112,96},{1... | collective-permute-start | bytes 884744 | tf_op jit(solution)/shard_map/ppermute | solution.py:14
  60.6 5.2 %collective-permute-start.6 = (bf16[144,1024]{1,0:T(8,128)(2,1)}, bf16[144,1024]{1,0:T(8,128)(2,1)S(1)}, u32[]{:S(2)}, u32[]{:S(2)}) collective-permute-start(bf16[144,1024]{1,0:T(8,128)(2,1)} %get-tuple-element.34.own_ref), channel_id=1, source_target_pairs={{0,64},{16,80},{32,96},{48,112},{64,0},{80,16},{96,32},{112,48},{1... | collective-permute-start | bytes 884744 | tf_op jit(solution)/shard_map/ppermute | solution.py:14
  65.9 2.9 %shard_map.67 = bf16[4,144,256]{2,1,0:T(8,128)(2,1)} custom-call(s32[5]{0:T(128)S(1)} %pad_add_fusion.place_ref, bf16[256,1152]{1,0:T(8,128)(2,1)} %bitcast.13.rows_ref, bf16[216,1152]{1,0:T(8,128)(2,1)S(1)} %bitcast.21, bf16[224,1152]{1,0:T(8,128)(2,1)} %collective-permute-done.1.mine_ref, bf16[224,1152]{1,0:T(8,128)(2,1)} %collective-permute-done.2.other_ref, ...), custom_call_target="tpu_custom_call" | custom-call | flops 509607936 | bytes 1179648 | tf_op jit(solution)/shard_map/pallas_call | solution.py:156
  68.8 4.9 %all-to-all-start.2 = ((bf16[4,144,256]{2,1,0:T(8,128)(2,1)}), bf16[4,144,256]{2,1,0:T(8,128)(2,1)S(1)}, u32[]{:S(2)}, u32[]{:S(2)}) async-start(bf16[4,144,256]{2,1,0:T(8,128)(2,1)} %shard_map.67), calls=%async_computation.2 | async-start | bytes 589824 | tf_op jit(solution)/shard_map/all_to_all | solution.py:329
  73.7 4.5 %shard_map.68 = (f32[72,1024]{1,0:T(8,128)S(1)}, f32[80,1024]{1,0:T(8,128)S(1)}, f32[1,1024]{1,0:T(1,128)S(1)}) custom-call(s32[3]{0:T(128)S(1)} %bitcast.24, bf16[72,1024]{1,0:T(8,128)(2,1)S(1)} %copy-done.2, bf16[144,1024]{1,0:T(8,128)(2,1)} %get-tuple-element.34.own_ref, bf16[144,1024]{1,0:T(8,128)(2,1)S(1)} %collective-permute-done.5.far_ref), custom_call_target="tpu_custom_call" | custom-call | flops 2147483648 | bytes 589824 | tf_op jit(solution)/shard_map/pallas_call | solution.py:280
  78.2 1.3 %collective-permute-done.6.far_ref = bf16[144,1024]{1,0:T(8,128)(2,1)S(1)} collective-permute-done((bf16[144,1024]{1,0:T(8,128)(2,1)}, bf16[144,1024]{1,0:T(8,128)(2,1)S(1)}, u32[]{:S(2)}, u32[]{:S(2)}) %collective-permute-start.6) | collective-permute-done | bytes 294944 | tf_op jit(solution)/shard_map/ppermute | solution.py:14
  79.5 1.1 %all-to-all-done.2.parts_ref = bf16[4,144,256]{2,1,0:T(8,128)(2,1)S(1)} async-done(((bf16[4,144,256]{2,1,0:T(8,128)(2,1)}), bf16[4,144,256]{2,1,0:T(8,128)(2,1)S(1)}, u32[]{:S(2)}, u32[]{:S(2)}) %all-to-all-start.2) | async-done | bytes 294944 | tf_op jit(solution)/shard_map/all_to_all | solution.py:329
  80.7 2.4 %shard_map.70 = (f32[80,1024]{1,0:T(8,128)S(1)}, f32[1,1024]{1,0:T(1,128)S(1)}) custom-call(s32[3]{0:T(128)S(1)} %bitcast.25, bf16[72,1024]{1,0:T(8,128)(2,1)S(1)} %copy-done.2, f32[80,1024]{1,0:T(8,128)S(1)} %get-tuple-element.39.state_ref, f32[1,1024]{1,0:T(1,128)S(1)} %get-tuple-element.40.best_ref, bf16[144,1024]{1,0:T(8,128)(2,1)S(1)} %shard_map.69.far_ref), custom_call_target="tpu_custom_call" | custom-call | flops 1073741824 | bytes 294912 | tf_op jit(solution)/shard_map/pallas_call | solution.py:280
  83.1 2.4 %shard_map.71 = bf16[4,80,256]{2,1,0:T(8,128)(2,1)S(1)} custom-call(s32[3]{0:T(128)S(1)} %bitcast.26, bf16[72,1024]{1,0:T(8,128)(2,1)S(1)} %copy-done.2, f32[72,1024]{1,0:T(8,128)S(1)} %get-tuple-element.38.own_in_ref, f32[80,1024]{1,0:T(8,128)S(1)} %get-tuple-element.42.state_ref, f32[1,1024]{1,0:T(1,128)S(1)} %get-tuple-element.43.best_ref, ...), custom_call_target="tpu_custom_call" | custom-call | flops 1073741824 | bytes 294912 | tf_op jit(solution)/shard_map/pallas_call | solution.py:280
  85.5 9.7 %all_to_all.25.parts_ref = bf16[4,80,256]{2,1,0:T(8,128)(2,1)S(1)} all-to-all(bf16[4,80,256]{2,1,0:T(8,128)(2,1)S(1)} %shard_map.71), channel_id=1, replica_groups={{0,4,8,12},{1,5,9,13},{2,6,10,14},{3,7,11,15},{16,20,24,28},{17,21,25,2..., dimensions={0} | all-to-all | bytes 327680 | tf_op jit(solution)/shard_map/all_to_all | solution.py:329
  95.2 2.2 %shard_map.72 = bf16[4,64,1152]{2,1,0:T(8,128)(2,1)S(1)} custom-call(s32[5]{0:T(128)S(1)} %pad_add_fusion.place_ref, bf16[4,80,256]{2,1,0:T(8,128)(2,1)S(1)} %all_to_all.25.parts_ref, bf16[224,1152]{1,0:T(8,128)(2,1)S(1)} %pad_maximum_fusion.weight_ref, bf16[224,1152]{1,0:T(8,128)(2,1)} %collective-permute-done.1.mine_ref, ...), custom_call_target="tpu_custom_call" | custom-call | flops 188743680 | bytes 1327104 | tf_op jit(solution)/shard_map/pallas_call | solution.py:379
  97.4 13.0 %all_to_all.26 = bf16[4,64,1152]{2,1,0:T(8,128)(2,1)S(1)} all-to-all(bf16[4,64,1152]{2,1,0:T(8,128)(2,1)S(1)} %shard_map.72), channel_id=1, replica_groups={{0,1,2,3},{4,5,6,7},{8,9,10,11},{12,13,14,15},{16,17,18,19},{20,21,22,2..., dimensions={0} | all-to-all | bytes 1179648 | tf_op jit(solution)/shard_map/all_to_all | solution.py:329
  (26 shorter events, 3.7 us)
Async XLA Ops:
  3.4 7.3 %copy-start = (bf16[1,216,1152]{2,1,0:T(8,128)(2,1)S(1)}, bf16[1,216,1152]{2,1,0:T(8,128)(2,1)}, u32[]{:S(2)}) copy-start(bf16[1,216,1152]{2,1,0:T(8,128)(2,1)} %param.8) | copy-start | bytes 1492996
  3.4 43.2 %all-to-all-start = ((bf16[16,64,1152]{2,1,0:T(8,128)(2,1)}), bf16[16,64,1152]{2,1,0:T(8,128)(2,1)S(1)}, u32[]{:S(2)}, u32[]{:S(2)}) async-start(bf16[16,64,1152]{2,1,0:T(8,128)(2,1)} %get-tuple-element.27), calls=%async_computation | async-start | bytes 4718592 | tf_op jit(solution)/shard_map/all_to_all | solution.py:83
  10.6 20.7 %copy-start.4 = (f32[1,2,72]{2,1,0:T(2,128)S(1)}, f32[1,2,72]{2,1,0:T(2,128)}, u32[]{:S(2)}) copy-start(f32[1,2,72]{2,1,0:T(2,128)} %param.9) | copy-start | bytes 1732
  11.8 34.8 %collective-permute-start.1 = (bf16[224,1152]{1,0:T(8,128)(2,1)S(1)}, bf16[224,1152]{1,0:T(8,128)(2,1)}, u32[]{:S(2)}, u32[]{:S(2)}) collective-permute-start(bf16[224,1152]{1,0:T(8,128)(2,1)S(1)} %pad_maximum_fusion.weight_ref), channel_id=1, source_target_pairs={{4,0},{5,1},{6,2},{7,3},{8,4},{9,5},{10,6},{11,7},{12,8},{13,9},{1... | collective-permute-start | bytes 1548296 | tf_op jit(solution)/shard_map/ppermute | solution.py:346
  16.8 22.5 %collective-permute-start = (bf16[64,1152]{1,0:T(8,128)(2,1)}, bf16[64,1152]{1,0:T(8,128)(2,1)}, u32[]{:S(2)}, u32[]{:S(2)}) collective-permute-start(bf16[64,1152]{1,0:T(8,128)(2,1)} %get-tuple-element.25), channel_id=1, source_target_pairs={{0,256},{16,272},{32,288},{48,304},{64,320},{80,336},{96,352},{112... | collective-permute-start | bytes 442376 | tf_op jit(solution)/shard_map/ppermute | solution.py:14
  28.5 25.2 %collective-permute-start.3 = (bf16[112,1152]{1,0:T(8,128)(2,1)}, bf16[112,1152]{1,0:T(8,128)(2,1)}, u32[]{:S(2)}, u32[]{:S(2)}) collective-permute-start(bf16[112,1152]{1,0:T(8,128)(2,1)} %slice_select_fusion), channel_id=1, source_target_pairs={{0,8},{1,9},{2,10},{3,11},{4,12},{5,13},{6,14},{7,15},{8,0},{9,1},... | collective-permute-start | bytes 774152 | tf_op jit(solution)/shard_map/ppermute | solution.py:349
  46.6 19.3 %collective-permute-start.2 = (bf16[224,1152]{1,0:T(8,128)(2,1)}, bf16[224,1152]{1,0:T(8,128)(2,1)}, u32[]{:S(2)}, u32[]{:S(2)}) collective-permute-start(bf16[224,1152]{1,0:T(8,128)(2,1)} %collective-permute-done.1.mine_ref), channel_id=1, source_target_pairs={{0,16},{16,0},{32,48},{48,32},{64,80},{80,64},{96,112},{112,96},{1... | collective-permute-start | bytes 1548296 | tf_op jit(solution)/shard_map/ppermute | solution.py:14
  49.5 16.4 %all-to-all-start.1 = ((bf16[4,64,1152]{2,1,0:T(8,128)(2,1)}), bf16[4,64,1152]{2,1,0:T(8,128)(2,1)}, u32[]{:S(2)}, u32[]{:S(2)}) async-start(bf16[4,64,1152]{2,1,0:T(8,128)(2,1)} %shard_map.65), calls=%async_computation.1 | async-start | bytes 1179648 | tf_op jit(solution)/shard_map/all_to_all | solution.py:329
  53.7 12.2 %collective-permute-start.4 = (bf16[112,1152]{1,0:T(8,128)(2,1)}, bf16[112,1152]{1,0:T(8,128)(2,1)}, u32[]{:S(2)}, u32[]{:S(2)}) collective-permute-start(bf16[112,1152]{1,0:T(8,128)(2,1)} %collective-permute-done.3.mine_half_ref), channel_id=1, source_target_pairs={{0,16},{16,0},{32,48},{48,32},{64,80},{80,64},{96,112},{112,96},{1... | collective-permute-start | bytes 774152 | tf_op jit(solution)/shard_map/ppermute | solution.py:14
  57.3 0.7 copy-start.1
  58.0 15.8 %copy-start.3 = (s32[3,1]{0,1:T(1,128)S(1)}, s32[3,1]{0,1:T(1,128)}, u32[]{:S(2)}) copy-start(s32[3,1]{0,1:T(1,128)} %param.11) | copy-start | bytes 40
  58.0 15.8 %copy-start.2 = (bf16[72,1024]{1,0:T(8,128)(2,1)S(1)}, bf16[72,1024]{1,0:T(8,128)(2,1)}, u32[]{:S(2)}) copy-start(bf16[72,1024]{1,0:T(8,128)(2,1)} %copy-done.1) | copy-start | bytes 442372
  58.0 15.7 %collective-permute-start.5 = (bf16[144,1024]{1,0:T(8,128)(2,1)}, bf16[144,1024]{1,0:T(8,128)(2,1)S(1)}, u32[]{:S(2)}, u32[]{:S(2)}) collective-permute-start(bf16[144,1024]{1,0:T(8,128)(2,1)} %get-tuple-element.34.own_ref), channel_id=1, source_target_pairs={{0,16},{16,0},{32,48},{48,32},{64,80},{80,64},{96,112},{112,96},{1... | collective-permute-start | bytes 884744 | tf_op jit(solution)/shard_map/ppermute | solution.py:14
  60.6 18.9 %collective-permute-start.6 = (bf16[144,1024]{1,0:T(8,128)(2,1)}, bf16[144,1024]{1,0:T(8,128)(2,1)S(1)}, u32[]{:S(2)}, u32[]{:S(2)}) collective-permute-start(bf16[144,1024]{1,0:T(8,128)(2,1)} %get-tuple-element.34.own_ref), channel_id=1, source_target_pairs={{0,64},{16,80},{32,96},{48,112},{64,0},{80,16},{96,32},{112,48},{1... | collective-permute-start | bytes 884744 | tf_op jit(solution)/shard_map/ppermute | solution.py:14
  68.8 11.8 %all-to-all-start.2 = ((bf16[4,144,256]{2,1,0:T(8,128)(2,1)}), bf16[4,144,256]{2,1,0:T(8,128)(2,1)S(1)}, u32[]{:S(2)}, u32[]{:S(2)}) async-start(bf16[4,144,256]{2,1,0:T(8,128)(2,1)} %shard_map.67), calls=%async_computation.2 | async-start | bytes 589824 | tf_op jit(solution)/shard_map/all_to_all | solution.py:329

commit v18 on v16

--- a/solution.py
+++ b/solution.py
@@ -418,12 +418,13 @@
     far_parts = project_far(place, far_tokens, weight, column, head_dim)
     far_parts = exchange(far_parts, 1)
     own_result, state, best = attend_near(active, query, own, near[0])
-    far_parts, own_result, state, best, near[1] = lax.optimization_barrier(
-        (far_parts, own_result, state, best, near[1])
+    out_rows = [rows[: head_dim + PAD] for rows in [packed] + column]
+    far_parts, own_result, state, best, near[1], out_rows = lax.optimization_barrier(
+        (far_parts, own_result, state, best, near[1], out_rows)
     )
     state, best = attend_middle(active, rounds - 1, query, state, best, settle(far_parts, gain))
     attended = attend_last(active, 1, query, own_result, state, best, near[1])
-    mixed = project_out(place, exchange(attended, 1), [packed] + column)
+    mixed = project_out(place, exchange(attended, 1), out_rows)
     return mixed.reshape(loc_len, view_dev, width)
 
 

time: 112 us -> 114 us (1.018)
  the two profiles are of different devices: /device:TPU:128 before, /device:TPU:160 now
where the time goes in v18:
time: 114 us; the launch traced here: 113 us
  starting transfers between devices  46.5 us (41%)
  blocking collectives  23.8 us (21%)
  Pallas kernels  18.9 us (17%)
  waiting for transfers between devices  14.4 us (13%)
  local copies, waits for them, and re-layouts  5.58 us (5%)
  other arithmetic  3.56 us (3%)
    all_to_all x2, blocking collectives, exchange(): lax.all_to_all(slots, 'head', split_axis=0, concat_axis=0, tiled=True, ax...  23.8 us
    ppermute x5, starting transfers between devices, partner(): lax.ppermute(array, 'view', [(i, i ^ 1 << bit) for i in range(lax.axis_si...  22.4 us
    pallas_call x3, Pallas kernels, call_attend(): pl.pallas_call(kernel, out_shape=out_shape, in_specs=[smem] + [vmem] * (l...  9.27 us
    all_to_all x2, starting transfers between devices, exchange(): lax.all_to_all(slots, 'head', split_axis=0, concat_axis=0, tiled=True, ax...  9.13 us
    ppermute x1, waiting for transfers between devices, column_weights(): beside = lax.ppermute(packed, ('view', 'head'), pairs)  9.12 us
    all_to_all x1, starting transfers between devices, gather_tokens(): lax.all_to_all(slots, 'head', split_axis=0, concat_axis=0, tiled=True)  7.18 us
    ppermute x5, waiting for transfers between devices, partner(): lax.ppermute(array, 'view', [(i, i ^ 1 << bit) for i in range(lax.axis_si...  5.27 us
    ppermute x1, starting transfers between devices, column_weights(): beside = lax.ppermute(packed, ('view', 'head'), pairs)  5.03 us
  transfers between devices with their start and end apart: 10, of which 2 were waited for; matrix products, arithmetic and copies ran while one was open for 7% of the time, Pallas kernels for 9%

profile of v18, /device:TPU:160, one launch (start us, length us, event | category | flops | bytes accessed | tf_op | source)
XLA Modules:
  0.0 112.9 jit_solution(7669660810406221168)
XLA Ops:
  0.0 2.7 %shard_map.64 = (bf16[64,1152]{1,0:T(8,128)(2,1)S(1)}, bf16[16,64,1152]{2,1,0:T(8,128)(2,1)}) custom-call(bf16[64,1152]{1,0:T(8,128)(2,1)} %bitcast.30, f32[1152]{0:T(1024)} %gain_ref.1), custom_call_target="tpu_custom_call" | custom-call | flops 589824 | bytes 2359296 | tf_op jit(solution)/shard_map/pallas_call | solution.py:49
  2.7 7.2 %all-to-all-start = ((bf16[16,64,1152]{2,1,0:T(8,128)(2,1)}), bf16[16,64,1152]{2,1,0:T(8,128)(2,1)S(1)}, u32[]{:S(2)}, u32[]{:S(2)}) async-start(bf16[16,64,1152]{2,1,0:T(8,128)(2,1)} %get-tuple-element.32), calls=%async_computation | async-start | bytes 4718592 | tf_op jit(solution)/shard_map/all_to_all | solution.py:83
  11.0 5.0 %collective-permute-start.1 = (bf16[224,1152]{1,0:T(8,128)(2,1)}, bf16[224,1152]{1,0:T(8,128)(2,1)}, u32[]{:S(2)}, u32[]{:S(2)}) collective-permute-start(bf16[224,1152]{1,0:T(8,128)(2,1)} %pad_maximum_fusion), channel_id=1, source_target_pairs={{4,0},{5,1},{6,2},{7,3},{8,4},{9,5},{10,6},{11,7},{12,8},{13,9},{1... | collective-permute-start | bytes 1548296 | tf_op jit(solution)/shard_map/ppermute | solution.py:346
  16.0 10.0 %collective-permute-start = (bf16[64,1152]{1,0:T(8,128)(2,1)S(1)}, bf16[64,1152]{1,0:T(8,128)(2,1)S(1)}, u32[]{:S(2)}, u32[]{:S(2)}) collective-permute-start(bf16[64,1152]{1,0:T(8,128)(2,1)S(1)} %get-tuple-element.30), channel_id=1, source_target_pairs={{0,256},{16,272},{32,288},{48,304},{64,320},{80,336},{96,352},{112... | collective-permute-start | bytes 442376 | tf_op jit(solution)/shard_map/ppermute | solution.py:14
  26.1 1.7 %slice_select_fusion = bf16[112,1152]{1,0:T(8,128)(2,1)} fusion(bf16[224,1152]{1,0:T(8,128)(2,1)} %pad_maximum_fusion, bf16[1,216,1152]{2,1,0:T(8,128)(2,1)S(1)} %copy-done, pred[]{:T(512)S(6)} %eq.9), kind=kLoop, calls=%fused_computation.2 | loop fusion | flops 129024 | bytes 774145 | tf_op jit(solution)/shard_map/jit(_where)/select_n | solution.py:347
  27.8 2.8 %collective-permute-start.3 = (bf16[112,1152]{1,0:T(8,128)(2,1)}, bf16[112,1152]{1,0:T(8,128)(2,1)}, u32[]{:S(2)}, u32[]{:S(2)}) collective-permute-start(bf16[112,1152]{1,0:T(8,128)(2,1)} %slice_select_fusion), channel_id=1, source_target_pairs={{0,8},{1,9},{2,10},{3,11},{4,12},{5,13},{6,14},{7,15},{8,0},{9,1},... | collective-permute-start | bytes 774152 | tf_op jit(solution)/shard_map/ppermute | solution.py:349
  30.7 5.3 %collective-permute-done.source_ref = bf16[64,1152]{1,0:T(8,128)(2,1)S(1)} collective-permute-done((bf16[64,1152]{1,0:T(8,128)(2,1)S(1)}, bf16[64,1152]{1,0:T(8,128)(2,1)S(1)}, u32[]{:S(2)}, u32[]{:S(2)}) %collective-permute-start) | collective-permute-done | bytes 147488 | tf_op jit(solution)/shard_map/ppermute | solution.py:14
  36.8 9.1 %collective-permute-done.1.mine_ref = bf16[224,1152]{1,0:T(8,128)(2,1)} collective-permute-done((bf16[224,1152]{1,0:T(8,128)(2,1)}, bf16[224,1152]{1,0:T(8,128)(2,1)}, u32[]{:S(2)}, u32[]{:S(2)}) %collective-permute-start.1) | collective-permute-done | bytes 516128 | tf_op jit(solution)/shard_map/ppermute | solution.py:346
  45.9 2.9 %collective-permute-start.2 = (bf16[224,1152]{1,0:T(8,128)(2,1)}, bf16[224,1152]{1,0:T(8,128)(2,1)}, u32[]{:S(2)}, u32[]{:S(2)}) collective-permute-start(bf16[224,1152]{1,0:T(8,128)(2,1)} %collective-permute-done.1.mine_ref), channel_id=1, source_target_pairs={{0,16},{16,0},{32,48},{48,32},{64,80},{80,64},{96,112},{112,96},{1... | collective-permute-start | bytes 1548296 | tf_op jit(solution)/shard_map/ppermute | solution.py:14
  48.8 4.2 %all-to-all-start.1 = ((bf16[4,64,1152]{2,1,0:T(8,128)(2,1)}), bf16[4,64,1152]{2,1,0:T(8,128)(2,1)S(1)}, u32[]{:S(2)}, u32[]{:S(2)}) async-start(bf16[4,64,1152]{2,1,0:T(8,128)(2,1)} %shard_map.65), calls=%async_computation.1 | async-start | bytes 1179648 | tf_op jit(solution)/shard_map/all_to_all | solution.py:329
  53.1 1.9 %collective-permute-start.4 = (bf16[112,1152]{1,0:T(8,128)(2,1)}, bf16[112,1152]{1,0:T(8,128)(2,1)}, u32[]{:S(2)}, u32[]{:S(2)}) collective-permute-start(bf16[112,1152]{1,0:T(8,128)(2,1)} %collective-permute-done.3.mine_half_ref), channel_id=1, source_target_pairs={{0,16},{16,0},{32,48},{48,32},{64,80},{80,64},{96,112},{112,96},{1... | collective-permute-start | bytes 774152 | tf_op jit(solution)/shard_map/ppermute | solution.py:14
  55.0 1.7 %shard_map.66 = (bf16[72,1024]{1,0:T(8,128)(2,1)S(1)}, bf16[144,1024]{1,0:T(8,128)(2,1)}) custom-call(bf16[1024,1152]{1,0:T(8,128)(2,1)S(1)} %bitcast.19, bf16[216,1152]{1,0:T(8,128)(2,1)S(1)} %bitcast.20, f32[72,2]{1,0:T(8,128)S(1)} %bitcast.23), custom_call_target="tpu_custom_call" | custom-call | flops 509607936 | bytes 2359296 | tf_op jit(solution)/shard_map/pallas_call | solution.py:107
  57.3 2.4 %collective-permute-start.5 = (bf16[144,1024]{1,0:T(8,128)(2,1)}, bf16[144,1024]{1,0:T(8,128)(2,1)S(1)}, u32[]{:S(2)}, u32[]{:S(2)}) collective-permute-start(bf16[144,1024]{1,0:T(8,128)(2,1)} %get-tuple-element.39.own_ref), channel_id=1, source_target_pairs={{0,16},{16,0},{32,48},{48,32},{64,80},{80,64},{96,112},{112,96},{1... | collective-permute-start | bytes 884744 | tf_op jit(solution)/shard_map/ppermute | solution.py:14
  59.8 5.2 %collective-permute-start.6 = (bf16[144,1024]{1,0:T(8,128)(2,1)}, bf16[144,1024]{1,0:T(8,128)(2,1)S(1)}, u32[]{:S(2)}, u32[]{:S(2)}) collective-permute-start(bf16[144,1024]{1,0:T(8,128)(2,1)} %get-tuple-element.39.own_ref), channel_id=1, source_target_pairs={{0,64},{16,80},{32,96},{48,112},{64,0},{80,16},{96,32},{112,48},{1... | collective-permute-start | bytes 884744 | tf_op jit(solution)/shard_map/ppermute | solution.py:14
  65.1 2.8 %shard_map.67 = bf16[4,144,256]{2,1,0:T(8,128)(2,1)} custom-call(s32[5]{0:T(128)S(1)} %pad_add_fusion.place_ref, bf16[256,1152]{1,0:T(8,128)(2,1)S(1)} %bitcast.22, bf16[216,1152]{1,0:T(8,128)(2,1)S(1)} %bitcast.21, bf16[224,1152]{1,0:T(8,128)(2,1)} %collective-permute-done.1.mine_ref, bf16[224,1152]{1,0:T(8,128)(2,1)} %collective-permute-done.2.other_ref, ...), custom_call_target="tpu_custom_call" | custom-call | flops 509607936 | bytes 1179648 | tf_op jit(solution)/shard_map/pallas_call | solution.py:156
  67.9 4.9 %all-to-all-start.2 = ((bf16[4,144,256]{2,1,0:T(8,128)(2,1)}), bf16[4,144,256]{2,1,0:T(8,128)(2,1)S(1)}, u32[]{:S(2)}, u32[]{:S(2)}) async-start(bf16[4,144,256]{2,1,0:T(8,128)(2,1)} %shard_map.67), calls=%async_computation.2 | async-start | bytes 589824 | tf_op jit(solution)/shard_map/all_to_all | solution.py:329
  73.7 0.9 slice.41.mine_half_ref
  76.5 4.5 %shard_map.68 = (f32[72,1024]{1,0:T(8,128)S(1)}, f32[80,1024]{1,0:T(8,128)S(1)}, f32[1,1024]{1,0:T(1,128)S(1)}) custom-call(s32[3]{0:T(128)S(1)} %bitcast.25, bf16[72,1024]{1,0:T(8,128)(2,1)S(1)} %copy-done.2, bf16[144,1024]{1,0:T(8,128)(2,1)} %get-tuple-element.39.own_ref, bf16[144,1024]{1,0:T(8,128)(2,1)S(1)} %collective-permute-done.5.far_ref), custom_call_target="tpu_custom_call" | custom-call | flops 2147483648 | bytes 589824 | tf_op jit(solution)/shard_map/pallas_call | solution.py:280
  81.0 0.9 slice.40.other_ref
  82.1 2.4 %shard_map.70 = (f32[80,1024]{1,0:T(8,128)S(1)}, f32[1,1024]{1,0:T(1,128)S(1)}) custom-call(s32[3]{0:T(128)S(1)} %bitcast.26, bf16[72,1024]{1,0:T(8,128)(2,1)S(1)} %copy-done.2, f32[80,1024]{1,0:T(8,128)S(1)} %get-tuple-element.44.state_ref, f32[1,1024]{1,0:T(1,128)S(1)} %get-tuple-element.45.best_ref, bf16[144,1024]{1,0:T(8,128)(2,1)S(1)} %shard_map.69.far_ref), custom_call_target="tpu_custom_call" | custom-call | flops 1073741824 | bytes 294912 | tf_op jit(solution)/shard_map/pallas_call | solution.py:280
  84.5 2.4 %shard_map.71 = bf16[4,80,256]{2,1,0:T(8,128)(2,1)S(1)} custom-call(s32[3]{0:T(128)S(1)} %bitcast.27, bf16[72,1024]{1,0:T(8,128)(2,1)S(1)} %copy-done.2, f32[72,1024]{1,0:T(8,128)S(1)} %get-tuple-element.43.own_in_ref, f32[80,1024]{1,0:T(8,128)S(1)} %get-tuple-element.47.state_ref, f32[1,1024]{1,0:T(1,128)S(1)} %get-tuple-element.48.best_ref, ...), custom_call_target="tpu_custom_call" | custom-call | flops 1073741824 | bytes 294912 | tf_op jit(solution)/shard_map/pallas_call | solution.py:280
  86.9 10.7 %all_to_all.25.parts_ref = bf16[4,80,256]{2,1,0:T(8,128)(2,1)S(1)} all-to-all(bf16[4,80,256]{2,1,0:T(8,128)(2,1)S(1)} %shard_map.71), channel_id=1, replica_groups={{0,4,8,12},{1,5,9,13},{2,6,10,14},{3,7,11,15},{16,20,24,28},{17,21,25,2..., dimensions={0} | all-to-all | bytes 327680 | tf_op jit(solution)/shard_map/all_to_all | solution.py:329
  97.7 1.5 %shard_map.72 = bf16[4,64,1152]{2,1,0:T(8,128)(2,1)S(1)} custom-call(s32[5]{0:T(128)S(1)} %pad_add_fusion.place_ref, bf16[4,80,256]{2,1,0:T(8,128)(2,1)S(1)} %all_to_all.25.parts_ref, bf16[80,1152]{1,0:T(8,128)(2,1)S(1)} %concatenate.11.weight_ref, bf16[80,1152]{1,0:T(8,128)(2,1)S(1)} %slice.35.mine_ref, bf16[80,1152]{1,0:T(8,128)(2,1)S(1)} %slice.40.other_ref, ...), custom_call_target="tpu_custom_call" | custom-call | flops 188743680 | bytes 1327104 | tf_op jit(solution)/shard_map/pallas_call | solution.py:379
  99.1 13.0 %all_to_all.26 = bf16[4,64,1152]{2,1,0:T(8,128)(2,1)S(1)} all-to-all(bf16[4,64,1152]{2,1,0:T(8,128)(2,1)S(1)} %shard_map.72), channel_id=1, replica_groups={{0,1,2,3},{4,5,6,7},{8,9,10,11},{12,13,14,15},{16,17,18,19},{20,21,22,2..., dimensions={0} | all-to-all | bytes 1179648 | tf_op jit(solution)/shard_map/all_to_all | solution.py:329
  (33 shorter events, 6.5 us)
Async XLA Ops:
  2.7 7.3 %copy-start = (bf16[1,216,1152]{2,1,0:T(8,128)(2,1)S(1)}, bf16[1,216,1152]{2,1,0:T(8,128)(2,1)}, u32[]{:S(2)}) copy-start(bf16[1,216,1152]{2,1,0:T(8,128)(2,1)} %param.8) | copy-start | bytes 1492996
  2.7 7.3 %copy-start.4 = (bf16[1,72,1152]{2,1,0:T(8,128)(2,1)S(1)}, bf16[1,72,1152]{2,1,0:T(8,128)(2,1)}, u32[]{:S(2)}) copy-start(bf16[1,72,1152]{2,1,0:T(8,128)(2,1)} %param.10) | copy-start | bytes 497668
  2.7 43.2 %all-to-all-start = ((bf16[16,64,1152]{2,1,0:T(8,128)(2,1)}), bf16[16,64,1152]{2,1,0:T(8,128)(2,1)S(1)}, u32[]{:S(2)}, u32[]{:S(2)}) async-start(bf16[16,64,1152]{2,1,0:T(8,128)(2,1)} %get-tuple-element.32), calls=%async_computation | async-start | bytes 4718592 | tf_op jit(solution)/shard_map/all_to_all | solution.py:83
  9.9 20.6 %copy-start.5 = (f32[1,2,72]{2,1,0:T(2,128)S(1)}, f32[1,2,72]{2,1,0:T(2,128)}, u32[]{:S(2)}) copy-start(f32[1,2,72]{2,1,0:T(2,128)} %param.9) | copy-start | bytes 1732
  11.0 34.9 %collective-permute-start.1 = (bf16[224,1152]{1,0:T(8,128)(2,1)}, bf16[224,1152]{1,0:T(8,128)(2,1)}, u32[]{:S(2)}, u32[]{:S(2)}) collective-permute-start(bf16[224,1152]{1,0:T(8,128)(2,1)} %pad_maximum_fusion), channel_id=1, source_target_pairs={{4,0},{5,1},{6,2},{7,3},{8,4},{9,5},{10,6},{11,7},{12,8},{13,9},{1... | collective-permute-start | bytes 1548296 | tf_op jit(solution)/shard_map/ppermute | solution.py:346
  16.0 19.9 %collective-permute-start = (bf16[64,1152]{1,0:T(8,128)(2,1)S(1)}, bf16[64,1152]{1,0:T(8,128)(2,1)S(1)}, u32[]{:S(2)}, u32[]{:S(2)}) collective-permute-start(bf16[64,1152]{1,0:T(8,128)(2,1)S(1)} %get-tuple-element.30), channel_id=1, source_target_pairs={{0,256},{16,272},{32,288},{48,304},{64,320},{80,336},{96,352},{112... | collective-permute-start | bytes 442376 | tf_op jit(solution)/shard_map/ppermute | solution.py:14
  27.8 25.3 %collective-permute-start.3 = (bf16[112,1152]{1,0:T(8,128)(2,1)}, bf16[112,1152]{1,0:T(8,128)(2,1)}, u32[]{:S(2)}, u32[]{:S(2)}) collective-permute-start(bf16[112,1152]{1,0:T(8,128)(2,1)} %slice_select_fusion), channel_id=1, source_target_pairs={{0,8},{1,9},{2,10},{3,11},{4,12},{5,13},{6,14},{7,15},{8,0},{9,1},... | collective-permute-start | bytes 774152 | tf_op jit(solution)/shard_map/ppermute | solution.py:349
  45.9 19.2 %collective-permute-start.2 = (bf16[224,1152]{1,0:T(8,128)(2,1)}, bf16[224,1152]{1,0:T(8,128)(2,1)}, u32[]{:S(2)}, u32[]{:S(2)}) collective-permute-start(bf16[224,1152]{1,0:T(8,128)(2,1)} %collective-permute-done.1.mine_ref), channel_id=1, source_target_pairs={{0,16},{16,0},{32,48},{48,32},{64,80},{80,64},{96,112},{112,96},{1... | collective-permute-start | bytes 1548296 | tf_op jit(solution)/shard_map/ppermute | solution.py:14
  48.8 16.3 %all-to-all-start.1 = ((bf16[4,64,1152]{2,1,0:T(8,128)(2,1)}), bf16[4,64,1152]{2,1,0:T(8,128)(2,1)S(1)}, u32[]{:S(2)}, u32[]{:S(2)}) async-start(bf16[4,64,1152]{2,1,0:T(8,128)(2,1)} %shard_map.65), calls=%async_computation.1 | async-start | bytes 1179648 | tf_op jit(solution)/shard_map/all_to_all | solution.py:329
  53.1 12.0 %collective-permute-start.4 = (bf16[112,1152]{1,0:T(8,128)(2,1)}, bf16[112,1152]{1,0:T(8,128)(2,1)}, u32[]{:S(2)}, u32[]{:S(2)}) collective-permute-start(bf16[112,1152]{1,0:T(8,128)(2,1)} %collective-permute-done.3.mine_half_ref), channel_id=1, source_target_pairs={{0,16},{16,0},{32,48},{48,32},{64,80},{80,64},{96,112},{112,96},{1... | collective-permute-start | bytes 774152 | tf_op jit(solution)/shard_map/ppermute | solution.py:14
  56.6 0.7 copy-start.1
  57.3 19.2 %collective-permute-start.5 = (bf16[144,1024]{1,0:T(8,128)(2,1)}, bf16[144,1024]{1,0:T(8,128)(2,1)S(1)}, u32[]{:S(2)}, u32[]{:S(2)}) collective-permute-start(bf16[144,1024]{1,0:T(8,128)(2,1)} %get-tuple-element.39.own_ref), channel_id=1, source_target_pairs={{0,16},{16,0},{32,48},{48,32},{64,80},{80,64},{96,112},{112,96},{1... | collective-permute-start | bytes 884744 | tf_op jit(solution)/shard_map/ppermute | solution.py:14
  59.8 22.2 %collective-permute-start.6 = (bf16[144,1024]{1,0:T(8,128)(2,1)}, bf16[144,1024]{1,0:T(8,128)(2,1)S(1)}, u32[]{:S(2)}, u32[]{:S(2)}) collective-permute-start(bf16[144,1024]{1,0:T(8,128)(2,1)} %get-tuple-element.39.own_ref), channel_id=1, source_target_pairs={{0,64},{16,80},{32,96},{48,112},{64,0},{80,16},{96,32},{112,48},{1... | collective-permute-start | bytes 884744 | tf_op jit(solution)/shard_map/ppermute | solution.py:14
  65.1 11.5 %copy-start.2 = (bf16[72,1024]{1,0:T(8,128)(2,1)S(1)}, bf16[72,1024]{1,0:T(8,128)(2,1)}, u32[]{:S(2)}) copy-start(bf16[72,1024]{1,0:T(8,128)(2,1)} %copy-done.1) | copy-start | bytes 442372
  65.1 11.5 %copy-start.3 = (s32[3,1]{0,1:T(1,128)S(1)}, s32[3,1]{0,1:T(1,128)}, u32[]{:S(2)}) copy-start(s32[3,1]{0,1:T(1,128)} %param.11) | copy-start | bytes 40
  67.9 14.1 %all-to-all-start.2 = ((bf16[4,144,256]{2,1,0:T(8,128)(2,1)}), bf16[4,144,256]{2,1,0:T(8,128)(2,1)S(1)}, u32[]{:S(2)}, u32[]{:S(2)}) async-start(bf16[4,144,256]{2,1,0:T(8,128)(2,1)} %shard_map.67), calls=%async_computation.2 | async-start | bytes 589824 | tf_op jit(solution)/shard_map/all_to_all | solution.py:329
